TPU v7x, 32 devices: a whole 2x2x4 slice. The times are simulated.
32 devices in a mesh: seq: 8 (over y, x, core), head: 4 (over z).
Axes of the slice: x: 2, y: 2, z: 4, core: 2. Of those that a mesh axis runs over, the one named last changes fastest.
Arguments:
- grad_out: bfloat16 [2048, 8192], P('seq', 'head'), may hold values from -6 to 6
- out_weight: bfloat16 [16384, 8192], P('head', 'seq'), may hold values from -0.046875 to 0.046875
- ssm_input: bfloat16 [2048, 16384], P('seq', 'head'), may hold values from -6 to 6
- step_size: float32 [2048, 128], P('seq', 'head'), may hold values from 0.02 to 0.2
- log_decay: float32 [2048, 128], P('seq', 'head'), may hold values from -1 to 0, as said below
- b_in: bfloat16 [2048, 256], P('seq'), may hold values from -1.5 to 1.5
- c_in: bfloat16 [2048, 256], P('seq'), may hold values from -1.5 to 1.5
- skip: float32 [128], P('head'), may hold values from 0.5 to 1.5
Outputs:
- grad_input: bfloat16 [2048, 16384], P('seq', 'head')
- grad_step: float32 [2048, 128], P('seq', 'head')
- grad_decay: float32 [2048, 128], P('seq', 'head')
- grad_b: float32 [2048, 256], P('seq')
- grad_c: float32 [2048, 256], P('seq')
Inputs may be any that keep to these rules, and one draw needn't show every extreme that they name: `log_decay`: every entry is negative.
All inputs are finite; a program needn't handle non-finite values.
Results may differ from a plain program's by a relative error of at most 0.0049.
Values may be sent and summed in bfloat16 or wider, within the bound.
No kernel may reach another device: no remote copies, remote signals or barrier semaphores. Data moves between devices by JAX's collectives and lax.ppermute only.
A program may use at most 128 MiB of HBM per device.

v0:
```python
import jax
import jax.numpy as jnp
from jax import lax
from jax.sharding import PartitionSpec as P

HIGH = lax.Precision.HIGHEST


def entering(part, axis, combine, identity, reverse):
    count = lax.axis_size(axis)
    place = lax.axis_index(axis)
    ahead = count - 1 - place if reverse else place
    gathered = jax.tree.map(lambda a: lax.all_gather(a, axis), part)
    state = jax.tree.map(lambda a, e: jnp.zeros_like(a) + jnp.asarray(e, a.dtype), part, identity)

    def one(hop, state):
        source = count - 1 - hop if reverse else hop
        return combine(
            state, jax.tree.map(lambda a: lax.dynamic_index_in_dim(a, source, 0, False), gathered)
        )

    return lax.fori_loop(0, ahead, one, state)


def inner_terms(inputs, strides, running, b_rows, c_rows, skips):
    span = inputs.shape[0]
    row_pos = lax.broadcasted_iota(jnp.int32, (span, span), 0)
    col_pos = lax.broadcasted_iota(jnp.int32, (span, span), 1)
    causal = row_pos >= col_pos
    running_t = running.T
    gaps = running_t[:, :, None] - running_t[:, None, :]
    weights = jnp.exp(jnp.where(causal[None], gaps, -jnp.inf)) * strides.T[:, None, :]
    intersection = jnp.dot(c_rows, b_rows.T, precision=HIGH)
    mixed_sum = jnp.einsum("hts,shp->thp", weights * intersection[None], inputs, precision=HIGH)
    return mixed_sum + skips[None, :, None] * inputs


def carried(c_rows, running, carried_state):
    readout = jnp.einsum("tn,hpn->thp", c_rows, carried_state, precision=HIGH)
    return readout * jnp.exp(running)[:, :, None]


def closing(inputs, strides, b_rows, running, carried_state):
    block_end = running[-1]
    input_scale = strides * jnp.exp(block_end[None, :] - running)
    fresh = jnp.einsum("thp,tn->hpn", inputs * input_scale[:, :, None], b_rows, precision=HIGH)
    return jnp.exp(block_end)[:, None, None] * carried_state + fresh


def block_forward(inputs, strides, decays, b_rows, c_rows, skips, carried_state):
    running = jnp.cumsum(decays, axis=0)
    outputs = inner_terms(inputs, strides, running, b_rows, c_rows, skips) + carried(
        c_rows, running, carried_state
    )
    return (outputs, closing(inputs, strides, b_rows, running, carried_state))


def compose(first_part, second_part):
    return (
        first_part[0] * second_part[0],
        second_part[0][:, None, None] * first_part[1] + second_part[1],
    )


def local(grad_out, out_weight, ssm_input, step_size, log_decay, b_in, c_in, skip):
    full_grad = lax.all_gather(grad_out, "head", axis=1, tiled=True)
    span = ssm_input.shape[0]
    head_count = step_size.shape[1]
    head_width = ssm_input.shape[1] // head_count
    state_count = b_in.shape[1]
    grad_y = lax.dot_general(
        full_grad,
        lax.all_gather(out_weight, "seq", axis=1, tiled=True),
        (((1,), (1,)), ((), ())),
        preferred_element_type=jnp.float32,
    ).astype(jnp.bfloat16)
    inputs = ssm_input.astype(jnp.float32).reshape(span, head_count, head_width)
    upstream = grad_y.astype(jnp.float32).reshape(span, head_count, head_width)
    b_float = b_in.astype(jnp.float32)
    c_float = c_in.astype(jnp.float32)
    zero_state = jnp.zeros((head_count, head_width, state_count), jnp.float32)
    running = jnp.cumsum(log_decay, axis=0)
    block_decay = jnp.exp(running[-1])
    local_states = closing(inputs, step_size, b_float, running, zero_state)
    local_grads = jnp.einsum(
        "thp,tn->hpn", upstream * jnp.exp(running)[:, :, None], c_float, precision=HIGH
    )
    identity = (jnp.ones((head_count,), jnp.float32), jnp.zeros_like(zero_state))
    incoming = entering((block_decay, local_states), "seq", compose, identity, False)[1]
    outgoing = entering((block_decay, local_grads), "seq", compose, identity, True)[1]

    def forward_full(inputs_v, strides_v, decays_v, b_rows, c_rows):
        return block_forward(inputs_v, strides_v, decays_v, b_rows, c_rows, skip, incoming)

    pull_full = jax.vjp(forward_full, inputs, step_size, log_decay, b_float, c_float)[1]
    gradients = pull_full((upstream, outgoing))
    grad_b, grad_c = lax.psum((gradients[3], gradients[4]), "head")
    grad_input = gradients[0].reshape(span, head_count * head_width).astype(jnp.bfloat16)
    return (grad_input, gradients[1], gradients[2], grad_b, grad_c)


def solution(mesh):
    in_specs = (
        P("seq", "head"),
        P("head", "seq"),
        P("seq", "head"),
        P("seq", "head"),
        P("seq", "head"),
        P("seq", None),
        P("seq", None),
        P("head"),
    )
    out_specs = (
        P("seq", "head"),
        P("seq", "head"),
        P("seq", "head"),
        P("seq", None),
        P("seq", None),
    )
    return jax.shard_map(local, mesh=mesh, in_specs=in_specs, out_specs=out_specs, check_vma=False)
```

profile of v0, /device:TPU:0, one launch (start us, length us, event | category | flops | bytes accessed | tf_op | source)
XLA Modules:
  0.0 927.2 jit_solution(3332845225254604746)
XLA Ops:
  9.6 83.4 %all-gather.8.cloned.1.call-done = bf16[256,8192]{1,0:T(8,128)(2,1)} async-done(((bf16[256,2048]{1,0:T(8,128)(2,1)}), bf16[256,8192]{1,0:T(8,128)(2,1)}) %all-gather.8.cloned.1.call-update) | async-done | bytes 4194320 | tf_op jit(solution)/shard_map/all_gather | solution.py:66
  93.1 303.3 %all-gather.10.cloned.1.call-done = bf16[4096,8192]{1,0:T(8,128)(2,1)} async-done(((bf16[4096,1024]{1,0:T(8,128)(2,1)}), bf16[4096,8192]{1,0:T(8,128)(2,1)}) %all-gather.10.cloned.1.call-update) | async-done | bytes 67108880 | tf_op jit(solution)/shard_map/all_gather | solution.py:73
  396.4 27.4 %convolution_convert_fusion = bf16[256,4096]{1,0:T(8,128)(2,1)S(1)} fusion(bf16[256,8192]{1,0:T(8,128)(2,1)} %all-gather.8.cloned.1.call-done, bf16[4096,8192]{1,0:T(8,128)(2,1)} %all-gather.10.cloned.1.call-done), kind=kOutput, calls=%fused_computation.16 | convolution fusion | flops 17180917760 | bytes 73400320 | tf_op jit(solution)/shard_map/dot_general | solution.py:71
  423.9 2.0 copy.83
  425.9 3.0 copy.60
  428.9 4.2 fusion.7
  433.2 4.1 copy.63
  437.6 8.7 all-gather.2
  446.3 147.8 %all-gather.12.cloned.1.call-done = f32[256,128,256]{2,1,0:T(8,128)} async-done(((f32[32,128,256]{2,1,0:T(8,128)}), f32[256,128,256]{2,1,0:T(8,128)}) %all-gather.12.cloned.1.call-update) | async-done | bytes 33554448 | tf_op jit(solution)/shard_map/all_gather | solution.py:13
  594.1 2.4 broadcast.24.clone
  596.5 45.6 %while.26 = (s32[]{:T(128)}, f32[32,128,256]{2,1,0:T(8,128)}, s32[]{:T(128)}, f32[8,32]{1,0:T(8,128)S(1)}, f32[8,32,128,256]{3,2,1,0:T(8,128)}, /*index=5*/s32[]{:T(128)}, s32[]{:T(128)}, s32[]{:T(128)}, s32[]{:T(128)}) while((s32[]{:T(128)}, f32[32,128,256]{2,1,0:T(8,128)}, s32[]{:T(128)}, f32[8,32]{1,0:T(8,128)S(1)}, ...), condition=%wide.region_3.4_spmd, body=%wide.region_2.3_spmd.sunk | while | flops 2097158 | bytes 12583451 | solution.py:22
  596.5 6.5 bitcast_add_fusion.6
  603.0 6.5 bitcast_add_fusion.6
  609.5 6.5 bitcast_add_fusion.6
  616.0 6.5 bitcast_add_fusion.6
  622.4 6.5 bitcast_add_fusion.6
  628.9 6.5 bitcast_add_fusion.6
  635.4 6.5 bitcast_add_fusion.6
  642.1 7.1 fusion.10
  649.4 4.2 fusion.21
  654.0 7.2 fusion.9
  661.2 9.0 fusion.13
  670.2 4.3 copy.71
  674.6 9.7 %fusion.34 = f32[256,256]{1,0:T(8,128)S(1)} fusion(f32[32,128,256]{2,1,0:T(8,128)} %get-tuple-element.133, bf16[256,32,128]{0,2,1:T(8,128)(2,1)} %bitcast.144, f32[256,32]{0,1:T(8,128)S(1)} %get-tuple-element.186), kind=kOutput, calls=%fused_computation.46 | convolution fusion | flops 3223322624 | bytes 6586368 | tf_op jit(solution)/shard_map/transpose(jvp(thp,tn->hpn))/dot_general | solution.py:46
  685.3 128.4 %all-gather.14.cloned.1.call-done = f32[256,128,256]{2,1,0:T(8,128)} async-done(((f32[32,128,256]{2,1,0:T(8,128)}), f32[256,128,256]{2,1,0:T(8,128)}) %all-gather.14.cloned.1.call-update) | async-done | bytes 33554448 | tf_op jit(solution)/shard_map/all_gather | solution.py:13
  813.7 2.5 broadcast.24
  816.5 4.5 fusion.14
  821.0 2.9 multiply_reduce_fusion.2
  823.9 6.9 fusion.33
  832.7 2.5 reduce-window.16
  836.0 80.8 %all-reduce.4.cloned.1.call-done = (f32[256,256]{1,0:T(8,128)}, f32[256,256]{1,0:T(8,128)}) async-done(((f32[256,256]{1,0:T(8,128)}, f32[256,256]{1,0:T(8,128)}), (f32[256,256]{1,0:T(8,128)}, f32[256,256]{1,0:T(8,128)})) %all-reduce.4.cloned.1.call-update) | async-done | bytes 524304 | tf_op jit(solution)/shard_map/psum | solution.py:97
  916.9 1.7 copy.133
  (62 shorter events, 9.1 us)
Async XLA Ops:
  7.2 634.9 %copy-start = (bf16[256,256]{1,0:T(8,128)(2,1)S(1)}, bf16[256,256]{1,0:T(8,128)(2,1)}, u32[]{:S(2)}) copy-start(bf16[256,256]{1,0:T(8,128)(2,1)} %param.17) | copy-start | bytes 393220
  7.2 85.9 %all-gather.8.cloned.1.call-start = ((), (), s32[]{:S(2)}) async-start(), calls=%async_computation | async-start | bytes 5242880 | tf_op jit(solution)/shard_map/all_gather | solution.py:66
  7.9 0.8 copy-start.8
  7.9 388.5 %all-gather.10.cloned.1.call-start = ((), (), s32[]{:S(2)}) async-start(), calls=%async_computation.1 | async-start | bytes 75497472 | tf_op jit(solution)/shard_map/all_gather | solution.py:73
  8.7 585.4 %all-gather.12.cloned.1.call-start = ((), (), s32[]{:S(2)}) async-start(), calls=%async_computation.2 | async-start | bytes 37748736 | tf_op jit(solution)/shard_map/all_gather | solution.py:13
  423.8 2.0 copy-start.6
  423.9 5.0 copy-start.5
  433.1 380.6 %all-gather.14.cloned.1.call-start = ((), (), s32[]{:S(2)}) async-start(), calls=%async_computation.3 | async-start | bytes 37748736 | tf_op jit(solution)/shard_map/all_gather | solution.py:13
  642.1 7.1 copy-start.7
  642.1 7.3 copy-start.2
  653.7 263.2 %all-reduce.4.cloned.1.call-start = ((), (), s32[]{:S(2)}) async-start(), calls=%async_computation.4 | async-start | bytes 1048576 | tf_op jit(solution)/shard_map/psum | solution.py:97
  654.0 7.2 copy-start.3
  654.0 7.2 copy-start.4
  654.0 7.2 copy-start.9
  816.5 4.5 copy-start.1
Sparse Core Ops, SparseCore 0:
  9.6 83.4 all-gather.7
  95.0 301.3 all-gather.9
  433.2 160.7 all-gather.11
  653.8 159.8 all-gather.13
  832.1 84.7 all-reduce.3
where the time goes:
time: 934 us; the launch traced here: 927 us
  waiting for transfers between devices  745 us (80%)
  matrix products  82.5 us (9%)
  other arithmetic  53.3 us (6%)
  local copies, waits for them, and re-layouts  22.3 us (2%)
  between operations  14.5 us (2%)
    all_gather x1, waiting for transfers between devices, local(): lax.all_gather(out_weight, 'seq', axis=1, tiled=True)  303 us
    all_gather x2, waiting for transfers between devices, entering(): gathered = jax.tree.map(lambda a: lax.all_gather(a, axis), part)  276 us
    all_gather x1, waiting for transfers between devices, local(): full_grad = lax.all_gather(grad_out, 'head', axis=1, tiled=True)  83.4 us
    psum x1, waiting for transfers between devices, local(): grad_b, grad_c = lax.psum((gradients[3], gradients[4]), 'head')  80.8 us
    add x7, other arithmetic, compose(): second_part[0][:, None, None] * first_part[1] + second_part[1]  45.4 us
    dot_general x1, matrix products, local(): lax.dot_general(full_grad, lax.all_gather(out_weight, 'seq', axis=1, tile...  27.4 us
    dot_general x3, matrix products, closing(): jnp.einsum('thp,tn->hpn', inputs * input_scale[:, :, None], b_rows, preci...  21 us
  transfers between devices with their start and end apart: 5, of which 5 were waited for; matrix products, arithmetic and copies ran while one was open for 4% of the time, Pallas kernels for 0%

commit v1 on v0

v1 whole, which is shorter than its diff:
```python
import jax
import jax.numpy as jnp
from jax import lax
from jax.experimental import pallas as pl
from jax.experimental.pallas import tpu as pltpu
from jax.sharding import PartitionSpec as P

BF16 = jnp.bfloat16
F32 = jnp.float32
HIGH = lax.Precision.HIGHEST
CHUNKS = 2
NN = (((1,), (0,)), ((), ()))
NT = (((1,), (1,)), ((), ()))
TN = (((0,), (0,)), ((), ()))


def mm(a, b, dims):
    return lax.dot_general(a, b, dims, preferred_element_type=F32)


def halves(a):
    high = a.astype(BF16)
    return high, (a - high.astype(F32)).astype(BF16)


def mm_left(a, b, dims):
    high, low = halves(a)
    return mm(high, b, dims) + mm(low, b, dims)


def mm_right(a, b, dims):
    high, low = halves(b)
    return mm(a, high, dims) + mm(a, low, dims)


def pick(table, head):
    lanes = lax.broadcasted_iota(jnp.int32, table.shape, 1)
    return jnp.sum(jnp.where(lanes == head, table, 0.0), axis=1, keepdims=True)


def place(ref, column, head):
    lanes = lax.broadcasted_iota(jnp.int32, ref.shape, 1)
    ref[...] = jnp.where(lanes == head, column, ref[...])


def states_kernel(v_ref, scale_ref, rows_ref, out_ref):
    head = pl.program_id(0)
    scaled = v_ref[...].astype(F32) * pick(scale_ref[...], head)
    out_ref[0] = mm_left(scaled, rows_ref[...], TN)


def span_states(values, scale, rows):
    span, heads = scale.shape
    width = values.shape[1] // heads
    states = rows.shape[1]
    return pl.pallas_call(
        states_kernel,
        grid=(heads,),
        in_specs=[
            pl.BlockSpec((span, width), lambda h: (0, h)),
            pl.BlockSpec((span, heads), lambda h: (0, 0)),
            pl.BlockSpec((span, states), lambda h: (0, 0)),
        ],
        out_specs=pl.BlockSpec((1, width, states), lambda h: (h, 0, 0)),
        out_shape=jax.ShapeDtypeStruct((heads, width, states), F32),
        compiler_params=pltpu.CompilerParams(vmem_limit_bytes=32 << 20),
        cost_estimate=pl.CostEstimate(
            flops=4 * span * heads * width * states,
            bytes_accessed=heads * width * (2 * span + 4 * states),
            transcendentals=0,
        ),
    )(values, scale, rows)


def inner_kernel(
    x_ref, y_ref, b_ref, c_ref, run_ref, run_t_ref, step_ref, skip_ref, state_ref,
    partial_ref, grad_b_ref, grad_c_ref, col_ref, carry_ref, row_ref,
    cross, mix, grad_c_acc,
):
    head = pl.program_id(0)
    span = x_ref.shape[0]

    @pl.when(head == 0)
    def _():
        cross[...] = mm(b_ref[...], c_ref[...], NT)
        mix[...] = jnp.zeros_like(mix)
        grad_c_acc[...] = jnp.zeros_like(grad_c_acc)
        col_ref[...] = jnp.zeros_like(col_ref)
        carry_ref[...] = jnp.zeros_like(carry_ref)

    x = x_ref[...]
    y = y_ref[...]
    run_col = pick(run_ref[...], head)
    step_col = pick(step_ref[...], head)
    run_row = run_t_ref[pl.ds(head, 1), :]
    source = lax.broadcasted_iota(jnp.int32, (span, span), 0)
    target = lax.broadcasted_iota(jnp.int32, (span, span), 1)
    decay = jnp.exp(jnp.where(source <= target, run_row - run_col, -jnp.inf))
    weights = decay * cross[...]
    pairs = mm(x, y, NT)
    mix[...] += decay * pairs * step_col
    terms = weights * pairs
    place(col_ref, jnp.sum(terms, axis=1, keepdims=True), head)
    row_ref[pl.ds(head, 1), :] = jnp.sum(terms * step_col, axis=0, keepdims=True)
    inner = mm_left(weights, y, NN)
    partial_ref[...] = step_col * inner + skip_ref[pl.ds(head, 1), :] * y.astype(F32)
    readout = mm_right(y, state_ref[0], NN) * jnp.exp(run_col)
    grad_c_acc[...] += readout
    place(
        carry_ref,
        jnp.sum(readout * c_ref[...].astype(F32), axis=1, keepdims=True),
        head,
    )

    @pl.when(head == pl.num_programs(0) - 1)
    def _():
        high, low = halves(mix[...])
        grad_b_ref[...] = mm(high, c_ref[...], NN) + mm(low, c_ref[...], NN)
        grad_c_ref[...] = (
            grad_c_acc[...] + mm(high, b_ref[...], TN) + mm(low, b_ref[...], TN)
        )


def inner_part(x, y, b, c, running, running_t, steps, skip_rows, incoming):
    span, heads = steps.shape
    width = x.shape[1] // heads
    states = b.shape[1]
    whole = lambda *shape: pl.BlockSpec(shape, lambda h: (0,) * len(shape))
    block = pl.BlockSpec((span, width), lambda h: (0, h))
    return pl.pallas_call(
        inner_kernel,
        grid=(heads,),
        in_specs=[
            block,
            block,
            whole(span, states),
            whole(span, states),
            whole(span, heads),
            whole(heads, span),
            whole(span, heads),
            whole(heads, width),
            pl.BlockSpec((1, width, states), lambda h: (h, 0, 0)),
        ],
        out_specs=[
            block,
            whole(span, states),
            whole(span, states),
            whole(span, heads),
            whole(span, heads),
            whole(heads, span),
        ],
        out_shape=[
            jax.ShapeDtypeStruct((span, heads * width), F32),
            jax.ShapeDtypeStruct((span, states), F32),
            jax.ShapeDtypeStruct((span, states), F32),
            jax.ShapeDtypeStruct((span, heads), F32),
            jax.ShapeDtypeStruct((span, heads), F32),
            jax.ShapeDtypeStruct((heads, span), F32),
        ],
        scratch_shapes=[
            pltpu.VMEM((span, span), F32),
            pltpu.VMEM((span, span), F32),
            pltpu.VMEM((span, states), F32),
        ],
        compiler_params=pltpu.CompilerParams(vmem_limit_bytes=32 << 20),
        cost_estimate=pl.CostEstimate(
            flops=10 * span * heads * width * states,
            bytes_accessed=8 * span * heads * width + 4 * heads * width * states,
            transcendentals=heads * span * span,
        ),
    )(x, y, b, c, running, running_t, steps, skip_rows, incoming)


def outer_kernel(
    x_ref, part_ref, b_ref, state_ref, grad_state_ref, tail_ref, step_ref, run_ref,
    col_ref, carry_ref, row_ref, grad_b_in_ref,
    grad_x_ref, grad_b_ref, grad_step_ref, grad_decay_ref,
    overlap, late,
):
    head = pl.program_id(0)

    @pl.when(head == 0)
    def _():
        grad_b_ref[...] = grad_b_in_ref[...]
        late[...] = jnp.zeros_like(late)
        overlap[...] = jnp.zeros_like(overlap)

    tail_col = pick(tail_ref[...], head)
    step_col = pick(step_ref[...], head)
    grad_state = grad_state_ref[0]
    b = b_ref[...]
    spread = mm_right(x_ref[...], grad_state, NN) * tail_col
    grad_b_ref[...] += spread * step_col
    place(late, jnp.sum(spread * b.astype(F32), axis=1, keepdims=True), head)
    outer = mm_right(b, grad_state, NT)
    grad_x_ref[...] = (part_ref[...] + (step_col * tail_col) * outer).astype(BF16)
    shared = jnp.sum(grad_state * state_ref[0], axis=0, keepdims=True)
    place(overlap, jnp.sum(shared, axis=1, keepdims=True), head)

    @pl.when(head == pl.num_programs(0) - 1)
    def _():
        span = step_ref.shape[0]
        steps = step_ref[...]
        grad_step = col_ref[...] + late[...]
        grad_step_ref[...] = grad_step
        change = carry_ref[...] + row_ref[...].T - steps * grad_step
        end = jnp.exp(run_ref[span - 1 : span, :]) * overlap[...]
        end += jnp.sum(steps * late[...], axis=0, keepdims=True)
        from_here = lax.broadcasted_iota(jnp.int32, (span, span), 0) <= (
            lax.broadcasted_iota(jnp.int32, (span, span), 1)
        )
        grad_decay_ref[...] = end + lax.dot_general(
            from_here.astype(F32), change, NN, precision=HIGH, preferred_element_type=F32
        )


def outer_part(x, part, b, state, grad_state, tail, steps, running, cols, carries, rows, grad_b):
    span, heads = steps.shape
    width = x.shape[1] // heads
    states = b.shape[1]
    whole = lambda *shape: pl.BlockSpec(shape, lambda h: (0,) * len(shape))
    block = pl.BlockSpec((span, width), lambda h: (0, h))
    per_head = pl.BlockSpec((1, width, states), lambda h: (h, 0, 0))
    table = whole(span, heads)
    return pl.pallas_call(
        outer_kernel,
        grid=(heads,),
        in_specs=[
            block, block, whole(span, states), per_head, per_head, table, table, table,
            table, table, whole(heads, span), whole(span, states),
        ],
        out_specs=[block, whole(span, states), table, table],
        out_shape=[
            jax.ShapeDtypeStruct((span, heads * width), BF16),
            jax.ShapeDtypeStruct((span, states), F32),
            jax.ShapeDtypeStruct((span, heads), F32),
            jax.ShapeDtypeStruct((span, heads), F32),
        ],
        scratch_shapes=[pltpu.VMEM((1, heads), F32), pltpu.VMEM((span, heads), F32)],
        compiler_params=pltpu.CompilerParams(vmem_limit_bytes=32 << 20),
        cost_estimate=pl.CostEstimate(
            flops=4 * span * heads * width * states,
            bytes_accessed=8 * span * heads * width + 8 * heads * width * states,
            transcendentals=0,
        ),
    )(x, part, b, state, grad_state, tail, steps, running, cols, carries, rows, grad_b)


def across(value, hop, chips):
    pairs = [(2 * i + core, 2 * (i ^ hop) + core) for i in range(chips) for core in range(2)]
    return lax.ppermute(value, "seq", pairs)


def other_core(value, chips):
    return lax.ppermute(value, "seq", [(i, i ^ 1) for i in range(2 * chips)])


def sum_over_heads(value):
    count = lax.axis_size("head")
    here = lax.axis_index("head")
    shares = value.reshape((count, value.shape[0] // count) + value.shape[1:])
    shift = lambda hop: [(i, (i + hop) % count) for i in range(count)]
    share = lambda hop: lax.dynamic_index_in_dim(shares, (here + hop) % count, 0, False)
    total = share(0)
    for hop in range(1, count):
        total = total + lax.ppermute(share(hop), "head", shift(hop))
    parts = [total] + [lax.ppermute(total, "head", shift(hop)) for hop in range(1, count)]
    stacked = jnp.stack(parts)
    ordered = [
        lax.dynamic_index_in_dim(stacked, (here - i) % count, 0, False) for i in range(count)
    ]
    return jnp.concatenate(ordered, axis=0)


def project(grad_out, out_weight, chips, chip, core):
    span = grad_out.shape[0]
    width = out_weight.shape[1]
    half = out_weight.shape[0] // 2
    weights = jnp.concatenate([out_weight, other_core(out_weight, chips)], axis=1)
    lanes = [weights[:half], weights[half:]]
    bits = [1 << i for i in range(chips.bit_length() - 1)]
    orders = [bits, bits[::-1]]
    rows = span // CHUNKS
    done = []
    for chunk in range(CHUNKS):
        full = lax.all_gather(
            grad_out[chunk * rows : (chunk + 1) * rows], "head", axis=1, tiled=True
        )
        blocks = []
        for hop in range(chips):
            first = 2 * (chip ^ hop)
            block = jnp.concatenate(
                [
                    lax.dynamic_slice_in_dim(full, (first + core) * width, width, 1),
                    lax.dynamic_slice_in_dim(full, (first + 1 - core) * width, width, 1),
                ],
                axis=1,
            )
            blocks.append(across(block, hop, chips) if hop else block)
        pieces = []
        for lane, order in zip(lanes, orders):
            hops = [0]
            for bit in order[::-1]:
                hops = hops + [hop | bit for hop in hops]
            middle = chips // 2

            def partial(which):
                left = jnp.concatenate([blocks[hop] for hop in which], axis=0)
                return mm(left, lane, NT)

            send = partial(hops[middle:]).astype(BF16)
            keep = partial(hops[:middle])
            for bit in order:
                keep = keep + across(send, bit, chips).astype(F32)
                size = keep.shape[0] // 2
                if size >= rows:
                    send = keep[size:].astype(BF16)
                    keep = keep[:size]
            pieces.append(keep.astype(BF16))
        done.append(jnp.concatenate(pieces, axis=1))
    return jnp.concatenate(done, axis=0)


def exchange(states, ends, chips, chip, core, reverse):
    half = states.shape[0] // 2
    mine = lax.dynamic_slice_in_dim(states, core * half, half, 0)
    theirs = other_core(
        lax.dynamic_slice_in_dim(states, (1 - core) * half, half, 0), chips
    )
    ends = lax.dynamic_slice_in_dim(ends, core * half, half, 1)
    by_chip = ends.reshape(chips, 2, half)
    own_ends = lax.dynamic_index_in_dim(by_chip, chip, 0, False)
    scale = lambda logs, value: jnp.exp(logs)[:, None, None] * value
    near_first = (core == 0) != reverse
    first = jnp.where(near_first, mine, theirs)
    second = jnp.where(near_first, theirs, mine)
    first_end, second_end = (own_ends[1], own_ends[0]) if reverse else (own_ends[0], own_ends[1])
    both = (scale(second_end, first) + second).astype(BF16)
    chip_ends = by_chip[:, 0] + by_chip[:, 1]
    index = jnp.arange(chips)[:, None]
    total = jnp.zeros_like(first)
    for hop in range(1, chips):
        source = chip ^ hop
        before = source > chip if reverse else source < chip
        low = jnp.minimum(chip, source)
        high = jnp.maximum(chip, source)
        between = jnp.sum(jnp.where((index > low) & (index < high), chip_ends, 0.0), axis=0)
        pairs = [
            (2 * (i ^ hop) + c, 2 * i + c)
            for i in range(chips)
            for c in range(2)
            if ((i ^ hop) > i) == reverse
        ]
        arrived = lax.ppermute(both, "seq", pairs).astype(F32)
        total = total + scale(jnp.where(before, between, -jnp.inf), arrived)
    after = scale(first_end, total) + first
    for_mine = jnp.where(near_first, total, after)
    for_theirs = jnp.where(near_first, after, total)
    arrived = other_core(for_theirs, chips)
    return jnp.where(
        core == 0,
        jnp.concatenate([for_mine, arrived], axis=0),
        jnp.concatenate([arrived, for_mine], axis=0),
    )


def local(grad_out, out_weight, ssm_input, step_size, log_decay, b_in, c_in, skip):
    place_on_seq = lax.axis_index("seq")
    chips = lax.axis_size("seq") // 2
    chip, core = place_on_seq // 2, place_on_seq % 2
    span, heads = step_size.shape
    width = ssm_input.shape[1] // heads
    upto = jnp.tril(jnp.ones((span, span), F32))
    running = jnp.dot(upto, log_decay, precision=HIGH)
    running_t = running.T
    tail = jnp.exp(running[-1:] - running)
    ends = lax.all_gather(running[-1], "seq")
    skip_rows = jnp.broadcast_to(skip[:, None], (heads, width))

    own_states = span_states(ssm_input, step_size * tail, b_in)
    incoming = exchange(own_states, ends, chips, chip, core, False)

    grad_y = project(grad_out, out_weight, chips, chip, core)
    own_grads = span_states(grad_y, jnp.exp(running), c_in)
    outgoing = exchange(own_grads, ends, chips, chip, core, True)
    part, grad_b, grad_c, cols, carries, rows = inner_part(
        ssm_input, grad_y, b_in, c_in, running, running_t, step_size, skip_rows, incoming
    )
    grad_c = sum_over_heads(grad_c)
    grad_input, grad_b, grad_step, grad_decay = outer_part(
        ssm_input, part, b_in, incoming, outgoing, tail, step_size, running,
        cols, carries, rows, grad_b,
    )
    grad_b = sum_over_heads(grad_b)
    return (grad_input, grad_step, grad_decay, grad_b, grad_c)


def solution(mesh):
    in_specs = (
        P("seq", "head"),
        P("head", "seq"),
        P("seq", "head"),
        P("seq", "head"),
        P("seq", "head"),
        P("seq", None),
        P("seq", None),
        P("head"),
    )
    out_specs = (
        P("seq", "head"),
        P("seq", "head"),
        P("seq", "head"),
        P("seq", None),
        P("seq", None),
    )
    return jax.shard_map(local, mesh=mesh, in_specs=in_specs, out_specs=out_specs, check_vma=False)
```

time: 934 us -> 460 us (0.49)
  waiting for transfers between devices: 745 us -> 229 us
  starting transfers between devices: 0.2 us -> 58.8 us
  Pallas kernels: 0 us -> 58.1 us
  matrix products: 82.5 us -> 32.6 us
  other arithmetic: 53.3 us -> 27 us
    all_gather x4 -> x2, waiting for transfers between devices: 663 us -> 86.4 us  [project(): lax.all_gather(grad_out[chunk * rows:(chunk + 1) * rows], 'head', axis=1,...]
    ppermute x0 -> x37, waiting for transfers between devices: none -> 142 us  [the longest x6 86.8 us: exchange(): arrived = lax.ppermute(both, 'seq', pairs).astype(F32)]
    psum x1 -> x0, waiting for transfers between devices: 80.8 us -> none  [local(): grad_b, grad_c = lax.psum((gradients[3], gradients[4]), 'head')]
    ppermute x0 -> x37, starting transfers between devices: none -> 58.7 us  [the longest x14 28.8 us: across(): return lax.ppermute(value, 'seq', pairs)]
    pallas_call x0 -> x4, Pallas kernels: none -> 58.1 us  [the longest x2 22.4 us: span_states(): pl.pallas_call(states_kernel, grid=(heads,), in_specs=[pl.BlockSpec((span...]
    dot_general x12 -> x9, matrix products: 82.5 us -> 32.6 us  [the longest x8 32.3 us: mm(): return lax.dot_general(a, b, dims, preferred_element_type=F32)]
    add x7 -> x3, other arithmetic: 45.4 us -> 0.04 us  [the longest x2 0.03 us: sum_over_heads(): total = total + lax.ppermute(share(hop), 'head', shift(hop))]
    select_n x0 -> x4, other arithmetic: none -> 18.5 us  [the longest x2 11.6 us: exchange(): for_mine = jnp.where(near_first, total, after)]
  transfers between devices with their start and end apart: 5 -> 39, of which waited for: 5 -> 15; matrix products, arithmetic and copies ran while one was open for 4% -> 15% of each run, Pallas kernels for 0% -> 2%
where the time goes in v1:
time: 460 us; the launch traced here: 459 us
  waiting for transfers between devices  229 us (50%)
  starting transfers between devices  58.8 us (13%)
  Pallas kernels  58.1 us (13%)
  matrix products  32.6 us (7%)
  local copies, waits for them, and re-layouts  31.1 us (7%)
  other arithmetic  27 us (6%)
  between operations  14.8 us (3%)
  blocking collectives  8.33 us (2%)
    ppermute x6, waiting for transfers between devices, exchange(): arrived = lax.ppermute(both, 'seq', pairs).astype(F32)  86.8 us
    all_gather x2, waiting for transfers between devices, project(): lax.all_gather(grad_out[chunk * rows:(chunk + 1) * rows], 'head', axis=1,...  86.4 us
    ppermute x14, waiting for transfers between devices, across(): return lax.ppermute(value, 'seq', pairs)  45 us
    dot_general x8, matrix products, mm(): return lax.dot_general(a, b, dims, preferred_element_type=F32)  32.3 us
    ppermute x14, starting transfers between devices, across(): return lax.ppermute(value, 'seq', pairs)  28.8 us
    pallas_call x2, Pallas kernels, span_states(): pl.pallas_call(states_kernel, grid=(heads,), in_specs=[pl.BlockSpec((span...  22.4 us
    pallas_call x1, Pallas kernels, inner_part(): pl.pallas_call(inner_kernel, grid=(heads,), in_specs=[block, block, whole...  18.1 us
    pallas_call x1, Pallas kernels, outer_part(): pl.pallas_call(outer_kernel, grid=(heads,), in_specs=[block, block, whole...  17.6 us
  transfers between devices with their start and end apart: 39, of which 15 were waited for; matrix products, arithmetic and copies ran while one was open for 15% of the time, Pallas kernels for 2%

profile of v1, /device:TPU:0, one launch (start us, length us, event | category | flops | bytes accessed | tf_op | source)
XLA Modules:
  0.0 459.4 jit_solution(17995943328796025921)
XLA Ops:
  11.4 7.6 %constant_dynamic-update-slice_fusion.1 = bf16[4096,2048]{1,0:T(8,128)(2,1)} fusion(bf16[4096,1024]{1,0:T(8,128)(2,1)} %param.9), kind=kLoop, calls=%fused_computation.127 | loop fusion | bytes 16777216
  19.0 39.5 %all-gather.6.cloned.1.call-done = bf16[128,8192]{1,0:T(8,128)(2,1)} async-done(((bf16[128,2048]{1,0:T(8,128)(2,1)}), bf16[128,8192]{1,0:T(8,128)(2,1)}) %all-gather.6.cloned.1.call-update) | async-done | bytes 2097168 | tf_op jit(solution)/shard_map/all_gather | solution.py:286
  58.5 46.8 %all-gather.4.cloned.1.call-done = bf16[128,8192]{1,0:T(8,128)(2,1)} async-done(((bf16[128,2048]{1,0:T(8,128)(2,1)}), bf16[128,8192]{1,0:T(8,128)(2,1)}) %all-gather.4.cloned.1.call-update) | async-done | bytes 2097168 | tf_op jit(solution)/shard_map/all_gather | solution.py:286
  105.4 2.9 constant_dynamic-slice_fusion.11
  115.3 7.6 %constant_dynamic-update-slice_fusion = bf16[4096,2048]{1,0:T(8,128)(2,1)} fusion(bf16[4096,2048]{1,0:T(8,128)(2,1)} %constant_dynamic-update-slice_fusion.1, bf16[4096,1024]{1,0:T(8,128)(2,1)} %collective-permute-done.1), kind=kLoop, calls=%fused_computation.126 | loop fusion | bytes 16777216 | tf_op jit(solution)/shard_map/concatenate | solution.py:279
  125.6 9.8 %collective-permute-done.8 = bf16[128,2048]{1,0:T(8,128)(2,1)S(1)} collective-permute-done((bf16[128,2048]{1,0:T(8,128)(2,1)S(1)}, bf16[128,2048]{1,0:T(8,128)(2,1)S(1)}, u32[]{:S(2)}, u32[]{:S(2)}) %collective-permute-start.8) | collective-permute-done | bytes 524320 | tf_op jit(solution)/shard_map/ppermute | solution.py:251
  135.4 5.7 %fusion.37 = bf16[256,2048]{1,0:T(8,128)(2,1)S(1)} fusion(bf16[4096,2048]{1,0:T(8,128)(2,1)} %constant_dynamic-update-slice_fusion, bf16[128,2048]{1,0:T(8,128)(2,1)S(1)} %collective-permute-done.10, bf16[128,2048]{1,0:T(8,128)(2,1)S(1)} %collective-permute-done.8), kind=kOutput, calls=%fused_computation.25 | convolution fusion | flops 2150105088 | bytes 10485760 | tf_op jit(solution)/shard_map/dot_general | solution.py:18
  143.5 3.3 fusion.31
  146.9 10.4 %collective-permute-start.11 = (bf16[256,2048]{1,0:T(8,128)(2,1)}, bf16[256,2048]{1,0:T(8,128)(2,1)S(1)}, u32[]{:S(2)}, u32[]{:S(2)}) collective-permute-start(bf16[256,2048]{1,0:T(8,128)(2,1)} %fusion.31), channel_id=1, source_target_pairs={{0,8},{4,12},{8,0},{12,4},{16,24},{20,28},{24,16},{28,20},{1,9},{5... | collective-permute-start | bytes 3145736 | tf_op jit(solution)/shard_map/ppermute | solution.py:251
  157.3 4.6 %fusion.34 = bf16[256,2048]{1,0:T(8,128)(2,1)} fusion(bf16[4096,2048]{1,0:T(8,128)(2,1)S(1)} %copy-done.11, bf16[128,2048]{1,0:T(8,128)(2,1)} %collective-permute-done.3, bf16[128,2048]{1,0:T(8,128)(2,1)S(1)} %collective-permute-done), kind=kOutput, calls=%fused_computation.24 | convolution fusion | flops 2150105088 | bytes 10485760 | tf_op jit(solution)/shard_map/dot_general | solution.py:18
  162.8 4.8 %fusion.28 = bf16[256,2048]{1,0:T(8,128)(2,1)} fusion(bf16[4096,2048]{1,0:T(8,128)(2,1)S(1)} %copy-done.11, bf16[128,2048]{1,0:T(8,128)(2,1)} %collective-permute-done.3, bf16[128,2048]{1,0:T(8,128)(2,1)S(1)} %collective-permute-done.2), kind=kOutput, calls=%fused_computation.22 | convolution fusion | flops 2150105088 | bytes 10485760 | tf_op jit(solution)/shard_map/dot_general | solution.py:18
  169.1 10.0 %collective-permute-done.13 = bf16[256,2048]{1,0:T(8,128)(2,1)S(1)} collective-permute-done((bf16[256,2048]{1,0:T(8,128)(2,1)S(1)}, bf16[256,2048]{1,0:T(8,128)(2,1)S(1)}, u32[]{:S(2)}, u32[]{:S(2)}) %collective-permute-start.13) | collective-permute-done | bytes 1048608 | tf_op jit(solution)/shard_map/ppermute | solution.py:251
  187.2 14.5 %collective-permute-done.6 = bf16[256,2048]{1,0:T(8,128)(2,1)} collective-permute-done((bf16[256,2048]{1,0:T(8,128)(2,1)}, bf16[256,2048]{1,0:T(8,128)(2,1)}, u32[]{:S(2)}, u32[]{:S(2)}) %collective-permute-start.6) | collective-permute-done | bytes 1048608 | tf_op jit(solution)/shard_map/ppermute | solution.py:251
  201.7 3.8 fusion.22
  207.1 5.3 %fusion.16 = f32[256,2048]{1,0:T(8,128)} fusion(bf16[4096,2048]{1,0:T(8,128)(2,1)S(1)} %copy-done.11, bf16[256,2048]{1,0:T(8,128)(2,1)} %collective-permute-done.4, bf16[128,2048]{1,0:T(8,128)(2,1)} %copy-done.19, bf16[128,1024]{1,0:T(8,128)(2,1)} %copy-done.15, bf16[128,1024]{1,0:T(8,128)(2,1)} %copy-done.16), kind=kOutput, calls=%fused_computation.18 | convolution fusion | flops 2151677952 | bytes 12582912 | tf_op jit(solution)/shard_map/dot_general | solution.py:18
  216.7 7.5 %collective-permute-done.7 = bf16[128,2048]{1,0:T(8,128)(2,1)} collective-permute-done((bf16[128,2048]{1,0:T(8,128)(2,1)S(1)}, bf16[128,2048]{1,0:T(8,128)(2,1)}, u32[]{:S(2)}, u32[]{:S(2)}) %collective-permute-start.7) | collective-permute-done | bytes 524320 | tf_op jit(solution)/shard_map/ppermute | solution.py:251
  228.2 11.2 %shard_map.121 = f32[32,128,256]{2,1,0:T(8,128)S(1)} custom-call(bf16[256,4096]{1,0:T(8,128)(2,1)S(1)} %maximum_maximum_fusion.y_ref.v_ref, f32[256,32]{1,0:T(8,128)S(1)} %copy.47.scale_ref, bf16[256,256]{1,0:T(8,128)(2,1)S(1)} %copy-done.9), custom_call_target="tpu_custom_call" | custom-call | flops 1073741824 | bytes 6291456 | tf_op jit(solution)/shard_map/pallas_call | solution.py:56
  242.8 11.2 %shard_map.119 = f32[32,128,256]{2,1,0:T(8,128)S(1)} custom-call(bf16[256,4096]{1,0:T(8,128)(2,1)S(1)} %copy-done.5, f32[256,32]{1,0:T(8,128)S(1)} %get-tuple-element.48.scale_ref, bf16[256,256]{1,0:T(8,128)(2,1)S(1)} %copy-done.8), custom_call_target="tpu_custom_call" | custom-call | flops 1073741824 | bytes 6291456 | tf_op jit(solution)/shard_map/pallas_call | solution.py:56
  257.2 8.3 %all-gather = f32[8,1,32]{2,1,0:T(1,128)S(1)} all-gather(f32[1,1,32]{2,1,0:T(1,128)S(1)} %bitcast.77), channel_id=1, replica_groups=mesh['seq'=8,'head'=4] {'seq'}, dimensions={0}, use_global_device_ids=true | all-gather | bytes 1152 | tf_op jit(solution)/shard_map/all_gather | solution.py:377
  265.6 3.7 add_convert_fusion
  273.5 25.0 %collective-permute-done.23 = bf16[16,128,256]{2,1,0:T(8,128)(2,1)} collective-permute-done((bf16[16,128,256]{2,1,0:T(8,128)(2,1)}, bf16[16,128,256]{2,1,0:T(8,128)(2,1)}, u32[]{:S(2)}, u32[]{:S(2)}) %collective-permute-start.23) | collective-permute-done | bytes 1048608 | tf_op jit(solution)/shard_map/ppermute | solution.py:354
  298.5 21.8 %collective-permute-done.22 = bf16[16,128,256]{2,1,0:T(8,128)(2,1)} collective-permute-done((bf16[16,128,256]{2,1,0:T(8,128)(2,1)}, bf16[16,128,256]{2,1,0:T(8,128)(2,1)}, u32[]{:S(2)}, u32[]{:S(2)}) %collective-permute-start.22) | collective-permute-done | bytes 1048608 | tf_op jit(solution)/shard_map/ppermute | solution.py:354
  320.3 8.2 %fusion.41 = (f32[16,128,256]{2,1,0:T(8,128)}, f32[16,128,256]{2,1,0:T(8,128)}, bf16[16,128,256]{2,1,0:T(8,128)(2,1)S(1)}) fusion(f32[16]{0:T(128)S(1)} %get-tuple-element.86, pred[]{:T(512)S(6)} %ne.63, f32[16,128,256]{2,1,0:T(8,128)} %collective-permute-done.20, f32[32,128,256]{2,1,0:T(8,128)} %copy-done.4, s32[]{:T(128)S(6)} %select_n.278, ...), kind=kLoop, calls=%fused_computation.29 | loop fusion | flops 9437184 | bytes 16777478 | tf_op jit(solution)/shard_map/jit(_where)/select_n | solution.py:357
  332.4 3.5 collective-permute-start.16
  336.0 18.2 %collective-permute-done.18 = bf16[16,128,256]{2,1,0:T(8,128)(2,1)S(1)} collective-permute-done((bf16[16,128,256]{2,1,0:T(8,128)(2,1)S(1)}, bf16[16,128,256]{2,1,0:T(8,128)(2,1)S(1)}, u32[]{:S(2)}, u32[]{:S(2)}) %collective-permute-start.18) | collective-permute-done | bytes 1048608 | tf_op jit(solution)/shard_map/ppermute | solution.py:354
  354.2 21.7 %collective-permute-done.17 = bf16[16,128,256]{2,1,0:T(8,128)(2,1)S(1)} collective-permute-done((bf16[16,128,256]{2,1,0:T(8,128)(2,1)S(1)}, bf16[16,128,256]{2,1,0:T(8,128)(2,1)S(1)}, u32[]{:S(2)}, u32[]{:S(2)}) %collective-permute-start.17) | collective-permute-done | bytes 1048608 | tf_op jit(solution)/shard_map/ppermute | solution.py:354
  375.9 3.3 fusion.43
  380.9 4.2 maximum_select_fusion.1.grad_state_ref
  388.0 18.1 %shard_map.120 = (f32[256,4096]{1,0:T(8,128)S(1)}, f32[256,256]{1,0:T(8,128)S(1)}, f32[256,256]{1,0:T(8,128)S(1)}, f32[256,32]{1,0:T(8,128)S(1)}, f32[256,32]{1,0:T(8,128)S(1)}, /*index=5*/f32[32,256]{1,0:T(8,128)S(1)}) custom-call(bf16[256,4096]{1,0:T(8,128)(2,1)S(1)} %copy-done.5, bf16[256,4096]{1,0:T(8,128)(2,1)S(1)} %copy-done.7, ...), custom_call_target="tpu_custom_call" | custom-call | flops 2684354560 | bytes 12582912 | tf_op jit(solution)/shard_map/pallas_call | solution.py:130
  406.1 17.6 %shard_map.122 = (bf16[256,4096]{1,0:T(8,128)(2,1)}, f32[256,256]{1,0:T(8,128)S(1)}, f32[256,32]{1,0:T(8,128)S(1)}, f32[256,32]{1,0:T(8,128)S(1)}) custom-call(bf16[256,4096]{1,0:T(8,128)(2,1)S(1)} %copy-done.5, f32[256,4096]{1,0:T(8,128)S(1)} %get-tuple-element.15.part_ref, bf16[256,256]{1,0:T(8,128)(2,1)S(1)} %copy-done.8, ...), custom_call_target="tpu_custom_call" | custom-call | flops 1073741824 | bytes 16777216 | tf_op jit(solution)/shard_map/pallas_call | solution.py:225
  432.2 3.1 collective-permute-done.26
  446.2 4.9 %collective-permute-done.35 = f32[64,256]{1,0:T(8,128)S(1)} collective-permute-done((f32[64,256]{1,0:T(8,128)S(1)}, f32[64,256]{1,0:T(8,128)S(1)}, u32[]{:S(2)}, u32[]{:S(2)}) %collective-permute-start.35) | collective-permute-done | bytes 65568 | tf_op jit(solution)/shard_map/ppermute | solution.py:267
  (162 shorter events, 76.2 us)
Async XLA Ops:
  7.2 51.4 %all-gather.6.cloned.1.call-start = ((), (), s32[]{:S(2)}) async-start(), calls=%async_computation.1 | async-start | bytes 2621440 | tf_op jit(solution)/shard_map/all_gather | solution.py:286
  7.2 107.4 %collective-permute-start.1 = (bf16[4096,1024]{1,0:T(8,128)(2,1)}, bf16[4096,1024]{1,0:T(8,128)(2,1)}, u32[]{:S(2)}, u32[]{:S(2)}) collective-permute-start(bf16[4096,1024]{1,0:T(8,128)(2,1)} %param.9), channel_id=1, source_target_pairs={{0,4},{4,0},{8,12},{12,8},{16,20},{20,16},{24,28},{28,24},{1,5},{5... | collective-permute-start | bytes 25165832 | tf_op jit(solution)/shard_map/ppermute | solution.py:255
  10.0 95.3 %all-gather.4.cloned.1.call-start = ((), (), s32[]{:S(2)}) async-start(), calls=%async_computation | async-start | bytes 2621440 | tf_op jit(solution)/shard_map/all_gather | solution.py:286
  108.3 15.8 %collective-permute-start.10 = (bf16[128,2048]{1,0:T(8,128)(2,1)S(1)}, bf16[128,2048]{1,0:T(8,128)(2,1)S(1)}, u32[]{:S(2)}, u32[]{:S(2)}) collective-permute-start(bf16[128,2048]{1,0:T(8,128)(2,1)S(1)} %pad_maximum_fusion.19), channel_id=1, source_target_pairs={{0,24},{4,28},{8,16},{12,20},{16,8},{20,12},{24,0},{28,4},{1,25},{... | collective-permute-start | bytes 1572872 | tf_op jit(solution)/shard_map/ppermute | solution.py:251
  110.8 24.7 %collective-permute-start.8 = (bf16[128,2048]{1,0:T(8,128)(2,1)S(1)}, bf16[128,2048]{1,0:T(8,128)(2,1)S(1)}, u32[]{:S(2)}, u32[]{:S(2)}) collective-permute-start(bf16[128,2048]{1,0:T(8,128)(2,1)S(1)} %pad_maximum_fusion.17), channel_id=1, source_target_pairs={{0,16},{4,20},{8,24},{12,28},{16,0},{20,4},{24,8},{28,12},{1,17},{... | collective-permute-start | bytes 1572872 | tf_op jit(solution)/shard_map/ppermute | solution.py:251
  111.4 31.3 %collective-permute-start.9 = (bf16[128,2048]{1,0:T(8,128)(2,1)S(1)}, bf16[128,2048]{1,0:T(8,128)(2,1)S(1)}, u32[]{:S(2)}, u32[]{:S(2)}) collective-permute-start(bf16[128,2048]{1,0:T(8,128)(2,1)S(1)} %pad_maximum_fusion.18), channel_id=1, source_target_pairs={{0,8},{4,12},{8,0},{12,4},{16,24},{20,28},{24,16},{28,20},{1,9},{5... | collective-permute-start | bytes 1572872 | tf_op jit(solution)/shard_map/ppermute | solution.py:251
  112.1 45.2 %collective-permute-start.3 = (bf16[128,2048]{1,0:T(8,128)(2,1)S(1)}, bf16[128,2048]{1,0:T(8,128)(2,1)}, u32[]{:S(2)}, u32[]{:S(2)}) collective-permute-start(bf16[128,2048]{1,0:T(8,128)(2,1)S(1)} %pad_maximum_fusion.16), channel_id=1, source_target_pairs={{0,24},{4,28},{8,16},{12,20},{16,8},{20,12},{24,0},{28,4},{1,25},{... | collective-permute-start | bytes 1572872 | tf_op jit(solution)/shard_map/ppermute | solution.py:251
  114.6 42.7 %collective-permute-start = (bf16[128,2048]{1,0:T(8,128)(2,1)S(1)}, bf16[128,2048]{1,0:T(8,128)(2,1)S(1)}, u32[]{:S(2)}, u32[]{:S(2)}) collective-permute-start(bf16[128,2048]{1,0:T(8,128)(2,1)S(1)} %pad_maximum_fusion.14), channel_id=1, source_target_pairs={{0,16},{4,20},{8,24},{12,28},{16,0},{20,4},{24,8},{28,12},{1,17},{... | collective-permute-start | bytes 1572872 | tf_op jit(solution)/shard_map/ppermute | solution.py:251
  124.1 38.6 %collective-permute-start.2 = (bf16[128,2048]{1,0:T(8,128)(2,1)S(1)}, bf16[128,2048]{1,0:T(8,128)(2,1)S(1)}, u32[]{:S(2)}, u32[]{:S(2)}) collective-permute-start(bf16[128,2048]{1,0:T(8,128)(2,1)S(1)} %pad_maximum_fusion.15), channel_id=1, source_target_pairs={{0,8},{4,12},{8,0},{12,4},{16,24},{20,28},{24,16},{28,20},{1,9},{5... | collective-permute-start | bytes 1572872 | tf_op jit(solution)/shard_map/ppermute | solution.py:251
  141.2 38.0 %collective-permute-start.13 = (bf16[256,2048]{1,0:T(8,128)(2,1)S(1)}, bf16[256,2048]{1,0:T(8,128)(2,1)S(1)}, u32[]{:S(2)}, u32[]{:S(2)}) collective-permute-start(bf16[256,2048]{1,0:T(8,128)(2,1)S(1)} %fusion.37), channel_id=1, source_target_pairs={{0,16},{4,20},{8,24},{12,28},{16,0},{20,4},{24,8},{28,12},{1,17},{... | collective-permute-start | bytes 3145736 | tf_op jit(solution)/shard_map/ppermute | solution.py:251
  146.9 36.3 %collective-permute-start.11 = (bf16[256,2048]{1,0:T(8,128)(2,1)}, bf16[256,2048]{1,0:T(8,128)(2,1)S(1)}, u32[]{:S(2)}, u32[]{:S(2)}) collective-permute-start(bf16[256,2048]{1,0:T(8,128)(2,1)} %fusion.31), channel_id=1, source_target_pairs={{0,8},{4,12},{8,0},{12,4},{16,24},{20,28},{24,16},{28,20},{1,9},{5... | collective-permute-start | bytes 3145736 | tf_op jit(solution)/shard_map/ppermute | solution.py:251
  161.9 39.8 %collective-permute-start.6 = (bf16[256,2048]{1,0:T(8,128)(2,1)}, bf16[256,2048]{1,0:T(8,128)(2,1)}, u32[]{:S(2)}, u32[]{:S(2)}) collective-permute-start(bf16[256,2048]{1,0:T(8,128)(2,1)} %fusion.34), channel_id=1, source_target_pairs={{0,16},{4,20},{8,24},{12,28},{16,0},{20,4},{24,8},{28,12},{1,17},{... | collective-permute-start | bytes 3145736 | tf_op jit(solution)/shard_map/ppermute | solution.py:251
  167.6 39.5 %collective-permute-start.4 = (bf16[256,2048]{1,0:T(8,128)(2,1)}, bf16[256,2048]{1,0:T(8,128)(2,1)}, u32[]{:S(2)}, u32[]{:S(2)}) collective-permute-start(bf16[256,2048]{1,0:T(8,128)(2,1)} %fusion.28), channel_id=1, source_target_pairs={{0,8},{4,12},{8,0},{12,4},{16,24},{20,28},{24,16},{28,20},{1,9},{5... | collective-permute-start | bytes 3145736 | tf_op jit(solution)/shard_map/ppermute | solution.py:251
  181.6 33.7 %collective-permute-start.14 = (bf16[128,2048]{1,0:T(8,128)(2,1)S(1)}, bf16[128,2048]{1,0:T(8,128)(2,1)S(1)}, u32[]{:S(2)}, u32[]{:S(2)}) collective-permute-start(bf16[128,2048]{1,0:T(8,128)(2,1)S(1)} %slice.145), channel_id=1, source_target_pairs={{0,8},{4,12},{8,0},{12,4},{16,24},{20,28},{24,16},{28,20},{1,9},{5... | collective-permute-start | bytes 1572872 | tf_op jit(solution)/shard_map/ppermute | solution.py:251
  185.6 29.8 %collective-permute-start.12 = (bf16[128,2048]{1,0:T(8,128)(2,1)S(1)}, bf16[128,2048]{1,0:T(8,128)(2,1)}, u32[]{:S(2)}, u32[]{:S(2)}) collective-permute-start(bf16[128,2048]{1,0:T(8,128)(2,1)S(1)} %slice.146), channel_id=1, source_target_pairs={{0,16},{4,20},{8,24},{12,28},{16,0},{20,4},{24,8},{28,12},{1,17},{... | collective-permute-start | bytes 1572872 | tf_op jit(solution)/shard_map/ppermute | solution.py:251
  205.6 18.6 %collective-permute-start.7 = (bf16[128,2048]{1,0:T(8,128)(2,1)S(1)}, bf16[128,2048]{1,0:T(8,128)(2,1)}, u32[]{:S(2)}, u32[]{:S(2)}) collective-permute-start(bf16[128,2048]{1,0:T(8,128)(2,1)S(1)} %slice.147), channel_id=1, source_target_pairs={{0,8},{4,12},{8,0},{12,4},{16,24},{20,28},{24,16},{28,20},{1,9},{5... | collective-permute-start | bytes 1572872 | tf_op jit(solution)/shard_map/ppermute | solution.py:251
  213.7 13.5 %collective-permute-start.5 = (bf16[128,2048]{1,0:T(8,128)(2,1)S(1)}, bf16[128,2048]{1,0:T(8,128)(2,1)S(1)}, u32[]{:S(2)}, u32[]{:S(2)}) collective-permute-start(bf16[128,2048]{1,0:T(8,128)(2,1)S(1)} %slice.148), channel_id=1, source_target_pairs={{0,16},{4,20},{8,24},{12,28},{16,0},{20,4},{24,8},{28,12},{1,17},{... | collective-permute-start | bytes 1572872 | tf_op jit(solution)/shard_map/ppermute | solution.py:251
  242.3 23.3 %collective-permute-start.20 = (f32[16,128,256]{2,1,0:T(8,128)}, f32[16,128,256]{2,1,0:T(8,128)}, u32[]{:S(2)}, u32[]{:S(2)}) collective-permute-start(f32[16,128,256]{2,1,0:T(8,128)} %constant_dynamic-slice_fusion), channel_id=1, source_target_pairs={{0,4},{4,0},{8,12},{12,8},{16,20},{20,16},{24,28},{28,24},{1,5},{5... | collective-permute-start | bytes 6291464 | tf_op jit(solution)/shard_map/ppermute | solution.py:255
  256.7 16.8 %collective-permute-start.15 = (f32[16,128,256]{2,1,0:T(8,128)}, f32[16,128,256]{2,1,0:T(8,128)}, u32[]{:S(2)}, u32[]{:S(2)}) collective-permute-start(f32[16,128,256]{2,1,0:T(8,128)} %constant_dynamic-slice_fusion.1), channel_id=1, source_target_pairs={{0,4},{4,0},{8,12},{12,8},{16,20},{20,16},{24,28},{28,24},{1,5},{5... | collective-permute-start | bytes 6291464 | tf_op jit(solution)/shard_map/ppermute | solution.py:255
  269.4 29.1 %collective-permute-start.23 = (bf16[16,128,256]{2,1,0:T(8,128)(2,1)}, bf16[16,128,256]{2,1,0:T(8,128)(2,1)}, u32[]{:S(2)}, u32[]{:S(2)}) collective-permute-start(bf16[16,128,256]{2,1,0:T(8,128)(2,1)} %add_convert_fusion), channel_id=1, source_target_pairs={{24,0},{28,4},{16,8},{20,12},{25,1},{29,5},{17,9},{21,13},{26,2},{... | collective-permute-start | bytes 3145736 | tf_op jit(solution)/shard_map/ppermute | solution.py:354
  270.7 49.7 %collective-permute-start.22 = (bf16[16,128,256]{2,1,0:T(8,128)(2,1)}, bf16[16,128,256]{2,1,0:T(8,128)(2,1)}, u32[]{:S(2)}, u32[]{:S(2)}) collective-permute-start(bf16[16,128,256]{2,1,0:T(8,128)(2,1)} %add_convert_fusion), channel_id=1, source_target_pairs={{16,0},{20,4},{24,8},{28,12},{17,1},{21,5},{25,9},{29,13},{18,2},{... | collective-permute-start | bytes 3145736 | tf_op jit(solution)/shard_map/ppermute | solution.py:354
  272.0 48.4 %collective-permute-start.21 = (bf16[16,128,256]{2,1,0:T(8,128)(2,1)}, bf16[16,128,256]{2,1,0:T(8,128)(2,1)}, u32[]{:S(2)}, u32[]{:S(2)}) collective-permute-start(bf16[16,128,256]{2,1,0:T(8,128)(2,1)} %add_convert_fusion), channel_id=1, source_target_pairs={{8,0},{12,4},{24,16},{28,20},{9,1},{13,5},{25,17},{29,21},{10,2},{... | collective-permute-start | bytes 3145736 | tf_op jit(solution)/shard_map/ppermute | solution.py:354
  328.6 25.7 %collective-permute-start.18 = (bf16[16,128,256]{2,1,0:T(8,128)(2,1)S(1)}, bf16[16,128,256]{2,1,0:T(8,128)(2,1)S(1)}, u32[]{:S(2)}, u32[]{:S(2)}) collective-permute-start(bf16[16,128,256]{2,1,0:T(8,128)(2,1)S(1)} %get-tuple-element.88), channel_id=1, source_target_pairs={{8,16},{12,20},{0,24},{4,28},{9,17},{13,21},{1,25},{5,29},{10,18},... | collective-permute-start | bytes 3145736 | tf_op jit(solution)/shard_map/ppermute | solution.py:354
  330.6 45.3 %collective-permute-start.17 = (bf16[16,128,256]{2,1,0:T(8,128)(2,1)S(1)}, bf16[16,128,256]{2,1,0:T(8,128)(2,1)S(1)}, u32[]{:S(2)}, u32[]{:S(2)}) collective-permute-start(bf16[16,128,256]{2,1,0:T(8,128)(2,1)S(1)} %get-tuple-element.88), channel_id=1, source_target_pairs={{0,16},{4,20},{8,24},{12,28},{1,17},{5,21},{9,25},{13,29},{2,18},{... | collective-permute-start | bytes 3145736 | tf_op jit(solution)/shard_map/ppermute | solution.py:354
  332.4 43.5 %collective-permute-start.16 = (bf16[16,128,256]{2,1,0:T(8,128)(2,1)S(1)}, bf16[16,128,256]{2,1,0:T(8,128)(2,1)S(1)}, u32[]{:S(2)}, u32[]{:S(2)}) collective-permute-start(bf16[16,128,256]{2,1,0:T(8,128)(2,1)S(1)} %get-tuple-element.88), channel_id=1, source_target_pairs={{0,8},{4,12},{16,24},{20,28},{1,9},{5,13},{17,25},{21,29},{2,10},{... | collective-permute-start | bytes 3145736 | tf_op jit(solution)/shard_map/ppermute | solution.py:354
  335.9 44.9 %collective-permute-start.24 = (f32[16,128,256]{2,1,0:T(8,128)}, f32[16,128,256]{2,1,0:T(8,128)}, u32[]{:S(2)}, u32[]{:S(2)}) collective-permute-start(f32[16,128,256]{2,1,0:T(8,128)} %get-tuple-element.51), channel_id=1, source_target_pairs={{0,4},{4,0},{8,12},{12,8},{16,20},{20,16},{24,28},{28,24},{1,5},{5... | collective-permute-start | bytes 6291464 | tf_op jit(solution)/shard_map/ppermute | solution.py:255
  426.5 8.7 %collective-permute-start.26 = (f32[64,256]{1,0:T(8,128)S(1)}, f32[64,256]{1,0:T(8,128)S(1)}, u32[]{:S(2)}, u32[]{:S(2)}) collective-permute-start(f32[64,256]{1,0:T(8,128)S(1)} %get-tuple-element.85), channel_id=1, source_target_pairs={{0,2},{1,3},{2,0},{3,1},{4,6},{5,7},{6,4},{7,5},{8,10},{9,11},{10,... | collective-permute-start | bytes 196616 | tf_op jit(solution)/shard_map/ppermute | solution.py:266
  426.5 8.7 %collective-permute-start.25 = (f32[64,256]{1,0:T(8,128)S(1)}, f32[64,256]{1,0:T(8,128)S(1)}, u32[]{:S(2)}, u32[]{:S(2)}) collective-permute-start(f32[64,256]{1,0:T(8,128)S(1)} %get-tuple-element.83), channel_id=1, source_target_pairs={{0,1},{1,2},{2,3},{3,0},{4,5},{5,6},{6,7},{7,4},{8,9},{9,10},{10,1... | collective-permute-start | bytes 196616 | tf_op jit(solution)/shard_map/ppermute | solution.py:266
  428.2 10.7 %collective-permute-start.33 = (f32[64,256]{1,0:T(8,128)S(1)}, f32[64,256]{1,0:T(8,128)S(1)}, u32[]{:S(2)}, u32[]{:S(2)}) collective-permute-start(f32[64,256]{1,0:T(8,128)S(1)} %get-tuple-element.77), channel_id=1, source_target_pairs={{0,3},{1,0},{2,1},{3,2},{4,7},{5,4},{6,5},{7,6},{8,11},{9,8},{10,9... | collective-permute-start | bytes 196616 | tf_op jit(solution)/shard_map/ppermute | solution.py:266
  430.4 10.5 %collective-permute-start.32 = (f32[64,256]{1,0:T(8,128)S(1)}, f32[64,256]{1,0:T(8,128)S(1)}, u32[]{:S(2)}, u32[]{:S(2)}) collective-permute-start(f32[64,256]{1,0:T(8,128)S(1)} %get-tuple-element.78), channel_id=1, source_target_pairs={{0,2},{1,3},{2,0},{3,1},{4,6},{5,7},{6,4},{7,5},{8,10},{9,11},{10,... | collective-permute-start | bytes 196616 | tf_op jit(solution)/shard_map/ppermute | solution.py:266
  431.6 9.4 %collective-permute-start.31 = (f32[64,256]{1,0:T(8,128)S(1)}, f32[64,256]{1,0:T(8,128)S(1)}, u32[]{:S(2)}, u32[]{:S(2)}) collective-permute-start(f32[64,256]{1,0:T(8,128)S(1)} %get-tuple-element.76), channel_id=1, source_target_pairs={{0,1},{1,2},{2,3},{3,0},{4,5},{5,6},{6,7},{7,4},{8,9},{9,10},{10,1... | collective-permute-start | bytes 196616 | tf_op jit(solution)/shard_map/ppermute | solution.py:266
  437.7 8.4 %collective-permute-start.29 = (f32[64,256]{1,0:T(8,128)S(1)}, f32[64,256]{1,0:T(8,128)S(1)}, u32[]{:S(2)}, u32[]{:S(2)}) collective-permute-start(f32[64,256]{1,0:T(8,128)S(1)} %fusion.67), channel_id=1, source_target_pairs={{0,2},{1,3},{2,0},{3,1},{4,6},{5,7},{6,4},{7,5},{8,10},{9,11},{10,... | collective-permute-start | bytes 196616 | tf_op jit(solution)/shard_map/ppermute | solution.py:267
  (30 other events, 433.8 us)
Sparse Core Ops, SparseCore 0:
  10.2 48.3 all-gather.5
  60.7 44.6 all-gather.3

commit v2 on v0

v2 whole, which is shorter than its diff:
```python
import jax
import jax.numpy as jnp
from jax import lax
from jax.experimental import pallas as pl
from jax.experimental.pallas import tpu as pltpu
from jax.sharding import PartitionSpec as P

BF16 = jnp.bfloat16
F32 = jnp.float32
HIGH = lax.Precision.HIGHEST
CHUNK_ROWS = 64
GROUP = 8
NN = (((1,), (0,)), ((), ()))
NT = (((1,), (1,)), ((), ()))
TN = (((0,), (0,)), ((), ()))
PARAMS = pltpu.CompilerParams(vmem_limit_bytes=48 << 20)


def mm(a, b, dims):
    return lax.dot_general(a, b, dims, preferred_element_type=F32)


def halves(a):
    high = a.astype(BF16)
    return high, (a - high.astype(F32)).astype(BF16)


def mm_left(a, b, dims):
    high, low = halves(a)
    return mm(high, b, dims) + mm(low, b, dims)


def mm_right(a, b):
    width = b.shape[1]
    both = mm(a, jnp.concatenate(halves(b), axis=1), NN)
    return both[:, :width] + both[:, width:]


def mm_wide(a, b):
    b = b.astype(BF16)
    return mm(jnp.concatenate(halves(a), axis=1), jnp.concatenate([b, b], axis=1), NT)


def whole(*shape):
    return pl.BlockSpec(shape, lambda i, at: (0,) * len(shape))


def cost(flops, size, exps=0):
    return pl.CostEstimate(flops=flops, bytes_accessed=size, transcendentals=exps)


def states_kernel(at_ref, v_ref, scale_ref, rows_ref, out_ref):
    del at_ref
    group = scale_ref.shape[2]
    width = v_ref.shape[1] // group
    for j in range(group):
        scaled = v_ref[:, j * width : (j + 1) * width].astype(F32) * scale_ref[0, :, j : j + 1]
        out_ref[j] = mm_right(rows_ref[...], scaled)


def span_states(values, scale, rows_t, at, count):
    groups, span, group = scale.shape
    width = values.shape[1] // (groups * group)
    states = rows_t.shape[0]
    return pl.pallas_call(
        states_kernel,
        grid_spec=pltpu.PrefetchScalarGridSpec(
            num_scalar_prefetch=1,
            grid=(count,),
            in_specs=[
                pl.BlockSpec((span, group * width), lambda i, at: (0, at[0] + i)),
                pl.BlockSpec((1, span, group), lambda i, at: (at[0] + i, 0, 0)),
                whole(states, span),
            ],
            out_specs=pl.BlockSpec((group, states, width), lambda i, at: (i, 0, 0)),
        ),
        out_shape=jax.ShapeDtypeStruct((count * group, states, width), F32),
        compiler_params=PARAMS,
        cost_estimate=cost(
            4 * span * count * group * width * states,
            count * group * width * (2 * span + 4 * states),
        ),
    )(at, values, scale, rows_t)


def inner_kernel(
    at_ref, x_ref, y_ref, b_ref, c_ref, run_ref, run_t_ref, step_ref, skip_ref, state_ref,
    partial_ref, grad_b_ref, grad_c_ref, col_ref, carry_ref,
    cross, mix, grad_c_acc, rows,
):
    del at_ref
    index = pl.program_id(0)
    group = step_ref.shape[2]
    span = x_ref.shape[0]
    width = x_ref.shape[1] // group

    @pl.when(index == 0)
    def _():
        cross[...] = mm(b_ref[...], c_ref[...], NT)
        mix[...] = jnp.zeros_like(mix)
        grad_c_acc[...] = jnp.zeros_like(grad_c_acc)

    source = lax.broadcasted_iota(jnp.int32, (span, span), 0)
    target = lax.broadcasted_iota(jnp.int32, (span, span), 1)
    causal = source <= target
    for j in range(group):
        columns = slice(j * width, (j + 1) * width)
        x = x_ref[:, columns]
        y = y_ref[:, columns]
        run_col = run_ref[0, :, j : j + 1]
        step_col = step_ref[0, :, j : j + 1]
        run_row = run_t_ref[0, j : j + 1, :]
        decay = jnp.exp(jnp.where(causal, run_row - run_col, -jnp.inf))
        weights = decay * cross[...]
        pairs = mm(x, y, NT)
        mix[...] += decay * pairs * step_col
        terms = weights * pairs
        col_ref[0, :, j : j + 1] = jnp.sum(terms, axis=1, keepdims=True)
        rows[j : j + 1, :] = jnp.sum(terms * step_col, axis=0, keepdims=True)
        inner = mm_left(weights, y, NN)
        y_wide = y.astype(F32)
        partial_ref[:, columns] = step_col * inner + skip_ref[0, j : j + 1, :] * y_wide
        state = state_ref[j]
        scaled = y_wide * jnp.exp(run_col)
        grad_c_acc[...] += mm_wide(scaled, state)
        carry_ref[0, :, j : j + 1] = jnp.sum(
            scaled * mm_right(c_ref[...], state), axis=1, keepdims=True
        )
    carry_ref[0] += rows[...].T

    @pl.when(index == pl.num_programs(0) - 1)
    def _():
        high, low = halves(mix[...])
        grad_b_ref[...] = mm(high, c_ref[...], NN) + mm(low, c_ref[...], NN)
        grad_c_ref[...] = (
            grad_c_acc[...] + mm(high, b_ref[...], TN) + mm(low, b_ref[...], TN)
        )


def inner_part(x, y, b, c, running, running_t, steps, skip_rows, incoming):
    groups, span, group = steps.shape
    heads = groups * group
    width = x.shape[1] // heads
    states = b.shape[1]
    block = pl.BlockSpec((span, group * width), lambda i, at: (0, i))
    table = pl.BlockSpec((1, span, group), lambda i, at: (i, 0, 0))
    return pl.pallas_call(
        inner_kernel,
        grid_spec=pltpu.PrefetchScalarGridSpec(
            num_scalar_prefetch=1,
            grid=(groups,),
            in_specs=[
                block,
                block,
                whole(span, states),
                whole(span, states),
                table,
                pl.BlockSpec((1, group, span), lambda i, at: (i, 0, 0)),
                table,
                pl.BlockSpec((1, group, width), lambda i, at: (i, 0, 0)),
                pl.BlockSpec((group, states, width), lambda i, at: (i, 0, 0)),
            ],
            out_specs=[block, whole(span, states), whole(span, states), table, table],
            scratch_shapes=[
                pltpu.VMEM((span, span), F32),
                pltpu.VMEM((span, span), F32),
                pltpu.VMEM((span, states), F32),
                pltpu.VMEM((group, span), F32),
            ],
        ),
        out_shape=[
            jax.ShapeDtypeStruct((span, heads * width), F32),
            jax.ShapeDtypeStruct((span, states), F32),
            jax.ShapeDtypeStruct((span, states), F32),
            jax.ShapeDtypeStruct((groups, span, group), F32),
            jax.ShapeDtypeStruct((groups, span, group), F32),
        ],
        compiler_params=PARAMS,
        cost_estimate=cost(
            14 * span * heads * width * states,
            8 * span * heads * width + 4 * heads * width * states,
            heads * span * span,
        ),
    )(jnp.zeros((1,), jnp.int32), x, y, b, c, running, running_t, steps, skip_rows, incoming)


def outer_kernel(
    at_ref, x_ref, part_ref, b_ref, state_ref, grad_state_ref, run_ref, step_ref,
    col_ref, carry_ref, grad_b_in_ref, *rest,
):
    del at_ref
    grad_x_ref, grad_b_ref, grad_step_ref, grad_decay_ref, late, overlap = rest[-6:]
    group = step_ref.shape[2]
    span = x_ref.shape[0]
    width = x_ref.shape[1] // group

    @pl.when(pl.program_id(0) == 0)
    def _():
        grad_b_ref[...] = grad_b_in_ref[...]

    running = run_ref[0]
    end = running[span - 1 : span, :]
    tails = jnp.exp(end - running)
    steps = step_ref[0]
    for j in range(group):
        columns = slice(j * width, (j + 1) * width)
        tail_col = tails[:, j : j + 1]
        step_col = steps[:, j : j + 1]
        grad_state = grad_state_ref[j]
        x = x_ref[:, columns].astype(F32)
        outer = mm_right(b_ref[...], grad_state) * tail_col
        late[:, j : j + 1] = jnp.sum(x * outer, axis=1, keepdims=True)
        grad_x_ref[:, columns] = (part_ref[:, columns] + step_col * outer).astype(BF16)
        grad_b_ref[...] += mm_wide(x * (step_col * tail_col), grad_state)
        shared = jnp.sum(grad_state * state_ref[j], axis=0, keepdims=True)
        overlap[:, j : j + 1] = jnp.sum(shared, axis=1, keepdims=True)

    grad_step = col_ref[0] + late[...]
    grad_step_ref[0] = grad_step
    change = carry_ref[0] - steps * grad_step
    last = jnp.exp(end) * overlap[...] + jnp.sum(steps * late[...], axis=0, keepdims=True)
    source = lax.broadcasted_iota(jnp.int32, (span, span), 0)
    target = lax.broadcasted_iota(jnp.int32, (span, span), 1)
    from_here = (source <= target).astype(BF16)
    high, low = halves(change)
    lowest = (change - high.astype(F32) - low.astype(F32)).astype(BF16)
    grad_decay_ref[0] = last + (
        mm(from_here, high, NN) + mm(from_here, low, NN) + mm(from_here, lowest, NN)
    )


def outer_part(x, part, b, state, grad_state, running, steps, cols, carries, grad_b, at, before):
    groups, span, group = steps.shape
    heads = groups * group
    count = grad_state.shape[0] // group
    width = x.shape[1] // heads
    states = b.shape[1]
    block = pl.BlockSpec((span, group * width), lambda i, at: (0, at[0] + i))
    table = pl.BlockSpec((1, span, group), lambda i, at: (at[0] + i, 0, 0))
    held = [] if before is None else list(before)
    return pl.pallas_call(
        outer_kernel,
        grid_spec=pltpu.PrefetchScalarGridSpec(
            num_scalar_prefetch=1,
            grid=(count,),
            in_specs=[
                block,
                block,
                whole(span, states),
                pl.BlockSpec((group, states, width), lambda i, at: (at[0] + i, 0, 0)),
                pl.BlockSpec((group, states, width), lambda i, at: (i, 0, 0)),
                table,
                table,
                table,
                table,
                whole(span, states),
            ]
            + [pl.BlockSpec(memory_space=pl.ANY)] * len(held),
            out_specs=[block, whole(span, states), table, table],
            scratch_shapes=[pltpu.VMEM((span, group), F32), pltpu.VMEM((1, group), F32)],
        ),
        out_shape=[
            jax.ShapeDtypeStruct((span, heads * width), BF16),
            jax.ShapeDtypeStruct((span, states), F32),
            jax.ShapeDtypeStruct((groups, span, group), F32),
            jax.ShapeDtypeStruct((groups, span, group), F32),
        ],
        input_output_aliases={11: 0, 12: 2, 13: 3} if held else {},
        compiler_params=PARAMS,
        cost_estimate=cost(
            8 * span * count * group * width * states,
            count * group * width * (8 * span + 8 * states),
        ),
    )(at, x, part, b, state, grad_state, running, steps, cols, carries, grad_b, *held)


def project_kernel(hops, at_ref, *refs):
    count = len(hops)
    pieces, (own_ref, other_ref, send_ref, keep_ref, left) = refs[:count], refs[count:]
    rows = pieces[0].shape[0]
    depth = own_ref.shape[1]

    @pl.when(pl.program_id(0) == 0)
    def _():
        first = pl.multiple_of(at_ref[0] * depth, depth)
        second = pl.multiple_of((1 - at_ref[0]) * depth, depth)
        for place, hop in enumerate(hops):
            left[pl.ds(place * rows, rows), :depth] = pieces[hop][:, pl.ds(first, depth)]
            left[pl.ds(place * rows, rows), depth:] = pieces[hop][:, pl.ds(second, depth)]

    total = mm(left[:, :depth], own_ref[...], NT) + mm(left[:, depth:], other_ref[...], NT)
    middle = rows * (count // 2)
    keep_ref[...] = total[:middle]
    send_ref[...] = total[middle:].astype(BF16)


def partial_sums(pieces, hops, own, other, lane, core):
    rows, both = pieces[0].shape
    depth = own.shape[1]
    half = own.shape[0] // 2
    tile = min(512, half)
    steps = half // tile
    middle = rows * (len(hops) // 2)
    weight = pl.BlockSpec((tile, depth), lambda i, at: (lane * steps + i, 0))
    return pl.pallas_call(
        lambda *refs: project_kernel(hops, *refs),
        grid_spec=pltpu.PrefetchScalarGridSpec(
            num_scalar_prefetch=1,
            grid=(steps,),
            in_specs=[whole(rows, both)] * len(hops) + [weight, weight],
            out_specs=[pl.BlockSpec((middle, tile), lambda i, at: (0, i))] * 2,
            scratch_shapes=[pltpu.VMEM((rows * len(hops), both), BF16)],
        ),
        out_shape=[
            jax.ShapeDtypeStruct((middle, half), BF16),
            jax.ShapeDtypeStruct((middle, half), F32),
        ],
        compiler_params=PARAMS,
        cost_estimate=cost(
            2 * rows * len(hops) * both * half, 2 * both * half + 6 * middle * half
        ),
    )(core, *pieces, own, other)


def across(value, hop, chips):
    pairs = [(2 * i + core, 2 * (i ^ hop) + core) for i in range(chips) for core in range(2)]
    return lax.ppermute(value, "seq", pairs)


def other_core(value, chips):
    return lax.ppermute(value, "seq", [(i, i ^ 1) for i in range(2 * chips)])


def orders(chips):
    bits = [1 << i for i in range(chips.bit_length() - 1)]
    return [bits, bits[::-1]]


def sum_over_heads(value):
    count = lax.axis_size("head")
    here = lax.axis_index("head")
    shares = value.reshape((count, value.shape[0] // count) + value.shape[1:])
    shift = lambda hop: [(i, (i + hop) % count) for i in range(count)]
    share = lambda hop: lax.dynamic_index_in_dim(shares, (here + hop) % count, 0, False)
    total = share(0)
    for hop in range(1, count):
        total = total + lax.ppermute(share(hop), "head", shift(hop))
    parts = [total] + [lax.ppermute(total, "head", shift(hop)) for hop in range(1, count)]
    stacked = jnp.stack(parts)
    ordered = [
        lax.dynamic_index_in_dim(stacked, (here - i) % count, 0, False) for i in range(count)
    ]
    return jnp.concatenate(ordered, axis=0)


def project(grad_out, out_weight, chips, chip, core, after):
    span = grad_out.shape[0]
    both = 2 * out_weight.shape[1]
    other = other_core(out_weight, chips)
    core_at = core.astype(jnp.int32).reshape(1)
    rows = min(CHUNK_ROWS, span)
    done = []
    for start in range(0, span, rows):
        full = lax.all_gather(grad_out[start : start + rows], "head", axis=1, tiled=True)
        base = chip if start == 0 else chip + after
        blocks = []
        for hop in range(chips):
            block = lax.dynamic_slice_in_dim(full, (base ^ hop) * both, both, 1)
            blocks.append(across(block, hop, chips) if hop else block)
        pieces = []
        for lane, order in enumerate(orders(chips)):
            hops = [0]
            for bit in order[::-1]:
                hops = hops + [hop | bit for hop in hops]
            send, keep = partial_sums(blocks, hops, out_weight, other, lane, core_at)
            for bit in order:
                keep = keep + across(send, bit, chips).astype(F32)
                size = keep.shape[0] // 2
                if size >= rows:
                    send = keep[size:].astype(BF16)
                    keep = keep[:size]
            pieces.append(keep.astype(BF16))
        done.append(jnp.concatenate(pieces, axis=1))
    return jnp.concatenate(done, axis=0)


def exchange(mine, to_other, ends, chips, chip, core, reverse):
    half = mine.shape[0]
    theirs = other_core(to_other, chips)
    ends = lax.dynamic_slice_in_dim(ends, core * half, half, 1)
    by_chip = ends.reshape(chips, 2, half)
    own_ends = lax.dynamic_index_in_dim(by_chip, chip, 0, False)
    chip_ends = by_chip[:, 0] + by_chip[:, 1]
    index = jnp.arange(chips)[:, None]
    scale = lambda logs, value: jnp.exp(logs)[:, None, None] * value.astype(F32)

    def carry(source, target):
        before = source > target if reverse else source < target
        inside = (index > jnp.minimum(source, target)) & (index < jnp.maximum(source, target))
        between = jnp.sum(jnp.where(inside, chip_ends, 0.0), axis=0)
        return jnp.where(before, between, -jnp.inf)

    near_first = (core == 0) != reverse
    first = jnp.where(near_first, mine, theirs)
    second = jnp.where(near_first, theirs, mine)
    first_end, second_end = (own_ends[1], own_ends[0]) if reverse else (own_ends[0], own_ends[1])
    chip_state = scale(second_end, first) + second
    totals = []
    for lane, order in enumerate(orders(chips)):
        heads = slice(lane * (half // 2), (lane + 1) * (half // 2))
        items = {0: chip_state[heads].astype(BF16)}
        for bit in order[:-1]:
            items.update({o | bit: across(item, bit, chips) for o, item in items.items()})
        bit = order[-1]
        gather = lambda target: sum(
            scale(carry(chip ^ o, target)[heads], item) for o, item in items.items()
        )
        arrived = across(gather(chip ^ bit).astype(BF16), bit, chips)
        totals.append(gather(chip) + arrived.astype(F32))
    total = jnp.concatenate(totals, axis=0)
    after = scale(first_end, total) + first
    for_mine = jnp.where(near_first, total, after)
    for_theirs = jnp.where(near_first, after, total)
    return for_mine, other_core(for_theirs, chips)


def local(grad_out, out_weight, ssm_input, step_size, log_decay, b_in, c_in, skip):
    place_on_seq = lax.axis_index("seq")
    chips = lax.axis_size("seq") // 2
    chip, core = place_on_seq // 2, place_on_seq % 2
    span, heads = step_size.shape
    width = ssm_input.shape[1] // heads
    group = min(GROUP, heads // 2)
    groups = heads // group
    by_group = lambda t: t.reshape(span, groups, group).transpose(1, 0, 2)
    flat = lambda t: t.transpose(1, 0, 2).reshape(span, heads)
    mine_at = (core * (groups // 2)).astype(jnp.int32).reshape(1)
    other_at = ((1 - core) * (groups // 2)).astype(jnp.int32).reshape(1)

    upto = jnp.tril(jnp.ones((span, span), F32))
    running = jnp.dot(upto, log_decay, precision=HIGH)
    ends = lax.all_gather(running[-1], "seq")
    tail = jnp.exp(running[-1:] - running)
    running_g = by_group(running)
    running_t = running.T.reshape(groups, group, span)
    steps_g = by_group(step_size)
    skip_rows = jnp.broadcast_to(skip.reshape(groups, group, 1), (groups, group, width))

    def states(values, scale, rows, reverse):
        rows_t = rows.T
        to_other = span_states(values, scale, rows_t, other_at, groups // 2)
        mine = span_states(values, scale, rows_t, mine_at, groups // 2)
        return exchange(mine, to_other, ends, chips, chip, core, reverse)

    for_mine, for_other = states(ssm_input, by_group(step_size * tail), b_in, False)
    incoming = jnp.where(
        core == 0,
        jnp.concatenate([for_mine, for_other], axis=0),
        jnp.concatenate([for_other, for_mine], axis=0),
    )
    corner = incoming[0, 0, 0]
    after = (corner != corner).astype(chip.dtype)

    grad_y = project(grad_out, out_weight, chips, chip, core, after)
    out_mine, out_other = states(grad_y, by_group(jnp.exp(running)), c_in, True)
    part, grad_b, grad_c, cols, carries = inner_part(
        ssm_input, grad_y, b_in, c_in, running_g, running_t, steps_g, skip_rows, incoming
    )
    grad_c = sum_over_heads(grad_c)
    shared = (running_g, steps_g, cols, carries)
    grad_x, grad_b, grad_step, grad_decay = outer_part(
        ssm_input, part, b_in, incoming, out_mine, *shared, grad_b, mine_at, None
    )
    grad_x, grad_b, grad_step, grad_decay = outer_part(
        ssm_input, part, b_in, incoming, out_other, *shared, grad_b, other_at,
        (grad_x, grad_step, grad_decay),
    )
    grad_b = sum_over_heads(grad_b)
    return (grad_x, flat(grad_step), flat(grad_decay), grad_b, grad_c)


def solution(mesh):
    in_specs = (
        P("seq", "head"),
        P("head", "seq"),
        P("seq", "head"),
        P("seq", "head"),
        P("seq", "head"),
        P("seq", None),
        P("seq", None),
        P("head"),
    )
    out_specs = (
        P("seq", "head"),
        P("seq", "head"),
        P("seq", "head"),
        P("seq", None),
        P("seq", None),
    )
    return jax.shard_map(local, mesh=mesh, in_specs=in_specs, out_specs=out_specs, check_vma=False)
```

time: 934 us -> 390 us (0.42)
  waiting for transfers between devices: 745 us -> 132 us
  Pallas kernels: 0 us -> 90.1 us
  matrix products: 82.5 us -> 0.34 us
  starting transfers between devices: 0.2 us -> 62.5 us
  other arithmetic: 53.3 us -> 43.6 us
    all_gather x4, waiting for transfers between devices: 663 us -> 38.8 us  [project(): lax.all_gather(grad_out[start:start + rows], 'head', axis=1, tiled=True)]
    ppermute x0 -> x53, waiting for transfers between devices: none -> 93.2 us  [the longest x36 72.8 us: across(): return lax.ppermute(value, 'seq', pairs)]
    pallas_call x0 -> x15, Pallas kernels: none -> 90.1 us  [the longest x8 46.1 us: partial_sums(): pl.pallas_call(lambda *refs: project_kernel(hops, *refs), grid_spec=pltpu...]
    dot_general x12 -> x1, matrix products: 82.5 us -> 0.34 us  [local(): running = jnp.dot(upto, log_decay, precision=HIGH)]
    psum x1 -> x0, waiting for transfers between devices: 80.8 us -> none  [local(): grad_b, grad_c = lax.psum((gradients[3], gradients[4]), 'head')]
    ppermute x0 -> x53, starting transfers between devices: none -> 62.1 us  [the longest x36 45.7 us: across(): return lax.ppermute(value, 'seq', pairs)]
    add x7 -> x13, other arithmetic: 45.4 us -> 9.66 us  [the longest x8 6.06 us: project(): keep = keep + across(send, bit, chips).astype(F32)]
    concatenate x0 -> x3, other arithmetic: none -> 14.8 us  [the longest x1 13.3 us: project(): return jnp.concatenate(done, axis=0)]
  transfers between devices with their start and end apart: 5 -> 57, of which waited for: 5 -> 27; matrix products, arithmetic and copies ran while one was open for 4% -> 9% of each run, Pallas kernels for 0% -> 21%
where the time goes in v2:
time: 390 us; the launch traced here: 386 us
  waiting for transfers between devices  132 us (34%)
  Pallas kernels  90.1 us (23%)
  starting transfers between devices  62.5 us (16%)
  other arithmetic  43.6 us (11%)
  local copies, waits for them, and re-layouts  28.2 us (7%)
  between operations  16.5 us (4%)
  blocking collectives  12.5 us (3%)
    ppermute x36, waiting for transfers between devices, across(): return lax.ppermute(value, 'seq', pairs)  72.8 us
    pallas_call x8, Pallas kernels, partial_sums(): pl.pallas_call(lambda *refs: project_kernel(hops, *refs), grid_spec=pltpu...  46.1 us
    ppermute x36, starting transfers between devices, across(): return lax.ppermute(value, 'seq', pairs)  45.7 us
    all_gather x4, waiting for transfers between devices, project(): lax.all_gather(grad_out[start:start + rows], 'head', axis=1, tiled=True)  38.8 us
    pallas_call x1, Pallas kernels, inner_part(): pl.pallas_call(inner_kernel, grid_spec=pltpu.PrefetchScalarGridSpec(num_s...  19.9 us
    pallas_call x2, Pallas kernels, outer_part(): pl.pallas_call(outer_kernel, grid_spec=pltpu.PrefetchScalarGridSpec(num_s...  15.9 us
    concatenate x1, other arithmetic, project(): return jnp.concatenate(done, axis=0)  13.3 us
    all_gather x1, blocking collectives, local(): ends = lax.all_gather(running[-1], 'seq')  12.5 us
  transfers between devices with their start and end apart: 57, of which 27 were waited for; matrix products, arithmetic and copies ran while one was open for 9% of the time, Pallas kernels for 21%

profile of v2, /device:TPU:0, one launch (start us, length us, event | category | flops | bytes accessed | tf_op | source)
XLA Modules:
  0.0 385.7 jit_solution(10899167697751130865)
XLA Ops:
  13.9 12.5 %all-gather = f32[8,1,32]{2,1,0:T(1,128)S(1)} all-gather(f32[1,1,32]{2,1,0:T(1,128)S(1)} %bitcast.118), channel_id=1, replica_groups=mesh['seq'=8,'head'=4] {'seq'}, dimensions={0}, use_global_device_ids=true | all-gather | bytes 1152 | tf_op jit(solution)/shard_map/all_gather | solution.py:442
  31.8 2.7 collective-permute-start.9
  36.1 11.0 %collective-permute-done.9 = bf16[8,256,128]{2,1,0:T(8,128)(2,1)} collective-permute-done((bf16[8,256,128]{2,1,0:T(8,128)(2,1)}, bf16[8,256,128]{2,1,0:T(8,128)(2,1)}, u32[]{:S(2)}, u32[]{:S(2)}) %collective-permute-start.9) | collective-permute-done | bytes 524320 | tf_op jit(solution)/shard_map/ppermute | solution.py:327
  48.6 2.7 fusion.7
  53.7 10.9 %collective-permute-done.10 = bf16[8,256,128]{2,1,0:T(8,128)(2,1)} collective-permute-done((bf16[8,256,128]{2,1,0:T(8,128)(2,1)}, bf16[8,256,128]{2,1,0:T(8,128)(2,1)}, u32[]{:S(2)}, u32[]{:S(2)}) %collective-permute-start.10) | collective-permute-done | bytes 524320 | tf_op jit(solution)/shard_map/ppermute | solution.py:327
  68.0 2.7 fusion.3
  75.2 2.8 maximum_select_fusion.state_ref
  87.5 11.4 %all-gather.10.cloned.1.call-done = bf16[64,8192]{1,0:T(8,128)(2,1)} async-done(((bf16[64,2048]{1,0:T(8,128)(2,1)}), bf16[64,8192]{1,0:T(8,128)(2,1)}) %all-gather.10.cloned.1.call-update) | async-done | bytes 1048592 | tf_op jit(solution)/shard_map/all_gather | solution.py:364
  101.0 27.4 %all-gather.8.cloned.1.call-done = bf16[64,8192]{1,0:T(8,128)(2,1)} async-done(((bf16[64,2048]{1,0:T(8,128)(2,1)}), bf16[64,8192]{1,0:T(8,128)(2,1)}) %all-gather.8.cloned.1.call-update) | async-done | bytes 1048592 | tf_op jit(solution)/shard_map/all_gather | solution.py:364
  134.9 5.9 %shard_map.128 = (bf16[128,2048]{1,0:T(8,128)(2,1)S(1)}, f32[128,2048]{1,0:T(8,128)S(1)}) custom-call(s32[1]{0:T(128)} %bitcast.1.refs_0_, bf16[64,2048]{1,0:T(8,128)(2,1)S(1)} %get-tuple-element.95.refs_1_, bf16[64,2048]{1,0:T(8,128)(2,1)} %collective-permute-done.28.refs_2_, bf16[64,2048]{1,0:T(8,128)(2,1)} %collective-permute-done.29.refs_3_, ...), custom_call_target="tpu_custom_call" | custom-call | flops 2147483648 | bytes 9961472 | tf_op jit(solution)/shard_map/pallas_call | solution.py:305
  140.8 5.9 %shard_map.127 = (bf16[128,2048]{1,0:T(8,128)(2,1)S(1)}, f32[128,2048]{1,0:T(8,128)S(1)}) custom-call(s32[1]{0:T(128)} %bitcast.1.refs_0_, bf16[64,2048]{1,0:T(8,128)(2,1)S(1)} %get-tuple-element.95.refs_1_, bf16[64,2048]{1,0:T(8,128)(2,1)} %collective-permute-done.28.refs_2_, bf16[64,2048]{1,0:T(8,128)(2,1)} %collective-permute-done.29.refs_3_, ...), custom_call_target="tpu_custom_call" | custom-call | flops 2147483648 | bytes 9961472 | tf_op jit(solution)/shard_map/pallas_call | solution.py:305
  151.9 5.7 %shard_map.126 = (bf16[128,2048]{1,0:T(8,128)(2,1)S(1)}, f32[128,2048]{1,0:T(8,128)S(1)}) custom-call(s32[1]{0:T(128)} %bitcast.1.refs_0_, bf16[64,2048]{1,0:T(8,128)(2,1)S(1)} %get-tuple-element.91.refs_1_, bf16[64,2048]{1,0:T(8,128)(2,1)S(1)} %collective-permute-done.21.refs_2_, bf16[64,2048]{1,0:T(8,128)(2,1)S(1)} %collective-permute-done.22.refs_3_, ...), custom_call_target="tpu_custom_call" | custom-call | flops 2147483648 | bytes 9961472 | tf_op jit(solution)/shard_map/pallas_call | solution.py:305
  157.7 5.7 %shard_map.125 = (bf16[128,2048]{1,0:T(8,128)(2,1)S(1)}, f32[128,2048]{1,0:T(8,128)S(1)}) custom-call(s32[1]{0:T(128)} %bitcast.1.refs_0_, bf16[64,2048]{1,0:T(8,128)(2,1)S(1)} %get-tuple-element.91.refs_1_, bf16[64,2048]{1,0:T(8,128)(2,1)S(1)} %collective-permute-done.21.refs_2_, bf16[64,2048]{1,0:T(8,128)(2,1)S(1)} %collective-permute-done.22.refs_3_, ...), custom_call_target="tpu_custom_call" | custom-call | flops 2147483648 | bytes 9961472 | tf_op jit(solution)/shard_map/pallas_call | solution.py:305
  167.0 5.7 %shard_map.124 = (bf16[128,2048]{1,0:T(8,128)(2,1)S(1)}, f32[128,2048]{1,0:T(8,128)S(1)}) custom-call(s32[1]{0:T(128)} %bitcast.1.refs_0_, bf16[64,2048]{1,0:T(8,128)(2,1)S(1)} %get-tuple-element.87.refs_1_, bf16[64,2048]{1,0:T(8,128)(2,1)S(1)} %collective-permute-done.14.refs_2_, bf16[64,2048]{1,0:T(8,128)(2,1)S(1)} %collective-permute-done.15.refs_3_, ...), custom_call_target="tpu_custom_call" | custom-call | flops 2147483648 | bytes 9961472 | tf_op jit(solution)/shard_map/pallas_call | solution.py:305
  172.7 5.7 %shard_map.123 = (bf16[128,2048]{1,0:T(8,128)(2,1)S(1)}, f32[128,2048]{1,0:T(8,128)S(1)}) custom-call(s32[1]{0:T(128)} %bitcast.1.refs_0_, bf16[64,2048]{1,0:T(8,128)(2,1)S(1)} %get-tuple-element.87.refs_1_, bf16[64,2048]{1,0:T(8,128)(2,1)S(1)} %collective-permute-done.14.refs_2_, bf16[64,2048]{1,0:T(8,128)(2,1)S(1)} %collective-permute-done.15.refs_3_, ...), custom_call_target="tpu_custom_call" | custom-call | flops 2147483648 | bytes 9961472 | tf_op jit(solution)/shard_map/pallas_call | solution.py:305
  181.1 5.8 %shard_map.120 = (bf16[128,2048]{1,0:T(8,128)(2,1)S(1)}, f32[128,2048]{1,0:T(8,128)S(1)}) custom-call(s32[1]{0:T(128)} %bitcast.1.refs_0_, bf16[64,2048]{1,0:T(8,128)(2,1)S(1)} %get-tuple-element.79.refs_1_, bf16[64,2048]{1,0:T(8,128)(2,1)} %collective-permute-done.refs_2_, bf16[64,2048]{1,0:T(8,128)(2,1)S(1)} %collective-permute-done.1.refs_3_, ...), custom_call_target="tpu_custom_call" | custom-call | flops 2147483648 | bytes 9961472 | tf_op jit(solution)/shard_map/pallas_call | solution.py:305
  186.8 5.7 %shard_map.119 = (bf16[128,2048]{1,0:T(8,128)(2,1)S(1)}, f32[128,2048]{1,0:T(8,128)S(1)}) custom-call(s32[1]{0:T(128)} %bitcast.1.refs_0_, bf16[64,2048]{1,0:T(8,128)(2,1)S(1)} %get-tuple-element.79.refs_1_, bf16[64,2048]{1,0:T(8,128)(2,1)} %collective-permute-done.refs_2_, bf16[64,2048]{1,0:T(8,128)(2,1)S(1)} %collective-permute-done.1.refs_3_, ...), custom_call_target="tpu_custom_call" | custom-call | flops 2147483648 | bytes 9961472 | tf_op jit(solution)/shard_map/pallas_call | solution.py:305
  209.2 6.8 %collective-permute-done.6 = bf16[128,2048]{1,0:T(8,128)(2,1)S(1)} collective-permute-done((bf16[128,2048]{1,0:T(8,128)(2,1)S(1)}, bf16[128,2048]{1,0:T(8,128)(2,1)S(1)}, u32[]{:S(2)}, u32[]{:S(2)}) %collective-permute-start.6) | collective-permute-done | bytes 524320 | tf_op jit(solution)/shard_map/ppermute | solution.py:327
  220.4 4.0 %collective-permute-done.34 = bf16[64,2048]{1,0:T(8,128)(2,1)S(1)} collective-permute-done((bf16[64,2048]{1,0:T(8,128)(2,1)S(1)}, bf16[64,2048]{1,0:T(8,128)(2,1)S(1)}, u32[]{:S(2)}, u32[]{:S(2)}) %collective-permute-start.34) | collective-permute-done | bytes 262176 | tf_op jit(solution)/shard_map/ppermute | solution.py:327
  231.6 3.9 %collective-permute-done.20 = bf16[64,2048]{1,0:T(8,128)(2,1)S(1)} collective-permute-done((bf16[64,2048]{1,0:T(8,128)(2,1)S(1)}, bf16[64,2048]{1,0:T(8,128)(2,1)S(1)}, u32[]{:S(2)}, u32[]{:S(2)}) %collective-permute-start.20) | collective-permute-done | bytes 262176 | tf_op jit(solution)/shard_map/ppermute | solution.py:327
  235.6 2.7 collective-permute-done.7
  238.5 13.3 %maximum_maximum_fusion.y_ref.v_ref = bf16[256,4096]{1,0:T(8,128)(2,1)S(1)} fusion(bf16[64,2048]{1,0:T(8,128)(2,1)S(1)} %fusion.20, bf16[64,2048]{1,0:T(8,128)(2,1)S(1)} %fusion.21, bf16[64,2048]{1,0:T(8,128)(2,1)S(1)} %fusion.22, bf16[64,2048]{1,0:T(8,128)(2,1)S(1)} %fusion.23, bf16[64,2048]{1,0:T(8,128)(2,1)S(1)} %fusion.24, ...), kind=kLoop, calls=%fused_computation.2 | loop fusion | flops 16777216 | bytes 4194304 | tf_op jit(solution)/shard_map/concatenate | solution.py:384
  263.1 11.9 %collective-permute-done.36 = bf16[8,256,128]{2,1,0:T(8,128)(2,1)S(1)} collective-permute-done((bf16[8,256,128]{2,1,0:T(8,128)(2,1)S(1)}, bf16[8,256,128]{2,1,0:T(8,128)(2,1)S(1)}, u32[]{:S(2)}, u32[]{:S(2)}) %collective-permute-start.36) | collective-permute-done | bytes 524320 | tf_op jit(solution)/shard_map/ppermute | solution.py:327
  278.2 10.6 %collective-permute-done.37 = bf16[8,256,128]{2,1,0:T(8,128)(2,1)S(1)} collective-permute-done((bf16[8,256,128]{2,1,0:T(8,128)(2,1)S(1)}, bf16[8,256,128]{2,1,0:T(8,128)(2,1)S(1)}, u32[]{:S(2)}, u32[]{:S(2)}) %collective-permute-start.37) | collective-permute-done | bytes 524320 | tf_op jit(solution)/shard_map/ppermute | solution.py:327
  290.4 4.5 %fusion = (f32[16,256,128]{2,1,0:T(8,128)}, f32[16,256,128]{2,1,0:T(8,128)}) fusion(f32[8,256,128]{2,1,0:T(8,128)S(1)} %get-tuple-element.71, f32[8,256,128]{2,1,0:T(8,128)S(1)} %get-tuple-element.70, f32[16]{0:T(128)S(1)} %get-tuple-element.119, pred[]{:T(512)S(6)} %ne.68, f32[16,256,128]{2,1,0:T(8,128)S(1)} %shard_map.130, ...), kind=kLoop, calls=%fused_computation.5 | loop fusion | flops 3145728 | bytes 10485825 | tf_op jit(solution)/shard_map/jit(_where)/select_n | solution.py:422
  295.5 19.9 %shard_map.129 = (f32[256,4096]{1,0:T(8,128)}, f32[256,256]{1,0:T(8,128)S(1)}, f32[256,256]{1,0:T(8,128)S(1)}, f32[4,256,8]{2,1,0:T(8,128)S(1)}, f32[4,256,8]{2,1,0:T(8,128)S(1)}) custom-call(s32[1]{0:T(128)} %constant.141.clone.1.at_ref, bf16[256,4096]{1,0:T(8,128)(2,1)S(1)} %copy-done.2, bf16[256,4096]{1,0:T(8,128)(2,1)} %copy-done.3, ...), custom_call_target="tpu_custom_call" | custom-call | flops 3758096384 | bytes 12582912 | tf_op jit(solution)/shard_map/pallas_call | solution.py:147
  324.3 5.1 %collective-permute-done.48 = f32[64,256]{1,0:T(8,128)S(1)} collective-permute-done((f32[64,256]{1,0:T(8,128)}, f32[64,256]{1,0:T(8,128)S(1)}, u32[]{:S(2)}, u32[]{:S(2)}) %collective-permute-start.48) | collective-permute-done | bytes 65568 | tf_op jit(solution)/shard_map/ppermute | solution.py:347
  334.6 4.5 %collective-permute-done.51 = f32[64,256]{1,0:T(8,128)S(1)} collective-permute-done((f32[64,256]{1,0:T(8,128)S(1)}, f32[64,256]{1,0:T(8,128)S(1)}, u32[]{:S(2)}, u32[]{:S(2)}) %collective-permute-start.51) | collective-permute-done | bytes 65568 | tf_op jit(solution)/shard_map/ppermute | solution.py:348
  343.1 8.0 %shard_map.132 = (bf16[256,4096]{1,0:T(8,128)(2,1)}, f32[256,256]{1,0:T(8,128)S(1)}, f32[4,256,8]{2,1,0:T(8,128)S(1)}, f32[4,256,8]{2,1,0:T(8,128)S(1)}) custom-call(s32[1]{0:T(128)} %bitcast.5.at_ref, bf16[256,4096]{1,0:T(8,128)(2,1)S(1)} %copy-done.2, f32[256,4096]{1,0:T(8,128)} %get-tuple-element.50.part_ref, bf16[256,256]{1,0:T(8,128)(2,1)S(1)} %copy-done.17, ...), custom_call_target="tpu_custom_call" | custom-call | flops 1073741824 | bytes 8388608 | tf_op jit(solution)/shard_map/pallas_call | solution.py:241
  351.0 8.0 %shard_map.133 = (bf16[256,4096]{1,0:T(8,128)(2,1)}, f32[256,256]{1,0:T(8,128)S(1)}, f32[4,256,8]{2,1,0:T(8,128)S(1)}, f32[4,256,8]{2,1,0:T(8,128)S(1)}) custom-call(s32[1]{0:T(128)} %bitcast.at_ref, bf16[256,4096]{1,0:T(8,128)(2,1)S(1)} %copy-done.2, ...), custom_call_target="tpu_custom_call", output_to_operand_aliasing={{0}: (11, {}), {2}: (12, {}), {3}: (13, {})} | custom-call | flops 1073741824 | bytes 8388608 | tf_op jit(solution)/shard_map/pallas_call | solution.py:241
  364.9 4.3 %collective-permute-done.42 = f32[64,256]{1,0:T(8,128)S(1)} collective-permute-done((f32[64,256]{1,0:T(8,128)S(1)}, f32[64,256]{1,0:T(8,128)S(1)}, u32[]{:S(2)}, u32[]{:S(2)}) %collective-permute-start.42) | collective-permute-done | bytes 65568 | tf_op jit(solution)/shard_map/ppermute | solution.py:347
  375.3 2.6 collective-permute-done.45
  (255 shorter events, 128.9 us)
Async XLA Ops:
  7.2 64.5 %all-gather.6.cloned.1.call-start = ((), (), s32[]{:S(2)}) async-start(), calls=%async_computation | async-start | bytes 1310720 | tf_op jit(solution)/shard_map/all_gather | solution.py:364
  9.6 72.3 %all-gather.12.cloned.1.call-start = ((), (), s32[]{:S(2)}) async-start(), calls=%async_computation.3 | async-start | bytes 1310720 | tf_op jit(solution)/shard_map/all_gather | solution.py:364
  9.6 123.7 %collective-permute-start.3 = (bf16[4096,1024]{1,0:T(8,128)(2,1)}, bf16[4096,1024]{1,0:T(8,128)(2,1)}, u32[]{:S(2)}, u32[]{:S(2)}) collective-permute-start(bf16[4096,1024]{1,0:T(8,128)(2,1)} %refs_5_.15), channel_id=1, source_target_pairs={{0,4},{4,0},{8,12},{12,8},{16,20},{20,16},{24,28},{28,24},{1,5},{5... | collective-permute-start | bytes 25165832 | tf_op jit(solution)/shard_map/ppermute | solution.py:331
  13.7 85.2 %all-gather.10.cloned.1.call-start = ((), (), s32[]{:S(2)}) async-start(), calls=%async_computation.2 | async-start | bytes 1310720 | tf_op jit(solution)/shard_map/all_gather | solution.py:364
  31.8 15.4 %collective-permute-start.9 = (bf16[8,256,128]{2,1,0:T(8,128)(2,1)}, bf16[8,256,128]{2,1,0:T(8,128)(2,1)}, u32[]{:S(2)}, u32[]{:S(2)}) collective-permute-start(bf16[8,256,128]{2,1,0:T(8,128)(2,1)} %get-tuple-element.100), channel_id=1, source_target_pairs={{0,8},{4,12},{8,0},{12,4},{16,24},{20,28},{24,16},{28,20},{1,9},{5... | collective-permute-start | bytes 1572872 | tf_op jit(solution)/shard_map/ppermute | solution.py:327
  53.4 75.0 %all-gather.8.cloned.1.call-start = ((), (), s32[]{:S(2)}) async-start(), calls=%async_computation.1 | async-start | bytes 1310720 | tf_op jit(solution)/shard_map/all_gather | solution.py:364
  74.0 104.5 %collective-permute-start = (bf16[64,2048]{1,0:T(8,128)(2,1)}, bf16[64,2048]{1,0:T(8,128)(2,1)}, u32[]{:S(2)}, u32[]{:S(2)}) collective-permute-start(bf16[64,2048]{1,0:T(8,128)(2,1)} %get-tuple-element.78), channel_id=1, source_target_pairs={{0,8},{4,12},{8,0},{12,4},{16,24},{20,28},{24,16},{28,20},{1,9},{5... | collective-permute-start | bytes 786440 | tf_op jit(solution)/shard_map/ppermute | solution.py:327
  84.0 45.8 %collective-permute-start.28 = (bf16[64,2048]{1,0:T(8,128)(2,1)}, bf16[64,2048]{1,0:T(8,128)(2,1)}, u32[]{:S(2)}, u32[]{:S(2)}) collective-permute-start(bf16[64,2048]{1,0:T(8,128)(2,1)} %get-tuple-element.94), channel_id=1, source_target_pairs={{0,8},{4,12},{8,0},{12,4},{16,24},{20,28},{24,16},{28,20},{1,9},{5... | collective-permute-start | bytes 786440 | tf_op jit(solution)/shard_map/ppermute | solution.py:327
  84.8 46.6 %collective-permute-start.29 = (bf16[64,2048]{1,0:T(8,128)(2,1)}, bf16[64,2048]{1,0:T(8,128)(2,1)}, u32[]{:S(2)}, u32[]{:S(2)}) collective-permute-start(bf16[64,2048]{1,0:T(8,128)(2,1)} %get-tuple-element.93), channel_id=1, source_target_pairs={{0,16},{4,20},{8,24},{12,28},{16,0},{20,4},{24,8},{28,12},{1,17},{... | collective-permute-start | bytes 786440 | tf_op jit(solution)/shard_map/ppermute | solution.py:327
  85.3 47.5 %collective-permute-start.30 = (bf16[64,2048]{1,0:T(8,128)(2,1)}, bf16[64,2048]{1,0:T(8,128)(2,1)}, u32[]{:S(2)}, u32[]{:S(2)}) collective-permute-start(bf16[64,2048]{1,0:T(8,128)(2,1)} %get-tuple-element.92), channel_id=1, source_target_pairs={{0,24},{4,28},{8,16},{12,20},{16,8},{20,12},{24,0},{28,4},{1,25},{... | collective-permute-start | bytes 786440 | tf_op jit(solution)/shard_map/ppermute | solution.py:327
  129.8 50.2 %collective-permute-start.1 = (bf16[64,2048]{1,0:T(8,128)(2,1)S(1)}, bf16[64,2048]{1,0:T(8,128)(2,1)S(1)}, u32[]{:S(2)}, u32[]{:S(2)}) collective-permute-start(bf16[64,2048]{1,0:T(8,128)(2,1)S(1)} %copy-done.27), channel_id=1, source_target_pairs={{0,16},{4,20},{8,24},{12,28},{16,0},{20,4},{24,8},{28,12},{1,17},{... | collective-permute-start | bytes 786440 | tf_op jit(solution)/shard_map/ppermute | solution.py:327
  131.3 15.3 %collective-permute-start.21 = (bf16[64,2048]{1,0:T(8,128)(2,1)S(1)}, bf16[64,2048]{1,0:T(8,128)(2,1)S(1)}, u32[]{:S(2)}, u32[]{:S(2)}) collective-permute-start(bf16[64,2048]{1,0:T(8,128)(2,1)S(1)} %copy-done.30), channel_id=1, source_target_pairs={{0,8},{4,12},{8,0},{12,4},{16,24},{20,28},{24,16},{28,20},{1,9},{5... | collective-permute-start | bytes 786440 | tf_op jit(solution)/shard_map/ppermute | solution.py:327
  132.8 16.2 %collective-permute-start.22 = (bf16[64,2048]{1,0:T(8,128)(2,1)S(1)}, bf16[64,2048]{1,0:T(8,128)(2,1)S(1)}, u32[]{:S(2)}, u32[]{:S(2)}) collective-permute-start(bf16[64,2048]{1,0:T(8,128)(2,1)S(1)} %copy-done.29), channel_id=1, source_target_pairs={{0,16},{4,20},{8,24},{12,28},{16,0},{20,4},{24,8},{28,12},{1,17},{... | collective-permute-start | bytes 786440 | tf_op jit(solution)/shard_map/ppermute | solution.py:327
  133.4 17.1 %collective-permute-start.23 = (bf16[64,2048]{1,0:T(8,128)(2,1)S(1)}, bf16[64,2048]{1,0:T(8,128)(2,1)S(1)}, u32[]{:S(2)}, u32[]{:S(2)}) collective-permute-start(bf16[64,2048]{1,0:T(8,128)(2,1)S(1)} %copy-done.28), channel_id=1, source_target_pairs={{0,24},{4,28},{8,16},{12,20},{16,8},{20,12},{24,0},{28,4},{1,25},{... | collective-permute-start | bytes 786440 | tf_op jit(solution)/shard_map/ppermute | solution.py:327
  146.7 16.7 %collective-permute-start.14 = (bf16[64,2048]{1,0:T(8,128)(2,1)S(1)}, bf16[64,2048]{1,0:T(8,128)(2,1)S(1)}, u32[]{:S(2)}, u32[]{:S(2)}) collective-permute-start(bf16[64,2048]{1,0:T(8,128)(2,1)S(1)} %get-tuple-element.86), channel_id=1, source_target_pairs={{0,8},{4,12},{8,0},{12,4},{16,24},{20,28},{24,16},{28,20},{1,9},{5... | collective-permute-start | bytes 786440 | tf_op jit(solution)/shard_map/ppermute | solution.py:327
  149.0 16.0 %collective-permute-start.15 = (bf16[64,2048]{1,0:T(8,128)(2,1)S(1)}, bf16[64,2048]{1,0:T(8,128)(2,1)S(1)}, u32[]{:S(2)}, u32[]{:S(2)}) collective-permute-start(bf16[64,2048]{1,0:T(8,128)(2,1)S(1)} %get-tuple-element.85), channel_id=1, source_target_pairs={{0,16},{4,20},{8,24},{12,28},{16,0},{20,4},{24,8},{28,12},{1,17},{... | collective-permute-start | bytes 786440 | tf_op jit(solution)/shard_map/ppermute | solution.py:327
  150.5 15.0 %collective-permute-start.16 = (bf16[64,2048]{1,0:T(8,128)(2,1)S(1)}, bf16[64,2048]{1,0:T(8,128)(2,1)S(1)}, u32[]{:S(2)}, u32[]{:S(2)}) collective-permute-start(bf16[64,2048]{1,0:T(8,128)(2,1)S(1)} %get-tuple-element.84), channel_id=1, source_target_pairs={{0,24},{4,28},{8,16},{12,20},{16,8},{20,12},{24,0},{28,4},{1,25},{... | collective-permute-start | bytes 786440 | tf_op jit(solution)/shard_map/ppermute | solution.py:327
  163.4 17.1 %collective-permute-start.2 = (bf16[64,2048]{1,0:T(8,128)(2,1)S(1)}, bf16[64,2048]{1,0:T(8,128)(2,1)S(1)}, u32[]{:S(2)}, u32[]{:S(2)}) collective-permute-start(bf16[64,2048]{1,0:T(8,128)(2,1)S(1)} %copy-done.26), channel_id=1, source_target_pairs={{0,24},{4,28},{8,16},{12,20},{16,8},{20,12},{24,0},{28,4},{1,25},{... | collective-permute-start | bytes 786440 | tf_op jit(solution)/shard_map/ppermute | solution.py:327
  165.0 27.6 %collective-permute-start.33 = (bf16[128,2048]{1,0:T(8,128)(2,1)S(1)}, bf16[128,2048]{1,0:T(8,128)(2,1)}, u32[]{:S(2)}, u32[]{:S(2)}) collective-permute-start(bf16[128,2048]{1,0:T(8,128)(2,1)S(1)} %get-tuple-element.49), channel_id=1, source_target_pairs={{0,16},{4,20},{8,24},{12,28},{16,0},{20,4},{24,8},{28,12},{1,17},{... | collective-permute-start | bytes 1572872 | tf_op jit(solution)/shard_map/ppermute | solution.py:327
  165.5 29.8 %collective-permute-start.31 = (bf16[128,2048]{1,0:T(8,128)(2,1)S(1)}, bf16[128,2048]{1,0:T(8,128)(2,1)}, u32[]{:S(2)}, u32[]{:S(2)}) collective-permute-start(bf16[128,2048]{1,0:T(8,128)(2,1)S(1)} %get-tuple-element.47), channel_id=1, source_target_pairs={{0,8},{4,12},{8,0},{12,4},{16,24},{20,28},{24,16},{28,20},{1,9},{5... | collective-permute-start | bytes 1572872 | tf_op jit(solution)/shard_map/ppermute | solution.py:327
  178.4 19.6 %collective-permute-start.26 = (bf16[128,2048]{1,0:T(8,128)(2,1)S(1)}, bf16[128,2048]{1,0:T(8,128)(2,1)}, u32[]{:S(2)}, u32[]{:S(2)}) collective-permute-start(bf16[128,2048]{1,0:T(8,128)(2,1)S(1)} %get-tuple-element.45), channel_id=1, source_target_pairs={{0,16},{4,20},{8,24},{12,28},{16,0},{20,4},{24,8},{28,12},{1,17},{... | collective-permute-start | bytes 1572872 | tf_op jit(solution)/shard_map/ppermute | solution.py:327
  180.0 19.9 %collective-permute-start.24 = (bf16[128,2048]{1,0:T(8,128)(2,1)S(1)}, bf16[128,2048]{1,0:T(8,128)(2,1)}, u32[]{:S(2)}, u32[]{:S(2)}) collective-permute-start(bf16[128,2048]{1,0:T(8,128)(2,1)S(1)} %get-tuple-element.43), channel_id=1, source_target_pairs={{0,8},{4,12},{8,0},{12,4},{16,24},{20,28},{24,16},{28,20},{1,9},{5... | collective-permute-start | bytes 1572872 | tf_op jit(solution)/shard_map/ppermute | solution.py:327
  180.5 24.4 %collective-permute-start.19 = (bf16[128,2048]{1,0:T(8,128)(2,1)S(1)}, bf16[128,2048]{1,0:T(8,128)(2,1)}, u32[]{:S(2)}, u32[]{:S(2)}) collective-permute-start(bf16[128,2048]{1,0:T(8,128)(2,1)S(1)} %get-tuple-element.41), channel_id=1, source_target_pairs={{0,16},{4,20},{8,24},{12,28},{16,0},{20,4},{24,8},{28,12},{1,17},{... | collective-permute-start | bytes 1572872 | tf_op jit(solution)/shard_map/ppermute | solution.py:327
  192.6 14.9 %collective-permute-start.17 = (bf16[128,2048]{1,0:T(8,128)(2,1)S(1)}, bf16[128,2048]{1,0:T(8,128)(2,1)S(1)}, u32[]{:S(2)}, u32[]{:S(2)}) collective-permute-start(bf16[128,2048]{1,0:T(8,128)(2,1)S(1)} %get-tuple-element.39), channel_id=1, source_target_pairs={{0,8},{4,12},{8,0},{12,4},{16,24},{20,28},{24,16},{28,20},{1,9},{5... | collective-permute-start | bytes 1572872 | tf_op jit(solution)/shard_map/ppermute | solution.py:327
  195.3 20.7 %collective-permute-start.6 = (bf16[128,2048]{1,0:T(8,128)(2,1)S(1)}, bf16[128,2048]{1,0:T(8,128)(2,1)S(1)}, u32[]{:S(2)}, u32[]{:S(2)}) collective-permute-start(bf16[128,2048]{1,0:T(8,128)(2,1)S(1)} %get-tuple-element.37), channel_id=1, source_target_pairs={{0,16},{4,20},{8,24},{12,28},{16,0},{20,4},{24,8},{28,12},{1,17},{... | collective-permute-start | bytes 1572872 | tf_op jit(solution)/shard_map/ppermute | solution.py:327
  198.0 20.8 %collective-permute-start.4 = (bf16[128,2048]{1,0:T(8,128)(2,1)S(1)}, bf16[128,2048]{1,0:T(8,128)(2,1)S(1)}, u32[]{:S(2)}, u32[]{:S(2)}) collective-permute-start(bf16[128,2048]{1,0:T(8,128)(2,1)S(1)} %get-tuple-element.35), channel_id=1, source_target_pairs={{0,8},{4,12},{8,0},{12,4},{16,24},{20,28},{24,16},{28,20},{1,9},{5... | collective-permute-start | bytes 1572872 | tf_op jit(solution)/shard_map/ppermute | solution.py:327
  199.8 24.5 %collective-permute-start.34 = (bf16[64,2048]{1,0:T(8,128)(2,1)S(1)}, bf16[64,2048]{1,0:T(8,128)(2,1)S(1)}, u32[]{:S(2)}, u32[]{:S(2)}) collective-permute-start(bf16[64,2048]{1,0:T(8,128)(2,1)S(1)} %slice.272), channel_id=1, source_target_pairs={{0,8},{4,12},{8,0},{12,4},{16,24},{20,28},{24,16},{28,20},{1,9},{5... | collective-permute-start | bytes 786440 | tf_op jit(solution)/shard_map/ppermute | solution.py:327
  204.9 21.0 %collective-permute-start.32 = (bf16[64,2048]{1,0:T(8,128)(2,1)S(1)}, bf16[64,2048]{1,0:T(8,128)(2,1)S(1)}, u32[]{:S(2)}, u32[]{:S(2)}) collective-permute-start(bf16[64,2048]{1,0:T(8,128)(2,1)S(1)} %slice.273), channel_id=1, source_target_pairs={{0,16},{4,20},{8,24},{12,28},{16,0},{20,4},{24,8},{28,12},{1,17},{... | collective-permute-start | bytes 786440 | tf_op jit(solution)/shard_map/ppermute | solution.py:327
  207.5 22.5 %collective-permute-start.27 = (bf16[64,2048]{1,0:T(8,128)(2,1)S(1)}, bf16[64,2048]{1,0:T(8,128)(2,1)S(1)}, u32[]{:S(2)}, u32[]{:S(2)}) collective-permute-start(bf16[64,2048]{1,0:T(8,128)(2,1)S(1)} %slice.274), channel_id=1, source_target_pairs={{0,8},{4,12},{8,0},{12,4},{16,24},{20,28},{24,16},{28,20},{1,9},{5... | collective-permute-start | bytes 786440 | tf_op jit(solution)/shard_map/ppermute | solution.py:327
  216.0 15.5 %collective-permute-start.25 = (bf16[64,2048]{1,0:T(8,128)(2,1)S(1)}, bf16[64,2048]{1,0:T(8,128)(2,1)S(1)}, u32[]{:S(2)}, u32[]{:S(2)}) collective-permute-start(bf16[64,2048]{1,0:T(8,128)(2,1)S(1)} %slice.275), channel_id=1, source_target_pairs={{0,16},{4,20},{8,24},{12,28},{16,0},{20,4},{24,8},{28,12},{1,17},{... | collective-permute-start | bytes 786440 | tf_op jit(solution)/shard_map/ppermute | solution.py:327
  218.8 16.7 %collective-permute-start.20 = (bf16[64,2048]{1,0:T(8,128)(2,1)S(1)}, bf16[64,2048]{1,0:T(8,128)(2,1)S(1)}, u32[]{:S(2)}, u32[]{:S(2)}) collective-permute-start(bf16[64,2048]{1,0:T(8,128)(2,1)S(1)} %slice.276), channel_id=1, source_target_pairs={{0,8},{4,12},{8,0},{12,4},{16,24},{20,28},{24,16},{28,20},{1,9},{5... | collective-permute-start | bytes 786440 | tf_op jit(solution)/shard_map/ppermute | solution.py:327
  294.9 56.1 %collective-permute-start.40 = (f32[16,256,128]{2,1,0:T(8,128)}, f32[16,256,128]{2,1,0:T(8,128)}, u32[]{:S(2)}, u32[]{:S(2)}) collective-permute-start(f32[16,256,128]{2,1,0:T(8,128)} %get-tuple-element.67), channel_id=1, source_target_pairs={{0,4},{4,0},{8,12},{12,8},{16,20},{20,16},{24,28},{28,24},{1,5},{5... | collective-permute-start | bytes 6291464 | tf_op jit(solution)/shard_map/ppermute | solution.py:331
  (58 other events, 380.0 us)
Sparse Core Ops, SparseCore 0:
  10.2 30.6 all-gather.5
  42.4 27.4 all-gather.11
  71.5 27.4 all-gather.9
  100.9 27.4 all-gather.7

commit v3 on v2

--- a/solution.py
+++ b/solution.py
@@ -8,7 +8,7 @@
 BF16 = jnp.bfloat16
 F32 = jnp.float32
 HIGH = lax.Precision.HIGHEST
-CHUNK_ROWS = 64
+CHUNKS = 2
 GROUP = 8
 NN = (((1,), (0,)), ((), ()))
 NT = (((1,), (1,)), ((), ()))
@@ -43,6 +43,10 @@
 
 def whole(*shape):
     return pl.BlockSpec(shape, lambda i, at: (0,) * len(shape))
+
+
+def tie(value, *before):
+    return lax.optimization_barrier((value, *before))[0]
 
 
 def cost(flops, size, exps=0):
@@ -84,11 +88,12 @@
 
 
 def inner_kernel(
-    at_ref, x_ref, y_ref, b_ref, c_ref, run_ref, run_t_ref, step_ref, skip_ref, state_ref,
-    partial_ref, grad_b_ref, grad_c_ref, col_ref, carry_ref,
-    cross, mix, grad_c_acc, rows,
+    first, last, at_ref, x_ref, y_ref, b_ref, c_ref, run_ref, run_t_ref, step_ref, skip_ref,
+    state_ref, *rest,
 ):
     del at_ref
+    held = rest[: 0 if first else 5]
+    partial_ref, col_ref, carry_ref, mix_ref, grad_c_ref, cross, rows = rest[len(held) :]
     index = pl.program_id(0)
     group = step_ref.shape[2]
     span = x_ref.shape[0]
@@ -97,8 +102,8 @@
     @pl.when(index == 0)
     def _():
         cross[...] = mm(b_ref[...], c_ref[...], NT)
-        mix[...] = jnp.zeros_like(mix)
-        grad_c_acc[...] = jnp.zeros_like(grad_c_acc)
+        mix_ref[...] = jnp.zeros_like(mix_ref) if first else held[3][...]
+        grad_c_ref[...] = jnp.zeros_like(grad_c_ref) if first else held[4][...]
 
     source = lax.broadcasted_iota(jnp.int32, (span, span), 0)
     target = lax.broadcasted_iota(jnp.int32, (span, span), 1)
@@ -113,7 +118,7 @@
         decay = jnp.exp(jnp.where(causal, run_row - run_col, -jnp.inf))
         weights = decay * cross[...]
         pairs = mm(x, y, NT)
-        mix[...] += decay * pairs * step_col
+        mix_ref[...] += decay * pairs * step_col
         terms = weights * pairs
         col_ref[0, :, j : j + 1] = jnp.sum(terms, axis=1, keepdims=True)
         rows[j : j + 1, :] = jnp.sum(terms * step_col, axis=0, keepdims=True)
@@ -122,66 +127,67 @@
         partial_ref[:, columns] = step_col * inner + skip_ref[0, j : j + 1, :] * y_wide
         state = state_ref[j]
         scaled = y_wide * jnp.exp(run_col)
-        grad_c_acc[...] += mm_wide(scaled, state)
+        grad_c_ref[...] += mm_wide(scaled, state)
         carry_ref[0, :, j : j + 1] = jnp.sum(
             scaled * mm_right(c_ref[...], state), axis=1, keepdims=True
         )
     carry_ref[0] += rows[...].T
 
-    @pl.when(index == pl.num_programs(0) - 1)
-    def _():
-        high, low = halves(mix[...])
-        grad_b_ref[...] = mm(high, c_ref[...], NN) + mm(low, c_ref[...], NN)
-        grad_c_ref[...] = (
-            grad_c_acc[...] + mm(high, b_ref[...], TN) + mm(low, b_ref[...], TN)
-        )
-
-
-def inner_part(x, y, b, c, running, running_t, steps, skip_rows, incoming):
+    if last:
+
+        @pl.when(index == pl.num_programs(0) - 1)
+        def _():
+            high, low = halves(mix_ref[...])
+            mix_ref[...] = mm(high, c_ref[...], NN) + mm(low, c_ref[...], NN)
+            grad_c_ref[...] += mm(high, b_ref[...], TN) + mm(low, b_ref[...], TN)
+
+
+def inner_part(x, y, b, c, running, running_t, steps, skip_rows, incoming, at, count, held, last):
     groups, span, group = steps.shape
     heads = groups * group
     width = x.shape[1] // heads
     states = b.shape[1]
-    block = pl.BlockSpec((span, group * width), lambda i, at: (0, i))
-    table = pl.BlockSpec((1, span, group), lambda i, at: (i, 0, 0))
+    block = pl.BlockSpec((span, group * width), lambda i, at: (0, at[0] + i))
+    table = pl.BlockSpec((1, span, group), lambda i, at: (at[0] + i, 0, 0))
+    any_place = pl.BlockSpec(memory_space=pl.ANY)
     return pl.pallas_call(
-        inner_kernel,
+        lambda *refs: inner_kernel(not held, last, *refs),
         grid_spec=pltpu.PrefetchScalarGridSpec(
             num_scalar_prefetch=1,
-            grid=(groups,),
+            grid=(count,),
             in_specs=[
                 block,
                 block,
                 whole(span, states),
                 whole(span, states),
                 table,
-                pl.BlockSpec((1, group, span), lambda i, at: (i, 0, 0)),
+                pl.BlockSpec((1, group, span), lambda i, at: (at[0] + i, 0, 0)),
                 table,
-                pl.BlockSpec((1, group, width), lambda i, at: (i, 0, 0)),
-                pl.BlockSpec((group, states, width), lambda i, at: (i, 0, 0)),
-            ],
-            out_specs=[block, whole(span, states), whole(span, states), table, table],
-            scratch_shapes=[
-                pltpu.VMEM((span, span), F32),
-                pltpu.VMEM((span, span), F32),
-                pltpu.VMEM((span, states), F32),
-                pltpu.VMEM((group, span), F32),
-            ],
+                pl.BlockSpec((1, group, width), lambda i, at: (at[0] + i, 0, 0)),
+                pl.BlockSpec((group, states, width), lambda i, at: (at[0] + i, 0, 0)),
+            ]
+            + ([any_place] * 3 + [whole(span, states)] * 2 if held else []),
+            out_specs=[block, table, table, whole(span, states), whole(span, states)],
+            scratch_shapes=[pltpu.VMEM((span, span), F32), pltpu.VMEM((group, span), F32)],
         ),
         out_shape=[
             jax.ShapeDtypeStruct((span, heads * width), F32),
+            jax.ShapeDtypeStruct((groups, span, group), F32),
+            jax.ShapeDtypeStruct((groups, span, group), F32),
             jax.ShapeDtypeStruct((span, states), F32),
             jax.ShapeDtypeStruct((span, states), F32),
-            jax.ShapeDtypeStruct((groups, span, group), F32),
-            jax.ShapeDtypeStruct((groups, span, group), F32),
         ],
+        input_output_aliases={10: 0, 11: 1, 12: 2} if held else {},
         compiler_params=PARAMS,
         cost_estimate=cost(
-            14 * span * heads * width * states,
-            8 * span * heads * width + 4 * heads * width * states,
-            heads * span * span,
-        ),
-    )(jnp.zeros((1,), jnp.int32), x, y, b, c, running, running_t, steps, skip_rows, incoming)
+            14 * span * count * group * width * states,
+            count * group * width * (8 * span + 4 * states),
+            count * group * span * span,
+        ),
+    )(
+        jnp.full((1,), at, jnp.int32), x, y, b, c, running, running_t, steps, skip_rows,
+        incoming, *held,
+    )
 
 
 def outer_kernel(
@@ -322,6 +328,38 @@
     )(core, *pieces, own, other)
 
 
+def finish_kernel(count, *refs):
+    keeps, arrived, out_ref = refs[: 2 * count], refs[2 * count : -1], refs[-1]
+    steps = pl.num_programs(0) // 2
+    rows = keeps[0].shape[0]
+    for lane in range(2):
+
+        @pl.when(pl.program_id(0) // steps == lane)
+        def _():
+            for chunk in range(count):
+                at = lane * count + chunk
+                total = keeps[at][...] + arrived[at][...].astype(F32)
+                out_ref[chunk * rows : (chunk + 1) * rows, :] = total.astype(BF16)
+
+
+def finish(keeps, arrived):
+    count = len(keeps) // 2
+    rows, half = keeps[0].shape
+    tile = min(1024, half)
+    steps = half // tile
+    place = [lambda i: (0, jnp.minimum(i, steps - 1)), lambda i: (0, jnp.maximum(i - steps, 0))]
+    specs = [pl.BlockSpec((rows, tile), place[lane]) for lane in range(2) for _ in range(count)]
+    return pl.pallas_call(
+        lambda *refs: finish_kernel(count, *refs),
+        grid=(2 * steps,),
+        in_specs=specs + specs,
+        out_specs=pl.BlockSpec((rows * count, tile), lambda i: (0, i)),
+        out_shape=jax.ShapeDtypeStruct((rows * count, 2 * half), BF16),
+        compiler_params=PARAMS,
+        cost_estimate=cost(4 * rows * count * half, 16 * rows * count * half),
+    )(*keeps, *arrived)
+
+
 def across(value, hop, chips):
     pairs = [(2 * i + core, 2 * (i ^ hop) + core) for i in range(chips) for core in range(2)]
     return lax.ppermute(value, "seq", pairs)
@@ -353,40 +391,56 @@
     return jnp.concatenate(ordered, axis=0)
 
 
-def project(grad_out, out_weight, chips, chip, core, after):
+def project(grad_out, out_weight, chips, chip, core, before):
     span = grad_out.shape[0]
     both = 2 * out_weight.shape[1]
     other = other_core(out_weight, chips)
     core_at = core.astype(jnp.int32).reshape(1)
-    rows = min(CHUNK_ROWS, span)
-    done = []
-    for start in range(0, span, rows):
-        full = lax.all_gather(grad_out[start : start + rows], "head", axis=1, tiled=True)
-        base = chip if start == 0 else chip + after
-        blocks = []
-        for hop in range(chips):
-            block = lax.dynamic_slice_in_dim(full, (base ^ hop) * both, both, 1)
-            blocks.append(across(block, hop, chips) if hop else block)
-        pieces = []
-        for lane, order in enumerate(orders(chips)):
-            hops = [0]
-            for bit in order[::-1]:
-                hops = hops + [hop | bit for hop in hops]
-            send, keep = partial_sums(blocks, hops, out_weight, other, lane, core_at)
-            for bit in order:
-                keep = keep + across(send, bit, chips).astype(F32)
-                size = keep.shape[0] // 2
-                if size >= rows:
+    rows = span // CHUNKS
+    fulls = [
+        lax.all_gather(grad_out[i * rows : (i + 1) * rows], "head", axis=1, tiled=True)
+        for i in range(CHUNKS)
+    ]
+    lanes = []
+    for order in orders(chips):
+        hops = [0]
+        for bit in order[::-1]:
+            hops = hops + [hop | bit for hop in hops]
+        lanes.append((order, hops))
+    waiting = [[], []]
+
+    def reduce_last(blocks):
+        for lane, (order, _) in enumerate(lanes):
+            keep, send = waiting[lane][-1]
+            for step, bit in enumerate(order):
+                arrived = across(send, bit, chips)
+                if step == 0 and blocks is not None:
+                    arrived = tie(arrived, *blocks)
+                if step < len(order) - 1:
+                    keep = keep + arrived.astype(F32)
+                    size = keep.shape[0] // 2
                     send = keep[size:].astype(BF16)
                     keep = keep[:size]
-            pieces.append(keep.astype(BF16))
-        done.append(jnp.concatenate(pieces, axis=1))
-    return jnp.concatenate(done, axis=0)
-
-
-def exchange(mine, to_other, ends, chips, chip, core, reverse):
+            waiting[lane][-1] = (keep, arrived)
+
+    for chunk in range(CHUNKS):
+        full = tie(fulls[chunk], *before[chunk], *[w[-1][1] for w in waiting if w])
+        own = [
+            lax.dynamic_slice_in_dim(full, (chip ^ hop) * both, both, 1) for hop in range(chips)
+        ]
+        if chunk:
+            reduce_last(own)
+        blocks = [across(block, hop, chips) if hop else block for hop, block in enumerate(own)]
+        for lane, (_, hops) in enumerate(lanes):
+            send, keep = partial_sums(blocks, hops, out_weight, other, lane, core_at)
+            waiting[lane].append((keep, send))
+    reduce_last(None)
+    ends = waiting[0] + waiting[1]
+    return finish([keep for keep, _ in ends], [arrived for _, arrived in ends])
+
+
+def exchange(mine, theirs, ends, chips, chip, core, reverse, fill):
     half = mine.shape[0]
-    theirs = other_core(to_other, chips)
     ends = lax.dynamic_slice_in_dim(ends, core * half, half, 1)
     by_chip = ends.reshape(chips, 2, half)
     own_ends = lax.dynamic_index_in_dim(by_chip, chip, 0, False)
@@ -405,23 +459,33 @@
     second = jnp.where(near_first, theirs, mine)
     first_end, second_end = (own_ends[1], own_ends[0]) if reverse else (own_ends[0], own_ends[1])
     chip_state = scale(second_end, first) + second
+    lanes = []
+    for lane in range(2):
+        heads = slice(lane * (half // 2), (lane + 1) * (half // 2))
+        lanes.append((heads, {0: chip_state[heads].astype(BF16)}))
+    bits = orders(chips)
+    for step in range(len(bits[0])):
+        last = step == len(bits[0]) - 1
+        sent = []
+        for order, (heads, items) in zip(bits, lanes):
+            if last:
+                target = chip ^ order[step]
+                total = sum(scale(carry(chip ^ o, target)[heads], i) for o, i in items.items())
+                sent.append({0: total.astype(BF16)})
+            else:
+                sent.append(dict(items))
+        done = fill(step, [item for items in sent for item in items.values()])
+        for order, (heads, items), going in zip(bits, lanes, sent):
+            for o, item in going.items():
+                items[o | order[step]] = tie(across(item, order[step], chips), *done)
     totals = []
-    for lane, order in enumerate(orders(chips)):
-        heads = slice(lane * (half // 2), (lane + 1) * (half // 2))
-        items = {0: chip_state[heads].astype(BF16)}
-        for bit in order[:-1]:
-            items.update({o | bit: across(item, bit, chips) for o, item in items.items()})
-        bit = order[-1]
-        gather = lambda target: sum(
-            scale(carry(chip ^ o, target)[heads], item) for o, item in items.items()
-        )
-        arrived = across(gather(chip ^ bit).astype(BF16), bit, chips)
-        totals.append(gather(chip) + arrived.astype(F32))
+    for order, (heads, items) in zip(bits, lanes):
+        arrived = items.pop(order[-1])
+        total = sum(scale(carry(chip ^ o, chip)[heads], i) for o, i in items.items())
+        totals.append(total + arrived.astype(F32))
     total = jnp.concatenate(totals, axis=0)
     after = scale(first_end, total) + first
-    for_mine = jnp.where(near_first, total, after)
-    for_theirs = jnp.where(near_first, after, total)
-    return for_mine, other_core(for_theirs, chips)
+    return jnp.where(near_first, total, after), jnp.where(near_first, after, total)
 
 
 def local(grad_out, out_weight, ssm_input, step_size, log_decay, b_in, c_in, skip):
@@ -441,42 +505,67 @@
     running = jnp.dot(upto, log_decay, precision=HIGH)
     ends = lax.all_gather(running[-1], "seq")
     tail = jnp.exp(running[-1:] - running)
+    rise = by_group(jnp.exp(running))
     running_g = by_group(running)
     running_t = running.T.reshape(groups, group, span)
     steps_g = by_group(step_size)
     skip_rows = jnp.broadcast_to(skip.reshape(groups, group, 1), (groups, group, width))
-
-    def states(values, scale, rows, reverse):
-        rows_t = rows.T
+    b_rows, c_rows = b_in.T, c_in.T
+
+    def span_both(values, scale, rows_t):
         to_other = span_states(values, scale, rows_t, other_at, groups // 2)
-        mine = span_states(values, scale, rows_t, mine_at, groups // 2)
-        return exchange(mine, to_other, ends, chips, chip, core, reverse)
-
-    for_mine, for_other = states(ssm_input, by_group(step_size * tail), b_in, False)
+        theirs = other_core(to_other, chips)
+        return span_states(values, scale, rows_t, mine_at, groups // 2), theirs
+
+    last_sent = []
+
+    def note(step, sent):
+        last_sent[:] = sent
+        return []
+
+    mine, theirs = span_both(ssm_input, by_group(step_size * tail), b_rows)
+    for_mine, for_theirs = exchange(mine, theirs, ends, chips, chip, core, False, note)
+    arrived = other_core(for_theirs, chips)
     incoming = jnp.where(
         core == 0,
-        jnp.concatenate([for_mine, for_other], axis=0),
-        jnp.concatenate([for_other, for_mine], axis=0),
-    )
-    corner = incoming[0, 0, 0]
-    after = (corner != corner).astype(chip.dtype)
-
-    grad_y = project(grad_out, out_weight, chips, chip, core, after)
-    out_mine, out_other = states(grad_y, by_group(jnp.exp(running)), c_in, True)
-    part, grad_b, grad_c, cols, carries = inner_part(
-        ssm_input, grad_y, b_in, c_in, running_g, running_t, steps_g, skip_rows, incoming
-    )
-    grad_c = sum_over_heads(grad_c)
+        jnp.concatenate([for_mine, arrived], axis=0),
+        jnp.concatenate([arrived, for_mine], axis=0),
+    )
+    tables = (running_g, running_t, steps_g, skip_rows)
+    before = [[*last_sent, *tables, rise, c_rows]] + [[incoming]] * (CHUNKS - 1)
+    grad_y = project(grad_out, out_weight, chips, chip, core, before)
+
+    few = max(1, groups // 4)
+    counts = [few, groups - 2 * few, few]
+    held = ()
+
+    def fill(step, sent):
+        nonlocal held
+        count = counts[step] if step < len(counts) else 0
+        if count:
+            held = inner_part(
+                ssm_input, grad_y, b_in, c_in, tie(running_g, *sent), running_t, steps_g,
+                skip_rows, incoming, sum(counts[:step]), count, held, step == len(counts) - 1,
+            )
+        return list(held)
+
+    mine, theirs = span_both(grad_y, rise, c_rows)
+    theirs = tie(theirs, *fill(0, [mine]))
+    for_mine, for_theirs = exchange(
+        mine, theirs, ends, chips, chip, core, True, lambda step, sent: fill(step + 1, sent)
+    )
+    for_other = other_core(for_theirs, chips)
+    part, cols, carries, grad_b, grad_c = held
     shared = (running_g, steps_g, cols, carries)
     grad_x, grad_b, grad_step, grad_decay = outer_part(
-        ssm_input, part, b_in, incoming, out_mine, *shared, grad_b, mine_at, None
+        ssm_input, part, b_in, incoming, for_mine, *shared, grad_b, mine_at, None
     )
     grad_x, grad_b, grad_step, grad_decay = outer_part(
-        ssm_input, part, b_in, incoming, out_other, *shared, grad_b, other_at,
+        ssm_input, part, b_in, incoming, for_other, *shared, grad_b, other_at,
         (grad_x, grad_step, grad_decay),
     )
-    grad_b = sum_over_heads(grad_b)
-    return (grad_x, flat(grad_step), flat(grad_decay), grad_b, grad_c)
+    both = sum_over_heads(jnp.stack([grad_b, grad_c], axis=1))
+    return (grad_x, flat(grad_step), flat(grad_decay), both[:, 0], both[:, 1])
 
 
 def solution(mesh):

time: 390 us -> 343 us (0.88)
  starting transfers between devices: 62.5 us -> 37.6 us
  other arithmetic: 43.6 us -> 33.1 us
  Pallas kernels: 90.1 us -> 80.9 us
  waiting for transfers between devices: 132 us -> 137 us
    ppermute x36 -> x22, waiting for transfers between devices: 72.8 us -> 119 us  [across(): return lax.ppermute(value, 'seq', pairs)]
    all_gather x4 -> x2, waiting for transfers between devices: 38.8 us -> 0.02 us  [project(): lax.all_gather(grad_out[i * rows:(i + 1) * rows], 'head', axis=1, tiled=T...]
    ppermute x36 -> x22, starting transfers between devices: 45.7 us -> 25.9 us  [across(): return lax.ppermute(value, 'seq', pairs)]
    pallas_call x8 -> x4, Pallas kernels: 46.1 us -> 29.2 us  [partial_sums(): pl.pallas_call(lambda *refs: project_kernel(hops, *refs), grid_spec=pltpu...]
    concatenate x1 -> x0, other arithmetic: 13.3 us -> none  [project(): return jnp.concatenate(done, axis=0)]
    pallas_call x1 -> x4, Pallas kernels: 19.9 us -> 27.7 us  [the longest x3 23.7 us: inner_part(): pl.pallas_call(lambda *refs: inner_kernel(not held, last, *refs), grid_sp...]
    dynamic_slice x4 -> x2, local copies, waits for them, and re-layouts: 7.81 us -> 3.84 us  [project(): lax.dynamic_slice_in_dim(full, (chip ^ hop) * both, both, 1)]
    unnamed x68 -> x98, local copies, waits for them, and re-layouts: 12.2 us -> 15.5 us
  transfers between devices with their start and end apart: 57 -> 35, of which waited for: 27 -> 22; matrix products, arithmetic and copies ran while one was open for 9% -> 10% of each run, Pallas kernels for 21% -> 19%
where the time goes in v3:
time: 343 us; the launch traced here: 342 us
  waiting for transfers between devices  137 us (40%)
  Pallas kernels  80.9 us (24%)
  starting transfers between devices  37.6 us (11%)
  other arithmetic  33.1 us (10%)
  local copies, waits for them, and re-layouts  28 us (8%)
  between operations  14.8 us (4%)
  blocking collectives  9.76 us (3%)
    ppermute x22, waiting for transfers between devices, across(): return lax.ppermute(value, 'seq', pairs)  119 us
    pallas_call x4, Pallas kernels, partial_sums(): pl.pallas_call(lambda *refs: project_kernel(hops, *refs), grid_spec=pltpu...  29.2 us
    ppermute x22, starting transfers between devices, across(): return lax.ppermute(value, 'seq', pairs)  25.9 us
    pallas_call x3, Pallas kernels, inner_part(): pl.pallas_call(lambda *refs: inner_kernel(not held, last, *refs), grid_sp...  23.7 us
    pallas_call x2, Pallas kernels, outer_part(): pl.pallas_call(outer_kernel, grid_spec=pltpu.PrefetchScalarGridSpec(num_s...  15.9 us
    unnamed x98, local copies, waits for them, and re-layouts  15.5 us
    ppermute x3, waiting for transfers between devices, sum_over_heads(): lax.ppermute(total, 'head', shift(hop))  10 us
    all_gather x1, blocking collectives, local(): ends = lax.all_gather(running[-1], 'seq')  9.76 us
  transfers between devices with their start and end apart: 35, of which 22 were waited for; matrix products, arithmetic and copies ran while one was open for 10% of the time, Pallas kernels for 19%

profile of v3, /device:TPU:0, one launch (start us, length us, event | category | flops | bytes accessed | tf_op | source)
XLA Modules:
  0.0 341.8 jit_solution(17516334871669959095)
XLA Ops:
  16.3 9.8 %all-gather = f32[8,1,32]{2,1,0:T(1,128)S(1)} all-gather(f32[1,1,32]{2,1,0:T(1,128)S(1)} %bitcast.100), channel_id=1, replica_groups=mesh['seq'=8,'head'=4] {'seq'}, dimensions={0}, use_global_device_ids=true | all-gather | bytes 1152 | tf_op jit(solution)/shard_map/all_gather | solution.py:506
  35.0 11.2 %collective-permute-done.1 = bf16[8,256,128]{2,1,0:T(8,128)(2,1)} collective-permute-done((bf16[8,256,128]{2,1,0:T(8,128)(2,1)}, bf16[8,256,128]{2,1,0:T(8,128)(2,1)}, u32[]{:S(2)}, u32[]{:S(2)}) %collective-permute-start.1) | collective-permute-done | bytes 524320 | tf_op jit(solution)/shard_map/ppermute | solution.py:365
  49.2 11.7 %collective-permute-done.8 = bf16[8,256,128]{2,1,0:T(8,128)(2,1)S(1)} collective-permute-done((bf16[8,256,128]{2,1,0:T(8,128)(2,1)S(1)}, bf16[8,256,128]{2,1,0:T(8,128)(2,1)S(1)}, u32[]{:S(2)}, u32[]{:S(2)}) %collective-permute-start.8) | collective-permute-done | bytes 524320 | tf_op jit(solution)/shard_map/ppermute | solution.py:365
  60.9 2.7 fusion.7
  65.2 11.2 %collective-permute-done.9 = bf16[8,256,128]{2,1,0:T(8,128)(2,1)} collective-permute-done((bf16[8,256,128]{2,1,0:T(8,128)(2,1)}, bf16[8,256,128]{2,1,0:T(8,128)(2,1)}, u32[]{:S(2)}, u32[]{:S(2)}) %collective-permute-start.9) | collective-permute-done | bytes 524320 | tf_op jit(solution)/shard_map/ppermute | solution.py:365
  78.0 3.9 %fusion.3 = (f32[16,256,128]{2,1,0:T(8,128)}, f32[16,256,128]{2,1,0:T(8,128)}) fusion(f32[8,256,128]{2,1,0:T(8,128)S(1)} %fusion.11, f32[8,256,128]{2,1,0:T(8,128)} %get-tuple-element.112, f32[16]{0:T(128)S(1)} %get-tuple-element.129, pred[]{:T(512)S(6)} %eq.15, f32[16,256,128]{2,1,0:T(8,128)S(1)} %copy-done.7, f32[16,256,128]{2,1,0:T(8,128)} %collective-permute-done), kind=kLoop, calls=%fused_computation.13 | loop fusion | flops 3145728 | bytes 10485825 | tf_op jit(solution)/shard_map/jit(_where)/select_n | solution.py:488
  89.1 4.9 %maximum_select_fusion.refs_9_.state_ref = f32[32,256,128]{2,1,0:T(8,128)} fusion(f32[16,256,128]{2,1,0:T(8,128)} %collective-permute-done.10, f32[16,256,128]{2,1,0:T(8,128)S(1)} %copy-done.34, pred[]{:T(512)S(6)} %eq.15), kind=kLoop, calls=%fused_computation | loop fusion | flops 3145728 | bytes 8388609 | tf_op jit(solution)/shard_map/jit(_where)/select_n | solution.py:529
  94.1 7.2 %collective-permute-done.5.refs_4_ = bf16[128,2048]{1,0:T(8,128)(2,1)S(1)} collective-permute-done((bf16[128,2048]{1,0:T(8,128)(2,1)S(1)}, bf16[128,2048]{1,0:T(8,128)(2,1)S(1)}, u32[]{:S(2)}, u32[]{:S(2)}) %collective-permute-start.5) | collective-permute-done | bytes 524320 | tf_op jit(solution)/shard_map/ppermute | solution.py:365
  101.3 10.8 %collective-permute-done.4.refs_3_ = bf16[128,2048]{1,0:T(8,128)(2,1)S(1)} collective-permute-done((bf16[128,2048]{1,0:T(8,128)(2,1)S(1)}, bf16[128,2048]{1,0:T(8,128)(2,1)S(1)}, u32[]{:S(2)}, u32[]{:S(2)}) %collective-permute-start.4) | collective-permute-done | bytes 524320 | tf_op jit(solution)/shard_map/ppermute | solution.py:365
  112.2 7.3 %shard_map.122 = (bf16[256,2048]{1,0:T(8,128)(2,1)S(1)}, f32[256,2048]{1,0:T(8,128)S(1)}) custom-call(s32[1]{0:T(128)} %bitcast.1.refs_0_, bf16[128,2048]{1,0:T(8,128)(2,1)S(1)} %get-tuple-element.105.refs_1_, bf16[128,2048]{1,0:T(8,128)(2,1)S(1)} %collective-permute-done.3.refs_2_, bf16[128,2048]{1,0:T(8,128)(2,1)S(1)} %collective-permute-done.4.refs_3_, ...), custom_call_target="tpu_custom_call" | custom-call | flops 4294967296 | bytes 11534336 | tf_op jit(solution)/shard_map/pallas_call | solution.py:311
  121.8 7.3 %shard_map.121 = (bf16[256,2048]{1,0:T(8,128)(2,1)S(1)}, f32[256,2048]{1,0:T(8,128)S(1)}) custom-call(s32[1]{0:T(128)} %bitcast.1.refs_0_, bf16[128,2048]{1,0:T(8,128)(2,1)S(1)} %get-tuple-element.105.refs_1_, bf16[128,2048]{1,0:T(8,128)(2,1)S(1)} %collective-permute-done.3.refs_2_, bf16[128,2048]{1,0:T(8,128)(2,1)S(1)} %collective-permute-done.4.refs_3_, ...), custom_call_target="tpu_custom_call" | custom-call | flops 4294967296 | bytes 11534336 | tf_op jit(solution)/shard_map/pallas_call | solution.py:311
  139.1 10.0 %collective-permute-done.13.refs_4_ = bf16[128,2048]{1,0:T(8,128)(2,1)S(1)} collective-permute-done((bf16[128,2048]{1,0:T(8,128)(2,1)S(1)}, bf16[128,2048]{1,0:T(8,128)(2,1)S(1)}, u32[]{:S(2)}, u32[]{:S(2)}) %collective-permute-start.13) | collective-permute-done | bytes 524320 | tf_op jit(solution)/shard_map/ppermute | solution.py:365
  149.1 10.3 %collective-permute-done.12.refs_3_ = bf16[128,2048]{1,0:T(8,128)(2,1)S(1)} collective-permute-done((bf16[128,2048]{1,0:T(8,128)(2,1)S(1)}, bf16[128,2048]{1,0:T(8,128)(2,1)S(1)}, u32[]{:S(2)}, u32[]{:S(2)}) %collective-permute-start.12) | collective-permute-done | bytes 524320 | tf_op jit(solution)/shard_map/ppermute | solution.py:365
  160.3 7.3 %shard_map.124 = (bf16[256,2048]{1,0:T(8,128)(2,1)S(1)}, f32[256,2048]{1,0:T(8,128)S(1)}) custom-call(s32[1]{0:T(128)} %bitcast.1.refs_0_, bf16[128,2048]{1,0:T(8,128)(2,1)S(1)} %get-tuple-element.101.refs_1_, bf16[128,2048]{1,0:T(8,128)(2,1)S(1)} %collective-permute-done.11.refs_2_, bf16[128,2048]{1,0:T(8,128)(2,1)S(1)} %collective-permute-done.12.refs_3_, ...), custom_call_target="tpu_custom_call" | custom-call | flops 4294967296 | bytes 11534336 | tf_op jit(solution)/shard_map/pallas_call | solution.py:311
  168.3 7.3 %shard_map.123 = (bf16[256,2048]{1,0:T(8,128)(2,1)S(1)}, f32[256,2048]{1,0:T(8,128)S(1)}) custom-call(s32[1]{0:T(128)} %bitcast.1.refs_0_, bf16[128,2048]{1,0:T(8,128)(2,1)S(1)} %get-tuple-element.101.refs_1_, bf16[128,2048]{1,0:T(8,128)(2,1)S(1)} %collective-permute-done.11.refs_2_, bf16[128,2048]{1,0:T(8,128)(2,1)S(1)} %collective-permute-done.12.refs_3_, ...), custom_call_target="tpu_custom_call" | custom-call | flops 4294967296 | bytes 11534336 | tf_op jit(solution)/shard_map/pallas_call | solution.py:311
  177.1 5.8 %collective-permute-done.7 = bf16[256,2048]{1,0:T(8,128)(2,1)} collective-permute-done((bf16[256,2048]{1,0:T(8,128)(2,1)S(1)}, bf16[256,2048]{1,0:T(8,128)(2,1)}, u32[]{:S(2)}, u32[]{:S(2)}) %collective-permute-start.7) | collective-permute-done | bytes 1048608 | tf_op jit(solution)/shard_map/ppermute | solution.py:365
  188.4 16.1 %collective-permute-done.16 = bf16[256,2048]{1,0:T(8,128)(2,1)} collective-permute-done((bf16[256,2048]{1,0:T(8,128)(2,1)S(1)}, bf16[256,2048]{1,0:T(8,128)(2,1)}, u32[]{:S(2)}, u32[]{:S(2)}) %collective-permute-start.16) | collective-permute-done | bytes 1048608 | tf_op jit(solution)/shard_map/ppermute | solution.py:365
  210.0 5.6 %collective-permute-done.17.refs_4_ = bf16[128,2048]{1,0:T(8,128)(2,1)S(1)} collective-permute-done((bf16[128,2048]{1,0:T(8,128)(2,1)S(1)}, bf16[128,2048]{1,0:T(8,128)(2,1)S(1)}, u32[]{:S(2)}, u32[]{:S(2)}) %collective-permute-start.17) | collective-permute-done | bytes 524320 | tf_op jit(solution)/shard_map/ppermute | solution.py:365
  216.5 10.3 %collective-permute-done.20.refs_7_ = bf16[128,2048]{1,0:T(8,128)(2,1)S(1)} collective-permute-done((bf16[128,2048]{1,0:T(8,128)(2,1)S(1)}, bf16[128,2048]{1,0:T(8,128)(2,1)S(1)}, u32[]{:S(2)}, u32[]{:S(2)}) %collective-permute-start.20) | collective-permute-done | bytes 524320 | tf_op jit(solution)/shard_map/ppermute | solution.py:365
  226.8 4.0 %shard_map.125.v_ref.refs_2_ = bf16[256,4096]{1,0:T(8,128)(2,1)} custom-call(f32[128,2048]{1,0:T(8,128)S(1)} %slice.156.refs_0_, f32[128,2048]{1,0:T(8,128)S(1)} %slice.157.refs_1_, f32[128,2048]{1,0:T(8,128)S(1)} %slice.158.refs_2_, f32[128,2048]{1,0:T(8,128)} %slice.159.refs_3_, bf16[128,2048]{1,0:T(8,128)(2,1)S(1)} %collective-permute-done.17.refs_4_, ...), custom_call_target="tpu_custom_call" | custom-call | flops 2097152 | bytes 8388608 | tf_op jit(solution)/shard_map/pallas_call | solution.py:352
  239.2 6.3 %shard_map.128 = (f32[256,4096]{1,0:T(8,128)}, f32[4,256,8]{2,1,0:T(8,128)S(1)}, f32[4,256,8]{2,1,0:T(8,128)S(1)}, f32[256,256]{1,0:T(8,128)S(1)}, f32[256,256]{1,0:T(8,128)S(1)}) custom-call(s32[1]{0:T(128)} %constant.123.clone.1.refs_0_, bf16[256,4096]{1,0:T(8,128)(2,1)S(1)} %copy-done.3, bf16[256,4096]{1,0:T(8,128)(2,1)} %shard_map.125.v_ref.refs_2_, ...), custom_call_target="tpu_custom_call" | custom-call | flops 939524096 | bytes 3145728 | tf_op jit(solution)/shard_map/pallas_call | solution.py:153
  250.0 11.0 %shard_map.129 = (f32[256,4096]{1,0:T(8,128)}, f32[4,256,8]{2,1,0:T(8,128)S(1)}, f32[4,256,8]{2,1,0:T(8,128)S(1)}, f32[256,256]{1,0:T(8,128)S(1)}, f32[256,256]{1,0:T(8,128)S(1)}) custom-call(s32[1]{0:T(128)} %constant.124.clone.1.refs_0_, bf16[256,4096]{1,0:T(8,128)(2,1)S(1)} %copy-done.3, ...), custom_call_target="tpu_custom_call", output_to_operand_aliasing={{0}: (10, {}), {1}: (11, {}), {2}: (12, {})} | custom-call | flops 1879048192 | bytes 6291456 | tf_op jit(solution)/shard_map/pallas_call | solution.py:153
  265.9 6.4 %shard_map.130 = (f32[256,4096]{1,0:T(8,128)}, f32[4,256,8]{2,1,0:T(8,128)S(1)}, f32[4,256,8]{2,1,0:T(8,128)S(1)}, f32[256,256]{1,0:T(8,128)S(1)}, f32[256,256]{1,0:T(8,128)S(1)}) custom-call(s32[1]{0:T(128)} %constant.111.clone.1.refs_0_, bf16[256,4096]{1,0:T(8,128)(2,1)S(1)} %copy-done.3, ...), custom_call_target="tpu_custom_call", output_to_operand_aliasing={{0}: (10, {}), {1}: (11, {}), {2}: (12, {})} | custom-call | flops 939524096 | bytes 3145728 | tf_op jit(solution)/shard_map/pallas_call | solution.py:153
  272.3 4.7 %collective-permute-done.25 = bf16[8,256,128]{2,1,0:T(8,128)(2,1)S(1)} collective-permute-done((bf16[8,256,128]{2,1,0:T(8,128)(2,1)S(1)}, bf16[8,256,128]{2,1,0:T(8,128)(2,1)S(1)}, u32[]{:S(2)}, u32[]{:S(2)}) %collective-permute-start.25) | collective-permute-done | bytes 524320 | tf_op jit(solution)/shard_map/ppermute | solution.py:365
  278.0 4.4 %fusion = (f32[16,256,128]{2,1,0:T(8,128)}, f32[16,256,128]{2,1,0:T(8,128)}) fusion(f32[8,256,128]{2,1,0:T(8,128)S(1)} %get-tuple-element.107, f32[8,256,128]{2,1,0:T(8,128)S(1)} %get-tuple-element.106, f32[16]{0:T(128)S(1)} %copy-done.39, pred[]{:T(512)S(6)} %ne.47, f32[16,256,128]{2,1,0:T(8,128)S(1)} %shard_map.126, f32[16,256,128]{2,1,0:T(8,128)} %collective-permute-done.21), kind=kLoop, calls=%fused_computation.4 | loop fusion | flops 3145728 | bytes 10485825 | tf_op jit(solution)/shard_map/jit(_where)/select_n | solution.py:488
  284.5 7.9 %shard_map.131 = (bf16[256,4096]{1,0:T(8,128)(2,1)}, f32[256,256]{1,0:T(8,128)S(1)}, f32[4,256,8]{2,1,0:T(8,128)S(1)}, f32[4,256,8]{2,1,0:T(8,128)S(1)}) custom-call(s32[1]{0:T(128)} %bitcast.6.at_ref, bf16[256,4096]{1,0:T(8,128)(2,1)S(1)} %copy-done.3, f32[256,4096]{1,0:T(8,128)} %get-tuple-element.76.part_ref, bf16[256,256]{1,0:T(8,128)(2,1)S(1)} %copy-done.12, ...), custom_call_target="tpu_custom_call" | custom-call | flops 1073741824 | bytes 8388608 | tf_op jit(solution)/shard_map/pallas_call | solution.py:247
  292.4 8.0 %shard_map.132 = (bf16[256,4096]{1,0:T(8,128)(2,1)}, f32[256,256]{1,0:T(8,128)}, f32[4,256,8]{2,1,0:T(8,128)S(1)}, f32[4,256,8]{2,1,0:T(8,128)S(1)}) custom-call(s32[1]{0:T(128)} %bitcast.at_ref, bf16[256,4096]{1,0:T(8,128)(2,1)S(1)} %copy-done.3, ...), custom_call_target="tpu_custom_call", output_to_operand_aliasing={{0}: (11, {}), {2}: (12, {}), {3}: (13, {})} | custom-call | flops 1073741824 | bytes 8388608 | tf_op jit(solution)/shard_map/pallas_call | solution.py:247
  304.6 2.6 collective-permute-start.28
  308.6 2.7 collective-permute-done.27
  311.2 5.2 %collective-permute-done.28 = f32[64,2,256]{2,0,1:T(8,128)S(1)} collective-permute-done((f32[64,2,256]{2,0,1:T(8,128)S(1)}, f32[64,2,256]{2,0,1:T(8,128)S(1)}, u32[]{:S(2)}, u32[]{:S(2)}) %collective-permute-start.28) | collective-permute-done | bytes 131104 | tf_op jit(solution)/shard_map/ppermute | solution.py:385
  317.4 4.4 %collective-permute-start.32 = (f32[64,2,256]{2,0,1:T(8,128)S(1)}, f32[64,2,256]{2,0,1:T(8,128)S(1)}, u32[]{:S(2)}, u32[]{:S(2)}) collective-permute-start(f32[64,2,256]{2,0,1:T(8,128)S(1)} %fusion.28), channel_id=1, source_target_pairs={{0,3},{1,0},{2,1},{3,2},{4,7},{5,4},{6,5},{7,6},{8,11},{9,8},{10,9... | collective-permute-start | bytes 393224 | tf_op jit(solution)/shard_map/ppermute | solution.py:386
  325.7 8.3 %collective-permute-done.31 = f32[64,2,256]{2,0,1:T(8,128)S(1)} collective-permute-done((f32[64,2,256]{2,0,1:T(8,128)S(1)}, f32[64,2,256]{2,0,1:T(8,128)S(1)}, u32[]{:S(2)}, u32[]{:S(2)}) %collective-permute-start.31) | collective-permute-done | bytes 131104 | tf_op jit(solution)/shard_map/ppermute | solution.py:386
  (218 shorter events, 90.5 us)
Async XLA Ops:
  7.2 76.4 %all-gather.4.cloned.1.call-start = ((), (), s32[]{:S(2)}) async-start(), calls=%async_computation | async-start | bytes 2621440 | tf_op jit(solution)/shard_map/all_gather | solution.py:401
  7.2 104.9 %collective-permute-start.6 = (bf16[4096,1024]{1,0:T(8,128)(2,1)}, bf16[4096,1024]{1,0:T(8,128)(2,1)}, u32[]{:S(2)}, u32[]{:S(2)}) collective-permute-start(bf16[4096,1024]{1,0:T(8,128)(2,1)} %refs_5_.7), channel_id=1, source_target_pairs={{0,4},{4,0},{8,12},{12,8},{16,20},{20,16},{24,28},{28,24},{1,5},{5... | collective-permute-start | bytes 25165832 | tf_op jit(solution)/shard_map/ppermute | solution.py:369
  14.6 13.9 %collective-permute-start = (f32[16,256,128]{2,1,0:T(8,128)}, f32[16,256,128]{2,1,0:T(8,128)}, u32[]{:S(2)}, u32[]{:S(2)}) collective-permute-start(f32[16,256,128]{2,1,0:T(8,128)} %shard_map.120), channel_id=1, source_target_pairs={{0,4},{4,0},{8,12},{12,8},{16,20},{20,16},{24,28},{28,24},{1,5},{5... | collective-permute-start | bytes 6291464 | tf_op jit(solution)/shard_map/ppermute | solution.py:369
  16.2 115.2 %all-gather.6.cloned.1.call-start = ((), (), s32[]{:S(2)}) async-start(), calls=%async_computation.1 | async-start | bytes 2621440 | tf_op jit(solution)/shard_map/all_gather | solution.py:401
  31.7 14.5 %collective-permute-start.1 = (bf16[8,256,128]{2,1,0:T(8,128)(2,1)}, bf16[8,256,128]{2,1,0:T(8,128)(2,1)}, u32[]{:S(2)}, u32[]{:S(2)}) collective-permute-start(bf16[8,256,128]{2,1,0:T(8,128)(2,1)} %get-tuple-element.117), channel_id=1, source_target_pairs={{0,8},{4,12},{8,0},{12,4},{16,24},{20,28},{24,16},{28,20},{1,9},{5... | collective-permute-start | bytes 1572872 | tf_op jit(solution)/shard_map/ppermute | solution.py:365
  33.8 15.4 %collective-permute-start.2 = (bf16[8,256,128]{2,1,0:T(8,128)(2,1)}, bf16[8,256,128]{2,1,0:T(8,128)(2,1)S(1)}, u32[]{:S(2)}, u32[]{:S(2)}) collective-permute-start(bf16[8,256,128]{2,1,0:T(8,128)(2,1)} %get-tuple-element.116), channel_id=1, source_target_pairs={{0,16},{4,20},{8,24},{12,28},{16,0},{20,4},{24,8},{28,12},{1,17},{... | collective-permute-start | bytes 1572872 | tf_op jit(solution)/shard_map/ppermute | solution.py:365
  47.5 13.4 %collective-permute-start.8 = (bf16[8,256,128]{2,1,0:T(8,128)(2,1)S(1)}, bf16[8,256,128]{2,1,0:T(8,128)(2,1)S(1)}, u32[]{:S(2)}, u32[]{:S(2)}) collective-permute-start(bf16[8,256,128]{2,1,0:T(8,128)(2,1)S(1)} %fusion.5), channel_id=1, source_target_pairs={{0,16},{4,20},{8,24},{12,28},{16,0},{20,4},{24,8},{28,12},{1,17},{... | collective-permute-start | bytes 1572872 | tf_op jit(solution)/shard_map/ppermute | solution.py:365
  63.6 12.8 %collective-permute-start.9 = (bf16[8,256,128]{2,1,0:T(8,128)(2,1)}, bf16[8,256,128]{2,1,0:T(8,128)(2,1)}, u32[]{:S(2)}, u32[]{:S(2)}) collective-permute-start(bf16[8,256,128]{2,1,0:T(8,128)(2,1)} %get-tuple-element.113), channel_id=1, source_target_pairs={{0,8},{4,12},{8,0},{12,4},{16,24},{20,28},{24,16},{28,20},{1,9},{5... | collective-permute-start | bytes 1572872 | tf_op jit(solution)/shard_map/ppermute | solution.py:365
  85.6 15.7 %collective-permute-start.5 = (bf16[128,2048]{1,0:T(8,128)(2,1)S(1)}, bf16[128,2048]{1,0:T(8,128)(2,1)S(1)}, u32[]{:S(2)}, u32[]{:S(2)}) collective-permute-start(bf16[128,2048]{1,0:T(8,128)(2,1)S(1)} %get-tuple-element.102), channel_id=1, source_target_pairs={{0,24},{4,28},{8,16},{12,20},{16,8},{20,12},{24,0},{28,4},{1,25},{... | collective-permute-start | bytes 1572872 | tf_op jit(solution)/shard_map/ppermute | solution.py:365
  87.7 24.4 %collective-permute-start.4 = (bf16[128,2048]{1,0:T(8,128)(2,1)S(1)}, bf16[128,2048]{1,0:T(8,128)(2,1)S(1)}, u32[]{:S(2)}, u32[]{:S(2)}) collective-permute-start(bf16[128,2048]{1,0:T(8,128)(2,1)S(1)} %get-tuple-element.103), channel_id=1, source_target_pairs={{0,16},{4,20},{8,24},{12,28},{16,0},{20,4},{24,8},{28,12},{1,17},{... | collective-permute-start | bytes 1572872 | tf_op jit(solution)/shard_map/ppermute | solution.py:365
  88.6 23.6 %collective-permute-start.3 = (bf16[128,2048]{1,0:T(8,128)(2,1)S(1)}, bf16[128,2048]{1,0:T(8,128)(2,1)S(1)}, u32[]{:S(2)}, u32[]{:S(2)}) collective-permute-start(bf16[128,2048]{1,0:T(8,128)(2,1)S(1)} %get-tuple-element.104), channel_id=1, source_target_pairs={{0,8},{4,12},{8,0},{12,4},{16,24},{20,28},{24,16},{28,20},{1,9},{5... | collective-permute-start | bytes 1572872 | tf_op jit(solution)/shard_map/ppermute | solution.py:365
  133.3 15.8 %collective-permute-start.13 = (bf16[128,2048]{1,0:T(8,128)(2,1)S(1)}, bf16[128,2048]{1,0:T(8,128)(2,1)S(1)}, u32[]{:S(2)}, u32[]{:S(2)}) collective-permute-start(bf16[128,2048]{1,0:T(8,128)(2,1)S(1)} %get-tuple-element.98), channel_id=1, source_target_pairs={{0,24},{4,28},{8,16},{12,20},{16,8},{20,12},{24,0},{28,4},{1,25},{... | collective-permute-start | bytes 1572872 | tf_op jit(solution)/shard_map/ppermute | solution.py:365
  135.1 24.4 %collective-permute-start.12 = (bf16[128,2048]{1,0:T(8,128)(2,1)S(1)}, bf16[128,2048]{1,0:T(8,128)(2,1)S(1)}, u32[]{:S(2)}, u32[]{:S(2)}) collective-permute-start(bf16[128,2048]{1,0:T(8,128)(2,1)S(1)} %get-tuple-element.99), channel_id=1, source_target_pairs={{0,16},{4,20},{8,24},{12,28},{16,0},{20,4},{24,8},{28,12},{1,17},{... | collective-permute-start | bytes 1572872 | tf_op jit(solution)/shard_map/ppermute | solution.py:365
  136.3 24.0 %collective-permute-start.11 = (bf16[128,2048]{1,0:T(8,128)(2,1)S(1)}, bf16[128,2048]{1,0:T(8,128)(2,1)S(1)}, u32[]{:S(2)}, u32[]{:S(2)}) collective-permute-start(bf16[128,2048]{1,0:T(8,128)(2,1)S(1)} %get-tuple-element.100), channel_id=1, source_target_pairs={{0,8},{4,12},{8,0},{12,4},{16,24},{20,28},{24,16},{28,20},{1,9},{5... | collective-permute-start | bytes 1572872 | tf_op jit(solution)/shard_map/ppermute | solution.py:365
  136.9 46.0 %collective-permute-start.7 = (bf16[256,2048]{1,0:T(8,128)(2,1)S(1)}, bf16[256,2048]{1,0:T(8,128)(2,1)}, u32[]{:S(2)}, u32[]{:S(2)}) collective-permute-start(bf16[256,2048]{1,0:T(8,128)(2,1)S(1)} %copy-done.33), channel_id=1, source_target_pairs={{0,8},{4,12},{8,0},{12,4},{16,24},{20,28},{24,16},{28,20},{1,9},{5... | collective-permute-start | bytes 3145736 | tf_op jit(solution)/shard_map/ppermute | solution.py:365
  138.3 47.0 %collective-permute-start.15 = (bf16[256,2048]{1,0:T(8,128)(2,1)S(1)}, bf16[256,2048]{1,0:T(8,128)(2,1)}, u32[]{:S(2)}, u32[]{:S(2)}) collective-permute-start(bf16[256,2048]{1,0:T(8,128)(2,1)S(1)} %copy-done.31), channel_id=1, source_target_pairs={{0,16},{4,20},{8,24},{12,28},{16,0},{20,4},{24,8},{28,12},{1,17},{... | collective-permute-start | bytes 3145736 | tf_op jit(solution)/shard_map/ppermute | solution.py:365
  167.6 36.8 %collective-permute-start.16 = (bf16[256,2048]{1,0:T(8,128)(2,1)S(1)}, bf16[256,2048]{1,0:T(8,128)(2,1)}, u32[]{:S(2)}, u32[]{:S(2)}) collective-permute-start(bf16[256,2048]{1,0:T(8,128)(2,1)S(1)} %get-tuple-element.59), channel_id=1, source_target_pairs={{0,16},{4,20},{8,24},{12,28},{16,0},{20,4},{24,8},{28,12},{1,17},{... | collective-permute-start | bytes 3145736 | tf_op jit(solution)/shard_map/ppermute | solution.py:365
  175.6 32.0 %collective-permute-start.14 = (bf16[256,2048]{1,0:T(8,128)(2,1)S(1)}, bf16[256,2048]{1,0:T(8,128)(2,1)S(1)}, u32[]{:S(2)}, u32[]{:S(2)}) collective-permute-start(bf16[256,2048]{1,0:T(8,128)(2,1)S(1)} %get-tuple-element.55), channel_id=1, source_target_pairs={{0,8},{4,12},{8,0},{12,4},{16,24},{20,28},{24,16},{28,20},{1,9},{5... | collective-permute-start | bytes 3145736 | tf_op jit(solution)/shard_map/ppermute | solution.py:365
  184.6 31.0 %collective-permute-start.17 = (bf16[128,2048]{1,0:T(8,128)(2,1)S(1)}, bf16[128,2048]{1,0:T(8,128)(2,1)S(1)}, u32[]{:S(2)}, u32[]{:S(2)}) collective-permute-start(bf16[128,2048]{1,0:T(8,128)(2,1)S(1)} %slice.202), channel_id=1, source_target_pairs={{0,16},{4,20},{8,24},{12,28},{16,0},{20,4},{24,8},{28,12},{1,17},{... | collective-permute-start | bytes 1572872 | tf_op jit(solution)/shard_map/ppermute | solution.py:365
  186.9 29.6 %collective-permute-start.19 = (bf16[128,2048]{1,0:T(8,128)(2,1)S(1)}, bf16[128,2048]{1,0:T(8,128)(2,1)S(1)}, u32[]{:S(2)}, u32[]{:S(2)}) collective-permute-start(bf16[128,2048]{1,0:T(8,128)(2,1)S(1)} %slice.200), channel_id=1, source_target_pairs={{0,8},{4,12},{8,0},{12,4},{16,24},{20,28},{24,16},{28,20},{1,9},{5... | collective-permute-start | bytes 1572872 | tf_op jit(solution)/shard_map/ppermute | solution.py:365
  206.0 20.8 %collective-permute-start.20 = (bf16[128,2048]{1,0:T(8,128)(2,1)S(1)}, bf16[128,2048]{1,0:T(8,128)(2,1)S(1)}, u32[]{:S(2)}, u32[]{:S(2)}) collective-permute-start(bf16[128,2048]{1,0:T(8,128)(2,1)S(1)} %slice.199), channel_id=1, source_target_pairs={{0,8},{4,12},{8,0},{12,4},{16,24},{20,28},{24,16},{28,20},{1,9},{5... | collective-permute-start | bytes 1572872 | tf_op jit(solution)/shard_map/ppermute | solution.py:365
  208.0 18.8 %collective-permute-start.18 = (bf16[128,2048]{1,0:T(8,128)(2,1)S(1)}, bf16[128,2048]{1,0:T(8,128)(2,1)S(1)}, u32[]{:S(2)}, u32[]{:S(2)}) collective-permute-start(bf16[128,2048]{1,0:T(8,128)(2,1)S(1)} %slice.201), channel_id=1, source_target_pairs={{0,16},{4,20},{8,24},{12,28},{16,0},{20,4},{24,8},{28,12},{1,17},{... | collective-permute-start | bytes 1572872 | tf_op jit(solution)/shard_map/ppermute | solution.py:365
  234.9 10.5 %collective-permute-start.21 = (f32[16,256,128]{2,1,0:T(8,128)}, f32[16,256,128]{2,1,0:T(8,128)}, u32[]{:S(2)}, u32[]{:S(2)}) collective-permute-start(f32[16,256,128]{2,1,0:T(8,128)} %shard_map.127), channel_id=1, source_target_pairs={{0,4},{4,0},{8,12},{12,8},{16,20},{20,16},{24,28},{28,24},{1,5},{5... | collective-permute-start | bytes 6291464 | tf_op jit(solution)/shard_map/ppermute | solution.py:369
  247.7 14.4 %collective-permute-start.23 = (bf16[8,256,128]{2,1,0:T(8,128)(2,1)S(1)}, bf16[8,256,128]{2,1,0:T(8,128)(2,1)S(1)}, u32[]{:S(2)}, u32[]{:S(2)}) collective-permute-start(bf16[8,256,128]{2,1,0:T(8,128)(2,1)S(1)} %get-tuple-element.110), channel_id=1, source_target_pairs={{0,16},{4,20},{8,24},{12,28},{16,0},{20,4},{24,8},{28,12},{1,17},{... | collective-permute-start | bytes 1572872 | tf_op jit(solution)/shard_map/ppermute | solution.py:365
  249.2 14.0 %collective-permute-start.22 = (bf16[8,256,128]{2,1,0:T(8,128)(2,1)S(1)}, bf16[8,256,128]{2,1,0:T(8,128)(2,1)S(1)}, u32[]{:S(2)}, u32[]{:S(2)}) collective-permute-start(bf16[8,256,128]{2,1,0:T(8,128)(2,1)S(1)} %get-tuple-element.111), channel_id=1, source_target_pairs={{0,8},{4,12},{8,0},{12,4},{16,24},{20,28},{24,16},{28,20},{1,9},{5... | collective-permute-start | bytes 1572872 | tf_op jit(solution)/shard_map/ppermute | solution.py:365
  263.7 13.3 %collective-permute-start.25 = (bf16[8,256,128]{2,1,0:T(8,128)(2,1)S(1)}, bf16[8,256,128]{2,1,0:T(8,128)(2,1)S(1)}, u32[]{:S(2)}, u32[]{:S(2)}) collective-permute-start(bf16[8,256,128]{2,1,0:T(8,128)(2,1)S(1)} %get-tuple-element.108), channel_id=1, source_target_pairs={{0,8},{4,12},{8,0},{12,4},{16,24},{20,28},{24,16},{28,20},{1,9},{5... | collective-permute-start | bytes 1572872 | tf_op jit(solution)/shard_map/ppermute | solution.py:365
  264.4 12.9 %collective-permute-start.24 = (bf16[8,256,128]{2,1,0:T(8,128)(2,1)S(1)}, bf16[8,256,128]{2,1,0:T(8,128)(2,1)S(1)}, u32[]{:S(2)}, u32[]{:S(2)}) collective-permute-start(bf16[8,256,128]{2,1,0:T(8,128)(2,1)S(1)} %get-tuple-element.109), channel_id=1, source_target_pairs={{0,16},{4,20},{8,24},{12,28},{16,0},{20,4},{24,8},{28,12},{1,17},{... | collective-permute-start | bytes 1572872 | tf_op jit(solution)/shard_map/ppermute | solution.py:365
  282.4 10.0 %collective-permute-start.26 = (f32[16,256,128]{2,1,0:T(8,128)}, f32[16,256,128]{2,1,0:T(8,128)}, u32[]{:S(2)}, u32[]{:S(2)}) collective-permute-start(f32[16,256,128]{2,1,0:T(8,128)} %get-tuple-element.95), channel_id=1, source_target_pairs={{0,4},{4,0},{8,12},{12,8},{16,20},{20,16},{24,28},{28,24},{1,5},{5... | collective-permute-start | bytes 6291464 | tf_op jit(solution)/shard_map/ppermute | solution.py:369
  304.6 11.9 %collective-permute-start.28 = (f32[64,2,256]{2,0,1:T(8,128)S(1)}, f32[64,2,256]{2,0,1:T(8,128)S(1)}, u32[]{:S(2)}, u32[]{:S(2)}) collective-permute-start(f32[64,2,256]{2,0,1:T(8,128)S(1)} %get-tuple-element.125), channel_id=1, source_target_pairs={{0,2},{1,3},{2,0},{3,1},{4,6},{5,7},{6,4},{7,5},{8,10},{9,11},{10,... | collective-permute-start | bytes 393224 | tf_op jit(solution)/shard_map/ppermute | solution.py:385
  307.2 9.3 %collective-permute-start.29 = (f32[64,2,256]{2,0,1:T(8,128)S(1)}, f32[64,2,256]{2,0,1:T(8,128)S(1)}, u32[]{:S(2)}, u32[]{:S(2)}) collective-permute-start(f32[64,2,256]{2,0,1:T(8,128)S(1)} %get-tuple-element.126), channel_id=1, source_target_pairs={{0,3},{1,0},{2,1},{3,2},{4,7},{5,4},{6,5},{7,6},{8,11},{9,8},{10,9... | collective-permute-start | bytes 393224 | tf_op jit(solution)/shard_map/ppermute | solution.py:385
  321.8 12.2 %collective-permute-start.31 = (f32[64,2,256]{2,0,1:T(8,128)S(1)}, f32[64,2,256]{2,0,1:T(8,128)S(1)}, u32[]{:S(2)}, u32[]{:S(2)}) collective-permute-start(f32[64,2,256]{2,0,1:T(8,128)S(1)} %fusion.28), channel_id=1, source_target_pairs={{0,2},{1,3},{2,0},{3,1},{4,6},{5,7},{6,4},{7,5},{8,10},{9,11},{10,... | collective-permute-start | bytes 393224 | tf_op jit(solution)/shard_map/ppermute | solution.py:386
  322.2 11.8 %collective-permute-start.30 = (f32[64,2,256]{2,0,1:T(8,128)S(1)}, f32[64,2,256]{2,0,1:T(8,128)S(1)}, u32[]{:S(2)}, u32[]{:S(2)}) collective-permute-start(f32[64,2,256]{2,0,1:T(8,128)S(1)} %fusion.28), channel_id=1, source_target_pairs={{0,1},{1,2},{2,3},{3,0},{4,5},{5,6},{6,7},{7,4},{8,9},{9,10},{10,1... | collective-permute-start | bytes 393224 | tf_op jit(solution)/shard_map/ppermute | solution.py:386
  (51 other events, 385.7 us)
Sparse Core Ops, SparseCore 0:
  16.3 48.5 all-gather.3
  66.5 44.9 all-gather.5

commit v4 on v3

--- a/solution.py
+++ b/solution.py
@@ -13,7 +13,7 @@
 NN = (((1,), (0,)), ((), ()))
 NT = (((1,), (1,)), ((), ()))
 TN = (((0,), (0,)), ((), ()))
-PARAMS = pltpu.CompilerParams(vmem_limit_bytes=48 << 20)
+PARAMS = pltpu.CompilerParams(vmem_limit_bytes=60 << 20)
 
 
 def mm(a, b, dims):
@@ -23,11 +23,6 @@
 def halves(a):
     high = a.astype(BF16)
     return high, (a - high.astype(F32)).astype(BF16)
-
-
-def mm_left(a, b, dims):
-    high, low = halves(a)
-    return mm(high, b, dims) + mm(low, b, dims)
 
 
 def mm_right(a, b):
@@ -36,9 +31,10 @@
     return both[:, :width] + both[:, width:]
 
 
-def mm_wide(a, b):
-    b = b.astype(BF16)
-    return mm(jnp.concatenate(halves(a), axis=1), jnp.concatenate([b, b], axis=1), NT)
+def mm_wide(lefts, rights):
+    left = [part for a in lefts for part in halves(a)]
+    right = [part for b in rights for part in [b.astype(BF16)] * 2]
+    return mm(jnp.concatenate(left, axis=1), jnp.concatenate(right, axis=1), NT)
 
 
 def whole(*shape):
@@ -87,68 +83,116 @@
     )(at, values, scale, rows_t)
 
 
-def inner_kernel(
-    first, last, at_ref, x_ref, y_ref, b_ref, c_ref, run_ref, run_t_ref, step_ref, skip_ref,
-    state_ref, *rest,
-):
-    del at_ref
-    held = rest[: 0 if first else 5]
-    partial_ref, col_ref, carry_ref, mix_ref, grad_c_ref, cross, rows = rest[len(held) :]
-    index = pl.program_id(0)
-    group = step_ref.shape[2]
-    span = x_ref.shape[0]
-    width = x_ref.shape[1] // group
-
-    @pl.when(index == 0)
+def decay_kernel(run_ref, run_t_ref, b_ref, c_ref, decay_ref, weight_ref, cross_ref):
+    group = run_ref.shape[2]
+    span = run_ref.shape[1]
+
+    @pl.when(pl.program_id(0) == 0)
     def _():
-        cross[...] = mm(b_ref[...], c_ref[...], NT)
-        mix_ref[...] = jnp.zeros_like(mix_ref) if first else held[3][...]
-        grad_c_ref[...] = jnp.zeros_like(grad_c_ref) if first else held[4][...]
+        cross_ref[...] = mm(b_ref[...], c_ref[...], NT)
 
     source = lax.broadcasted_iota(jnp.int32, (span, span), 0)
     target = lax.broadcasted_iota(jnp.int32, (span, span), 1)
     causal = source <= target
     for j in range(group):
+        gap = run_t_ref[0, j : j + 1, :] - run_ref[0, :, j : j + 1]
+        decay = jnp.exp(jnp.where(causal, gap, -jnp.inf))
+        decay_ref[j] = decay
+        high, low = halves(decay * cross_ref[...])
+        weight_ref[j, :, :span] = high
+        weight_ref[j, :, span:] = low
+
+
+def decays(running, running_t, b, c):
+    groups, span, group = running.shape
+    states = b.shape[1]
+    fixed = lambda *shape: pl.BlockSpec(shape, lambda i: (0,) * len(shape))
+    return pl.pallas_call(
+        decay_kernel,
+        grid=(groups,),
+        in_specs=[
+            pl.BlockSpec((1, span, group), lambda i: (i, 0, 0)),
+            pl.BlockSpec((1, group, span), lambda i: (i, 0, 0)),
+            fixed(span, states),
+            fixed(span, states),
+        ],
+        out_specs=[
+            pl.BlockSpec((group, span, span), lambda i: (i, 0, 0)),
+            pl.BlockSpec((group, span, 2 * span), lambda i: (i, 0, 0)),
+            fixed(span, span),
+        ],
+        out_shape=[
+            jax.ShapeDtypeStruct((groups * group, span, span), F32),
+            jax.ShapeDtypeStruct((groups * group, span, 2 * span), BF16),
+            jax.ShapeDtypeStruct((span, span), F32),
+        ],
+        compiler_params=PARAMS,
+        cost_estimate=cost(
+            8 * groups * group * span * span,
+            8 * groups * group * span * span,
+            groups * group * span * span,
+        ),
+    )(running, running_t, b, c)
+
+
+def inner_kernel(
+    first, last, at_ref, x_ref, y_ref, b_ref, c_ref, rise_ref, step_ref, skip_ref,
+    state_ref, decay_ref, weight_ref, cross_ref, *rest,
+):
+    del at_ref
+    held = rest[: 0 if first else 5]
+    partial_ref, col_ref, carry_ref, mix_ref, grad_c_ref, rows = rest[len(held) :]
+    group = step_ref.shape[2]
+    width = x_ref.shape[1] // group
+
+    @pl.when(pl.program_id(0) == 0)
+    def _():
+        mix_ref[...] = jnp.zeros_like(mix_ref) if first else held[3][...]
+        grad_c_ref[...] = jnp.zeros_like(grad_c_ref) if first else held[4][...]
+
+    lefts, rights = [], []
+    for j in range(group):
         columns = slice(j * width, (j + 1) * width)
-        x = x_ref[:, columns]
         y = y_ref[:, columns]
-        run_col = run_ref[0, :, j : j + 1]
+        x_wide = x_ref[:, columns].astype(F32)
+        y_wide = y.astype(F32)
         step_col = step_ref[0, :, j : j + 1]
-        run_row = run_t_ref[0, j : j + 1, :]
-        decay = jnp.exp(jnp.where(causal, run_row - run_col, -jnp.inf))
-        weights = decay * cross[...]
-        pairs = mm(x, y, NT)
-        mix_ref[...] += decay * pairs * step_col
-        terms = weights * pairs
-        col_ref[0, :, j : j + 1] = jnp.sum(terms, axis=1, keepdims=True)
-        rows[j : j + 1, :] = jnp.sum(terms * step_col, axis=0, keepdims=True)
-        inner = mm_left(weights, y, NN)
-        y_wide = y.astype(F32)
+        stepped = jnp.concatenate(halves(x_wide * step_col), axis=1)
+        pairs = decay_ref[j] * mm(stepped, jnp.concatenate([y, y], axis=1), NT)
+        mix_ref[...] += pairs
+        rows[j : j + 1, :] = jnp.sum(pairs * cross_ref[...], axis=0, keepdims=True)
+        inner = mm(weight_ref[j], jnp.concatenate([y, y], axis=0), NN)
+        col_ref[0, :, j : j + 1] = jnp.sum(x_wide * inner, axis=1, keepdims=True)
         partial_ref[:, columns] = step_col * inner + skip_ref[0, j : j + 1, :] * y_wide
         state = state_ref[j]
-        scaled = y_wide * jnp.exp(run_col)
-        grad_c_ref[...] += mm_wide(scaled, state)
+        scaled = y_wide * rise_ref[0, :, j : j + 1]
+        lefts.append(scaled)
+        rights.append(state)
         carry_ref[0, :, j : j + 1] = jnp.sum(
             scaled * mm_right(c_ref[...], state), axis=1, keepdims=True
         )
+    grad_c_ref[...] += mm_wide(lefts, rights)
     carry_ref[0] += rows[...].T
 
     if last:
 
-        @pl.when(index == pl.num_programs(0) - 1)
+        @pl.when(pl.program_id(0) == pl.num_programs(0) - 1)
         def _():
             high, low = halves(mix_ref[...])
             mix_ref[...] = mm(high, c_ref[...], NN) + mm(low, c_ref[...], NN)
             grad_c_ref[...] += mm(high, b_ref[...], TN) + mm(low, b_ref[...], TN)
 
 
-def inner_part(x, y, b, c, running, running_t, steps, skip_rows, incoming, at, count, held, last):
+def inner_part(
+    x, y, b, c, rise, steps, skip_rows, incoming, decay, weight, cross, at, count, held, last
+):
     groups, span, group = steps.shape
     heads = groups * group
     width = x.shape[1] // heads
     states = b.shape[1]
     block = pl.BlockSpec((span, group * width), lambda i, at: (0, at[0] + i))
     table = pl.BlockSpec((1, span, group), lambda i, at: (at[0] + i, 0, 0))
+    per_head = lambda *shape: pl.BlockSpec((group, *shape), lambda i, at: (at[0] + i, 0, 0))
     any_place = pl.BlockSpec(memory_space=pl.ANY)
     return pl.pallas_call(
         lambda *refs: inner_kernel(not held, last, *refs),
@@ -161,14 +205,16 @@
                 whole(span, states),
                 whole(span, states),
                 table,
-                pl.BlockSpec((1, group, span), lambda i, at: (at[0] + i, 0, 0)),
                 table,
                 pl.BlockSpec((1, group, width), lambda i, at: (at[0] + i, 0, 0)),
-                pl.BlockSpec((group, states, width), lambda i, at: (at[0] + i, 0, 0)),
+                per_head(states, width),
+                per_head(span, span),
+                per_head(span, 2 * span),
+                whole(span, span),
             ]
             + ([any_place] * 3 + [whole(span, states)] * 2 if held else []),
             out_specs=[block, table, table, whole(span, states), whole(span, states)],
-            scratch_shapes=[pltpu.VMEM((span, span), F32), pltpu.VMEM((group, span), F32)],
+            scratch_shapes=[pltpu.VMEM((group, span), F32)],
         ),
         out_shape=[
             jax.ShapeDtypeStruct((span, heads * width), F32),
@@ -177,16 +223,15 @@
             jax.ShapeDtypeStruct((span, states), F32),
             jax.ShapeDtypeStruct((span, states), F32),
         ],
-        input_output_aliases={10: 0, 11: 1, 12: 2} if held else {},
+        input_output_aliases={12: 0, 13: 1, 14: 2} if held else {},
         compiler_params=PARAMS,
         cost_estimate=cost(
             14 * span * count * group * width * states,
-            count * group * width * (8 * span + 4 * states),
-            count * group * span * span,
+            count * group * (8 * span * width + 4 * width * states + 8 * span * span),
         ),
     )(
-        jnp.full((1,), at, jnp.int32), x, y, b, c, running, running_t, steps, skip_rows,
-        incoming, *held,
+        jnp.full((1,), at, jnp.int32), x, y, b, c, rise, steps, skip_rows, incoming,
+        decay, weight, cross, *held,
     )
 
 
@@ -208,6 +253,7 @@
     end = running[span - 1 : span, :]
     tails = jnp.exp(end - running)
     steps = step_ref[0]
+    lefts, rights = [], []
     for j in range(group):
         columns = slice(j * width, (j + 1) * width)
         tail_col = tails[:, j : j + 1]
@@ -217,10 +263,12 @@
         outer = mm_right(b_ref[...], grad_state) * tail_col
         late[:, j : j + 1] = jnp.sum(x * outer, axis=1, keepdims=True)
         grad_x_ref[:, columns] = (part_ref[:, columns] + step_col * outer).astype(BF16)
-        grad_b_ref[...] += mm_wide(x * (step_col * tail_col), grad_state)
+        lefts.append(x * (step_col * tail_col))
+        rights.append(grad_state)
         shared = jnp.sum(grad_state * state_ref[j], axis=0, keepdims=True)
         overlap[:, j : j + 1] = jnp.sum(shared, axis=1, keepdims=True)
 
+    grad_b_ref[...] += mm_wide(lefts, rights)
     grad_step = col_ref[0] + late[...]
     grad_step_ref[0] = grad_step
     change = carry_ref[0] - steps * grad_step
@@ -331,7 +379,7 @@
 def finish_kernel(count, *refs):
     keeps, arrived, out_ref = refs[: 2 * count], refs[2 * count : -1], refs[-1]
     steps = pl.num_programs(0) // 2
-    rows = keeps[0].shape[0]
+    rows = arrived[0].shape[0]
     for lane in range(2):
 
         @pl.when(pl.program_id(0) // steps == lane)
@@ -344,7 +392,7 @@
 
 def finish(keeps, arrived):
     count = len(keeps) // 2
-    rows, half = keeps[0].shape
+    rows, half = arrived[0].shape
     tile = min(1024, half)
     steps = half // tile
     place = [lambda i: (0, jnp.minimum(i, steps - 1)), lambda i: (0, jnp.maximum(i - steps, 0))]
@@ -376,19 +424,15 @@
 
 def sum_over_heads(value):
     count = lax.axis_size("head")
-    here = lax.axis_index("head")
-    shares = value.reshape((count, value.shape[0] // count) + value.shape[1:])
-    shift = lambda hop: [(i, (i + hop) % count) for i in range(count)]
-    share = lambda hop: lax.dynamic_index_in_dim(shares, (here + hop) % count, 0, False)
-    total = share(0)
-    for hop in range(1, count):
-        total = total + lax.ppermute(share(hop), "head", shift(hop))
-    parts = [total] + [lax.ppermute(total, "head", shift(hop)) for hop in range(1, count)]
-    stacked = jnp.stack(parts)
-    ordered = [
-        lax.dynamic_index_in_dim(stacked, (here - i) % count, 0, False) for i in range(count)
+    value = value.astype(BF16)
+    terms = [
+        lax.ppermute(value, "head", [(i, i ^ hop) for i in range(count)]) if hop else value
+        for hop in range(count)
     ]
-    return jnp.concatenate(ordered, axis=0)
+    terms = [term.astype(F32) for term in terms]
+    while len(terms) > 1:
+        terms = [terms[i] + terms[i + 1] for i in range(0, len(terms), 2)]
+    return terms[0]
 
 
 def project(grad_out, out_weight, chips, chip, core, before):
@@ -420,7 +464,7 @@
                     keep = keep + arrived.astype(F32)
                     size = keep.shape[0] // 2
                     send = keep[size:].astype(BF16)
-                    keep = keep[:size]
+                    keep = keep[:size] if size > rows else keep
             waiting[lane][-1] = (keep, arrived)
 
     for chunk in range(CHUNKS):
@@ -477,7 +521,11 @@
         done = fill(step, [item for items in sent for item in items.values()])
         for order, (heads, items), going in zip(bits, lanes, sent):
             for o, item in going.items():
-                items[o | order[step]] = tie(across(item, order[step], chips), *done)
+                items[o | order[step]] = across(item, order[step], chips)
+        fresh = [(items, o | order[step]) for order, (_, items), going in zip(bits, lanes, sent) for o in going]
+        values = lax.optimization_barrier((*[items[o] for items, o in fresh], *done))
+        for (items, o), value in zip(fresh, values):
+            items[o] = value
     totals = []
     for order, (heads, items) in zip(bits, lanes):
         arrived = items.pop(order[-1])
@@ -523,7 +571,9 @@
         last_sent[:] = sent
         return []
 
-    mine, theirs = span_both(ssm_input, by_group(step_size * tail), b_rows)
+    first_rows = grad_out[: span // CHUNKS]
+    scale = tie(by_group(step_size * tail), first_rows)
+    mine, theirs = span_both(ssm_input, scale, b_rows)
     for_mine, for_theirs = exchange(mine, theirs, ends, chips, chip, core, False, note)
     arrived = other_core(for_theirs, chips)
     incoming = jnp.where(
@@ -531,8 +581,8 @@
         jnp.concatenate([for_mine, arrived], axis=0),
         jnp.concatenate([arrived, for_mine], axis=0),
     )
-    tables = (running_g, running_t, steps_g, skip_rows)
-    before = [[*last_sent, *tables, rise, c_rows]] + [[incoming]] * (CHUNKS - 1)
+    decay, weight, cross = decays(tie(running_g, *last_sent), running_t, b_in, c_in)
+    before = [[*last_sent, steps_g, skip_rows, rise, c_rows]] + [[incoming, cross]] * (CHUNKS - 1)
     grad_y = project(grad_out, out_weight, chips, chip, core, before)
 
     few = max(1, groups // 4)
@@ -544,8 +594,8 @@
         count = counts[step] if step < len(counts) else 0
         if count:
             held = inner_part(
-                ssm_input, grad_y, b_in, c_in, tie(running_g, *sent), running_t, steps_g,
-                skip_rows, incoming, sum(counts[:step]), count, held, step == len(counts) - 1,
+                ssm_input, grad_y, b_in, c_in, tie(rise, *sent), steps_g, skip_rows, incoming,
+                decay, weight, cross, sum(counts[:step]), count, held, step == len(counts) - 1,
             )
         return list(held)
 
@@ -556,6 +606,7 @@
     )
     for_other = other_core(for_theirs, chips)
     part, cols, carries, grad_b, grad_c = held
+    grad_c = sum_over_heads(grad_c)
     shared = (running_g, steps_g, cols, carries)
     grad_x, grad_b, grad_step, grad_decay = outer_part(
         ssm_input, part, b_in, incoming, for_mine, *shared, grad_b, mine_at, None
@@ -564,8 +615,8 @@
         ssm_input, part, b_in, incoming, for_other, *shared, grad_b, other_at,
         (grad_x, grad_step, grad_decay),
     )
-    both = sum_over_heads(jnp.stack([grad_b, grad_c], axis=1))
-    return (grad_x, flat(grad_step), flat(grad_decay), both[:, 0], both[:, 1])
+    grad_b = sum_over_heads(grad_b)
+    return (grad_x, flat(grad_step), flat(grad_decay), grad_b, grad_c)
 
 
 def solution(mesh):

time: 343 us -> 330 us (0.962)
  waiting for transfers between devices: 137 us -> 99.8 us
  Pallas kernels: 80.9 us -> 110 us
  starting transfers between devices: 37.6 us -> 33.3 us
    ppermute x22, waiting for transfers between devices: 119 us -> 94.9 us  [across(): return lax.ppermute(value, 'seq', pairs)]
    ppermute x6, waiting for transfers between devices: 17.9 us -> 4.86 us  [sum_over_heads(): lax.ppermute(value, 'head', [(i, i ^ hop) for i in range(count)])]
    pallas_call x0 -> x1, Pallas kernels: none -> 8.15 us  [decays(): pl.pallas_call(decay_kernel, grid=(groups,), in_specs=[pl.BlockSpec((1, s...]
    pallas_call x4, Pallas kernels: 29.2 us -> 35.8 us  [partial_sums(): pl.pallas_call(lambda *refs: project_kernel(hops, *refs), grid_spec=pltpu...]
    unnamed x98 -> x62, local copies, waits for them, and re-layouts: 15.5 us -> 9.25 us
    pallas_call x4, Pallas kernels: 8.15 us -> 14.3 us  [span_states(): pl.pallas_call(states_kernel, grid_spec=pltpu.PrefetchScalarGridSpec(num_...]
    pallas_call x3, Pallas kernels: 23.7 us -> 28 us  [inner_part(): pl.pallas_call(lambda *refs: inner_kernel(not held, last, *refs), grid_sp...]
  transfers between devices with their start and end apart: 35 -> 35, of which waited for: 22 -> 18; matrix products, arithmetic and copies ran while one was open for 10% -> 12% of each run, Pallas kernels for 19% -> 31%
where the time goes in v4:
time: 330 us; the launch traced here: 329 us
  Pallas kernels  110 us (33%)
  waiting for transfers between devices  99.8 us (30%)
  other arithmetic  33.7 us (10%)
  starting transfers between devices  33.3 us (10%)
  local copies, waits for them, and re-layouts  27.4 us (8%)
  between operations  14.5 us (4%)
  blocking collectives  10.2 us (3%)
    ppermute x22, waiting for transfers between devices, across(): return lax.ppermute(value, 'seq', pairs)  94.9 us
    pallas_call x4, Pallas kernels, partial_sums(): pl.pallas_call(lambda *refs: project_kernel(hops, *refs), grid_spec=pltpu...  35.8 us
    pallas_call x3, Pallas kernels, inner_part(): pl.pallas_call(lambda *refs: inner_kernel(not held, last, *refs), grid_sp...  28 us
    ppermute x22, starting transfers between devices, across(): return lax.ppermute(value, 'seq', pairs)  23.8 us
    pallas_call x2, Pallas kernels, outer_part(): pl.pallas_call(outer_kernel, grid_spec=pltpu.PrefetchScalarGridSpec(num_s...  18.1 us
    pallas_call x4, Pallas kernels, span_states(): pl.pallas_call(states_kernel, grid_spec=pltpu.PrefetchScalarGridSpec(num_...  14.3 us
    all_gather x1, blocking collectives, local(): ends = lax.all_gather(running[-1], 'seq')  10.2 us
    unnamed x62, local copies, waits for them, and re-layouts  9.25 us
  transfers between devices with their start and end apart: 35, of which 18 were waited for; matrix products, arithmetic and copies ran while one was open for 12% of the time, Pallas kernels for 31%

profile of v4, /device:TPU:0, one launch (start us, length us, event | category | flops | bytes accessed | tf_op | source)
XLA Modules:
  0.0 328.8 jit_solution(973035733915399733)
XLA Ops:
  14.1 3.5 %shard_map.120 = f32[16,256,128]{2,1,0:T(8,128)} custom-call(s32[1]{0:T(128)} %bitcast.at_ref, bf16[256,4096]{1,0:T(8,128)(2,1)} %x_ref.3, f32[4,256,8]{2,1,0:T(8,128)} %bitcast.41, bf16[256,256]{1,0:T(8,128)(2,1)} %bitcast.50), custom_call_target="tpu_custom_call" | custom-call | flops 536870912 | bytes 3145728 | tf_op jit(solution)/shard_map/pallas_call | solution.py:65
  17.8 3.6 %shard_map.119 = f32[16,256,128]{2,1,0:T(8,128)} custom-call(s32[1]{0:T(128)} %bitcast.6.at_ref, bf16[256,4096]{1,0:T(8,128)(2,1)} %x_ref.3, f32[4,256,8]{2,1,0:T(8,128)} %bitcast.42, bf16[256,256]{1,0:T(8,128)(2,1)} %bitcast.51), custom_call_target="tpu_custom_call" | custom-call | flops 536870912 | bytes 3145728 | tf_op jit(solution)/shard_map/pallas_call | solution.py:65
  21.4 10.2 %all-gather = f32[8,1,32]{2,1,0:T(1,128)S(1)} all-gather(f32[1,1,32]{2,1,0:T(1,128)S(1)} %bitcast.61), channel_id=1, replica_groups=mesh['seq'=8,'head'=4] {'seq'}, dimensions={0}, use_global_device_ids=true | all-gather | bytes 1152 | tf_op jit(solution)/shard_map/all_gather | solution.py:554
  37.1 12.3 %collective-permute-done.2 = bf16[8,256,128]{2,1,0:T(8,128)(2,1)} collective-permute-done((bf16[8,256,128]{2,1,0:T(8,128)(2,1)}, bf16[8,256,128]{2,1,0:T(8,128)(2,1)}, u32[]{:S(2)}, u32[]{:S(2)}) %collective-permute-start.2) | collective-permute-done | bytes 524320 | tf_op jit(solution)/shard_map/ppermute | solution.py:413
  50.6 2.7 fusion.9
  55.4 11.2 %collective-permute-done.9 = bf16[8,256,128]{2,1,0:T(8,128)(2,1)} collective-permute-done((bf16[8,256,128]{2,1,0:T(8,128)(2,1)}, bf16[8,256,128]{2,1,0:T(8,128)(2,1)}, u32[]{:S(2)}, u32[]{:S(2)}) %collective-permute-start.9) | collective-permute-done | bytes 524320 | tf_op jit(solution)/shard_map/ppermute | solution.py:413
  69.0 2.8 fusion.3
  75.3 2.9 constant_dynamic-slice_fusion.4
  82.8 8.2 %shard_map.122 = (f32[32,256,256]{2,1,0:T(8,128)}, bf16[32,256,512]{2,1,0:T(8,128)(2,1)}, f32[256,256]{1,0:T(8,128)}) custom-call(f32[4,256,8]{2,1,0:T(8,128)} %bitcast.43, f32[4,8,256]{2,1,0:T(8,128)} %bitcast.53, bf16[256,256]{1,0:T(8,128)(2,1)} %b_ref.5, bf16[256,256]{1,0:T(8,128)(2,1)} %refs_4_.5), custom_call_target="tpu_custom_call" | custom-call | flops 16777216 | bytes 16777216 | tf_op jit(solution)/shard_map/pallas_call | solution.py:110
  90.9 5.0 %maximum_select_fusion.refs_8_.state_ref = f32[32,256,128]{2,1,0:T(8,128)} fusion(f32[16,256,128]{2,1,0:T(8,128)} %collective-permute-done.10, f32[16,256,128]{2,1,0:T(8,128)S(1)} %copy-done.8, pred[]{:T(512)S(6)} %eq.4), kind=kLoop, calls=%fused_computation | loop fusion | flops 3145728 | bytes 8388609 | tf_op jit(solution)/shard_map/jit(_where)/select_n | solution.py:579
  95.9 9.0 %collective-permute-done.4.refs_3_ = bf16[128,2048]{1,0:T(8,128)(2,1)S(1)} collective-permute-done((bf16[128,2048]{1,0:T(8,128)(2,1)}, bf16[128,2048]{1,0:T(8,128)(2,1)S(1)}, u32[]{:S(2)}, u32[]{:S(2)}) %collective-permute-start.4) | collective-permute-done | bytes 524320 | tf_op jit(solution)/shard_map/ppermute | solution.py:413
  105.9 8.9 %shard_map.123 = (bf16[256,2048]{1,0:T(8,128)(2,1)}, f32[256,2048]{1,0:T(8,128)}) custom-call(s32[1]{0:T(128)} %bitcast.1.refs_0_, bf16[128,2048]{1,0:T(8,128)(2,1)} %get-tuple-element.123.refs_1_, bf16[128,2048]{1,0:T(8,128)(2,1)} %copy-done.13, bf16[128,2048]{1,0:T(8,128)(2,1)} %copy-done.11, bf16[128,2048]{1,0:T(8,128)(2,1)} %copy-done.10, ...), custom_call_target="tpu_custom_call" | custom-call | flops 4294967296 | bytes 11534336 | tf_op jit(solution)/shard_map/pallas_call | solution.py:359
  114.9 8.9 %shard_map.121 = (bf16[256,2048]{1,0:T(8,128)(2,1)}, f32[256,2048]{1,0:T(8,128)}) custom-call(s32[1]{0:T(128)} %bitcast.1.refs_0_, bf16[128,2048]{1,0:T(8,128)(2,1)} %get-tuple-element.123.refs_1_, bf16[128,2048]{1,0:T(8,128)(2,1)} %copy-done.13, bf16[128,2048]{1,0:T(8,128)(2,1)} %copy-done.11, bf16[128,2048]{1,0:T(8,128)(2,1)} %copy-done.10, ...), custom_call_target="tpu_custom_call" | custom-call | flops 4294967296 | bytes 11534336 | tf_op jit(solution)/shard_map/pallas_call | solution.py:359
  131.9 10.1 %collective-permute-done.13.refs_4_ = bf16[128,2048]{1,0:T(8,128)(2,1)S(1)} collective-permute-done((bf16[128,2048]{1,0:T(8,128)(2,1)S(1)}, bf16[128,2048]{1,0:T(8,128)(2,1)S(1)}, u32[]{:S(2)}, u32[]{:S(2)}) %collective-permute-start.13) | collective-permute-done | bytes 524320 | tf_op jit(solution)/shard_map/ppermute | solution.py:413
  142.0 10.5 %collective-permute-done.12.refs_3_ = bf16[128,2048]{1,0:T(8,128)(2,1)S(1)} collective-permute-done((bf16[128,2048]{1,0:T(8,128)(2,1)S(1)}, bf16[128,2048]{1,0:T(8,128)(2,1)S(1)}, u32[]{:S(2)}, u32[]{:S(2)}) %collective-permute-start.12) | collective-permute-done | bytes 524320 | tf_op jit(solution)/shard_map/ppermute | solution.py:413
  154.0 8.9 %shard_map.125 = (bf16[256,2048]{1,0:T(8,128)(2,1)}, f32[256,2048]{1,0:T(8,128)}) custom-call(s32[1]{0:T(128)} %bitcast.1.refs_0_, bf16[128,2048]{1,0:T(8,128)(2,1)} %get-tuple-element.119.refs_1_, bf16[128,2048]{1,0:T(8,128)(2,1)} %copy-done.15, bf16[128,2048]{1,0:T(8,128)(2,1)} %copy-done.14, bf16[128,2048]{1,0:T(8,128)(2,1)} %copy-done.12, ...), custom_call_target="tpu_custom_call" | custom-call | flops 4294967296 | bytes 11534336 | tf_op jit(solution)/shard_map/pallas_call | solution.py:359
  163.9 9.0 %shard_map.124 = (bf16[256,2048]{1,0:T(8,128)(2,1)}, f32[256,2048]{1,0:T(8,128)}) custom-call(s32[1]{0:T(128)} %bitcast.1.refs_0_, bf16[128,2048]{1,0:T(8,128)(2,1)} %get-tuple-element.119.refs_1_, bf16[128,2048]{1,0:T(8,128)(2,1)} %copy-done.15, bf16[128,2048]{1,0:T(8,128)(2,1)} %copy-done.14, bf16[128,2048]{1,0:T(8,128)(2,1)} %copy-done.12, ...), custom_call_target="tpu_custom_call" | custom-call | flops 4294967296 | bytes 11534336 | tf_op jit(solution)/shard_map/pallas_call | solution.py:359
  180.9 16.6 %collective-permute-done.16 = bf16[256,2048]{1,0:T(8,128)(2,1)} collective-permute-done((bf16[256,2048]{1,0:T(8,128)(2,1)}, bf16[256,2048]{1,0:T(8,128)(2,1)}, u32[]{:S(2)}, u32[]{:S(2)}) %collective-permute-start.16) | collective-permute-done | bytes 1048608 | tf_op jit(solution)/shard_map/ppermute | solution.py:413
  203.3 7.1 %collective-permute-done.19.refs_6_ = bf16[128,2048]{1,0:T(8,128)(2,1)S(1)} collective-permute-done((bf16[128,2048]{1,0:T(8,128)(2,1)S(1)}, bf16[128,2048]{1,0:T(8,128)(2,1)S(1)}, u32[]{:S(2)}, u32[]{:S(2)}) %collective-permute-start.19) | collective-permute-done | bytes 524320 | tf_op jit(solution)/shard_map/ppermute | solution.py:413
  210.4 9.9 %collective-permute-done.20.refs_7_ = bf16[128,2048]{1,0:T(8,128)(2,1)S(1)} collective-permute-done((bf16[128,2048]{1,0:T(8,128)(2,1)S(1)}, bf16[128,2048]{1,0:T(8,128)(2,1)S(1)}, u32[]{:S(2)}, u32[]{:S(2)}) %collective-permute-start.20) | collective-permute-done | bytes 524320 | tf_op jit(solution)/shard_map/ppermute | solution.py:413
  221.8 5.2 %shard_map.126.v_ref.refs_2_ = bf16[256,4096]{1,0:T(8,128)(2,1)} custom-call(f32[256,2048]{1,0:T(8,128)} %copy-done.4, f32[256,2048]{1,0:T(8,128)} %copy-done.7, f32[256,2048]{1,0:T(8,128)} %copy-done.5, f32[256,2048]{1,0:T(8,128)} %copy-done.6, bf16[128,2048]{1,0:T(8,128)(2,1)} %copy-done.24, bf16[128,2048]{1,0:T(8,128)(2,1)} %copy-done.26, ...), custom_call_target="tpu_custom_call" | custom-call | flops 2097152 | bytes 8388608 | tf_op jit(solution)/shard_map/pallas_call | solution.py:400
  227.0 3.5 %shard_map.128 = f32[16,256,128]{2,1,0:T(8,128)} custom-call(s32[1]{0:T(128)} %bitcast.at_ref, bf16[256,4096]{1,0:T(8,128)(2,1)} %shard_map.126.v_ref.refs_2_, f32[4,256,8]{2,1,0:T(8,128)} %bitcast.31, bf16[256,256]{1,0:T(8,128)(2,1)} %bitcast.48), custom_call_target="tpu_custom_call" | custom-call | flops 536870912 | bytes 3145728 | tf_op jit(solution)/shard_map/pallas_call | solution.py:65
  230.6 3.6 %shard_map.127 = f32[16,256,128]{2,1,0:T(8,128)} custom-call(s32[1]{0:T(128)} %bitcast.6.at_ref, bf16[256,4096]{1,0:T(8,128)(2,1)} %shard_map.126.v_ref.refs_2_, f32[4,256,8]{2,1,0:T(8,128)} %bitcast.32, bf16[256,256]{1,0:T(8,128)(2,1)} %bitcast.49), custom_call_target="tpu_custom_call" | custom-call | flops 536870912 | bytes 3145728 | tf_op jit(solution)/shard_map/pallas_call | solution.py:65
  234.1 7.7 %shard_map.129 = (f32[256,4096]{1,0:T(8,128)}, f32[4,256,8]{2,1,0:T(8,128)}, f32[4,256,8]{2,1,0:T(8,128)}, f32[256,256]{1,0:T(8,128)}, f32[256,256]{1,0:T(8,128)}) custom-call(s32[1]{0:T(128)} %constant.66.clone.1.refs_0_, bf16[256,4096]{1,0:T(8,128)(2,1)} %x_ref.3, bf16[256,4096]{1,0:T(8,128)(2,1)} %shard_map.126.v_ref.refs_2_, bf16[256,256]{1,0:T(8,128)(2,1)} %b_ref.5, ...), custom_call_target="tpu_custom_call" | custom-call | flops 939524096 | bytes 7340032 | tf_op jit(solution)/shard_map/pallas_call | solution.py:197
  247.1 12.5 %shard_map.130 = (f32[256,4096]{1,0:T(8,128)}, f32[4,256,8]{2,1,0:T(8,128)}, f32[4,256,8]{2,1,0:T(8,128)}, f32[256,256]{1,0:T(8,128)}, f32[256,256]{1,0:T(8,128)}) custom-call(s32[1]{0:T(128)} %constant.67.clone.1.refs_0_, bf16[256,4096]{1,0:T(8,128)(2,1)} %x_ref.3, ...), custom_call_target="tpu_custom_call", output_to_operand_aliasing={{0}: (12, {}), {1}: (13, {}), {2}: (14, {})} | custom-call | flops 1879048192 | bytes 14680064 | tf_op jit(solution)/shard_map/pallas_call | solution.py:197
  264.6 7.9 %shard_map.131 = (f32[256,4096]{1,0:T(8,128)}, f32[4,256,8]{2,1,0:T(8,128)}, f32[4,256,8]{2,1,0:T(8,128)}, f32[256,256]{1,0:T(8,128)}, f32[256,256]{1,0:T(8,128)}) custom-call(s32[1]{0:T(128)} %constant.54.clone.1.refs_0_, bf16[256,4096]{1,0:T(8,128)(2,1)} %x_ref.3, ...), custom_call_target="tpu_custom_call", output_to_operand_aliasing={{0}: (12, {}), {1}: (13, {}), {2}: (14, {})} | custom-call | flops 939524096 | bytes 7340032 | tf_op jit(solution)/shard_map/pallas_call | solution.py:197
  272.5 3.8 %collective-permute-done.25 = bf16[8,256,128]{2,1,0:T(8,128)(2,1)} collective-permute-done((bf16[8,256,128]{2,1,0:T(8,128)(2,1)}, bf16[8,256,128]{2,1,0:T(8,128)(2,1)}, u32[]{:S(2)}, u32[]{:S(2)}) %collective-permute-start.25) | collective-permute-done | bytes 524320 | tf_op jit(solution)/shard_map/ppermute | solution.py:413
  279.1 4.4 %fusion = (f32[16,256,128]{2,1,0:T(8,128)}, f32[16,256,128]{2,1,0:T(8,128)}) fusion(f32[8,256,128]{2,1,0:T(8,128)S(1)} %get-tuple-element.125, f32[8,256,128]{2,1,0:T(8,128)S(1)} %get-tuple-element.124, f32[16]{0:T(128)S(1)} %get-tuple-element.141, pred[]{:T(512)S(6)} %ne.17, f32[16,256,128]{2,1,0:T(8,128)S(1)} %copy-done.3, ...), kind=kLoop, calls=%fused_computation.4 | loop fusion | flops 3145728 | bytes 10485825 | tf_op jit(solution)/shard_map/jit(_where)/select_n | solution.py:536
  283.5 2.5 collective-permute-start.31
  288.0 9.1 %shard_map.132 = (bf16[256,4096]{1,0:T(8,128)(2,1)}, f32[256,256]{1,0:T(8,128)}, f32[4,256,8]{2,1,0:T(8,128)}, f32[4,256,8]{2,1,0:T(8,128)}) custom-call(s32[1]{0:T(128)} %bitcast.6.at_ref, bf16[256,4096]{1,0:T(8,128)(2,1)} %x_ref.3, f32[256,4096]{1,0:T(8,128)} %get-tuple-element.94.part_ref, bf16[256,256]{1,0:T(8,128)(2,1)} %b_ref.5, ...), custom_call_target="tpu_custom_call" | custom-call | flops 1073741824 | bytes 8388608 | tf_op jit(solution)/shard_map/pallas_call | solution.py:295
  298.4 9.1 %shard_map.133 = (bf16[256,4096]{1,0:T(8,128)(2,1)}, f32[256,256]{1,0:T(8,128)}, f32[4,256,8]{2,1,0:T(8,128)}, f32[4,256,8]{2,1,0:T(8,128)}) custom-call(s32[1]{0:T(128)} %bitcast.at_ref, bf16[256,4096]{1,0:T(8,128)(2,1)} %x_ref.3, f32[256,4096]{1,0:T(8,128)} %get-tuple-element.94.part_ref, ...), custom_call_target="tpu_custom_call", output_to_operand_aliasing={{0}: (11, {}), {2}: (12, {}), {3}: (13, {})} | custom-call | flops 1073741824 | bytes 8388608 | tf_op jit(solution)/shard_map/pallas_call | solution.py:295
  316.4 3.0 collective-permute-done.28
  (175 shorter events, 80.8 us)
Async XLA Ops:
  7.2 67.5 %all-gather.4.cloned.1.call-start = ((), (), s32[]{:S(2)}) async-start(), calls=%async_computation | async-start | bytes 2621440 | tf_op jit(solution)/shard_map/all_gather | solution.py:445
  7.2 97.8 %collective-permute-start.6 = (bf16[4096,1024]{1,0:T(8,128)(2,1)}, bf16[4096,1024]{1,0:T(8,128)(2,1)}, u32[]{:S(2)}, u32[]{:S(2)}) collective-permute-start(bf16[4096,1024]{1,0:T(8,128)(2,1)} %refs_5_.7), channel_id=1, source_target_pairs={{0,4},{4,0},{8,12},{12,8},{16,20},{20,16},{24,28},{28,24},{1,5},{5... | collective-permute-start | bytes 25165832 | tf_op jit(solution)/shard_map/ppermute | solution.py:417
  17.6 14.2 %collective-permute-start = (f32[16,256,128]{2,1,0:T(8,128)}, f32[16,256,128]{2,1,0:T(8,128)S(1)}, u32[]{:S(2)}, u32[]{:S(2)}) collective-permute-start(f32[16,256,128]{2,1,0:T(8,128)} %shard_map.120), channel_id=1, source_target_pairs={{0,4},{4,0},{8,12},{12,8},{16,20},{20,16},{24,28},{28,24},{1,5},{5... | collective-permute-start | bytes 6291464 | tf_op jit(solution)/shard_map/ppermute | solution.py:417
  17.7 106.1 %all-gather.6.cloned.1.call-start = ((), (), s32[]{:S(2)}) async-start(), calls=%async_computation.1 | async-start | bytes 2621440 | tf_op jit(solution)/shard_map/all_gather | solution.py:445
  34.9 14.5 %collective-permute-start.2 = (bf16[8,256,128]{2,1,0:T(8,128)(2,1)}, bf16[8,256,128]{2,1,0:T(8,128)(2,1)}, u32[]{:S(2)}, u32[]{:S(2)}) collective-permute-start(bf16[8,256,128]{2,1,0:T(8,128)(2,1)} %get-tuple-element.136), channel_id=1, source_target_pairs={{0,16},{4,20},{8,24},{12,28},{16,0},{20,4},{24,8},{28,12},{1,17},{... | collective-permute-start | bytes 1572872 | tf_op jit(solution)/shard_map/ppermute | solution.py:413
  36.4 14.2 %collective-permute-start.1 = (bf16[8,256,128]{2,1,0:T(8,128)(2,1)}, bf16[8,256,128]{2,1,0:T(8,128)(2,1)}, u32[]{:S(2)}, u32[]{:S(2)}) collective-permute-start(bf16[8,256,128]{2,1,0:T(8,128)(2,1)} %get-tuple-element.137), channel_id=1, source_target_pairs={{0,8},{4,12},{8,0},{12,4},{16,24},{20,28},{24,16},{28,20},{1,9},{5... | collective-permute-start | bytes 1572872 | tf_op jit(solution)/shard_map/ppermute | solution.py:413
  53.2 13.4 %collective-permute-start.9 = (bf16[8,256,128]{2,1,0:T(8,128)(2,1)}, bf16[8,256,128]{2,1,0:T(8,128)(2,1)}, u32[]{:S(2)}, u32[]{:S(2)}) collective-permute-start(bf16[8,256,128]{2,1,0:T(8,128)(2,1)} %get-tuple-element.134), channel_id=1, source_target_pairs={{0,8},{4,12},{8,0},{12,4},{16,24},{20,28},{24,16},{28,20},{1,9},{5... | collective-permute-start | bytes 1572872 | tf_op jit(solution)/shard_map/ppermute | solution.py:413
  53.7 13.2 %collective-permute-start.8 = (bf16[8,256,128]{2,1,0:T(8,128)(2,1)}, bf16[8,256,128]{2,1,0:T(8,128)(2,1)}, u32[]{:S(2)}, u32[]{:S(2)}) collective-permute-start(bf16[8,256,128]{2,1,0:T(8,128)(2,1)} %get-tuple-element.135), channel_id=1, source_target_pairs={{0,16},{4,20},{8,24},{12,28},{16,0},{20,4},{24,8},{28,12},{1,17},{... | collective-permute-start | bytes 1572872 | tf_op jit(solution)/shard_map/ppermute | solution.py:413
  71.8 19.1 %collective-permute-start.10 = (f32[16,256,128]{2,1,0:T(8,128)}, f32[16,256,128]{2,1,0:T(8,128)}, u32[]{:S(2)}, u32[]{:S(2)}) collective-permute-start(f32[16,256,128]{2,1,0:T(8,128)} %get-tuple-element.115), channel_id=1, source_target_pairs={{0,4},{4,0},{8,12},{12,8},{16,20},{20,16},{24,28},{28,24},{1,5},{5... | collective-permute-start | bytes 6291464 | tf_op jit(solution)/shard_map/ppermute | solution.py:417
  78.3 17.7 %collective-permute-start.5 = (bf16[128,2048]{1,0:T(8,128)(2,1)}, bf16[128,2048]{1,0:T(8,128)(2,1)S(1)}, u32[]{:S(2)}, u32[]{:S(2)}) collective-permute-start(bf16[128,2048]{1,0:T(8,128)(2,1)} %get-tuple-element.120), channel_id=1, source_target_pairs={{0,24},{4,28},{8,16},{12,20},{16,8},{20,12},{24,0},{28,4},{1,25},{... | collective-permute-start | bytes 1572872 | tf_op jit(solution)/shard_map/ppermute | solution.py:413
  79.8 25.2 %collective-permute-start.4 = (bf16[128,2048]{1,0:T(8,128)(2,1)}, bf16[128,2048]{1,0:T(8,128)(2,1)S(1)}, u32[]{:S(2)}, u32[]{:S(2)}) collective-permute-start(bf16[128,2048]{1,0:T(8,128)(2,1)} %get-tuple-element.121), channel_id=1, source_target_pairs={{0,16},{4,20},{8,24},{12,28},{16,0},{20,4},{24,8},{28,12},{1,17},{... | collective-permute-start | bytes 1572872 | tf_op jit(solution)/shard_map/ppermute | solution.py:413
  81.3 23.7 %collective-permute-start.3 = (bf16[128,2048]{1,0:T(8,128)(2,1)}, bf16[128,2048]{1,0:T(8,128)(2,1)S(1)}, u32[]{:S(2)}, u32[]{:S(2)}) collective-permute-start(bf16[128,2048]{1,0:T(8,128)(2,1)} %get-tuple-element.122), channel_id=1, source_target_pairs={{0,8},{4,12},{8,0},{12,4},{16,24},{20,28},{24,16},{28,20},{1,9},{5... | collective-permute-start | bytes 1572872 | tf_op jit(solution)/shard_map/ppermute | solution.py:413
  126.3 15.7 %collective-permute-start.13 = (bf16[128,2048]{1,0:T(8,128)(2,1)S(1)}, bf16[128,2048]{1,0:T(8,128)(2,1)S(1)}, u32[]{:S(2)}, u32[]{:S(2)}) collective-permute-start(bf16[128,2048]{1,0:T(8,128)(2,1)S(1)} %get-tuple-element.116), channel_id=1, source_target_pairs={{0,24},{4,28},{8,16},{12,20},{16,8},{20,12},{24,0},{28,4},{1,25},{... | collective-permute-start | bytes 1572872 | tf_op jit(solution)/shard_map/ppermute | solution.py:413
  127.9 24.6 %collective-permute-start.12 = (bf16[128,2048]{1,0:T(8,128)(2,1)S(1)}, bf16[128,2048]{1,0:T(8,128)(2,1)S(1)}, u32[]{:S(2)}, u32[]{:S(2)}) collective-permute-start(bf16[128,2048]{1,0:T(8,128)(2,1)S(1)} %get-tuple-element.117), channel_id=1, source_target_pairs={{0,16},{4,20},{8,24},{12,28},{16,0},{20,4},{24,8},{28,12},{1,17},{... | collective-permute-start | bytes 1572872 | tf_op jit(solution)/shard_map/ppermute | solution.py:413
  129.2 24.0 %collective-permute-start.11 = (bf16[128,2048]{1,0:T(8,128)(2,1)S(1)}, bf16[128,2048]{1,0:T(8,128)(2,1)S(1)}, u32[]{:S(2)}, u32[]{:S(2)}) collective-permute-start(bf16[128,2048]{1,0:T(8,128)(2,1)S(1)} %get-tuple-element.118), channel_id=1, source_target_pairs={{0,8},{4,12},{8,0},{12,4},{16,24},{20,28},{24,16},{28,20},{1,9},{5... | collective-permute-start | bytes 1572872 | tf_op jit(solution)/shard_map/ppermute | solution.py:413
  129.8 45.2 %collective-permute-start.15 = (bf16[256,2048]{1,0:T(8,128)(2,1)}, bf16[256,2048]{1,0:T(8,128)(2,1)S(1)}, u32[]{:S(2)}, u32[]{:S(2)}) collective-permute-start(bf16[256,2048]{1,0:T(8,128)(2,1)} %get-tuple-element.67), channel_id=1, source_target_pairs={{0,16},{4,20},{8,24},{12,28},{16,0},{20,4},{24,8},{28,12},{1,17},{... | collective-permute-start | bytes 3145736 | tf_op jit(solution)/shard_map/ppermute | solution.py:413
  131.2 43.8 %collective-permute-start.7 = (bf16[256,2048]{1,0:T(8,128)(2,1)}, bf16[256,2048]{1,0:T(8,128)(2,1)}, u32[]{:S(2)}, u32[]{:S(2)}) collective-permute-start(bf16[256,2048]{1,0:T(8,128)(2,1)} %get-tuple-element.62), channel_id=1, source_target_pairs={{0,8},{4,12},{8,0},{12,4},{16,24},{20,28},{24,16},{28,20},{1,9},{5... | collective-permute-start | bytes 3145736 | tf_op jit(solution)/shard_map/ppermute | solution.py:413
  163.0 34.5 %collective-permute-start.16 = (bf16[256,2048]{1,0:T(8,128)(2,1)}, bf16[256,2048]{1,0:T(8,128)(2,1)}, u32[]{:S(2)}, u32[]{:S(2)}) collective-permute-start(bf16[256,2048]{1,0:T(8,128)(2,1)} %get-tuple-element.75), channel_id=1, source_target_pairs={{0,16},{4,20},{8,24},{12,28},{16,0},{20,4},{24,8},{28,12},{1,17},{... | collective-permute-start | bytes 3145736 | tf_op jit(solution)/shard_map/ppermute | solution.py:413
  172.9 28.0 %collective-permute-start.14 = (bf16[256,2048]{1,0:T(8,128)(2,1)}, bf16[256,2048]{1,0:T(8,128)(2,1)S(1)}, u32[]{:S(2)}, u32[]{:S(2)}) collective-permute-start(bf16[256,2048]{1,0:T(8,128)(2,1)} %get-tuple-element.71), channel_id=1, source_target_pairs={{0,8},{4,12},{8,0},{12,4},{16,24},{20,28},{24,16},{28,20},{1,9},{5... | collective-permute-start | bytes 3145736 | tf_op jit(solution)/shard_map/ppermute | solution.py:413
  178.8 31.6 %collective-permute-start.19 = (bf16[128,2048]{1,0:T(8,128)(2,1)S(1)}, bf16[128,2048]{1,0:T(8,128)(2,1)S(1)}, u32[]{:S(2)}, u32[]{:S(2)}) collective-permute-start(bf16[128,2048]{1,0:T(8,128)(2,1)S(1)} %slice.169), channel_id=1, source_target_pairs={{0,8},{4,12},{8,0},{12,4},{16,24},{20,28},{24,16},{28,20},{1,9},{5... | collective-permute-start | bytes 1572872 | tf_op jit(solution)/shard_map/ppermute | solution.py:413
  180.3 30.1 %collective-permute-start.17 = (bf16[128,2048]{1,0:T(8,128)(2,1)S(1)}, bf16[128,2048]{1,0:T(8,128)(2,1)S(1)}, u32[]{:S(2)}, u32[]{:S(2)}) collective-permute-start(bf16[128,2048]{1,0:T(8,128)(2,1)S(1)} %slice.171), channel_id=1, source_target_pairs={{0,16},{4,20},{8,24},{12,28},{16,0},{20,4},{24,8},{28,12},{1,17},{... | collective-permute-start | bytes 1572872 | tf_op jit(solution)/shard_map/ppermute | solution.py:413
  199.3 20.9 %collective-permute-start.20 = (bf16[128,2048]{1,0:T(8,128)(2,1)S(1)}, bf16[128,2048]{1,0:T(8,128)(2,1)S(1)}, u32[]{:S(2)}, u32[]{:S(2)}) collective-permute-start(bf16[128,2048]{1,0:T(8,128)(2,1)S(1)} %slice.168), channel_id=1, source_target_pairs={{0,8},{4,12},{8,0},{12,4},{16,24},{20,28},{24,16},{28,20},{1,9},{5... | collective-permute-start | bytes 1572872 | tf_op jit(solution)/shard_map/ppermute | solution.py:413
  202.5 17.7 %collective-permute-start.18 = (bf16[128,2048]{1,0:T(8,128)(2,1)S(1)}, bf16[128,2048]{1,0:T(8,128)(2,1)S(1)}, u32[]{:S(2)}, u32[]{:S(2)}) collective-permute-start(bf16[128,2048]{1,0:T(8,128)(2,1)S(1)} %slice.170), channel_id=1, source_target_pairs={{0,16},{4,20},{8,24},{12,28},{16,0},{20,4},{24,8},{28,12},{1,17},{... | collective-permute-start | bytes 1572872 | tf_op jit(solution)/shard_map/ppermute | solution.py:413
  230.6 11.2 %collective-permute-start.21 = (f32[16,256,128]{2,1,0:T(8,128)}, f32[16,256,128]{2,1,0:T(8,128)}, u32[]{:S(2)}, u32[]{:S(2)}) collective-permute-start(f32[16,256,128]{2,1,0:T(8,128)} %shard_map.128), channel_id=1, source_target_pairs={{0,4},{4,0},{8,12},{12,8},{16,20},{20,16},{24,28},{28,24},{1,5},{5... | collective-permute-start | bytes 6291464 | tf_op jit(solution)/shard_map/ppermute | solution.py:417
  244.9 14.7 %collective-permute-start.23 = (bf16[8,256,128]{2,1,0:T(8,128)(2,1)}, bf16[8,256,128]{2,1,0:T(8,128)(2,1)S(1)}, u32[]{:S(2)}, u32[]{:S(2)}) collective-permute-start(bf16[8,256,128]{2,1,0:T(8,128)(2,1)} %get-tuple-element.128), channel_id=1, source_target_pairs={{0,16},{4,20},{8,24},{12,28},{16,0},{20,4},{24,8},{28,12},{1,17},{... | collective-permute-start | bytes 1572872 | tf_op jit(solution)/shard_map/ppermute | solution.py:413
  245.5 14.3 %collective-permute-start.22 = (bf16[8,256,128]{2,1,0:T(8,128)(2,1)}, bf16[8,256,128]{2,1,0:T(8,128)(2,1)}, u32[]{:S(2)}, u32[]{:S(2)}) collective-permute-start(bf16[8,256,128]{2,1,0:T(8,128)(2,1)} %get-tuple-element.129), channel_id=1, source_target_pairs={{0,8},{4,12},{8,0},{12,4},{16,24},{20,28},{24,16},{28,20},{1,9},{5... | collective-permute-start | bytes 1572872 | tf_op jit(solution)/shard_map/ppermute | solution.py:413
  262.4 13.9 %collective-permute-start.25 = (bf16[8,256,128]{2,1,0:T(8,128)(2,1)}, bf16[8,256,128]{2,1,0:T(8,128)(2,1)}, u32[]{:S(2)}, u32[]{:S(2)}) collective-permute-start(bf16[8,256,128]{2,1,0:T(8,128)(2,1)} %get-tuple-element.126), channel_id=1, source_target_pairs={{0,8},{4,12},{8,0},{12,4},{16,24},{20,28},{24,16},{28,20},{1,9},{5... | collective-permute-start | bytes 1572872 | tf_op jit(solution)/shard_map/ppermute | solution.py:413
  263.9 13.2 %collective-permute-start.24 = (bf16[8,256,128]{2,1,0:T(8,128)(2,1)}, bf16[8,256,128]{2,1,0:T(8,128)(2,1)}, u32[]{:S(2)}, u32[]{:S(2)}) collective-permute-start(bf16[8,256,128]{2,1,0:T(8,128)(2,1)} %get-tuple-element.127), channel_id=1, source_target_pairs={{0,16},{4,20},{8,24},{12,28},{16,0},{20,4},{24,8},{28,12},{1,17},{... | collective-permute-start | bytes 1572872 | tf_op jit(solution)/shard_map/ppermute | solution.py:413
  283.5 13.5 %collective-permute-start.26 = (f32[16,256,128]{2,1,0:T(8,128)}, f32[16,256,128]{2,1,0:T(8,128)S(1)}, u32[]{:S(2)}, u32[]{:S(2)}) collective-permute-start(f32[16,256,128]{2,1,0:T(8,128)} %get-tuple-element.113), channel_id=1, source_target_pairs={{0,4},{4,0},{8,12},{12,8},{16,20},{20,16},{24,28},{28,24},{1,5},{5... | collective-permute-start | bytes 6291464 | tf_op jit(solution)/shard_map/ppermute | solution.py:417
  283.5 29.2 %collective-permute-start.31 = (bf16[256,256]{1,0:T(8,128)(2,1)S(1)}, bf16[256,256]{1,0:T(8,128)(2,1)S(1)}, u32[]{:S(2)}, u32[]{:S(2)}) collective-permute-start(bf16[256,256]{1,0:T(8,128)(2,1)S(1)} %convert_element_type.131), channel_id=1, source_target_pairs={{0,2},{1,3},{2,0},{3,1},{4,6},{5,7},{6,4},{7,5},{8,10},{9,11},{10,... | collective-permute-start | bytes 393224 | tf_op jit(solution)/shard_map/ppermute | solution.py:429
  286.1 26.9 %collective-permute-start.30 = (bf16[256,256]{1,0:T(8,128)(2,1)S(1)}, bf16[256,256]{1,0:T(8,128)(2,1)S(1)}, u32[]{:S(2)}, u32[]{:S(2)}) collective-permute-start(bf16[256,256]{1,0:T(8,128)(2,1)S(1)} %convert_element_type.131), channel_id=1, source_target_pairs={{0,1},{1,0},{2,3},{3,2},{4,5},{5,4},{6,7},{7,6},{8,9},{9,8},{10,11... | collective-permute-start | bytes 393224 | tf_op jit(solution)/shard_map/ppermute | solution.py:429
  287.7 25.3 %collective-permute-start.32 = (bf16[256,256]{1,0:T(8,128)(2,1)S(1)}, bf16[256,256]{1,0:T(8,128)(2,1)S(1)}, u32[]{:S(2)}, u32[]{:S(2)}) collective-permute-start(bf16[256,256]{1,0:T(8,128)(2,1)S(1)} %convert_element_type.131), channel_id=1, source_target_pairs={{0,3},{1,2},{2,1},{3,0},{4,7},{5,6},{6,5},{7,4},{8,11},{9,10},{10,... | collective-permute-start | bytes 393224 | tf_op jit(solution)/shard_map/ppermute | solution.py:429
  (33 other events, 289.8 us)
Sparse Core Ops, SparseCore 0:
  17.8 48.6 all-gather.3
  68.1 44.8 all-gather.5

commit v5 on v4

--- a/solution.py
+++ b/solution.py
@@ -8,12 +8,11 @@
 BF16 = jnp.bfloat16
 F32 = jnp.float32
 HIGH = lax.Precision.HIGHEST
-CHUNKS = 2
 GROUP = 8
 NN = (((1,), (0,)), ((), ()))
 NT = (((1,), (1,)), ((), ()))
 TN = (((0,), (0,)), ((), ()))
-PARAMS = pltpu.CompilerParams(vmem_limit_bytes=60 << 20)
+PARAMS = pltpu.CompilerParams(vmem_limit_bytes=28 << 20)
 
 
 def mm(a, b, dims):
@@ -46,7 +45,10 @@
 
 
 def cost(flops, size, exps=0):
-    return pl.CostEstimate(flops=flops, bytes_accessed=size, transcendentals=exps)
+    scale = 256
+    return pl.CostEstimate(
+        flops=flops // scale, bytes_accessed=size // scale, transcendentals=exps // scale
+    )
 
 
 def states_kernel(at_ref, v_ref, scale_ref, rows_ref, out_ref):
@@ -379,32 +381,37 @@
 def finish_kernel(count, *refs):
     keeps, arrived, out_ref = refs[: 2 * count], refs[2 * count : -1], refs[-1]
     steps = pl.num_programs(0) // 2
-    rows = arrived[0].shape[0]
     for lane in range(2):
 
         @pl.when(pl.program_id(0) // steps == lane)
         def _():
+            start = 0
             for chunk in range(count):
                 at = lane * count + chunk
                 total = keeps[at][...] + arrived[at][...].astype(F32)
-                out_ref[chunk * rows : (chunk + 1) * rows, :] = total.astype(BF16)
+                rows = total.shape[0]
+                out_ref[start : start + rows, :] = total.astype(BF16)
+                start += rows
 
 
 def finish(keeps, arrived):
     count = len(keeps) // 2
-    rows, half = arrived[0].shape
+    half = arrived[0].shape[1]
+    span = sum(a.shape[0] for a in arrived) // 2
     tile = min(1024, half)
     steps = half // tile
     place = [lambda i: (0, jnp.minimum(i, steps - 1)), lambda i: (0, jnp.maximum(i - steps, 0))]
-    specs = [pl.BlockSpec((rows, tile), place[lane]) for lane in range(2) for _ in range(count)]
+    specs = [
+        pl.BlockSpec((a.shape[0], tile), place[i // count]) for i, a in enumerate(arrived)
+    ]
     return pl.pallas_call(
         lambda *refs: finish_kernel(count, *refs),
         grid=(2 * steps,),
         in_specs=specs + specs,
-        out_specs=pl.BlockSpec((rows * count, tile), lambda i: (0, i)),
-        out_shape=jax.ShapeDtypeStruct((rows * count, 2 * half), BF16),
+        out_specs=pl.BlockSpec((span, tile), lambda i: (0, i)),
+        out_shape=jax.ShapeDtypeStruct((span, 2 * half), BF16),
         compiler_params=PARAMS,
-        cost_estimate=cost(4 * rows * count * half, 16 * rows * count * half),
+        cost_estimate=cost(4 * span * half, 16 * span * half),
     )(*keeps, *arrived)
 
 
@@ -435,16 +442,21 @@
     return terms[0]
 
 
-def project(grad_out, out_weight, chips, chip, core, before):
-    span = grad_out.shape[0]
-    both = 2 * out_weight.shape[1]
-    other = other_core(out_weight, chips)
+def gather_halves(grad_out):
+    half = grad_out.shape[0] // 2
+    pieces = [grad_out[:half], grad_out[half:]]
+    return pieces[0], [lax.all_gather(p, "head", axis=1, tiled=True) for p in pieces]
+
+
+def blocks_of(full, start, rows, chips, chip):
+    both = full.shape[1] // chips
+    return [
+        lax.dynamic_slice(full, (start, (chip ^ hop) * both), (rows, both)) for hop in range(chips)
+    ]
+
+
+def project(fulls, own, out_weight, other, chips, chip, core, before):
     core_at = core.astype(jnp.int32).reshape(1)
-    rows = span // CHUNKS
-    fulls = [
-        lax.all_gather(grad_out[i * rows : (i + 1) * rows], "head", axis=1, tiled=True)
-        for i in range(CHUNKS)
-    ]
     lanes = []
     for order in orders(chips):
         hops = [0]
@@ -453,32 +465,42 @@
         lanes.append((order, hops))
     waiting = [[], []]
 
-    def reduce_last(blocks):
+    def reduce(chunk, rows, after):
         for lane, (order, _) in enumerate(lanes):
-            keep, send = waiting[lane][-1]
+            keep, send, arrived = waiting[lane][chunk]
             for step, bit in enumerate(order):
-                arrived = across(send, bit, chips)
-                if step == 0 and blocks is not None:
-                    arrived = tie(arrived, *blocks)
+                if step:
+                    arrived = across(send, bit, chips)
+                elif after:
+                    arrived = tie(arrived, *after)
                 if step < len(order) - 1:
                     keep = keep + arrived.astype(F32)
                     size = keep.shape[0] // 2
                     send = keep[size:].astype(BF16)
                     keep = keep[:size] if size > rows else keep
-            waiting[lane][-1] = (keep, arrived)
-
-    for chunk in range(CHUNKS):
-        full = tie(fulls[chunk], *before[chunk], *[w[-1][1] for w in waiting if w])
-        own = [
-            lax.dynamic_slice_in_dim(full, (chip ^ hop) * both, both, 1) for hop in range(chips)
-        ]
-        if chunk:
-            reduce_last(own)
+            waiting[lane][chunk] = (keep, arrived)
+
+    half = fulls[0].shape[0]
+    rows = [half, half // 2, half // 2]
+    count = len(rows)
+    for chunk in range(count):
         blocks = [across(block, hop, chips) if hop else block for hop, block in enumerate(own)]
-        for lane, (_, hops) in enumerate(lanes):
+        if chunk == 0:
+            blocks = lax.optimization_barrier((*blocks, *before))[:chips]
+        if chunk == 1:
+            full = tie(fulls[1], waiting[0][0][2], *own)
+            own = blocks_of(full, rows[1], rows[2], chips, chip)
+            blocks = lax.optimization_barrier((*blocks, *own))[:chips]
+        for lane, (order, hops) in enumerate(lanes):
             send, keep = partial_sums(blocks, hops, out_weight, other, lane, core_at)
-            waiting[lane].append((keep, send))
-    reduce_last(None)
+            waiting[lane].append((keep, send, across(send, order[0], chips)))
+        if chunk == 0:
+            full = tie(fulls[1], *[lane[0][1] for lane in waiting])
+            own = blocks_of(full, 0, rows[1], chips, chip)
+        if chunk == 1:
+            reduce(0, rows[0], own)
+    reduce(count - 2, rows[count - 2], None)
+    reduce(count - 1, rows[count - 1], None)
     ends = waiting[0] + waiting[1]
     return finish([keep for keep, _ in ends], [arrived for _, arrived in ends])
 
@@ -549,6 +571,11 @@
     mine_at = (core * (groups // 2)).astype(jnp.int32).reshape(1)
     other_at = ((1 - core) * (groups // 2)).astype(jnp.int32).reshape(1)
 
+    first_rows, fulls = gather_halves(grad_out)
+    log_decay, step_size, b_in, c_in, _ = lax.optimization_barrier(
+        (log_decay, step_size, b_in, c_in, first_rows)
+    )
+    other_weight = other_core(out_weight, chips)
     upto = jnp.tril(jnp.ones((span, span), F32))
     running = jnp.dot(upto, log_decay, precision=HIGH)
     ends = lax.all_gather(running[-1], "seq")
@@ -565,25 +592,27 @@
         theirs = other_core(to_other, chips)
         return span_states(values, scale, rows_t, mine_at, groups // 2), theirs
 
-    last_sent = []
-
-    def note(step, sent):
-        last_sent[:] = sent
-        return []
-
-    first_rows = grad_out[: span // CHUNKS]
-    scale = tie(by_group(step_size * tail), first_rows)
-    mine, theirs = span_both(ssm_input, scale, b_rows)
-    for_mine, for_theirs = exchange(mine, theirs, ends, chips, chip, core, False, note)
+    own = []
+
+    def first_blocks(step, sent):
+        if step < chips.bit_length() - 2:
+            return []
+        own[:] = blocks_of(tie(fulls[0], *sent), 0, span // 2, chips, chip)
+        return own
+
+    mine, theirs = span_both(ssm_input, by_group(step_size * tail), b_rows)
+    for_mine, for_theirs = exchange(
+        mine, theirs, ends, chips, chip, core, False, first_blocks
+    )
     arrived = other_core(for_theirs, chips)
     incoming = jnp.where(
         core == 0,
         jnp.concatenate([for_mine, arrived], axis=0),
         jnp.concatenate([arrived, for_mine], axis=0),
     )
-    decay, weight, cross = decays(tie(running_g, *last_sent), running_t, b_in, c_in)
-    before = [[*last_sent, steps_g, skip_rows, rise, c_rows]] + [[incoming, cross]] * (CHUNKS - 1)
-    grad_y = project(grad_out, out_weight, chips, chip, core, before)
+    decay, weight, cross = decays(tie(running_g, *own), running_t, b_in, c_in)
+    before = [incoming, cross, steps_g, skip_rows, rise, c_rows]
+    grad_y = project(fulls, own, out_weight, other_weight, chips, chip, core, before)
 
     few = max(1, groups // 4)
     counts = [few, groups - 2 * few, few]

time: 330 us -> 317 us (0.961)
  Pallas kernels: 110 us -> 81.7 us
  local copies, waits for them, and re-layouts: 27.4 us -> 39.3 us
  starting transfers between devices: 33.3 us -> 41.3 us
  other arithmetic: 33.7 us -> 27.8 us
    unnamed x62 -> x66, local copies, waits for them, and re-layouts: 9.25 us -> 26.1 us
    ppermute x22 -> x29, waiting for transfers between devices: 94.9 us -> 86.2 us  [across(): return lax.ppermute(value, 'seq', pairs)]
    ppermute x22 -> x29, starting transfers between devices: 23.8 us -> 31.6 us  [across(): return lax.ppermute(value, 'seq', pairs)]
    all_gather x2, waiting for transfers between devices: 0.01 us -> 7.05 us  [gather_halves(): lax.all_gather(p, 'head', axis=1, tiled=True)]
    pallas_call x3, Pallas kernels: 28 us -> 21.2 us  [inner_part(): pl.pallas_call(lambda *refs: inner_kernel(not held, last, *refs), grid_sp...]
    pallas_call x2, Pallas kernels: 18.1 us -> 12.3 us  [outer_part(): pl.pallas_call(outer_kernel, grid_spec=pltpu.PrefetchScalarGridSpec(num_s...]
    pallas_call x4, Pallas kernels: 14.3 us -> 8.46 us  [span_states(): pl.pallas_call(states_kernel, grid_spec=pltpu.PrefetchScalarGridSpec(num_...]
    pallas_call x1, Pallas kernels: 8.15 us -> 2.87 us  [decays(): pl.pallas_call(decay_kernel, grid=(groups,), in_specs=[pl.BlockSpec((1, s...]
  transfers between devices with their start and end apart: 35 -> 42, of which waited for: 18 -> 19; matrix products, arithmetic and copies ran while one was open for 12% -> 10% of each run, Pallas kernels for 31% -> 25%
where the time goes in v5:
time: 317 us; the launch traced here: 316 us
  waiting for transfers between devices  99.3 us (31%)
  Pallas kernels  81.7 us (26%)
  starting transfers between devices  41.3 us (13%)
  local copies, waits for them, and re-layouts  39.3 us (12%)
  other arithmetic  27.8 us (9%)
  between operations  14.7 us (5%)
  blocking collectives  11.5 us (4%)
    ppermute x29, waiting for transfers between devices, across(): return lax.ppermute(value, 'seq', pairs)  86.2 us
    pallas_call x6, Pallas kernels, partial_sums(): pl.pallas_call(lambda *refs: project_kernel(hops, *refs), grid_spec=pltpu...  35.6 us
    ppermute x29, starting transfers between devices, across(): return lax.ppermute(value, 'seq', pairs)  31.6 us
    unnamed x66, local copies, waits for them, and re-layouts  26.1 us
    pallas_call x3, Pallas kernels, inner_part(): pl.pallas_call(lambda *refs: inner_kernel(not held, last, *refs), grid_sp...  21.2 us
    pallas_call x2, Pallas kernels, outer_part(): pl.pallas_call(outer_kernel, grid_spec=pltpu.PrefetchScalarGridSpec(num_s...  12.3 us
    all_gather x1, blocking collectives, local(): ends = lax.all_gather(running[-1], 'seq')  11.5 us
    ppermute x6, starting transfers between devices, sum_over_heads(): lax.ppermute(value, 'head', [(i, i ^ hop) for i in range(count)])  8.9 us
  transfers between devices with their start and end apart: 42, of which 19 were waited for; matrix products, arithmetic and copies ran while one was open for 10% of the time, Pallas kernels for 25%

profile of v5, /device:TPU:0, one launch (start us, length us, event | category | flops | bytes accessed | tf_op | source)
XLA Modules:
  0.0 316.0 jit_solution(13828090739097430184)
XLA Ops:
  15.6 11.5 %all-gather = f32[8,1,32]{2,1,0:T(1,128)S(1)} all-gather(f32[1,1,32]{2,1,0:T(1,128)S(1)} %bitcast.61), channel_id=1, replica_groups=mesh['seq'=8,'head'=4] {'seq'}, dimensions={0}, use_global_device_ids=true | all-gather | bytes 1152 | tf_op jit(solution)/shard_map/all_gather | solution.py:581
  34.2 11.1 %collective-permute-done.2 = bf16[8,256,128]{2,1,0:T(8,128)(2,1)} collective-permute-done((bf16[8,256,128]{2,1,0:T(8,128)(2,1)}, bf16[8,256,128]{2,1,0:T(8,128)(2,1)}, u32[]{:S(2)}, u32[]{:S(2)}) %collective-permute-start.2) | collective-permute-done | bytes 524320 | tf_op jit(solution)/shard_map/ppermute | solution.py:420
  46.8 2.7 fusion.9
  51.5 7.1 %all-gather.4.cloned.1.call-done = bf16[128,8192]{1,0:T(8,128)(2,1)} async-done(((bf16[128,2048]{1,0:T(8,128)(2,1)}), bf16[128,8192]{1,0:T(8,128)(2,1)}) %all-gather.4.cloned.1.call-update) | async-done | bytes 2097168 | tf_op jit(solution)/shard_map/all_gather | solution.py:448
  58.6 2.9 constant_dynamic-slice_fusion.4
  75.8 2.9 shard_map.121
  78.7 3.3 %copy-done.9 = f32[32,256,256]{2,1,0:T(8,128)} copy-done((f32[32,256,256]{2,1,0:T(8,128)}, f32[32,256,256]{2,1,0:T(8,128)S(1)}, u32[]{:S(2)}) %copy-start.9) | copy-done | bytes 8388632
  82.1 3.3 %copy-done.11 = bf16[32,256,512]{2,1,0:T(8,128)(2,1)} copy-done((bf16[32,256,512]{2,1,0:T(8,128)(2,1)}, bf16[32,256,512]{2,1,0:T(8,128)(2,1)S(1)}, u32[]{:S(2)}) %copy-start.11) | copy-done | bytes 8388632
  85.4 6.4 %maximum_select_fusion.refs_8_.state_ref = f32[32,256,128]{2,1,0:T(8,128)} fusion(f32[16,256,128]{2,1,0:T(8,128)} %collective-permute-done.8, f32[16,256,128]{2,1,0:T(8,128)} %get-tuple-element.146, pred[]{:T(512)S(6)} %eq.4), kind=kLoop, calls=%fused_computation | loop fusion | flops 3145728 | bytes 8388609 | tf_op jit(solution)/shard_map/jit(_where)/select_n | solution.py:608
  91.8 3.5 %collective-permute-done.4.refs_3_ = bf16[128,2048]{1,0:T(8,128)(2,1)} collective-permute-done((bf16[128,2048]{1,0:T(8,128)(2,1)}, bf16[128,2048]{1,0:T(8,128)(2,1)}, u32[]{:S(2)}, u32[]{:S(2)}) %collective-permute-start.4) | collective-permute-done | bytes 524320 | tf_op jit(solution)/shard_map/ppermute | solution.py:420
  95.3 3.4 %copy-done.2 = bf16[4096,1024]{1,0:T(8,128)(2,1)S(1)} copy-done((bf16[4096,1024]{1,0:T(8,128)(2,1)S(1)}, bf16[4096,1024]{1,0:T(8,128)(2,1)}, u32[]{:S(2)}) %copy-start.2) | copy-done | bytes 8388632
  98.7 7.8 %shard_map.122 = (bf16[256,2048]{1,0:T(8,128)(2,1)}, f32[256,2048]{1,0:T(8,128)S(1)}) custom-call(s32[1]{0:T(128)} %bitcast.1.refs_0_, bf16[128,2048]{1,0:T(8,128)(2,1)S(1)} %copy-done.17, bf16[128,2048]{1,0:T(8,128)(2,1)} %collective-permute-done.3.refs_2_, bf16[128,2048]{1,0:T(8,128)(2,1)} %collective-permute-done.4.refs_3_, ...), custom_call_target="tpu_custom_call" | custom-call | flops 16777216 | bytes 45056 | tf_op jit(solution)/shard_map/pallas_call | solution.py:361
  108.8 7.9 %shard_map.123 = (bf16[256,2048]{1,0:T(8,128)(2,1)}, f32[256,2048]{1,0:T(8,128)S(1)}) custom-call(s32[1]{0:T(128)} %bitcast.1.refs_0_, bf16[128,2048]{1,0:T(8,128)(2,1)S(1)} %copy-done.17, bf16[128,2048]{1,0:T(8,128)(2,1)} %collective-permute-done.3.refs_2_, bf16[128,2048]{1,0:T(8,128)(2,1)} %collective-permute-done.4.refs_3_, ...), custom_call_target="tpu_custom_call" | custom-call | flops 16777216 | bytes 45056 | tf_op jit(solution)/shard_map/pallas_call | solution.py:361
  123.8 10.5 %collective-permute-done.10 = bf16[256,2048]{1,0:T(8,128)(2,1)} collective-permute-done((bf16[256,2048]{1,0:T(8,128)(2,1)}, bf16[256,2048]{1,0:T(8,128)(2,1)}, u32[]{:S(2)}, u32[]{:S(2)}) %collective-permute-start.10) | collective-permute-done | bytes 1048608 | tf_op jit(solution)/shard_map/ppermute | solution.py:420
  135.6 4.8 %collective-permute-done.13.refs_4_ = bf16[64,2048]{1,0:T(8,128)(2,1)S(1)} collective-permute-done((bf16[64,2048]{1,0:T(8,128)(2,1)S(1)}, bf16[64,2048]{1,0:T(8,128)(2,1)S(1)}, u32[]{:S(2)}, u32[]{:S(2)}) %collective-permute-start.13) | collective-permute-done | bytes 262176 | tf_op jit(solution)/shard_map/ppermute | solution.py:420
  141.3 19.8 %collective-permute-done.12.refs_3_ = bf16[64,2048]{1,0:T(8,128)(2,1)S(1)} collective-permute-done((bf16[64,2048]{1,0:T(8,128)(2,1)S(1)}, bf16[64,2048]{1,0:T(8,128)(2,1)S(1)}, u32[]{:S(2)}, u32[]{:S(2)}) %collective-permute-start.12) | collective-permute-done | bytes 262176 | tf_op jit(solution)/shard_map/ppermute | solution.py:420
  162.3 3.4 %copy-done.3 = bf16[4096,1024]{1,0:T(8,128)(2,1)S(1)} copy-done((bf16[4096,1024]{1,0:T(8,128)(2,1)S(1)}, bf16[4096,1024]{1,0:T(8,128)(2,1)}, u32[]{:S(2)}) %copy-start.3) | copy-done | bytes 8388632
  165.6 5.0 %shard_map.126 = (bf16[128,2048]{1,0:T(8,128)(2,1)S(1)}, f32[128,2048]{1,0:T(8,128)S(1)}) custom-call(s32[1]{0:T(128)} %bitcast.1.refs_0_, bf16[64,2048]{1,0:T(8,128)(2,1)S(1)} %get-tuple-element.94.refs_1_, bf16[64,2048]{1,0:T(8,128)(2,1)S(1)} %collective-permute-done.11.refs_2_, bf16[64,2048]{1,0:T(8,128)(2,1)S(1)} %collective-permute-done.12.refs_3_, ...), custom_call_target="tpu_custom_call" | custom-call | flops 8388608 | bytes 38912 | tf_op jit(solution)/shard_map/pallas_call | solution.py:361
  171.8 5.0 %shard_map.124 = (bf16[128,2048]{1,0:T(8,128)(2,1)S(1)}, f32[128,2048]{1,0:T(8,128)S(1)}) custom-call(s32[1]{0:T(128)} %bitcast.1.refs_0_, bf16[64,2048]{1,0:T(8,128)(2,1)S(1)} %get-tuple-element.94.refs_1_, bf16[64,2048]{1,0:T(8,128)(2,1)S(1)} %collective-permute-done.11.refs_2_, bf16[64,2048]{1,0:T(8,128)(2,1)S(1)} %collective-permute-done.12.refs_3_, ...), custom_call_target="tpu_custom_call" | custom-call | flops 8388608 | bytes 38912 | tf_op jit(solution)/shard_map/pallas_call | solution.py:361
  183.4 5.0 %shard_map.125 = (bf16[128,2048]{1,0:T(8,128)(2,1)S(1)}, f32[128,2048]{1,0:T(8,128)S(1)}) custom-call(s32[1]{0:T(128)} %bitcast.1.refs_0_, bf16[64,2048]{1,0:T(8,128)(2,1)S(1)} %get-tuple-element.151.refs_1_, bf16[64,2048]{1,0:T(8,128)(2,1)S(1)} %collective-permute-done.15.refs_2_, bf16[64,2048]{1,0:T(8,128)(2,1)S(1)} %collective-permute-done.16.refs_3_, ...), custom_call_target="tpu_custom_call" | custom-call | flops 8388608 | bytes 38912 | tf_op jit(solution)/shard_map/pallas_call | solution.py:361
  189.3 5.0 %shard_map.127 = (bf16[128,2048]{1,0:T(8,128)(2,1)S(1)}, f32[128,2048]{1,0:T(8,128)S(1)}) custom-call(s32[1]{0:T(128)} %bitcast.1.refs_0_, bf16[64,2048]{1,0:T(8,128)(2,1)S(1)} %get-tuple-element.151.refs_1_, bf16[64,2048]{1,0:T(8,128)(2,1)S(1)} %collective-permute-done.15.refs_2_, bf16[64,2048]{1,0:T(8,128)(2,1)S(1)} %collective-permute-done.16.refs_3_, ...), custom_call_target="tpu_custom_call" | custom-call | flops 8388608 | bytes 38912 | tf_op jit(solution)/shard_map/pallas_call | solution.py:361
  197.0 17.1 %collective-permute-done.18 = bf16[128,2048]{1,0:T(8,128)(2,1)S(1)} collective-permute-done((bf16[128,2048]{1,0:T(8,128)(2,1)S(1)}, bf16[128,2048]{1,0:T(8,128)(2,1)S(1)}, u32[]{:S(2)}, u32[]{:S(2)}) %collective-permute-start.18) | collective-permute-done | bytes 524320 | tf_op jit(solution)/shard_map/ppermute | solution.py:420
  220.5 2.8 collective-permute-done.24.refs_8_
  233.6 3.4 %copy-done.10 = f32[32,256,256]{2,1,0:T(8,128)S(1)} copy-done((f32[32,256,256]{2,1,0:T(8,128)S(1)}, f32[32,256,256]{2,1,0:T(8,128)}, u32[]{:S(2)}) %copy-start.10) | copy-done | bytes 8388632
  237.0 5.6 %shard_map.131 = (f32[256,4096]{1,0:T(8,128)S(1)}, f32[4,256,8]{2,1,0:T(8,128)S(1)}, f32[4,256,8]{2,1,0:T(8,128)S(1)}, f32[256,256]{1,0:T(8,128)S(1)}, f32[256,256]{1,0:T(8,128)S(1)}) custom-call(s32[1]{0:T(128)} %constant.68.clone.1.refs_0_, bf16[256,4096]{1,0:T(8,128)(2,1)S(1)} %copy-done.5, bf16[256,4096]{1,0:T(8,128)(2,1)S(1)} %copy-done.8, ...), custom_call_target="tpu_custom_call" | custom-call | flops 3670016 | bytes 28672 | tf_op jit(solution)/shard_map/pallas_call | solution.py:199
  246.7 9.9 %shard_map.132 = (f32[256,4096]{1,0:T(8,128)S(1)}, f32[4,256,8]{2,1,0:T(8,128)S(1)}, f32[4,256,8]{2,1,0:T(8,128)S(1)}, f32[256,256]{1,0:T(8,128)S(1)}, f32[256,256]{1,0:T(8,128)S(1)}) custom-call(s32[1]{0:T(128)} %constant.69.clone.1.refs_0_, bf16[256,4096]{1,0:T(8,128)(2,1)S(1)} %copy-done.5, ...), custom_call_target="tpu_custom_call", output_to_operand_aliasing={{0}: (12, {}), {1}: (13, {}), {2}: (14, {})} | custom-call | flops 7340032 | bytes 57344 | tf_op jit(solution)/shard_map/pallas_call | solution.py:199
  262.1 5.8 %shard_map.133 = (f32[256,4096]{1,0:T(8,128)S(1)}, f32[4,256,8]{2,1,0:T(8,128)S(1)}, f32[4,256,8]{2,1,0:T(8,128)S(1)}, f32[256,256]{1,0:T(8,128)S(1)}, f32[256,256]{1,0:T(8,128)S(1)}) custom-call(s32[1]{0:T(128)} %constant.55.clone.1.refs_0_, bf16[256,4096]{1,0:T(8,128)(2,1)S(1)} %copy-done.5, ...), custom_call_target="tpu_custom_call", output_to_operand_aliasing={{0}: (12, {}), {1}: (13, {}), {2}: (14, {})} | custom-call | flops 3670016 | bytes 28672 | tf_op jit(solution)/shard_map/pallas_call | solution.py:199
  267.8 5.7 %collective-permute-done.32 = bf16[8,256,128]{2,1,0:T(8,128)(2,1)S(1)} collective-permute-done((bf16[8,256,128]{2,1,0:T(8,128)(2,1)S(1)}, bf16[8,256,128]{2,1,0:T(8,128)(2,1)S(1)}, u32[]{:S(2)}, u32[]{:S(2)}) %collective-permute-start.32) | collective-permute-done | bytes 524320 | tf_op jit(solution)/shard_map/ppermute | solution.py:420
  277.2 2.7 collective-permute-start.38
  281.6 6.1 %shard_map.134 = (bf16[256,4096]{1,0:T(8,128)(2,1)}, f32[256,256]{1,0:T(8,128)S(1)}, f32[4,256,8]{2,1,0:T(8,128)S(1)}, f32[4,256,8]{2,1,0:T(8,128)S(1)}) custom-call(s32[1]{0:T(128)} %bitcast.6.at_ref, bf16[256,4096]{1,0:T(8,128)(2,1)S(1)} %copy-done.5, f32[256,4096]{1,0:T(8,128)S(1)} %get-tuple-element.126.part_ref, bf16[256,256]{1,0:T(8,128)(2,1)S(1)} %copy-done.16, ...), custom_call_target="tpu_custom_call" | custom-call | flops 4194304 | bytes 32768 | tf_op jit(solution)/shard_map/pallas_call | solution.py:297
  287.8 6.1 %shard_map.135 = (bf16[256,4096]{1,0:T(8,128)(2,1)}, f32[256,256]{1,0:T(8,128)S(1)}, f32[4,256,8]{2,1,0:T(8,128)S(1)}, f32[4,256,8]{2,1,0:T(8,128)S(1)}) custom-call(s32[1]{0:T(128)} %bitcast.at_ref, bf16[256,4096]{1,0:T(8,128)(2,1)S(1)} %copy-done.5, ...), custom_call_target="tpu_custom_call", output_to_operand_aliasing={{0}: (11, {}), {2}: (12, {}), {3}: (13, {})} | custom-call | flops 4194304 | bytes 32768 | tf_op jit(solution)/shard_map/pallas_call | solution.py:297
  301.5 4.1 %collective-permute-done.35 = bf16[256,256]{1,0:T(8,128)(2,1)S(1)} collective-permute-done((bf16[256,256]{1,0:T(8,128)(2,1)S(1)}, bf16[256,256]{1,0:T(8,128)(2,1)S(1)}, u32[]{:S(2)}, u32[]{:S(2)}) %collective-permute-start.35) | collective-permute-done | bytes 131104 | tf_op jit(solution)/shard_map/ppermute | solution.py:436
  (202 shorter events, 100.0 us)
Async XLA Ops:
  7.2 51.3 %all-gather.4.cloned.1.call-start = ((), (), s32[]{:S(2)}) async-start(), calls=%async_computation | async-start | bytes 2621440 | tf_op jit(solution)/shard_map/all_gather | solution.py:448
  9.8 109.0 %all-gather.6.cloned.1.call-start = ((), (), s32[]{:S(2)}) async-start(), calls=%async_computation.1 | async-start | bytes 2621440 | tf_op jit(solution)/shard_map/all_gather | solution.py:448
  9.8 85.5 %collective-permute-start.9 = (bf16[4096,1024]{1,0:T(8,128)(2,1)}, bf16[4096,1024]{1,0:T(8,128)(2,1)}, u32[]{:S(2)}, u32[]{:S(2)}) collective-permute-start(bf16[4096,1024]{1,0:T(8,128)(2,1)} %refs_5_.11), channel_id=1, source_target_pairs={{0,4},{4,0},{8,12},{12,8},{16,20},{20,16},{24,28},{28,24},{1,5},{5... | collective-permute-start | bytes 25165832 | tf_op jit(solution)/shard_map/ppermute | solution.py:424
  13.8 13.5 %collective-permute-start = (f32[16,256,128]{2,1,0:T(8,128)}, f32[16,256,128]{2,1,0:T(8,128)}, u32[]{:S(2)}, u32[]{:S(2)}) collective-permute-start(f32[16,256,128]{2,1,0:T(8,128)} %shard_map.120), channel_id=1, source_target_pairs={{0,4},{4,0},{8,12},{12,8},{16,20},{20,16},{24,28},{28,24},{1,5},{5... | collective-permute-start | bytes 6291464 | tf_op jit(solution)/shard_map/ppermute | solution.py:424
  30.5 14.8 %collective-permute-start.2 = (bf16[8,256,128]{2,1,0:T(8,128)(2,1)}, bf16[8,256,128]{2,1,0:T(8,128)(2,1)}, u32[]{:S(2)}, u32[]{:S(2)}) collective-permute-start(bf16[8,256,128]{2,1,0:T(8,128)(2,1)} %get-tuple-element.172), channel_id=1, source_target_pairs={{0,16},{4,20},{8,24},{12,28},{16,0},{20,4},{24,8},{28,12},{1,17},{... | collective-permute-start | bytes 1572872 | tf_op jit(solution)/shard_map/ppermute | solution.py:420
  32.6 14.2 %collective-permute-start.1 = (bf16[8,256,128]{2,1,0:T(8,128)(2,1)}, bf16[8,256,128]{2,1,0:T(8,128)(2,1)}, u32[]{:S(2)}, u32[]{:S(2)}) collective-permute-start(bf16[8,256,128]{2,1,0:T(8,128)(2,1)} %get-tuple-element.173), channel_id=1, source_target_pairs={{0,8},{4,12},{8,0},{12,4},{16,24},{20,28},{24,16},{28,20},{1,9},{5... | collective-permute-start | bytes 1572872 | tf_op jit(solution)/shard_map/ppermute | solution.py:420
  49.4 13.3 %collective-permute-start.7 = (bf16[8,256,128]{2,1,0:T(8,128)(2,1)}, bf16[8,256,128]{2,1,0:T(8,128)(2,1)}, u32[]{:S(2)}, u32[]{:S(2)}) collective-permute-start(bf16[8,256,128]{2,1,0:T(8,128)(2,1)} %get-tuple-element.170), channel_id=1, source_target_pairs={{0,8},{4,12},{8,0},{12,4},{16,24},{20,28},{24,16},{28,20},{1,9},{5... | collective-permute-start | bytes 1572872 | tf_op jit(solution)/shard_map/ppermute | solution.py:420
  69.0 16.4 %collective-permute-start.8 = (f32[16,256,128]{2,1,0:T(8,128)}, f32[16,256,128]{2,1,0:T(8,128)}, u32[]{:S(2)}, u32[]{:S(2)}) collective-permute-start(f32[16,256,128]{2,1,0:T(8,128)} %get-tuple-element.147), channel_id=1, source_target_pairs={{0,4},{4,0},{8,12},{12,8},{16,20},{20,16},{24,28},{28,24},{1,5},{5... | collective-permute-start | bytes 6291464 | tf_op jit(solution)/shard_map/ppermute | solution.py:424
  69.0 22.8 %collective-permute-start.5 = (bf16[128,2048]{1,0:T(8,128)(2,1)}, bf16[128,2048]{1,0:T(8,128)(2,1)}, u32[]{:S(2)}, u32[]{:S(2)}) collective-permute-start(bf16[128,2048]{1,0:T(8,128)(2,1)} %get-tuple-element.156), channel_id=1, source_target_pairs={{0,24},{4,28},{8,16},{12,20},{16,8},{20,12},{24,0},{28,4},{1,25},{... | collective-permute-start | bytes 1572872 | tf_op jit(solution)/shard_map/ppermute | solution.py:420
  70.2 25.1 %collective-permute-start.4 = (bf16[128,2048]{1,0:T(8,128)(2,1)}, bf16[128,2048]{1,0:T(8,128)(2,1)}, u32[]{:S(2)}, u32[]{:S(2)}) collective-permute-start(bf16[128,2048]{1,0:T(8,128)(2,1)} %get-tuple-element.157), channel_id=1, source_target_pairs={{0,16},{4,20},{8,24},{12,28},{16,0},{20,4},{24,8},{28,12},{1,17},{... | collective-permute-start | bytes 1572872 | tf_op jit(solution)/shard_map/ppermute | solution.py:420
  70.9 24.4 %collective-permute-start.3 = (bf16[128,2048]{1,0:T(8,128)(2,1)}, bf16[128,2048]{1,0:T(8,128)(2,1)}, u32[]{:S(2)}, u32[]{:S(2)}) collective-permute-start(bf16[128,2048]{1,0:T(8,128)(2,1)} %get-tuple-element.158), channel_id=1, source_target_pairs={{0,8},{4,12},{8,0},{12,4},{16,24},{20,28},{24,16},{28,20},{1,9},{5... | collective-permute-start | bytes 1572872 | tf_op jit(solution)/shard_map/ppermute | solution.py:420
  107.9 26.4 %collective-permute-start.10 = (bf16[256,2048]{1,0:T(8,128)(2,1)}, bf16[256,2048]{1,0:T(8,128)(2,1)}, u32[]{:S(2)}, u32[]{:S(2)}) collective-permute-start(bf16[256,2048]{1,0:T(8,128)(2,1)} %get-tuple-element.89), channel_id=1, source_target_pairs={{0,8},{4,12},{8,0},{12,4},{16,24},{20,28},{24,16},{28,20},{1,9},{5... | collective-permute-start | bytes 3145736 | tf_op jit(solution)/shard_map/ppermute | solution.py:420
  118.0 44.2 %collective-permute-start.19 = (bf16[256,2048]{1,0:T(8,128)(2,1)}, bf16[256,2048]{1,0:T(8,128)(2,1)}, u32[]{:S(2)}, u32[]{:S(2)}) collective-permute-start(bf16[256,2048]{1,0:T(8,128)(2,1)} %get-tuple-element.90), channel_id=1, source_target_pairs={{0,16},{4,20},{8,24},{12,28},{16,0},{20,4},{24,8},{28,12},{1,17},{... | collective-permute-start | bytes 3145736 | tf_op jit(solution)/shard_map/ppermute | solution.py:420
  120.3 20.1 %collective-permute-start.13 = (bf16[64,2048]{1,0:T(8,128)(2,1)S(1)}, bf16[64,2048]{1,0:T(8,128)(2,1)S(1)}, u32[]{:S(2)}, u32[]{:S(2)}) collective-permute-start(bf16[64,2048]{1,0:T(8,128)(2,1)S(1)} %get-tuple-element.152), channel_id=1, source_target_pairs={{0,24},{4,28},{8,16},{12,20},{16,8},{20,12},{24,0},{28,4},{1,25},{... | collective-permute-start | bytes 786440 | tf_op jit(solution)/shard_map/ppermute | solution.py:420
  122.1 39.1 %collective-permute-start.12 = (bf16[64,2048]{1,0:T(8,128)(2,1)S(1)}, bf16[64,2048]{1,0:T(8,128)(2,1)S(1)}, u32[]{:S(2)}, u32[]{:S(2)}) collective-permute-start(bf16[64,2048]{1,0:T(8,128)(2,1)S(1)} %get-tuple-element.153), channel_id=1, source_target_pairs={{0,16},{4,20},{8,24},{12,28},{16,0},{20,4},{24,8},{28,12},{1,17},{... | collective-permute-start | bytes 786440 | tf_op jit(solution)/shard_map/ppermute | solution.py:420
  123.2 39.1 %collective-permute-start.11 = (bf16[64,2048]{1,0:T(8,128)(2,1)S(1)}, bf16[64,2048]{1,0:T(8,128)(2,1)S(1)}, u32[]{:S(2)}, u32[]{:S(2)}) collective-permute-start(bf16[64,2048]{1,0:T(8,128)(2,1)S(1)} %get-tuple-element.154), channel_id=1, source_target_pairs={{0,8},{4,12},{8,0},{12,4},{16,24},{20,28},{24,16},{28,20},{1,9},{5... | collective-permute-start | bytes 786440 | tf_op jit(solution)/shard_map/ppermute | solution.py:420
  134.4 46.6 %collective-permute-start.17 = (bf16[64,2048]{1,0:T(8,128)(2,1)S(1)}, bf16[64,2048]{1,0:T(8,128)(2,1)S(1)}, u32[]{:S(2)}, u32[]{:S(2)}) collective-permute-start(bf16[64,2048]{1,0:T(8,128)(2,1)S(1)} %get-tuple-element.148), channel_id=1, source_target_pairs={{0,24},{4,28},{8,16},{12,20},{16,8},{20,12},{24,0},{28,4},{1,25},{... | collective-permute-start | bytes 786440 | tf_op jit(solution)/shard_map/ppermute | solution.py:420
  140.4 41.9 %collective-permute-start.16 = (bf16[64,2048]{1,0:T(8,128)(2,1)S(1)}, bf16[64,2048]{1,0:T(8,128)(2,1)S(1)}, u32[]{:S(2)}, u32[]{:S(2)}) collective-permute-start(bf16[64,2048]{1,0:T(8,128)(2,1)S(1)} %get-tuple-element.149), channel_id=1, source_target_pairs={{0,16},{4,20},{8,24},{12,28},{16,0},{20,4},{24,8},{28,12},{1,17},{... | collective-permute-start | bytes 786440 | tf_op jit(solution)/shard_map/ppermute | solution.py:420
  161.1 22.3 %collective-permute-start.15 = (bf16[64,2048]{1,0:T(8,128)(2,1)S(1)}, bf16[64,2048]{1,0:T(8,128)(2,1)S(1)}, u32[]{:S(2)}, u32[]{:S(2)}) collective-permute-start(bf16[64,2048]{1,0:T(8,128)(2,1)S(1)} %get-tuple-element.150), channel_id=1, source_target_pairs={{0,8},{4,12},{8,0},{12,4},{16,24},{20,28},{24,16},{28,20},{1,9},{5... | collective-permute-start | bytes 786440 | tf_op jit(solution)/shard_map/ppermute | solution.py:420
  170.6 23.7 %collective-permute-start.20 = (bf16[128,2048]{1,0:T(8,128)(2,1)S(1)}, bf16[128,2048]{1,0:T(8,128)(2,1)S(1)}, u32[]{:S(2)}, u32[]{:S(2)}) collective-permute-start(bf16[128,2048]{1,0:T(8,128)(2,1)S(1)} %get-tuple-element.105), channel_id=1, source_target_pairs={{0,16},{4,20},{8,24},{12,28},{16,0},{20,4},{24,8},{28,12},{1,17},{... | collective-permute-start | bytes 1572872 | tf_op jit(solution)/shard_map/ppermute | solution.py:420
  176.8 18.6 %collective-permute-start.14 = (bf16[128,2048]{1,0:T(8,128)(2,1)S(1)}, bf16[128,2048]{1,0:T(8,128)(2,1)S(1)}, u32[]{:S(2)}, u32[]{:S(2)}) collective-permute-start(bf16[128,2048]{1,0:T(8,128)(2,1)S(1)} %get-tuple-element.99), channel_id=1, source_target_pairs={{0,8},{4,12},{8,0},{12,4},{16,24},{20,28},{24,16},{28,20},{1,9},{5... | collective-permute-start | bytes 1572872 | tf_op jit(solution)/shard_map/ppermute | solution.py:420
  181.0 35.6 %collective-permute-start.22 = (bf16[128,2048]{1,0:T(8,128)(2,1)S(1)}, bf16[128,2048]{1,0:T(8,128)(2,1)S(1)}, u32[]{:S(2)}, u32[]{:S(2)}) collective-permute-start(bf16[128,2048]{1,0:T(8,128)(2,1)S(1)} %slice.182), channel_id=1, source_target_pairs={{0,16},{4,20},{8,24},{12,28},{16,0},{20,4},{24,8},{28,12},{1,17},{... | collective-permute-start | bytes 1572872 | tf_op jit(solution)/shard_map/ppermute | solution.py:420
  182.3 35.0 %collective-permute-start.25 = (bf16[128,2048]{1,0:T(8,128)(2,1)S(1)}, bf16[128,2048]{1,0:T(8,128)(2,1)S(1)}, u32[]{:S(2)}, u32[]{:S(2)}) collective-permute-start(bf16[128,2048]{1,0:T(8,128)(2,1)S(1)} %slice.181), channel_id=1, source_target_pairs={{0,8},{4,12},{8,0},{12,4},{16,24},{20,28},{24,16},{28,20},{1,9},{5... | collective-permute-start | bytes 1572872 | tf_op jit(solution)/shard_map/ppermute | solution.py:420
  188.4 25.8 %collective-permute-start.18 = (bf16[128,2048]{1,0:T(8,128)(2,1)S(1)}, bf16[128,2048]{1,0:T(8,128)(2,1)S(1)}, u32[]{:S(2)}, u32[]{:S(2)}) collective-permute-start(bf16[128,2048]{1,0:T(8,128)(2,1)S(1)} %get-tuple-element.101), channel_id=1, source_target_pairs={{0,8},{4,12},{8,0},{12,4},{16,24},{20,28},{24,16},{28,20},{1,9},{5... | collective-permute-start | bytes 1572872 | tf_op jit(solution)/shard_map/ppermute | solution.py:420
  194.3 20.9 %collective-permute-start.21 = (bf16[128,2048]{1,0:T(8,128)(2,1)S(1)}, bf16[128,2048]{1,0:T(8,128)(2,1)S(1)}, u32[]{:S(2)}, u32[]{:S(2)}) collective-permute-start(bf16[128,2048]{1,0:T(8,128)(2,1)S(1)} %get-tuple-element.107), channel_id=1, source_target_pairs={{0,16},{4,20},{8,24},{12,28},{16,0},{20,4},{24,8},{28,12},{1,17},{... | collective-permute-start | bytes 1572872 | tf_op jit(solution)/shard_map/ppermute | solution.py:420
  195.4 23.0 %collective-permute-start.26 = (bf16[64,2048]{1,0:T(8,128)(2,1)S(1)}, bf16[64,2048]{1,0:T(8,128)(2,1)S(1)}, u32[]{:S(2)}, u32[]{:S(2)}) collective-permute-start(bf16[64,2048]{1,0:T(8,128)(2,1)S(1)} %slice.184), channel_id=1, source_target_pairs={{0,8},{4,12},{8,0},{12,4},{16,24},{20,28},{24,16},{28,20},{1,9},{5... | collective-permute-start | bytes 786440 | tf_op jit(solution)/shard_map/ppermute | solution.py:420
  227.3 15.3 %collective-permute-start.28 = (f32[16,256,128]{2,1,0:T(8,128)}, f32[16,256,128]{2,1,0:T(8,128)}, u32[]{:S(2)}, u32[]{:S(2)}) collective-permute-start(f32[16,256,128]{2,1,0:T(8,128)} %shard_map.130), channel_id=1, source_target_pairs={{0,4},{4,0},{8,12},{12,8},{16,20},{20,16},{24,28},{28,24},{1,5},{5... | collective-permute-start | bytes 6291464 | tf_op jit(solution)/shard_map/ppermute | solution.py:424
  244.7 14.4 %collective-permute-start.30 = (bf16[8,256,128]{2,1,0:T(8,128)(2,1)S(1)}, bf16[8,256,128]{2,1,0:T(8,128)(2,1)S(1)}, u32[]{:S(2)}, u32[]{:S(2)}) collective-permute-start(bf16[8,256,128]{2,1,0:T(8,128)(2,1)S(1)} %get-tuple-element.164), channel_id=1, source_target_pairs={{0,16},{4,20},{8,24},{12,28},{16,0},{20,4},{24,8},{28,12},{1,17},{... | collective-permute-start | bytes 1572872 | tf_op jit(solution)/shard_map/ppermute | solution.py:420
  245.7 14.1 %collective-permute-start.29 = (bf16[8,256,128]{2,1,0:T(8,128)(2,1)S(1)}, bf16[8,256,128]{2,1,0:T(8,128)(2,1)S(1)}, u32[]{:S(2)}, u32[]{:S(2)}) collective-permute-start(bf16[8,256,128]{2,1,0:T(8,128)(2,1)S(1)} %get-tuple-element.165), channel_id=1, source_target_pairs={{0,8},{4,12},{8,0},{12,4},{16,24},{20,28},{24,16},{28,20},{1,9},{5... | collective-permute-start | bytes 1572872 | tf_op jit(solution)/shard_map/ppermute | solution.py:420
  277.2 21.8 %collective-permute-start.38 = (bf16[256,256]{1,0:T(8,128)(2,1)S(1)}, bf16[256,256]{1,0:T(8,128)(2,1)S(1)}, u32[]{:S(2)}, u32[]{:S(2)}) collective-permute-start(bf16[256,256]{1,0:T(8,128)(2,1)S(1)} %convert_element_type.141), channel_id=1, source_target_pairs={{0,2},{1,3},{2,0},{3,1},{4,6},{5,7},{6,4},{7,5},{8,10},{9,11},{10,... | collective-permute-start | bytes 393224 | tf_op jit(solution)/shard_map/ppermute | solution.py:436
  279.9 19.3 %collective-permute-start.37 = (bf16[256,256]{1,0:T(8,128)(2,1)S(1)}, bf16[256,256]{1,0:T(8,128)(2,1)S(1)}, u32[]{:S(2)}, u32[]{:S(2)}) collective-permute-start(bf16[256,256]{1,0:T(8,128)(2,1)S(1)} %convert_element_type.141), channel_id=1, source_target_pairs={{0,1},{1,0},{2,3},{3,2},{4,5},{5,4},{6,7},{7,6},{8,9},{9,8},{10,11... | collective-permute-start | bytes 393224 | tf_op jit(solution)/shard_map/ppermute | solution.py:436
  281.4 17.8 %collective-permute-start.39 = (bf16[256,256]{1,0:T(8,128)(2,1)S(1)}, bf16[256,256]{1,0:T(8,128)(2,1)S(1)}, u32[]{:S(2)}, u32[]{:S(2)}) collective-permute-start(bf16[256,256]{1,0:T(8,128)(2,1)S(1)} %convert_element_type.141), channel_id=1, source_target_pairs={{0,3},{1,2},{2,1},{3,0},{4,7},{5,6},{6,5},{7,4},{8,11},{9,10},{10,... | collective-permute-start | bytes 393224 | tf_op jit(solution)/shard_map/ppermute | solution.py:436
  (43 other events, 263.3 us)
Sparse Core Ops, SparseCore 0:
  9.9 48.6 all-gather.3
  60.1 44.6 all-gather.5

commit v6 on v5

--- a/solution.py
+++ b/solution.py
@@ -12,7 +12,7 @@
 NN = (((1,), (0,)), ((), ()))
 NT = (((1,), (1,)), ((), ()))
 TN = (((0,), (0,)), ((), ()))
-PARAMS = pltpu.CompilerParams(vmem_limit_bytes=28 << 20)
+PARAMS = pltpu.CompilerParams(vmem_limit_bytes=24 << 20)
 
 
 def mm(a, b, dims):
@@ -139,9 +139,8 @@
 
 def inner_kernel(
     first, last, at_ref, x_ref, y_ref, b_ref, c_ref, rise_ref, step_ref, skip_ref,
-    state_ref, decay_ref, weight_ref, cross_ref, *rest,
+    mine_ref, other_ref, decay_ref, weight_ref, cross_ref, *rest,
 ):
-    del at_ref
     held = rest[: 0 if first else 5]
     partial_ref, col_ref, carry_ref, mix_ref, grad_c_ref, rows = rest[len(held) :]
     group = step_ref.shape[2]
@@ -152,6 +151,7 @@
         mix_ref[...] = jnp.zeros_like(mix_ref) if first else held[3][...]
         grad_c_ref[...] = jnp.zeros_like(grad_c_ref) if first else held[4][...]
 
+    is_mine = (at_ref[0] + pl.program_id(0)) // at_ref[2] == at_ref[1]
     lefts, rights = [], []
     for j in range(group):
         columns = slice(j * width, (j + 1) * width)
@@ -166,7 +166,7 @@
         inner = mm(weight_ref[j], jnp.concatenate([y, y], axis=0), NN)
         col_ref[0, :, j : j + 1] = jnp.sum(x_wide * inner, axis=1, keepdims=True)
         partial_ref[:, columns] = step_col * inner + skip_ref[0, j : j + 1, :] * y_wide
-        state = state_ref[j]
+        state = jnp.where(is_mine, mine_ref[j], other_ref[j])
         scaled = y_wide * rise_ref[0, :, j : j + 1]
         lefts.append(scaled)
         rights.append(state)
@@ -186,7 +186,8 @@
 
 
 def inner_part(
-    x, y, b, c, rise, steps, skip_rows, incoming, decay, weight, cross, at, count, held, last
+    x, y, b, c, rise, steps, skip_rows, mine, other, core, decay, weight, cross, at, count, held,
+    last,
 ):
     groups, span, group = steps.shape
     heads = groups * group
@@ -196,6 +197,10 @@
     table = pl.BlockSpec((1, span, group), lambda i, at: (at[0] + i, 0, 0))
     per_head = lambda *shape: pl.BlockSpec((group, *shape), lambda i, at: (at[0] + i, 0, 0))
     any_place = pl.BlockSpec(memory_space=pl.ANY)
+    half = groups // 2
+    near = lambda i, at: (jnp.clip(at[0] + i - at[1] * half, 0, half - 1), 0, 0)
+    far = lambda i, at: (jnp.clip(at[0] + i - (1 - at[1]) * half, 0, half - 1), 0, 0)
+    at = jnp.stack([jnp.int32(at), core.astype(jnp.int32), jnp.int32(half)])
     return pl.pallas_call(
         lambda *refs: inner_kernel(not held, last, *refs),
         grid_spec=pltpu.PrefetchScalarGridSpec(
@@ -209,7 +214,8 @@
                 table,
                 table,
                 pl.BlockSpec((1, group, width), lambda i, at: (at[0] + i, 0, 0)),
-                per_head(states, width),
+                pl.BlockSpec((group, states, width), near),
+                pl.BlockSpec((group, states, width), far),
                 per_head(span, span),
                 per_head(span, 2 * span),
                 whole(span, span),
@@ -225,15 +231,14 @@
             jax.ShapeDtypeStruct((span, states), F32),
             jax.ShapeDtypeStruct((span, states), F32),
         ],
-        input_output_aliases={12: 0, 13: 1, 14: 2} if held else {},
+        input_output_aliases={13: 0, 14: 1, 15: 2} if held else {},
         compiler_params=PARAMS,
         cost_estimate=cost(
             14 * span * count * group * width * states,
             count * group * (8 * span * width + 4 * width * states + 8 * span * span),
         ),
     )(
-        jnp.full((1,), at, jnp.int32), x, y, b, c, rise, steps, skip_rows, incoming,
-        decay, weight, cross, *held,
+        at, x, y, b, c, rise, steps, skip_rows, mine, other, decay, weight, cross, *held
     )
 
 
@@ -303,7 +308,7 @@
                 block,
                 block,
                 whole(span, states),
-                pl.BlockSpec((group, states, width), lambda i, at: (at[0] + i, 0, 0)),
+                pl.BlockSpec((group, states, width), lambda i, at: (i, 0, 0)),
                 pl.BlockSpec((group, states, width), lambda i, at: (i, 0, 0)),
                 table,
                 table,
@@ -415,6 +420,78 @@
     )(*keeps, *arrived)
 
 
+def split_kernel(keep_ref, arrived_ref, out_ref, send_ref):
+    total = keep_ref[...] + arrived_ref[...].astype(F32)
+    size = out_ref.shape[0]
+    out_ref[...] = total[:size]
+    send_ref[...] = total[size:].astype(BF16)
+
+
+def add_and_split(keep, arrived):
+    rows, half = keep.shape
+    tile = min(1024, half)
+    column = lambda size: pl.BlockSpec((size, tile), lambda i: (0, i))
+    return pl.pallas_call(
+        split_kernel,
+        grid=(half // tile,),
+        in_specs=[column(rows), column(rows)],
+        out_specs=[column(rows // 2), column(rows // 2)],
+        out_shape=[
+            jax.ShapeDtypeStruct((rows // 2, half), F32),
+            jax.ShapeDtypeStruct((rows // 2, half), BF16),
+        ],
+        compiler_params=PARAMS,
+        cost_estimate=cost(rows * half, 9 * rows * half),
+    )(keep, arrived)
+
+
+def blend_kernel(count, step, at_ref, *refs):
+    del at_ref
+    weight_ref, terms, outs = refs[0], refs[1 : 1 + count], refs[1 + count :]
+    for j in range(step):
+        head = pl.program_id(0) * step + j
+        values = [term[j].astype(F32) for term in terms]
+        for k, out in enumerate(outs):
+            total = weight_ref[k * count, head] * values[0]
+            for i in range(1, count):
+                total += weight_ref[k * count + i, head] * values[i]
+            out[j] = total.astype(out.dtype)
+
+
+def blend(terms, starts, weights, heads, dtype):
+    count = len(terms)
+    step = max(1, min(4, heads // 2))
+    while any(start % step for start in starts):
+        step //= 2
+    rows, width = terms[0].shape[1:]
+    specs = []
+    for term, start in zip(terms, starts):
+        last = term.shape[0] // step - 1
+        shift = start // step
+        specs.append(
+            pl.BlockSpec(
+                (step, rows, width),
+                lambda i, at, last=last, shift=shift: (jnp.clip(i + shift, 0, last), 0, 0),
+            )
+        )
+    out = pl.BlockSpec((step, rows, width), lambda i, at: (i, 0, 0))
+    table = jnp.stack([weight for row in weights for weight in row])
+    return pl.pallas_call(
+        lambda *refs: blend_kernel(count, step, *refs),
+        grid_spec=pltpu.PrefetchScalarGridSpec(
+            num_scalar_prefetch=1,
+            grid=(heads // step,),
+            in_specs=[pl.BlockSpec(memory_space=pltpu.SMEM)] + specs,
+            out_specs=[out] * len(weights),
+        ),
+        out_shape=[jax.ShapeDtypeStruct((heads, rows, width), dtype)] * len(weights),
+        compiler_params=PARAMS,
+        cost_estimate=cost(
+            2 * count * len(weights) * heads * rows * width, 4 * count * heads * rows * width
+        ),
+    )(jnp.zeros((1,), jnp.int32), table, *terms)
+
+
 def across(value, hop, chips):
     pairs = [(2 * i + core, 2 * (i ^ hop) + core) for i in range(chips) for core in range(2)]
     return lax.ppermute(value, "seq", pairs)
@@ -455,7 +532,7 @@
     ]
 
 
-def project(fulls, own, out_weight, other, chips, chip, core, before):
+def project(fulls, blocks, second, out_weight, other, chips, chip, core, ahead, before):
     core_at = core.astype(jnp.int32).reshape(1)
     lanes = []
     for order in orders(chips):
@@ -465,7 +542,8 @@
         lanes.append((order, hops))
     waiting = [[], []]
 
-    def reduce(chunk, rows, after):
+    def reduce(chunk, after):
+        last = []
         for lane, (order, _) in enumerate(lanes):
             keep, send, arrived = waiting[lane][chunk]
             for step, bit in enumerate(order):
@@ -474,88 +552,108 @@
                 elif after:
                     arrived = tie(arrived, *after)
                 if step < len(order) - 1:
-                    keep = keep + arrived.astype(F32)
-                    size = keep.shape[0] // 2
-                    send = keep[size:].astype(BF16)
-                    keep = keep[:size] if size > rows else keep
+                    keep, send = add_and_split(keep, arrived)
             waiting[lane][chunk] = (keep, arrived)
-
-    half = fulls[0].shape[0]
-    rows = [half, half // 2, half // 2]
-    count = len(rows)
-    for chunk in range(count):
-        blocks = [across(block, hop, chips) if hop else block for hop, block in enumerate(own)]
-        if chunk == 0:
-            blocks = lax.optimization_barrier((*blocks, *before))[:chips]
-        if chunk == 1:
-            full = tie(fulls[1], waiting[0][0][2], *own)
-            own = blocks_of(full, rows[1], rows[2], chips, chip)
-            blocks = lax.optimization_barrier((*blocks, *own))[:chips]
+            last.append(send)
+        return last, [lane[chunk][1] for lane in waiting]
+
+    rows = fulls[0].shape[0] // 2
+    own = [None, second]
+    for chunk in range(4):
+        if chunk:
+            blocks = [
+                across(block, hop, chips) if hop else block
+                for hop, block in enumerate(own[chunk])
+            ]
+        blocks = lax.optimization_barrier((*blocks, *ahead))[:chips]
         for lane, (order, hops) in enumerate(lanes):
             send, keep = partial_sums(blocks, hops, out_weight, other, lane, core_at)
             waiting[lane].append((keep, send, across(send, order[0], chips)))
-        if chunk == 0:
-            full = tie(fulls[1], *[lane[0][1] for lane in waiting])
-            own = blocks_of(full, 0, rows[1], chips, chip)
+        ahead = [lane[chunk][1] for lane in waiting]
         if chunk == 1:
-            reduce(0, rows[0], own)
-    reduce(count - 2, rows[count - 2], None)
-    reduce(count - 1, rows[count - 1], None)
+            sent, first = reduce(0, ahead)
+            full = tie(fulls[1], *ahead, *first, *before(sent))
+            own += [blocks_of(full, i * rows, rows, chips, chip) for i in range(2)]
+            ahead = reduce(1, own[2])[1]
+    reduce(2, ahead)
+    reduce(3, None)
     ends = waiting[0] + waiting[1]
     return finish([keep for keep, _ in ends], [arrived for _, arrived in ends])
 
 
-def exchange(mine, theirs, ends, chips, chip, core, reverse, fill):
+def exchange(mine, theirs, ends, chips, chip, core, reverse):
     half = mine.shape[0]
     ends = lax.dynamic_slice_in_dim(ends, core * half, half, 1)
     by_chip = ends.reshape(chips, 2, half)
     own_ends = lax.dynamic_index_in_dim(by_chip, chip, 0, False)
     chip_ends = by_chip[:, 0] + by_chip[:, 1]
     index = jnp.arange(chips)[:, None]
-    scale = lambda logs, value: jnp.exp(logs)[:, None, None] * value.astype(F32)
 
     def carry(source, target):
         before = source > target if reverse else source < target
         inside = (index > jnp.minimum(source, target)) & (index < jnp.maximum(source, target))
         between = jnp.sum(jnp.where(inside, chip_ends, 0.0), axis=0)
-        return jnp.where(before, between, -jnp.inf)
+        return jnp.exp(jnp.where(before, between, -jnp.inf))
 
     near_first = (core == 0) != reverse
-    first = jnp.where(near_first, mine, theirs)
-    second = jnp.where(near_first, theirs, mine)
-    first_end, second_end = (own_ends[1], own_ends[0]) if reverse else (own_ends[0], own_ends[1])
-    chip_state = scale(second_end, first) + second
+    own_scale = jnp.exp(own_ends)
+    first_scale, second_scale = own_scale[int(reverse)], own_scale[1 - int(reverse)]
+    one = jnp.ones((half,), F32)
+    pick_near = lambda a, b: jnp.where(near_first, a, b)
+    few = half // 2
+    part = [slice(0, few), slice(few, half)]
+    parts = [pick_near(second_scale, one), pick_near(one, second_scale)]
     lanes = []
-    for lane in range(2):
-        heads = slice(lane * (half // 2), (lane + 1) * (half // 2))
-        lanes.append((heads, {0: chip_state[heads].astype(BF16)}))
+    for heads in part:
+        weights = [[weight[heads] for weight in parts]]
+        chip_state = blend([mine, theirs], [heads.start] * 2, weights, few, BF16)
+        lanes.append({0: chip_state[0]})
     bits = orders(chips)
     for step in range(len(bits[0])):
         last = step == len(bits[0]) - 1
         sent = []
-        for order, (heads, items) in zip(bits, lanes):
+        for order, heads, items in zip(bits, part, lanes):
             if last:
                 target = chip ^ order[step]
-                total = sum(scale(carry(chip ^ o, target)[heads], i) for o, i in items.items())
-                sent.append({0: total.astype(BF16)})
+                weights = [[carry(chip ^ o, target)[heads] for o in items]]
+                total = blend(list(items.values()), [0] * len(items), weights, few, BF16)
+                sent.append({0: total[0]})
             else:
                 sent.append(dict(items))
-        done = fill(step, [item for items in sent for item in items.values()])
-        for order, (heads, items), going in zip(bits, lanes, sent):
+        fresh = []
+        for order, items, going in zip(bits, lanes, sent):
             for o, item in going.items():
                 items[o | order[step]] = across(item, order[step], chips)
-        fresh = [(items, o | order[step]) for order, (_, items), going in zip(bits, lanes, sent) for o in going]
-        values = lax.optimization_barrier((*[items[o] for items, o in fresh], *done))
+                fresh.append((items, o | order[step]))
+        arrived = [items[o] for items, o in fresh]
+        done = yield [item for going in sent for item in going.values()], arrived
+        values = lax.optimization_barrier((*arrived, *done))
         for (items, o), value in zip(fresh, values):
             items[o] = value
-    totals = []
-    for order, (heads, items) in zip(bits, lanes):
-        arrived = items.pop(order[-1])
-        total = sum(scale(carry(chip ^ o, chip)[heads], i) for o, i in items.items())
-        totals.append(total + arrived.astype(F32))
-    total = jnp.concatenate(totals, axis=0)
-    after = scale(first_end, total) + first
-    return jnp.where(near_first, total, after), jnp.where(near_first, after, total)
+    terms, starts = [mine, theirs], [0, 0]
+    alphas = [pick_near(one, first_scale), pick_near(first_scale, one)]
+    zero = jnp.zeros((half,), F32)
+    weights = [[zero, pick_near(zero, one)], [pick_near(one, zero), zero]]
+    for order, heads, items in zip(bits, part, lanes):
+        here = (jnp.arange(half) >= heads.start) & (jnp.arange(half) < heads.stop)
+        for o, item in items.items():
+            if o == 0:
+                continue
+            scale = one if o == order[-1] else carry(chip ^ o, chip)
+            terms.append(item)
+            starts.append(-heads.start)
+            for row, alpha in zip(weights, alphas):
+                row.append(jnp.where(here, alpha * scale, 0.0))
+    return tuple(blend(terms, starts, weights, half, F32))
+
+
+def run_steps(steps, work, done=None):
+    for step in range(64):
+        try:
+            sent, _ = steps.send(done)
+        except StopIteration as stop:
+            return stop.value
+        done = work(step, sent)
 
 
 def local(grad_out, out_weight, ssm_input, step_size, log_decay, b_in, c_in, skip):
@@ -592,30 +690,30 @@
         theirs = other_core(to_other, chips)
         return span_states(values, scale, rows_t, mine_at, groups // 2), theirs
 
-    own = []
-
-    def first_blocks(step, sent):
-        if step < chips.bit_length() - 2:
-            return []
-        own[:] = blocks_of(tie(fulls[0], *sent), 0, span // 2, chips, chip)
-        return own
-
     mine, theirs = span_both(ssm_input, by_group(step_size * tail), b_rows)
-    for_mine, for_theirs = exchange(
-        mine, theirs, ends, chips, chip, core, False, first_blocks
-    )
-    arrived = other_core(for_theirs, chips)
-    incoming = jnp.where(
-        core == 0,
-        jnp.concatenate([for_mine, arrived], axis=0),
-        jnp.concatenate([arrived, for_mine], axis=0),
-    )
-    decay, weight, cross = decays(tie(running_g, *own), running_t, b_in, c_in)
-    before = [incoming, cross, steps_g, skip_rows, rise, c_rows]
-    grad_y = project(fulls, own, out_weight, other_weight, chips, chip, core, before)
-
-    few = max(1, groups // 4)
-    counts = [few, groups - 2 * few, few]
+    forward = exchange(mine, theirs, ends, chips, chip, core, False)
+    sent, raw = next(forward)
+    for _ in range(chips.bit_length() - 2):
+        sent, raw = forward.send([])
+    full = tie(fulls[0], other_weight, *sent)
+    rows = span // 4
+    own = blocks_of(full, 0, rows, chips, chip)
+    blocks = [across(block, hop, chips) if hop else block for hop, block in enumerate(own)]
+    second = blocks_of(tie(full, *blocks[1:]), rows, rows, chips, chip)
+    tables = []
+
+    def before(done):
+        in_mine, for_theirs = run_steps(forward, None, done)
+        in_other = other_core(for_theirs, chips)
+        tables[:] = [in_mine, in_other, *decays(tie(running_g, *done), running_t, b_in, c_in)]
+        return [in_mine, tables[-1], steps_g, skip_rows, rise, c_rows]
+
+    grad_y = project(
+        fulls, blocks, second, out_weight, other_weight, chips, chip, core, raw, before
+    )
+    in_mine, in_other, decay, weight, cross = tables
+
+    counts = [0, groups - groups // 2, groups // 2]
     held = ()
 
     def fill(step, sent):
@@ -623,25 +721,24 @@
         count = counts[step] if step < len(counts) else 0
         if count:
             held = inner_part(
-                ssm_input, grad_y, b_in, c_in, tie(rise, *sent), steps_g, skip_rows, incoming,
-                decay, weight, cross, sum(counts[:step]), count, held, step == len(counts) - 1,
+                ssm_input, grad_y, b_in, c_in, tie(rise, *sent), steps_g, skip_rows, in_mine,
+                in_other, core, decay, weight, cross, sum(counts[:step]), count, held, step == len(counts) - 1,
             )
         return list(held)
 
     mine, theirs = span_both(grad_y, rise, c_rows)
     theirs = tie(theirs, *fill(0, [mine]))
-    for_mine, for_theirs = exchange(
-        mine, theirs, ends, chips, chip, core, True, lambda step, sent: fill(step + 1, sent)
-    )
+    backward = exchange(mine, theirs, ends, chips, chip, core, True)
+    for_mine, for_theirs = run_steps(backward, lambda step, sent: fill(step + 1, sent))
     for_other = other_core(for_theirs, chips)
     part, cols, carries, grad_b, grad_c = held
     grad_c = sum_over_heads(grad_c)
     shared = (running_g, steps_g, cols, carries)
     grad_x, grad_b, grad_step, grad_decay = outer_part(
-        ssm_input, part, b_in, incoming, for_mine, *shared, grad_b, mine_at, None
+        ssm_input, part, b_in, in_mine, for_mine, *shared, grad_b, mine_at, None
     )
     grad_x, grad_b, grad_step, grad_decay = outer_part(
-        ssm_input, part, b_in, incoming, for_other, *shared, grad_b, other_at,
+        ssm_input, part, b_in, in_other, for_other, *shared, grad_b, other_at,
         (grad_x, grad_step, grad_decay),
     )
     grad_b = sum_over_heads(grad_b)

time: 317 us -> 344 us (1.085)
  Pallas kernels: 81.7 us -> 110 us
  other arithmetic: 27.8 us -> 5.16 us
  local copies, waits for them, and re-layouts: 39.3 us -> 60.5 us
  starting transfers between devices: 41.3 us -> 49.1 us
  waiting for transfers between devices: 99.3 us -> 92.1 us
    pallas_call x0 -> x18, Pallas kernels: none -> 23.2 us  [the longest x10 17.8 us: blend(): pl.pallas_call(lambda *refs: blend_kernel(count, step, *refs), grid_spec=...]
    unnamed x66 -> x148, local copies, waits for them, and re-layouts: 26.1 us -> 49.2 us
    select_n x5 -> x3, other arithmetic: 11.4 us -> 1.16 us  [the longest x2 1.15 us: exchange(): row.append(jnp.where(here, alpha * scale, 0.0))]
    ppermute x29 -> x36, waiting for transfers between devices: 86.2 us -> 76.6 us  [across(): return lax.ppermute(value, 'seq', pairs)]
    ppermute x29 -> x36, starting transfers between devices: 31.6 us -> 38.9 us  [across(): return lax.ppermute(value, 'seq', pairs)]
    add x8 -> x0, other arithmetic: 6.58 us -> none  [the longest x6 3.67 us: reduce(): keep = keep + arrived.astype(F32)]
    pallas_call x6 -> x8, Pallas kernels: 35.6 us -> 41 us  [partial_sums(): pl.pallas_call(lambda *refs: project_kernel(hops, *refs), grid_spec=pltpu...]
    another operation x2 -> x9, other arithmetic: 4.05 us -> 0.16 us  [the longest x8 0.08 us: blend(): table = jnp.stack([weight for row in weights for weight in row])]
  transfers between devices with their start and end apart: 42 -> 49, of which waited for: 19 -> 19; matrix products, arithmetic and copies ran while one was open for 10% -> 4% of each run, Pallas kernels for 25% -> 29%
where the time goes in v6:
time: 344 us; the launch traced here: 343 us
  Pallas kernels  110 us (32%)
  waiting for transfers between devices  92.1 us (27%)
  local copies, waits for them, and re-layouts  60.5 us (18%)
  starting transfers between devices  49.1 us (14%)
  between operations  15.1 us (4%)
  blocking collectives  10.1 us (3%)
  other arithmetic  5.16 us (2%)
    ppermute x36, waiting for transfers between devices, across(): return lax.ppermute(value, 'seq', pairs)  76.6 us
    unnamed x148, local copies, waits for them, and re-layouts  49.2 us
    pallas_call x8, Pallas kernels, partial_sums(): pl.pallas_call(lambda *refs: project_kernel(hops, *refs), grid_spec=pltpu...  41 us
    ppermute x36, starting transfers between devices, across(): return lax.ppermute(value, 'seq', pairs)  38.9 us
    pallas_call x2, Pallas kernels, inner_part(): pl.pallas_call(lambda *refs: inner_kernel(not held, last, *refs), grid_sp...  20.5 us
    pallas_call x10, Pallas kernels, blend(): pl.pallas_call(lambda *refs: blend_kernel(count, step, *refs), grid_spec=...  17.8 us
    pallas_call x2, Pallas kernels, outer_part(): pl.pallas_call(outer_kernel, grid_spec=pltpu.PrefetchScalarGridSpec(num_s...  12.5 us
    all_gather x1, blocking collectives, local(): ends = lax.all_gather(running[-1], 'seq')  10.1 us
  transfers between devices with their start and end apart: 49, of which 19 were waited for; matrix products, arithmetic and copies ran while one was open for 4% of the time, Pallas kernels for 29%

profile of v6, /device:TPU:0, one launch (start us, length us, event | category | flops | bytes accessed | tf_op | source)
XLA Modules:
  0.0 342.9 jit_solution(11979396715204722351)
XLA Ops:
  15.6 10.1 %all-gather = f32[8,1,32]{2,1,0:T(1,128)S(1)} all-gather(f32[1,1,32]{2,1,0:T(1,128)S(1)} %bitcast.117), channel_id=1, replica_groups=mesh['seq'=8,'head'=4] {'seq'}, dimensions={0}, use_global_device_ids=true | all-gather | bytes 1152 | tf_op jit(solution)/shard_map/all_gather | solution.py:679
  33.0 9.8 %collective-permute-done.3.refs_3_.refs_6_ = bf16[8,256,128]{2,1,0:T(8,128)(2,1)S(1)} collective-permute-done((bf16[8,256,128]{2,1,0:T(8,128)(2,1)S(1)}, bf16[8,256,128]{2,1,0:T(8,128)(2,1)S(1)}, u32[]{:S(2)}, u32[]{:S(2)}) %collective-permute-start.3) | collective-permute-done | bytes 524320 | tf_op jit(solution)/shard_map/ppermute | solution.py:497
  51.2 7.4 %all-gather.4.cloned.1.call-done = bf16[128,8192]{1,0:T(8,128)(2,1)} async-done(((bf16[128,2048]{1,0:T(8,128)(2,1)}), bf16[128,8192]{1,0:T(8,128)(2,1)}) %all-gather.4.cloned.1.call-update) | async-done | bytes 2097168 | tf_op jit(solution)/shard_map/all_gather | solution.py:525
  63.5 5.7 %collective-permute-done.4.refs_2_ = bf16[64,2048]{1,0:T(8,128)(2,1)S(1)} collective-permute-done((bf16[64,2048]{1,0:T(8,128)(2,1)S(1)}, bf16[64,2048]{1,0:T(8,128)(2,1)S(1)}, u32[]{:S(2)}, u32[]{:S(2)}) %collective-permute-start.4) | collective-permute-done | bytes 262176 | tf_op jit(solution)/shard_map/ppermute | solution.py:497
  69.2 5.6 %collective-permute-done.5.refs_3_ = bf16[64,2048]{1,0:T(8,128)(2,1)S(1)} collective-permute-done((bf16[64,2048]{1,0:T(8,128)(2,1)S(1)}, bf16[64,2048]{1,0:T(8,128)(2,1)S(1)}, u32[]{:S(2)}, u32[]{:S(2)}) %collective-permute-start.5) | collective-permute-done | bytes 262176 | tf_op jit(solution)/shard_map/ppermute | solution.py:497
  74.8 3.4 copy-done.2
  78.2 5.0 %shard_map.126 = (bf16[128,2048]{1,0:T(8,128)(2,1)S(1)}, f32[128,2048]{1,0:T(8,128)S(1)}) custom-call(s32[1]{0:T(128)} %bitcast.1.refs_0_, bf16[64,2048]{1,0:T(8,128)(2,1)S(1)} %get-tuple-element.108.refs_1_, bf16[64,2048]{1,0:T(8,128)(2,1)S(1)} %collective-permute-done.4.refs_2_, bf16[64,2048]{1,0:T(8,128)(2,1)S(1)} %collective-permute-done.5.refs_3_, ...), custom_call_target="tpu_custom_call" | custom-call | flops 8388608 | bytes 38912 | tf_op jit(solution)/shard_map/pallas_call | solution.py:366
  84.8 5.0 %shard_map.125 = (bf16[128,2048]{1,0:T(8,128)(2,1)S(1)}, f32[128,2048]{1,0:T(8,128)S(1)}) custom-call(s32[1]{0:T(128)} %bitcast.1.refs_0_, bf16[64,2048]{1,0:T(8,128)(2,1)S(1)} %get-tuple-element.108.refs_1_, bf16[64,2048]{1,0:T(8,128)(2,1)S(1)} %collective-permute-done.4.refs_2_, bf16[64,2048]{1,0:T(8,128)(2,1)S(1)} %collective-permute-done.5.refs_3_, ...), custom_call_target="tpu_custom_call" | custom-call | flops 8388608 | bytes 38912 | tf_op jit(solution)/shard_map/pallas_call | solution.py:366
  94.1 15.8 %collective-permute-done.10.refs_2_ = bf16[64,2048]{1,0:T(8,128)(2,1)S(1)} collective-permute-done((bf16[64,2048]{1,0:T(8,128)(2,1)S(1)}, bf16[64,2048]{1,0:T(8,128)(2,1)S(1)}, u32[]{:S(2)}, u32[]{:S(2)}) %collective-permute-start.10) | collective-permute-done | bytes 262176 | tf_op jit(solution)/shard_map/ppermute | solution.py:497
  109.9 3.6 %collective-permute-done.12.refs_4_ = bf16[64,2048]{1,0:T(8,128)(2,1)S(1)} collective-permute-done((bf16[64,2048]{1,0:T(8,128)(2,1)S(1)}, bf16[64,2048]{1,0:T(8,128)(2,1)S(1)}, u32[]{:S(2)}, u32[]{:S(2)}) %collective-permute-start.12) | collective-permute-done | bytes 262176 | tf_op jit(solution)/shard_map/ppermute | solution.py:497
  113.4 5.6 %shard_map.128 = (bf16[128,2048]{1,0:T(8,128)(2,1)}, f32[128,2048]{1,0:T(8,128)S(1)}) custom-call(s32[1]{0:T(128)} %bitcast.1.refs_0_, bf16[64,2048]{1,0:T(8,128)(2,1)S(1)} %get-tuple-element.116.refs_1_, bf16[64,2048]{1,0:T(8,128)(2,1)S(1)} %collective-permute-done.10.refs_2_, bf16[64,2048]{1,0:T(8,128)(2,1)S(1)} %collective-permute-done.11.refs_3_, ...), custom_call_target="tpu_custom_call" | custom-call | flops 8388608 | bytes 38912 | tf_op jit(solution)/shard_map/pallas_call | solution.py:366
  120.7 5.6 %shard_map.127 = (bf16[128,2048]{1,0:T(8,128)(2,1)}, f32[128,2048]{1,0:T(8,128)S(1)}) custom-call(s32[1]{0:T(128)} %bitcast.1.refs_0_, bf16[64,2048]{1,0:T(8,128)(2,1)S(1)} %get-tuple-element.116.refs_1_, bf16[64,2048]{1,0:T(8,128)(2,1)S(1)} %collective-permute-done.10.refs_2_, bf16[64,2048]{1,0:T(8,128)(2,1)S(1)} %collective-permute-done.11.refs_3_, ...), custom_call_target="tpu_custom_call" | custom-call | flops 8388608 | bytes 38912 | tf_op jit(solution)/shard_map/pallas_call | solution.py:366
  143.0 3.9 %shard_map.131 = (f32[16,256,128]{2,1,0:T(8,128)S(1)}, f32[16,256,128]{2,1,0:T(8,128)S(1)}) custom-call(s32[1]{0:T(128)} %constant.34.clone.1.refs_0_, f32[12,16]{1,0:T(8,128)S(1)} %stack.112.refs_1_, f32[16,256,128]{2,1,0:T(8,128)S(1)} %copy-done.12, f32[16,256,128]{2,1,0:T(8,128)} %collective-permute-done.1.refs_3_, bf16[8,256,128]{2,1,0:T(8,128)(2,1)S(1)} %copy-done.38, ...), custom_call_target="tpu_custom_call" | custom-call | flops 49152 | bytes 49152 | tf_op jit(solution)/shard_map/pallas_call | solution.py:479
  152.5 3.4 copy-done.15
  155.8 3.3 copy-done.17
  173.8 4.1 %collective-permute-done.20.refs_9_ = bf16[64,2048]{1,0:T(8,128)(2,1)S(1)} collective-permute-done((bf16[64,2048]{1,0:T(8,128)(2,1)S(1)}, bf16[64,2048]{1,0:T(8,128)(2,1)S(1)}, u32[]{:S(2)}, u32[]{:S(2)}) %collective-permute-start.20) | collective-permute-done | bytes 262176 | tf_op jit(solution)/shard_map/ppermute | solution.py:497
  179.9 7.0 %collective-permute-done.18.refs_3_ = bf16[64,2048]{1,0:T(8,128)(2,1)S(1)} collective-permute-done((bf16[64,2048]{1,0:T(8,128)(2,1)S(1)}, bf16[64,2048]{1,0:T(8,128)(2,1)S(1)}, u32[]{:S(2)}, u32[]{:S(2)}) %collective-permute-start.18) | collective-permute-done | bytes 262176 | tf_op jit(solution)/shard_map/ppermute | solution.py:497
  186.8 3.4 copy-done.3
  190.2 5.0 %shard_map.136 = (bf16[128,2048]{1,0:T(8,128)(2,1)S(1)}, f32[128,2048]{1,0:T(8,128)S(1)}) custom-call(s32[1]{0:T(128)} %bitcast.1.refs_0_, bf16[64,2048]{1,0:T(8,128)(2,1)S(1)} %get-tuple-element.142.refs_1_, bf16[64,2048]{1,0:T(8,128)(2,1)S(1)} %collective-permute-done.17.refs_2_, bf16[64,2048]{1,0:T(8,128)(2,1)S(1)} %collective-permute-done.18.refs_3_, ...), custom_call_target="tpu_custom_call" | custom-call | flops 8388608 | bytes 38912 | tf_op jit(solution)/shard_map/pallas_call | solution.py:366
  196.7 5.0 %shard_map.135 = (bf16[128,2048]{1,0:T(8,128)(2,1)S(1)}, f32[128,2048]{1,0:T(8,128)S(1)}) custom-call(s32[1]{0:T(128)} %bitcast.1.refs_0_, bf16[64,2048]{1,0:T(8,128)(2,1)S(1)} %get-tuple-element.142.refs_1_, bf16[64,2048]{1,0:T(8,128)(2,1)S(1)} %collective-permute-done.17.refs_2_, bf16[64,2048]{1,0:T(8,128)(2,1)S(1)} %collective-permute-done.18.refs_3_, ...), custom_call_target="tpu_custom_call" | custom-call | flops 8388608 | bytes 38912 | tf_op jit(solution)/shard_map/pallas_call | solution.py:366
  201.7 5.0 %shard_map.138 = (bf16[128,2048]{1,0:T(8,128)(2,1)S(1)}, f32[128,2048]{1,0:T(8,128)S(1)}) custom-call(s32[1]{0:T(128)} %bitcast.1.refs_0_, bf16[64,2048]{1,0:T(8,128)(2,1)S(1)} %get-tuple-element.149.refs_1_, bf16[64,2048]{1,0:T(8,128)(2,1)S(1)} %collective-permute-done.24.refs_2_, bf16[64,2048]{1,0:T(8,128)(2,1)S(1)} %collective-permute-done.25.refs_3_, ...), custom_call_target="tpu_custom_call" | custom-call | flops 8388608 | bytes 38912 | tf_op jit(solution)/shard_map/pallas_call | solution.py:366
  207.3 5.0 %shard_map.137 = (bf16[128,2048]{1,0:T(8,128)(2,1)S(1)}, f32[128,2048]{1,0:T(8,128)S(1)}) custom-call(s32[1]{0:T(128)} %bitcast.1.refs_0_, bf16[64,2048]{1,0:T(8,128)(2,1)S(1)} %get-tuple-element.149.refs_1_, bf16[64,2048]{1,0:T(8,128)(2,1)S(1)} %collective-permute-done.24.refs_2_, bf16[64,2048]{1,0:T(8,128)(2,1)S(1)} %collective-permute-done.25.refs_3_, ...), custom_call_target="tpu_custom_call" | custom-call | flops 8388608 | bytes 38912 | tf_op jit(solution)/shard_map/pallas_call | solution.py:366
  219.8 6.5 %collective-permute-done.27.arrived_ref = bf16[128,2048]{1,0:T(8,128)(2,1)S(1)} collective-permute-done((bf16[128,2048]{1,0:T(8,128)(2,1)S(1)}, bf16[128,2048]{1,0:T(8,128)(2,1)S(1)}, u32[]{:S(2)}, u32[]{:S(2)}) %collective-permute-start.27) | collective-permute-done | bytes 524320 | tf_op jit(solution)/shard_map/ppermute | solution.py:497
  227.0 4.9 %collective-permute-done.23.arrived_ref = bf16[128,2048]{1,0:T(8,128)(2,1)S(1)} collective-permute-done((bf16[128,2048]{1,0:T(8,128)(2,1)S(1)}, bf16[128,2048]{1,0:T(8,128)(2,1)S(1)}, u32[]{:S(2)}, u32[]{:S(2)}) %collective-permute-start.23) | collective-permute-done | bytes 524320 | tf_op jit(solution)/shard_map/ppermute | solution.py:497
  238.7 3.2 shard_map.143.v_ref.refs_2_
  251.5 9.9 %shard_map.148 = (f32[256,4096]{1,0:T(8,128)S(1)}, f32[4,256,8]{2,1,0:T(8,128)S(1)}, f32[4,256,8]{2,1,0:T(8,128)S(1)}, f32[256,256]{1,0:T(8,128)S(1)}, f32[256,256]{1,0:T(8,128)S(1)}) custom-call(s32[3]{0:T(128)S(1)} %get-tuple-element.268.refs_0_, bf16[256,4096]{1,0:T(8,128)(2,1)S(1)} %copy-done.4, bf16[256,4096]{1,0:T(8,128)(2,1)S(1)} %shard_map.143.v_ref.refs_2_, ...), custom_call_target="tpu_custom_call" | custom-call | flops 7340032 | bytes 57344 | tf_op jit(solution)/shard_map/pallas_call | solution.py:204
  275.4 3.4 copy-done.16
  286.9 10.6 %shard_map.151 = (f32[256,4096]{1,0:T(8,128)S(1)}, f32[4,256,8]{2,1,0:T(8,128)S(1)}, f32[4,256,8]{2,1,0:T(8,128)S(1)}, f32[256,256]{1,0:T(8,128)S(1)}, f32[256,256]{1,0:T(8,128)S(1)}) custom-call(s32[3]{0:T(128)S(1)} %get-tuple-element.269.refs_0_, bf16[256,4096]{1,0:T(8,128)(2,1)S(1)} %copy-done.4, ...), custom_call_target="tpu_custom_call", output_to_operand_aliasing={{0}: (13, {}), {1}: (14, {}), {2}: (15, {})} | custom-call | flops 7340032 | bytes 57344 | tf_op jit(solution)/shard_map/pallas_call | solution.py:204
  299.6 3.9 %shard_map.152 = (f32[16,256,128]{2,1,0:T(8,128)S(1)}, f32[16,256,128]{2,1,0:T(8,128)S(1)}) custom-call(s32[1]{0:T(128)} %constant.34.clone.1.refs_0_, f32[12,16]{1,0:T(8,128)S(1)} %stack.124.refs_1_, f32[16,256,128]{2,1,0:T(8,128)S(1)} %copy-done.14, f32[16,256,128]{2,1,0:T(8,128)S(1)} %copy-done.26, bf16[8,256,128]{2,1,0:T(8,128)(2,1)S(1)} %copy-done.42, ...), custom_call_target="tpu_custom_call" | custom-call | flops 49152 | bytes 49152 | tf_op jit(solution)/shard_map/pallas_call | solution.py:479
  308.1 6.4 %shard_map.153 = (bf16[256,4096]{1,0:T(8,128)(2,1)}, f32[256,256]{1,0:T(8,128)S(1)}, f32[4,256,8]{2,1,0:T(8,128)S(1)}, f32[4,256,8]{2,1,0:T(8,128)S(1)}) custom-call(s32[1]{0:T(128)} %bitcast.9.at_ref, bf16[256,4096]{1,0:T(8,128)(2,1)S(1)} %copy-done.4, f32[256,4096]{1,0:T(8,128)S(1)} %copy-done.10, bf16[256,256]{1,0:T(8,128)(2,1)S(1)} %copy-done.29, ...), custom_call_target="tpu_custom_call" | custom-call | flops 4194304 | bytes 32768 | tf_op jit(solution)/shard_map/pallas_call | solution.py:302
  314.4 6.1 %shard_map.154 = (bf16[256,4096]{1,0:T(8,128)(2,1)}, f32[256,256]{1,0:T(8,128)S(1)}, f32[4,256,8]{2,1,0:T(8,128)S(1)}, f32[4,256,8]{2,1,0:T(8,128)S(1)}) custom-call(s32[1]{0:T(128)} %bitcast.at_ref, bf16[256,4096]{1,0:T(8,128)(2,1)S(1)} %copy-done.4, f32[256,4096]{1,0:T(8,128)S(1)} %copy-done.10, ...), custom_call_target="tpu_custom_call", output_to_operand_aliasing={{0}: (11, {}), {2}: (12, {}), {3}: (13, {})} | custom-call | flops 4194304 | bytes 32768 | tf_op jit(solution)/shard_map/pallas_call | solution.py:302
  328.3 6.0 %collective-permute-done.42 = bf16[256,256]{1,0:T(8,128)(2,1)S(1)} collective-permute-done((bf16[256,256]{1,0:T(8,128)(2,1)S(1)}, bf16[256,256]{1,0:T(8,128)(2,1)S(1)}, u32[]{:S(2)}, u32[]{:S(2)}) %collective-permute-start.42) | collective-permute-done | bytes 131104 | tf_op jit(solution)/shard_map/ppermute | solution.py:513
  (311 shorter events, 139.6 us)
Async XLA Ops:
  7.2 51.4 %all-gather.4.cloned.1.call-start = ((), (), s32[]{:S(2)}) async-start(), calls=%async_computation | async-start | bytes 2621440 | tf_op jit(solution)/shard_map/all_gather | solution.py:525
  7.3 51.4 %collective-permute-start = (bf16[4096,1024]{1,0:T(8,128)(2,1)}, bf16[4096,1024]{1,0:T(8,128)(2,1)}, u32[]{:S(2)}, u32[]{:S(2)}) collective-permute-start(bf16[4096,1024]{1,0:T(8,128)(2,1)} %refs_5_.15), channel_id=1, source_target_pairs={{0,4},{4,0},{8,12},{12,8},{16,20},{20,16},{24,28},{28,24},{1,5},{5... | collective-permute-start | bytes 25165832 | tf_op jit(solution)/shard_map/ppermute | solution.py:501
  10.2 149.6 %all-gather.6.cloned.1.call-start = ((), (), s32[]{:S(2)}) async-start(), calls=%async_computation.1 | async-start | bytes 2621440 | tf_op jit(solution)/shard_map/all_gather | solution.py:525
  28.5 14.2 %collective-permute-start.3 = (bf16[8,256,128]{2,1,0:T(8,128)(2,1)S(1)}, bf16[8,256,128]{2,1,0:T(8,128)(2,1)S(1)}, u32[]{:S(2)}, u32[]{:S(2)}) collective-permute-start(bf16[8,256,128]{2,1,0:T(8,128)(2,1)S(1)} %shard_map.122.refs_2_), channel_id=1, source_target_pairs={{0,16},{4,20},{8,24},{12,28},{16,0},{20,4},{24,8},{28,12},{1,17},{... | collective-permute-start | bytes 1572872 | tf_op jit(solution)/shard_map/ppermute | solution.py:497
  31.4 14.0 %collective-permute-start.2 = (bf16[8,256,128]{2,1,0:T(8,128)(2,1)S(1)}, bf16[8,256,128]{2,1,0:T(8,128)(2,1)S(1)}, u32[]{:S(2)}, u32[]{:S(2)}) collective-permute-start(bf16[8,256,128]{2,1,0:T(8,128)(2,1)S(1)} %shard_map.121.refs_2_), channel_id=1, source_target_pairs={{0,8},{4,12},{8,0},{12,4},{16,24},{20,28},{24,16},{28,20},{1,9},{5... | collective-permute-start | bytes 1572872 | tf_op jit(solution)/shard_map/ppermute | solution.py:497
  47.7 15.8 %collective-permute-start.8 = (bf16[8,256,128]{2,1,0:T(8,128)(2,1)}, bf16[8,256,128]{2,1,0:T(8,128)(2,1)S(1)}, u32[]{:S(2)}, u32[]{:S(2)}) collective-permute-start(bf16[8,256,128]{2,1,0:T(8,128)(2,1)} %shard_map.124), channel_id=1, source_target_pairs={{0,8},{4,12},{8,0},{12,4},{16,24},{20,28},{24,16},{28,20},{1,9},{5... | collective-permute-start | bytes 1572872 | tf_op jit(solution)/shard_map/ppermute | solution.py:497
  83.2 45.5 %collective-permute-start.15 = (bf16[128,2048]{1,0:T(8,128)(2,1)S(1)}, bf16[128,2048]{1,0:T(8,128)(2,1)S(1)}, u32[]{:S(2)}, u32[]{:S(2)}) collective-permute-start(bf16[128,2048]{1,0:T(8,128)(2,1)S(1)} %get-tuple-element.115), channel_id=1, source_target_pairs={{0,16},{4,20},{8,24},{12,28},{16,0},{20,4},{24,8},{28,12},{1,17},{... | collective-permute-start | bytes 1572872 | tf_op jit(solution)/shard_map/ppermute | solution.py:497
  89.7 40.8 %collective-permute-start.9 = (bf16[128,2048]{1,0:T(8,128)(2,1)S(1)}, bf16[128,2048]{1,0:T(8,128)(2,1)S(1)}, u32[]{:S(2)}, u32[]{:S(2)}) collective-permute-start(bf16[128,2048]{1,0:T(8,128)(2,1)S(1)} %get-tuple-element.113), channel_id=1, source_target_pairs={{0,8},{4,12},{8,0},{12,4},{16,24},{20,28},{24,16},{28,20},{1,9},{5... | collective-permute-start | bytes 1572872 | tf_op jit(solution)/shard_map/ppermute | solution.py:497
  90.5 19.4 %collective-permute-start.10 = (bf16[64,2048]{1,0:T(8,128)(2,1)S(1)}, bf16[64,2048]{1,0:T(8,128)(2,1)S(1)}, u32[]{:S(2)}, u32[]{:S(2)}) collective-permute-start(bf16[64,2048]{1,0:T(8,128)(2,1)S(1)} %get-tuple-element.220), channel_id=1, source_target_pairs={{0,8},{4,12},{8,0},{12,4},{16,24},{20,28},{24,16},{28,20},{1,9},{5... | collective-permute-start | bytes 786440 | tf_op jit(solution)/shard_map/ppermute | solution.py:497
  92.0 17.9 %collective-permute-start.11 = (bf16[64,2048]{1,0:T(8,128)(2,1)S(1)}, bf16[64,2048]{1,0:T(8,128)(2,1)S(1)}, u32[]{:S(2)}, u32[]{:S(2)}) collective-permute-start(bf16[64,2048]{1,0:T(8,128)(2,1)S(1)} %get-tuple-element.219), channel_id=1, source_target_pairs={{0,16},{4,20},{8,24},{12,28},{16,0},{20,4},{24,8},{28,12},{1,17},{... | collective-permute-start | bytes 786440 | tf_op jit(solution)/shard_map/ppermute | solution.py:497
  92.6 20.8 %collective-permute-start.12 = (bf16[64,2048]{1,0:T(8,128)(2,1)S(1)}, bf16[64,2048]{1,0:T(8,128)(2,1)S(1)}, u32[]{:S(2)}, u32[]{:S(2)}) collective-permute-start(bf16[64,2048]{1,0:T(8,128)(2,1)S(1)} %get-tuple-element.218), channel_id=1, source_target_pairs={{0,24},{4,28},{8,16},{12,20},{16,8},{20,12},{24,0},{28,4},{1,25},{... | collective-permute-start | bytes 786440 | tf_op jit(solution)/shard_map/ppermute | solution.py:497
  120.0 41.8 %collective-permute-start.21 = (bf16[128,2048]{1,0:T(8,128)(2,1)}, bf16[128,2048]{1,0:T(8,128)(2,1)}, u32[]{:S(2)}, u32[]{:S(2)}) collective-permute-start(bf16[128,2048]{1,0:T(8,128)(2,1)} %get-tuple-element.121), channel_id=1, source_target_pairs={{0,16},{4,20},{8,24},{12,28},{16,0},{20,4},{24,8},{28,12},{1,17},{... | collective-permute-start | bytes 1572872 | tf_op jit(solution)/shard_map/ppermute | solution.py:497
  127.3 37.2 %collective-permute-start.13 = (bf16[128,2048]{1,0:T(8,128)(2,1)}, bf16[128,2048]{1,0:T(8,128)(2,1)}, u32[]{:S(2)}, u32[]{:S(2)}) collective-permute-start(bf16[128,2048]{1,0:T(8,128)(2,1)} %get-tuple-element.120), channel_id=1, source_target_pairs={{0,8},{4,12},{8,0},{12,4},{16,24},{20,28},{24,16},{28,20},{1,9},{5... | collective-permute-start | bytes 1572872 | tf_op jit(solution)/shard_map/ppermute | solution.py:497
  130.5 29.3 %collective-permute-start.16 = (bf16[64,2048]{1,0:T(8,128)(2,1)}, bf16[64,2048]{1,0:T(8,128)(2,1)}, u32[]{:S(2)}, u32[]{:S(2)}) collective-permute-start(bf16[64,2048]{1,0:T(8,128)(2,1)} %get-tuple-element.128), channel_id=1, source_target_pairs={{0,8},{4,12},{8,0},{12,4},{16,24},{20,28},{24,16},{28,20},{1,9},{5... | collective-permute-start | bytes 786440 | tf_op jit(solution)/shard_map/ppermute | solution.py:497
  132.8 27.0 %collective-permute-start.14 = (bf16[64,2048]{1,0:T(8,128)(2,1)}, bf16[64,2048]{1,0:T(8,128)(2,1)}, u32[]{:S(2)}, u32[]{:S(2)}) collective-permute-start(bf16[64,2048]{1,0:T(8,128)(2,1)} %get-tuple-element.125), channel_id=1, source_target_pairs={{0,16},{4,20},{8,24},{12,28},{16,0},{20,4},{24,8},{28,12},{1,17},{... | collective-permute-start | bytes 786440 | tf_op jit(solution)/shard_map/ppermute | solution.py:497
  167.1 19.8 %collective-permute-start.18 = (bf16[64,2048]{1,0:T(8,128)(2,1)S(1)}, bf16[64,2048]{1,0:T(8,128)(2,1)S(1)}, u32[]{:S(2)}, u32[]{:S(2)}) collective-permute-start(bf16[64,2048]{1,0:T(8,128)(2,1)S(1)} %get-tuple-element.215), channel_id=1, source_target_pairs={{0,16},{4,20},{8,24},{12,28},{16,0},{20,4},{24,8},{28,12},{1,17},{... | collective-permute-start | bytes 786440 | tf_op jit(solution)/shard_map/ppermute | solution.py:497
  168.4 18.4 %collective-permute-start.19 = (bf16[64,2048]{1,0:T(8,128)(2,1)S(1)}, bf16[64,2048]{1,0:T(8,128)(2,1)S(1)}, u32[]{:S(2)}, u32[]{:S(2)}) collective-permute-start(bf16[64,2048]{1,0:T(8,128)(2,1)S(1)} %get-tuple-element.214), channel_id=1, source_target_pairs={{0,24},{4,28},{8,16},{12,20},{16,8},{20,12},{24,0},{28,4},{1,25},{... | collective-permute-start | bytes 786440 | tf_op jit(solution)/shard_map/ppermute | solution.py:497
  172.3 29.3 %collective-permute-start.24 = (bf16[64,2048]{1,0:T(8,128)(2,1)S(1)}, bf16[64,2048]{1,0:T(8,128)(2,1)S(1)}, u32[]{:S(2)}, u32[]{:S(2)}) collective-permute-start(bf16[64,2048]{1,0:T(8,128)(2,1)S(1)} %get-tuple-element.212), channel_id=1, source_target_pairs={{0,8},{4,12},{8,0},{12,4},{16,24},{20,28},{24,16},{28,20},{1,9},{5... | collective-permute-start | bytes 786440 | tf_op jit(solution)/shard_map/ppermute | solution.py:497
  177.8 23.8 %collective-permute-start.25 = (bf16[64,2048]{1,0:T(8,128)(2,1)S(1)}, bf16[64,2048]{1,0:T(8,128)(2,1)S(1)}, u32[]{:S(2)}, u32[]{:S(2)}) collective-permute-start(bf16[64,2048]{1,0:T(8,128)(2,1)S(1)} %get-tuple-element.211), channel_id=1, source_target_pairs={{0,16},{4,20},{8,24},{12,28},{16,0},{20,4},{24,8},{28,12},{1,17},{... | collective-permute-start | bytes 786440 | tf_op jit(solution)/shard_map/ppermute | solution.py:497
  178.6 23.1 %collective-permute-start.26 = (bf16[64,2048]{1,0:T(8,128)(2,1)S(1)}, bf16[64,2048]{1,0:T(8,128)(2,1)S(1)}, u32[]{:S(2)}, u32[]{:S(2)}) collective-permute-start(bf16[64,2048]{1,0:T(8,128)(2,1)S(1)} %get-tuple-element.210), channel_id=1, source_target_pairs={{0,24},{4,28},{8,16},{12,20},{16,8},{20,12},{24,0},{28,4},{1,25},{... | collective-permute-start | bytes 786440 | tf_op jit(solution)/shard_map/ppermute | solution.py:497
  195.2 22.2 %collective-permute-start.28 = (bf16[128,2048]{1,0:T(8,128)(2,1)S(1)}, bf16[128,2048]{1,0:T(8,128)(2,1)S(1)}, u32[]{:S(2)}, u32[]{:S(2)}) collective-permute-start(bf16[128,2048]{1,0:T(8,128)(2,1)S(1)} %get-tuple-element.148), channel_id=1, source_target_pairs={{0,16},{4,20},{8,24},{12,28},{16,0},{20,4},{24,8},{28,12},{1,17},{... | collective-permute-start | bytes 1572872 | tf_op jit(solution)/shard_map/ppermute | solution.py:497
  212.3 14.0 %collective-permute-start.27 = (bf16[128,2048]{1,0:T(8,128)(2,1)S(1)}, bf16[128,2048]{1,0:T(8,128)(2,1)S(1)}, u32[]{:S(2)}, u32[]{:S(2)}) collective-permute-start(bf16[128,2048]{1,0:T(8,128)(2,1)S(1)} %get-tuple-element.153), channel_id=1, source_target_pairs={{0,8},{4,12},{8,0},{12,4},{16,24},{20,28},{24,16},{28,20},{1,9},{5... | collective-permute-start | bytes 1572872 | tf_op jit(solution)/shard_map/ppermute | solution.py:497
  213.2 18.8 %collective-permute-start.23 = (bf16[128,2048]{1,0:T(8,128)(2,1)S(1)}, bf16[128,2048]{1,0:T(8,128)(2,1)S(1)}, u32[]{:S(2)}, u32[]{:S(2)}) collective-permute-start(bf16[128,2048]{1,0:T(8,128)(2,1)S(1)} %get-tuple-element.147), channel_id=1, source_target_pairs={{0,8},{4,12},{8,0},{12,4},{16,24},{20,28},{24,16},{28,20},{1,9},{5... | collective-permute-start | bytes 1572872 | tf_op jit(solution)/shard_map/ppermute | solution.py:497
  217.4 17.4 %collective-permute-start.33 = (bf16[64,2048]{1,0:T(8,128)(2,1)S(1)}, bf16[64,2048]{1,0:T(8,128)(2,1)S(1)}, u32[]{:S(2)}, u32[]{:S(2)}) collective-permute-start(bf16[64,2048]{1,0:T(8,128)(2,1)S(1)} %get-tuple-element.169), channel_id=1, source_target_pairs={{0,8},{4,12},{8,0},{12,4},{16,24},{20,28},{24,16},{28,20},{1,9},{5... | collective-permute-start | bytes 786440 | tf_op jit(solution)/shard_map/ppermute | solution.py:497
  217.8 19.8 %collective-permute-start.32 = (bf16[64,2048]{1,0:T(8,128)(2,1)S(1)}, bf16[64,2048]{1,0:T(8,128)(2,1)S(1)}, u32[]{:S(2)}, u32[]{:S(2)}) collective-permute-start(bf16[64,2048]{1,0:T(8,128)(2,1)S(1)} %get-tuple-element.168), channel_id=1, source_target_pairs={{0,8},{4,12},{8,0},{12,4},{16,24},{20,28},{24,16},{28,20},{1,9},{5... | collective-permute-start | bytes 786440 | tf_op jit(solution)/shard_map/ppermute | solution.py:497
  249.8 15.3 %collective-permute-start.36 = (bf16[8,256,128]{2,1,0:T(8,128)(2,1)S(1)}, bf16[8,256,128]{2,1,0:T(8,128)(2,1)S(1)}, u32[]{:S(2)}, u32[]{:S(2)}) collective-permute-start(bf16[8,256,128]{2,1,0:T(8,128)(2,1)S(1)} %shard_map.147.refs_2_), channel_id=1, source_target_pairs={{0,16},{4,20},{8,24},{12,28},{16,0},{20,4},{24,8},{28,12},{1,17},{... | collective-permute-start | bytes 1572872 | tf_op jit(solution)/shard_map/ppermute | solution.py:497
  250.2 14.9 %collective-permute-start.35 = (bf16[8,256,128]{2,1,0:T(8,128)(2,1)S(1)}, bf16[8,256,128]{2,1,0:T(8,128)(2,1)S(1)}, u32[]{:S(2)}, u32[]{:S(2)}) collective-permute-start(bf16[8,256,128]{2,1,0:T(8,128)(2,1)S(1)} %shard_map.146.refs_2_), channel_id=1, source_target_pairs={{0,8},{4,12},{8,0},{12,4},{16,24},{20,28},{24,16},{28,20},{1,9},{5... | collective-permute-start | bytes 1572872 | tf_op jit(solution)/shard_map/ppermute | solution.py:497
  267.4 32.1 %collective-permute-start.39 = (bf16[8,256,128]{2,1,0:T(8,128)(2,1)}, bf16[8,256,128]{2,1,0:T(8,128)(2,1)}, u32[]{:S(2)}, u32[]{:S(2)}) collective-permute-start(bf16[8,256,128]{2,1,0:T(8,128)(2,1)} %shard_map.150), channel_id=1, source_target_pairs={{0,8},{4,12},{8,0},{12,4},{16,24},{20,28},{24,16},{28,20},{1,9},{5... | collective-permute-start | bytes 1572872 | tf_op jit(solution)/shard_map/ppermute | solution.py:497
  269.8 29.7 %collective-permute-start.38 = (bf16[8,256,128]{2,1,0:T(8,128)(2,1)}, bf16[8,256,128]{2,1,0:T(8,128)(2,1)}, u32[]{:S(2)}, u32[]{:S(2)}) collective-permute-start(bf16[8,256,128]{2,1,0:T(8,128)(2,1)} %shard_map.149), channel_id=1, source_target_pairs={{0,16},{4,20},{8,24},{12,28},{16,0},{20,4},{24,8},{28,12},{1,17},{... | collective-permute-start | bytes 1572872 | tf_op jit(solution)/shard_map/ppermute | solution.py:497
  303.6 20.3 %collective-permute-start.44 = (bf16[256,256]{1,0:T(8,128)(2,1)S(1)}, bf16[256,256]{1,0:T(8,128)(2,1)S(1)}, u32[]{:S(2)}, u32[]{:S(2)}) collective-permute-start(bf16[256,256]{1,0:T(8,128)(2,1)S(1)} %convert_element_type.35), channel_id=1, source_target_pairs={{0,1},{1,0},{2,3},{3,2},{4,5},{5,4},{6,7},{7,6},{8,9},{9,8},{10,11... | collective-permute-start | bytes 393224 | tf_op jit(solution)/shard_map/ppermute | solution.py:513
  304.5 21.4 %collective-permute-start.45 = (bf16[256,256]{1,0:T(8,128)(2,1)S(1)}, bf16[256,256]{1,0:T(8,128)(2,1)S(1)}, u32[]{:S(2)}, u32[]{:S(2)}) collective-permute-start(bf16[256,256]{1,0:T(8,128)(2,1)S(1)} %convert_element_type.35), channel_id=1, source_target_pairs={{0,2},{1,3},{2,0},{3,1},{4,6},{5,7},{6,4},{7,5},{8,10},{9,11},{10,... | collective-permute-start | bytes 393224 | tf_op jit(solution)/shard_map/ppermute | solution.py:513
  306.1 19.8 %collective-permute-start.46 = (bf16[256,256]{1,0:T(8,128)(2,1)S(1)}, bf16[256,256]{1,0:T(8,128)(2,1)S(1)}, u32[]{:S(2)}, u32[]{:S(2)}) collective-permute-start(bf16[256,256]{1,0:T(8,128)(2,1)S(1)} %convert_element_type.35), channel_id=1, source_target_pairs={{0,3},{1,2},{2,1},{3,0},{4,7},{5,6},{6,5},{7,4},{8,11},{9,10},{10,... | collective-permute-start | bytes 393224 | tf_op jit(solution)/shard_map/ppermute | solution.py:513
  (91 other events, 560.6 us)
Sparse Core Ops, SparseCore 0:
  10.4 48.2 all-gather.3
  60.2 44.6 all-gather.5

commit v7 on v6

--- a/solution.py
+++ b/solution.py
@@ -12,7 +12,7 @@
 NN = (((1,), (0,)), ((), ()))
 NT = (((1,), (1,)), ((), ()))
 TN = (((0,), (0,)), ((), ()))
-PARAMS = pltpu.CompilerParams(vmem_limit_bytes=24 << 20)
+PARAMS = pltpu.CompilerParams(vmem_limit_bytes=48 << 20)
 
 
 def mm(a, b, dims):
@@ -572,10 +572,11 @@
         ahead = [lane[chunk][1] for lane in waiting]
         if chunk == 1:
             sent, first = reduce(0, ahead)
-            full = tie(fulls[1], *ahead, *first, *before(sent))
+            full = tie(fulls[1], *ahead)
             own += [blocks_of(full, i * rows, rows, chips, chip) for i in range(2)]
-            ahead = reduce(1, own[2])[1]
-    reduce(2, ahead)
+            last = reduce(1, own[2])[1]
+            ahead = [*first, *before([*sent, *own[2]]), *own[3]]
+    reduce(2, [*ahead, *last])
     reduce(3, None)
     ends = waiting[0] + waiting[1]
     return finish([keep for keep, _ in ends], [arrived for _, arrived in ends])
@@ -692,10 +693,10 @@
 
     mine, theirs = span_both(ssm_input, by_group(step_size * tail), b_rows)
     forward = exchange(mine, theirs, ends, chips, chip, core, False)
-    sent, raw = next(forward)
+    _, raw = next(forward)
     for _ in range(chips.bit_length() - 2):
-        sent, raw = forward.send([])
-    full = tie(fulls[0], other_weight, *sent)
+        _, raw = forward.send([])
+    full = tie(fulls[0], other_weight, *raw)
     rows = span // 4
     own = blocks_of(full, 0, rows, chips, chip)
     blocks = [across(block, hop, chips) if hop else block for hop, block in enumerate(own)]
@@ -709,7 +710,7 @@
         return [in_mine, tables[-1], steps_g, skip_rows, rise, c_rows]
 
     grad_y = project(
-        fulls, blocks, second, out_weight, other_weight, chips, chip, core, raw, before
+        fulls, blocks, second, out_weight, other_weight, chips, chip, core, second, before
     )
     in_mine, in_other, decay, weight, cross = tables
 

time: 344 us -> 328 us (0.953)
  local copies, waits for them, and re-layouts: 60.5 us -> 37.1 us
  Pallas kernels: 110 us -> 133 us
  waiting for transfers between devices: 92.1 us -> 74.1 us
    unnamed x148 -> x134, local copies, waits for them, and re-layouts: 49.2 us -> 24.9 us
    ppermute x36, waiting for transfers between devices: 76.6 us -> 56.8 us  [across(): return lax.ppermute(value, 'seq', pairs)]
    pallas_call x8, Pallas kernels: 41 us -> 48.5 us  [partial_sums(): pl.pallas_call(lambda *refs: project_kernel(hops, *refs), grid_spec=pltpu...]
    pallas_call x1, Pallas kernels: 2.82 us -> 6.81 us  [decays(): pl.pallas_call(decay_kernel, grid=(groups,), in_specs=[pl.BlockSpec((1, s...]
    pallas_call x2, Pallas kernels: 20.5 us -> 24.4 us  [inner_part(): pl.pallas_call(lambda *refs: inner_kernel(not held, last, *refs), grid_sp...]
  transfers between devices with their start and end apart: 49 -> 49, of which waited for: 19 -> 16; matrix products, arithmetic and copies ran while one was open for 4% -> 5% of each run, Pallas kernels for 29% -> 37%
where the time goes in v7:
time: 328 us; the launch traced here: 327 us
  Pallas kernels  133 us (41%)
  waiting for transfers between devices  74.1 us (23%)
  starting transfers between devices  50.7 us (15%)
  local copies, waits for them, and re-layouts  37.1 us (11%)
  between operations  14.8 us (5%)
  blocking collectives  10.6 us (3%)
  other arithmetic  5.45 us (2%)
    ppermute x36, waiting for transfers between devices, across(): return lax.ppermute(value, 'seq', pairs)  56.8 us
    pallas_call x8, Pallas kernels, partial_sums(): pl.pallas_call(lambda *refs: project_kernel(hops, *refs), grid_spec=pltpu...  48.5 us
    ppermute x36, starting transfers between devices, across(): return lax.ppermute(value, 'seq', pairs)  40.6 us
    unnamed x134, local copies, waits for them, and re-layouts  24.9 us
    pallas_call x2, Pallas kernels, inner_part(): pl.pallas_call(lambda *refs: inner_kernel(not held, last, *refs), grid_sp...  24.4 us
    pallas_call x10, Pallas kernels, blend(): pl.pallas_call(lambda *refs: blend_kernel(count, step, *refs), grid_spec=...  20.4 us
    pallas_call x2, Pallas kernels, outer_part(): pl.pallas_call(outer_kernel, grid_spec=pltpu.PrefetchScalarGridSpec(num_s...  15.5 us
    all_gather x1, blocking collectives, local(): ends = lax.all_gather(running[-1], 'seq')  10.6 us
  transfers between devices with their start and end apart: 49, of which 16 were waited for; matrix products, arithmetic and copies ran while one was open for 5% of the time, Pallas kernels for 37%

profile of v7, /device:TPU:0, one launch (start us, length us, event | category | flops | bytes accessed | tf_op | source)
XLA Modules:
  0.0 326.6 jit_solution(16255353158056204828)
XLA Ops:
  14.0 10.6 %all-gather = f32[8,1,32]{2,1,0:T(1,128)S(1)} all-gather(f32[1,1,32]{2,1,0:T(1,128)S(1)} %bitcast.115), channel_id=1, replica_groups=mesh['seq'=8,'head'=4] {'seq'}, dimensions={0}, use_global_device_ids=true | all-gather | bytes 1152 | tf_op jit(solution)/shard_map/all_gather | solution.py:680
  34.4 9.4 %collective-permute-done.2.refs_3_.refs_4_ = bf16[8,256,128]{2,1,0:T(8,128)(2,1)S(1)} collective-permute-done((bf16[8,256,128]{2,1,0:T(8,128)(2,1)S(1)}, bf16[8,256,128]{2,1,0:T(8,128)(2,1)S(1)}, u32[]{:S(2)}, u32[]{:S(2)}) %collective-permute-start.2) | collective-permute-done | bytes 524320 | tf_op jit(solution)/shard_map/ppermute | solution.py:497
  43.8 2.8 collective-permute-done.3.refs_3_.refs_6_
  51.6 7.0 %all-gather.4.cloned.1.call-done = bf16[128,8192]{1,0:T(8,128)(2,1)} async-done(((bf16[128,2048]{1,0:T(8,128)(2,1)}), bf16[128,8192]{1,0:T(8,128)(2,1)}) %all-gather.4.cloned.1.call-update) | async-done | bytes 2097168 | tf_op jit(solution)/shard_map/all_gather | solution.py:525
  58.6 2.9 collective-permute-done.4.refs_5_
  61.5 2.7 collective-permute-done.5.refs_7_
  69.1 6.5 %collective-permute-done.8.refs_4_ = bf16[64,2048]{1,0:T(8,128)(2,1)S(1)} collective-permute-done((bf16[64,2048]{1,0:T(8,128)(2,1)S(1)}, bf16[64,2048]{1,0:T(8,128)(2,1)S(1)}, u32[]{:S(2)}, u32[]{:S(2)}) %collective-permute-start.8) | collective-permute-done | bytes 262176 | tf_op jit(solution)/shard_map/ppermute | solution.py:497
  81.9 6.3 %shard_map.125 = (bf16[128,2048]{1,0:T(8,128)(2,1)}, f32[128,2048]{1,0:T(8,128)S(1)}) custom-call(s32[1]{0:T(128)} %bitcast.1.refs_0_, bf16[64,2048]{1,0:T(8,128)(2,1)S(1)} %get-tuple-element.109.refs_1_, bf16[64,2048]{1,0:T(8,128)(2,1)S(1)} %collective-permute-done.6.refs_2_, bf16[64,2048]{1,0:T(8,128)(2,1)S(1)} %collective-permute-done.7.refs_3_, ...), custom_call_target="tpu_custom_call" | custom-call | flops 8388608 | bytes 38912 | tf_op jit(solution)/shard_map/pallas_call | solution.py:366
  89.0 6.3 %shard_map.126 = (bf16[128,2048]{1,0:T(8,128)(2,1)}, f32[128,2048]{1,0:T(8,128)S(1)}) custom-call(s32[1]{0:T(128)} %bitcast.1.refs_0_, bf16[64,2048]{1,0:T(8,128)(2,1)S(1)} %get-tuple-element.109.refs_1_, bf16[64,2048]{1,0:T(8,128)(2,1)S(1)} %collective-permute-done.6.refs_2_, bf16[64,2048]{1,0:T(8,128)(2,1)S(1)} %collective-permute-done.7.refs_3_, ...), custom_call_target="tpu_custom_call" | custom-call | flops 8388608 | bytes 38912 | tf_op jit(solution)/shard_map/pallas_call | solution.py:366
  96.3 6.3 %shard_map.127 = (bf16[128,2048]{1,0:T(8,128)(2,1)}, f32[128,2048]{1,0:T(8,128)S(1)}) custom-call(s32[1]{0:T(128)} %bitcast.1.refs_0_, bf16[64,2048]{1,0:T(8,128)(2,1)S(1)} %get-tuple-element.116.refs_1_, bf16[64,2048]{1,0:T(8,128)(2,1)S(1)} %collective-permute-done.10.refs_2_, bf16[64,2048]{1,0:T(8,128)(2,1)S(1)} %collective-permute-done.11.refs_3_, ...), custom_call_target="tpu_custom_call" | custom-call | flops 8388608 | bytes 38912 | tf_op jit(solution)/shard_map/pallas_call | solution.py:366
  104.7 6.3 %shard_map.128 = (bf16[128,2048]{1,0:T(8,128)(2,1)}, f32[128,2048]{1,0:T(8,128)S(1)}) custom-call(s32[1]{0:T(128)} %bitcast.1.refs_0_, bf16[64,2048]{1,0:T(8,128)(2,1)S(1)} %get-tuple-element.116.refs_1_, bf16[64,2048]{1,0:T(8,128)(2,1)S(1)} %collective-permute-done.10.refs_2_, bf16[64,2048]{1,0:T(8,128)(2,1)S(1)} %collective-permute-done.11.refs_3_, ...), custom_call_target="tpu_custom_call" | custom-call | flops 8388608 | bytes 38912 | tf_op jit(solution)/shard_map/pallas_call | solution.py:366
  112.0 2.7 constant_dynamic-slice_fusion.10
  121.4 3.4 %collective-permute-done.16.refs_4_ = bf16[64,2048]{1,0:T(8,128)(2,1)S(1)} collective-permute-done((bf16[64,2048]{1,0:T(8,128)(2,1)S(1)}, bf16[64,2048]{1,0:T(8,128)(2,1)S(1)}, u32[]{:S(2)}, u32[]{:S(2)}) %collective-permute-start.16) | collective-permute-done | bytes 262176 | tf_op jit(solution)/shard_map/ppermute | solution.py:497
  133.0 6.3 %collective-permute-done.17.refs_8_ = bf16[64,2048]{1,0:T(8,128)(2,1)S(1)} collective-permute-done((bf16[64,2048]{1,0:T(8,128)(2,1)S(1)}, bf16[64,2048]{1,0:T(8,128)(2,1)S(1)}, u32[]{:S(2)}, u32[]{:S(2)}) %collective-permute-start.17) | collective-permute-done | bytes 262176 | tf_op jit(solution)/shard_map/ppermute | solution.py:497
  148.3 5.2 %shard_map.132 = (f32[16,256,128]{2,1,0:T(8,128)S(1)}, f32[16,256,128]{2,1,0:T(8,128)}) custom-call(s32[1]{0:T(128)} %constant.34.clone.1.refs_0_, f32[12,16]{1,0:T(8,128)S(1)} %stack.112.refs_1_, f32[16,256,128]{2,1,0:T(8,128)} %copy-done.4, f32[16,256,128]{2,1,0:T(8,128)} %collective-permute-done.1.refs_3_, bf16[8,256,128]{2,1,0:T(8,128)(2,1)S(1)} %copy-done.24, ...), custom_call_target="tpu_custom_call" | custom-call | flops 49152 | bytes 49152 | tf_op jit(solution)/shard_map/pallas_call | solution.py:479
  154.8 6.8 %shard_map.133 = (f32[32,256,256]{2,1,0:T(8,128)}, bf16[32,256,512]{2,1,0:T(8,128)(2,1)}, f32[256,256]{1,0:T(8,128)S(1)}) custom-call(f32[4,256,8]{2,1,0:T(8,128)S(1)} %bitcast.95, f32[4,8,256]{2,1,0:T(8,128)S(1)} %bitcast.107, bf16[256,256]{1,0:T(8,128)(2,1)S(1)} %copy-done.10, bf16[256,256]{1,0:T(8,128)(2,1)S(1)} %copy-done.21), custom_call_target="tpu_custom_call" | custom-call | flops 65536 | bytes 65536 | tf_op jit(solution)/shard_map/pallas_call | solution.py:112
  164.1 5.7 %shard_map.135 = (bf16[128,2048]{1,0:T(8,128)(2,1)S(1)}, f32[128,2048]{1,0:T(8,128)S(1)}) custom-call(s32[1]{0:T(128)} %bitcast.1.refs_0_, bf16[64,2048]{1,0:T(8,128)(2,1)S(1)} %copy-done.20, bf16[64,2048]{1,0:T(8,128)(2,1)S(1)} %copy-done.41, bf16[64,2048]{1,0:T(8,128)(2,1)S(1)} %copy-done.39, bf16[64,2048]{1,0:T(8,128)(2,1)S(1)} %copy-done.37, ...), custom_call_target="tpu_custom_call" | custom-call | flops 8388608 | bytes 38912 | tf_op jit(solution)/shard_map/pallas_call | solution.py:366
  169.8 5.7 %shard_map.134 = (bf16[128,2048]{1,0:T(8,128)(2,1)S(1)}, f32[128,2048]{1,0:T(8,128)S(1)}) custom-call(s32[1]{0:T(128)} %bitcast.1.refs_0_, bf16[64,2048]{1,0:T(8,128)(2,1)S(1)} %copy-done.20, bf16[64,2048]{1,0:T(8,128)(2,1)S(1)} %copy-done.41, bf16[64,2048]{1,0:T(8,128)(2,1)S(1)} %copy-done.39, bf16[64,2048]{1,0:T(8,128)(2,1)S(1)} %copy-done.37, ...), custom_call_target="tpu_custom_call" | custom-call | flops 8388608 | bytes 38912 | tf_op jit(solution)/shard_map/pallas_call | solution.py:366
  178.0 5.9 %shard_map.137 = (bf16[128,2048]{1,0:T(8,128)(2,1)S(1)}, f32[128,2048]{1,0:T(8,128)S(1)}) custom-call(s32[1]{0:T(128)} %bitcast.1.refs_0_, bf16[64,2048]{1,0:T(8,128)(2,1)S(1)} %copy-done.19, bf16[64,2048]{1,0:T(8,128)(2,1)} %collective-permute-done.21.refs_2_, bf16[64,2048]{1,0:T(8,128)(2,1)} %collective-permute-done.22.refs_3_, ...), custom_call_target="tpu_custom_call" | custom-call | flops 8388608 | bytes 38912 | tf_op jit(solution)/shard_map/pallas_call | solution.py:366
  184.5 5.9 %shard_map.136 = (bf16[128,2048]{1,0:T(8,128)(2,1)S(1)}, f32[128,2048]{1,0:T(8,128)S(1)}) custom-call(s32[1]{0:T(128)} %bitcast.1.refs_0_, bf16[64,2048]{1,0:T(8,128)(2,1)S(1)} %copy-done.19, bf16[64,2048]{1,0:T(8,128)(2,1)} %collective-permute-done.21.refs_2_, bf16[64,2048]{1,0:T(8,128)(2,1)} %collective-permute-done.22.refs_3_, ...), custom_call_target="tpu_custom_call" | custom-call | flops 8388608 | bytes 38912 | tf_op jit(solution)/shard_map/pallas_call | solution.py:366
  193.7 14.1 %collective-permute-done.26.refs_13_ = bf16[64,2048]{1,0:T(8,128)(2,1)S(1)} collective-permute-done((bf16[64,2048]{1,0:T(8,128)(2,1)S(1)}, bf16[64,2048]{1,0:T(8,128)(2,1)S(1)}, u32[]{:S(2)}, u32[]{:S(2)}) %collective-permute-start.26) | collective-permute-done | bytes 262176 | tf_op jit(solution)/shard_map/ppermute | solution.py:497
  213.5 2.8 collective-permute-done.30.refs_10_
  216.8 2.8 collective-permute-done.33.refs_15_
  219.6 4.0 %shard_map.143.v_ref.refs_2_ = bf16[256,4096]{1,0:T(8,128)(2,1)} custom-call(f32[64,2048]{1,0:T(8,128)S(1)} %copy-done.50, f32[64,2048]{1,0:T(8,128)S(1)} %get-tuple-element.127.refs_1_, f32[64,2048]{1,0:T(8,128)S(1)} %get-tuple-element.156.refs_2_, f32[64,2048]{1,0:T(8,128)S(1)} %get-tuple-element.158.refs_3_, f32[64,2048]{1,0:T(8,128)S(1)} %copy-done.52, ...), custom_call_target="tpu_custom_call" | custom-call | flops 8192 | bytes 32768 | tf_op jit(solution)/shard_map/pallas_call | solution.py:412
  229.1 4.1 %collective-permute-done.34.refs_3_ = f32[16,256,128]{2,1,0:T(8,128)S(1)} collective-permute-done((f32[16,256,128]{2,1,0:T(8,128)S(1)}, f32[16,256,128]{2,1,0:T(8,128)S(1)}, u32[]{:S(2)}, u32[]{:S(2)}) %collective-permute-start.34) | collective-permute-done | bytes 2097184 | tf_op jit(solution)/shard_map/ppermute | solution.py:501
  237.8 11.9 %shard_map.148 = (f32[256,4096]{1,0:T(8,128)}, f32[4,256,8]{2,1,0:T(8,128)S(1)}, f32[4,256,8]{2,1,0:T(8,128)S(1)}, f32[256,256]{1,0:T(8,128)S(1)}, f32[256,256]{1,0:T(8,128)S(1)}) custom-call(s32[3]{0:T(128)S(1)} %get-tuple-element.268.refs_0_, bf16[256,4096]{1,0:T(8,128)(2,1)S(1)} %copy-done.2, bf16[256,4096]{1,0:T(8,128)(2,1)} %shard_map.143.v_ref.refs_2_, ...), custom_call_target="tpu_custom_call" | custom-call | flops 7340032 | bytes 57344 | tf_op jit(solution)/shard_map/pallas_call | solution.py:204
  261.9 12.5 %shard_map.151 = (f32[256,4096]{1,0:T(8,128)}, f32[4,256,8]{2,1,0:T(8,128)S(1)}, f32[4,256,8]{2,1,0:T(8,128)S(1)}, f32[256,256]{1,0:T(8,128)S(1)}, f32[256,256]{1,0:T(8,128)S(1)}) custom-call(s32[3]{0:T(128)S(1)} %get-tuple-element.269.refs_0_, bf16[256,4096]{1,0:T(8,128)(2,1)S(1)} %copy-done.2, ...), custom_call_target="tpu_custom_call", output_to_operand_aliasing={{0}: (13, {}), {1}: (14, {}), {2}: (15, {})} | custom-call | flops 7340032 | bytes 57344 | tf_op jit(solution)/shard_map/pallas_call | solution.py:204
  275.2 5.2 %shard_map.152 = (f32[16,256,128]{2,1,0:T(8,128)S(1)}, f32[16,256,128]{2,1,0:T(8,128)}) custom-call(s32[1]{0:T(128)} %constant.34.clone.1.refs_0_, f32[12,16]{1,0:T(8,128)S(1)} %stack.124.refs_1_, f32[16,256,128]{2,1,0:T(8,128)} %copy-done.5, f32[16,256,128]{2,1,0:T(8,128)} %copy-done.7, bf16[8,256,128]{2,1,0:T(8,128)(2,1)S(1)} %copy-done.28, ...), custom_call_target="tpu_custom_call" | custom-call | flops 49152 | bytes 49152 | tf_op jit(solution)/shard_map/pallas_call | solution.py:479
  281.9 3.0 collective-permute-start.45
  287.4 7.7 %shard_map.153 = (bf16[256,4096]{1,0:T(8,128)(2,1)}, f32[256,256]{1,0:T(8,128)S(1)}, f32[4,256,8]{2,1,0:T(8,128)S(1)}, f32[4,256,8]{2,1,0:T(8,128)S(1)}) custom-call(s32[1]{0:T(128)} %bitcast.9.at_ref, bf16[256,4096]{1,0:T(8,128)(2,1)S(1)} %copy-done.2, f32[256,4096]{1,0:T(8,128)} %get-tuple-element.182.part_ref, bf16[256,256]{1,0:T(8,128)(2,1)S(1)} %copy-done.10, ...), custom_call_target="tpu_custom_call" | custom-call | flops 4194304 | bytes 32768 | tf_op jit(solution)/shard_map/pallas_call | solution.py:302
  296.5 7.7 %shard_map.154 = (bf16[256,4096]{1,0:T(8,128)(2,1)}, f32[256,256]{1,0:T(8,128)S(1)}, f32[4,256,8]{2,1,0:T(8,128)S(1)}, f32[4,256,8]{2,1,0:T(8,128)S(1)}) custom-call(s32[1]{0:T(128)} %bitcast.at_ref, bf16[256,4096]{1,0:T(8,128)(2,1)S(1)} %copy-done.2, ...), custom_call_target="tpu_custom_call", output_to_operand_aliasing={{0}: (11, {}), {2}: (12, {}), {3}: (13, {})} | custom-call | flops 4194304 | bytes 32768 | tf_op jit(solution)/shard_map/pallas_call | solution.py:302
  311.9 4.3 %collective-permute-done.42 = bf16[256,256]{1,0:T(8,128)(2,1)S(1)} collective-permute-done((bf16[256,256]{1,0:T(8,128)(2,1)S(1)}, bf16[256,256]{1,0:T(8,128)(2,1)S(1)}, u32[]{:S(2)}, u32[]{:S(2)}) %collective-permute-start.42) | collective-permute-done | bytes 131104 | tf_op jit(solution)/shard_map/ppermute | solution.py:513
  (296 shorter events, 116.9 us)
Async XLA Ops:
  7.2 51.4 %all-gather.4.cloned.1.call-start = ((), (), s32[]{:S(2)}) async-start(), calls=%async_computation | async-start | bytes 2621440 | tf_op jit(solution)/shard_map/all_gather | solution.py:525
  7.3 57.0 %collective-permute-start = (bf16[4096,1024]{1,0:T(8,128)(2,1)}, bf16[4096,1024]{1,0:T(8,128)(2,1)}, u32[]{:S(2)}, u32[]{:S(2)}) collective-permute-start(bf16[4096,1024]{1,0:T(8,128)(2,1)} %refs_5_.15), channel_id=1, source_target_pairs={{0,4},{4,0},{8,12},{12,8},{16,20},{20,16},{24,28},{28,24},{1,5},{5... | collective-permute-start | bytes 25165832 | tf_op jit(solution)/shard_map/ppermute | solution.py:501
  10.3 101.7 %all-gather.6.cloned.1.call-start = ((), (), s32[]{:S(2)}) async-start(), calls=%async_computation.1 | async-start | bytes 2621440 | tf_op jit(solution)/shard_map/all_gather | solution.py:525
  13.9 14.0 %collective-permute-start.1 = (f32[16,256,128]{2,1,0:T(8,128)}, f32[16,256,128]{2,1,0:T(8,128)}, u32[]{:S(2)}, u32[]{:S(2)}) collective-permute-start(f32[16,256,128]{2,1,0:T(8,128)} %shard_map.120), channel_id=1, source_target_pairs={{0,4},{4,0},{8,12},{12,8},{16,20},{20,16},{24,28},{28,24},{1,5},{5... | collective-permute-start | bytes 6291464 | tf_op jit(solution)/shard_map/ppermute | solution.py:501
  29.2 14.6 %collective-permute-start.2 = (bf16[8,256,128]{2,1,0:T(8,128)(2,1)S(1)}, bf16[8,256,128]{2,1,0:T(8,128)(2,1)S(1)}, u32[]{:S(2)}, u32[]{:S(2)}) collective-permute-start(bf16[8,256,128]{2,1,0:T(8,128)(2,1)S(1)} %shard_map.121.refs_2_), channel_id=1, source_target_pairs={{0,8},{4,12},{8,0},{12,4},{16,24},{20,28},{24,16},{28,20},{1,9},{5... | collective-permute-start | bytes 1572872 | tf_op jit(solution)/shard_map/ppermute | solution.py:497
  32.7 13.9 %collective-permute-start.3 = (bf16[8,256,128]{2,1,0:T(8,128)(2,1)S(1)}, bf16[8,256,128]{2,1,0:T(8,128)(2,1)S(1)}, u32[]{:S(2)}, u32[]{:S(2)}) collective-permute-start(bf16[8,256,128]{2,1,0:T(8,128)(2,1)S(1)} %shard_map.122.refs_2_), channel_id=1, source_target_pairs={{0,16},{4,20},{8,24},{12,28},{16,0},{20,4},{24,8},{28,12},{1,17},{... | collective-permute-start | bytes 1572872 | tf_op jit(solution)/shard_map/ppermute | solution.py:497
  78.3 18.0 %collective-permute-start.12 = (bf16[64,2048]{1,0:T(8,128)(2,1)S(1)}, bf16[64,2048]{1,0:T(8,128)(2,1)S(1)}, u32[]{:S(2)}, u32[]{:S(2)}) collective-permute-start(bf16[64,2048]{1,0:T(8,128)(2,1)S(1)} %get-tuple-element.218), channel_id=1, source_target_pairs={{0,24},{4,28},{8,16},{12,20},{16,8},{20,12},{24,0},{28,4},{1,25},{... | collective-permute-start | bytes 786440 | tf_op jit(solution)/shard_map/ppermute | solution.py:497
  79.6 16.7 %collective-permute-start.11 = (bf16[64,2048]{1,0:T(8,128)(2,1)S(1)}, bf16[64,2048]{1,0:T(8,128)(2,1)S(1)}, u32[]{:S(2)}, u32[]{:S(2)}) collective-permute-start(bf16[64,2048]{1,0:T(8,128)(2,1)S(1)} %get-tuple-element.219), channel_id=1, source_target_pairs={{0,16},{4,20},{8,24},{12,28},{16,0},{20,4},{24,8},{28,12},{1,17},{... | collective-permute-start | bytes 786440 | tf_op jit(solution)/shard_map/ppermute | solution.py:497
  80.6 15.7 %collective-permute-start.10 = (bf16[64,2048]{1,0:T(8,128)(2,1)S(1)}, bf16[64,2048]{1,0:T(8,128)(2,1)S(1)}, u32[]{:S(2)}, u32[]{:S(2)}) collective-permute-start(bf16[64,2048]{1,0:T(8,128)(2,1)S(1)} %get-tuple-element.220), channel_id=1, source_target_pairs={{0,8},{4,12},{8,0},{12,4},{16,24},{20,28},{24,16},{28,20},{1,9},{5... | collective-permute-start | bytes 786440 | tf_op jit(solution)/shard_map/ppermute | solution.py:497
  88.2 28.9 %collective-permute-start.9 = (bf16[128,2048]{1,0:T(8,128)(2,1)}, bf16[128,2048]{1,0:T(8,128)(2,1)}, u32[]{:S(2)}, u32[]{:S(2)}) collective-permute-start(bf16[128,2048]{1,0:T(8,128)(2,1)} %get-tuple-element.114), channel_id=1, source_target_pairs={{0,8},{4,12},{8,0},{12,4},{16,24},{20,28},{24,16},{28,20},{1,9},{5... | collective-permute-start | bytes 1572872 | tf_op jit(solution)/shard_map/ppermute | solution.py:497
  95.3 24.8 %collective-permute-start.18 = (bf16[128,2048]{1,0:T(8,128)(2,1)}, bf16[128,2048]{1,0:T(8,128)(2,1)}, u32[]{:S(2)}, u32[]{:S(2)}) collective-permute-start(bf16[128,2048]{1,0:T(8,128)(2,1)} %get-tuple-element.115), channel_id=1, source_target_pairs={{0,16},{4,20},{8,24},{12,28},{16,0},{20,4},{24,8},{28,12},{1,17},{... | collective-permute-start | bytes 1572872 | tf_op jit(solution)/shard_map/ppermute | solution.py:497
  103.6 37.6 %collective-permute-start.13 = (bf16[128,2048]{1,0:T(8,128)(2,1)}, bf16[128,2048]{1,0:T(8,128)(2,1)}, u32[]{:S(2)}, u32[]{:S(2)}) collective-permute-start(bf16[128,2048]{1,0:T(8,128)(2,1)} %get-tuple-element.120), channel_id=1, source_target_pairs={{0,8},{4,12},{8,0},{12,4},{16,24},{20,28},{24,16},{28,20},{1,9},{5... | collective-permute-start | bytes 1572872 | tf_op jit(solution)/shard_map/ppermute | solution.py:497
  117.1 14.2 %collective-permute-start.14 = (bf16[64,2048]{1,0:T(8,128)(2,1)S(1)}, bf16[64,2048]{1,0:T(8,128)(2,1)S(1)}, u32[]{:S(2)}, u32[]{:S(2)}) collective-permute-start(bf16[64,2048]{1,0:T(8,128)(2,1)S(1)} %get-tuple-element.216), channel_id=1, source_target_pairs={{0,8},{4,12},{8,0},{12,4},{16,24},{20,28},{24,16},{28,20},{1,9},{5... | collective-permute-start | bytes 786440 | tf_op jit(solution)/shard_map/ppermute | solution.py:497
  120.1 19.2 %collective-permute-start.17 = (bf16[64,2048]{1,0:T(8,128)(2,1)S(1)}, bf16[64,2048]{1,0:T(8,128)(2,1)S(1)}, u32[]{:S(2)}, u32[]{:S(2)}) collective-permute-start(bf16[64,2048]{1,0:T(8,128)(2,1)S(1)} %get-tuple-element.128), channel_id=1, source_target_pairs={{0,16},{4,20},{8,24},{12,28},{16,0},{20,4},{24,8},{28,12},{1,17},{... | collective-permute-start | bytes 786440 | tf_op jit(solution)/shard_map/ppermute | solution.py:497
  125.5 64.9 %collective-permute-start.25 = (bf16[128,2048]{1,0:T(8,128)(2,1)}, bf16[128,2048]{1,0:T(8,128)(2,1)}, u32[]{:S(2)}, u32[]{:S(2)}) collective-permute-start(bf16[128,2048]{1,0:T(8,128)(2,1)} %get-tuple-element.121), channel_id=1, source_target_pairs={{0,16},{4,20},{8,24},{12,28},{16,0},{20,4},{24,8},{28,12},{1,17},{... | collective-permute-start | bytes 1572872 | tf_op jit(solution)/shard_map/ppermute | solution.py:497
  130.1 45.5 %collective-permute-start.23 = (bf16[64,2048]{1,0:T(8,128)(2,1)}, bf16[64,2048]{1,0:T(8,128)(2,1)}, u32[]{:S(2)}, u32[]{:S(2)}) collective-permute-start(bf16[64,2048]{1,0:T(8,128)(2,1)} %get-tuple-element.210), channel_id=1, source_target_pairs={{0,24},{4,28},{8,16},{12,20},{16,8},{20,12},{24,0},{28,4},{1,25},{... | collective-permute-start | bytes 786440 | tf_op jit(solution)/shard_map/ppermute | solution.py:497
  132.0 44.4 %collective-permute-start.22 = (bf16[64,2048]{1,0:T(8,128)(2,1)}, bf16[64,2048]{1,0:T(8,128)(2,1)}, u32[]{:S(2)}, u32[]{:S(2)}) collective-permute-start(bf16[64,2048]{1,0:T(8,128)(2,1)} %get-tuple-element.211), channel_id=1, source_target_pairs={{0,16},{4,20},{8,24},{12,28},{16,0},{20,4},{24,8},{28,12},{1,17},{... | collective-permute-start | bytes 786440 | tf_op jit(solution)/shard_map/ppermute | solution.py:497
  140.0 38.0 %collective-permute-start.21 = (bf16[64,2048]{1,0:T(8,128)(2,1)}, bf16[64,2048]{1,0:T(8,128)(2,1)}, u32[]{:S(2)}, u32[]{:S(2)}) collective-permute-start(bf16[64,2048]{1,0:T(8,128)(2,1)} %get-tuple-element.212), channel_id=1, source_target_pairs={{0,8},{4,12},{8,0},{12,4},{16,24},{20,28},{24,16},{28,20},{1,9},{5... | collective-permute-start | bytes 786440 | tf_op jit(solution)/shard_map/ppermute | solution.py:497
  141.3 21.6 %collective-permute-start.19 = (bf16[64,2048]{1,0:T(8,128)(2,1)}, bf16[64,2048]{1,0:T(8,128)(2,1)}, u32[]{:S(2)}, u32[]{:S(2)}) collective-permute-start(bf16[64,2048]{1,0:T(8,128)(2,1)} %get-tuple-element.131), channel_id=1, source_target_pairs={{0,8},{4,12},{8,0},{12,4},{16,24},{20,28},{24,16},{28,20},{1,9},{5... | collective-permute-start | bytes 786440 | tf_op jit(solution)/shard_map/ppermute | solution.py:497
  162.9 29.9 %collective-permute-start.24 = (bf16[64,2048]{1,0:T(8,128)(2,1)S(1)}, bf16[64,2048]{1,0:T(8,128)(2,1)S(1)}, u32[]{:S(2)}, u32[]{:S(2)}) collective-permute-start(bf16[64,2048]{1,0:T(8,128)(2,1)S(1)} %get-tuple-element.151), channel_id=1, source_target_pairs={{0,16},{4,20},{8,24},{12,28},{16,0},{20,4},{24,8},{28,12},{1,17},{... | collective-permute-start | bytes 786440 | tf_op jit(solution)/shard_map/ppermute | solution.py:497
  175.5 32.2 %collective-permute-start.20 = (bf16[128,2048]{1,0:T(8,128)(2,1)S(1)}, bf16[128,2048]{1,0:T(8,128)(2,1)S(1)}, u32[]{:S(2)}, u32[]{:S(2)}) collective-permute-start(bf16[128,2048]{1,0:T(8,128)(2,1)S(1)} %get-tuple-element.143), channel_id=1, source_target_pairs={{0,8},{4,12},{8,0},{12,4},{16,24},{20,28},{24,16},{28,20},{1,9},{5... | collective-permute-start | bytes 1572872 | tf_op jit(solution)/shard_map/ppermute | solution.py:497
  176.4 31.8 %collective-permute-start.28 = (bf16[128,2048]{1,0:T(8,128)(2,1)S(1)}, bf16[128,2048]{1,0:T(8,128)(2,1)S(1)}, u32[]{:S(2)}, u32[]{:S(2)}) collective-permute-start(bf16[128,2048]{1,0:T(8,128)(2,1)S(1)} %get-tuple-element.144), channel_id=1, source_target_pairs={{0,16},{4,20},{8,24},{12,28},{16,0},{20,4},{24,8},{28,12},{1,17},{... | collective-permute-start | bytes 1572872 | tf_op jit(solution)/shard_map/ppermute | solution.py:497
  183.9 26.7 %collective-permute-start.29 = (bf16[128,2048]{1,0:T(8,128)(2,1)S(1)}, bf16[128,2048]{1,0:T(8,128)(2,1)S(1)}, u32[]{:S(2)}, u32[]{:S(2)}) collective-permute-start(bf16[128,2048]{1,0:T(8,128)(2,1)S(1)} %get-tuple-element.150), channel_id=1, source_target_pairs={{0,16},{4,20},{8,24},{12,28},{16,0},{20,4},{24,8},{28,12},{1,17},{... | collective-permute-start | bytes 1572872 | tf_op jit(solution)/shard_map/ppermute | solution.py:497
  190.4 21.7 %collective-permute-start.27 = (bf16[128,2048]{1,0:T(8,128)(2,1)S(1)}, bf16[128,2048]{1,0:T(8,128)(2,1)S(1)}, u32[]{:S(2)}, u32[]{:S(2)}) collective-permute-start(bf16[128,2048]{1,0:T(8,128)(2,1)S(1)} %get-tuple-element.149), channel_id=1, source_target_pairs={{0,8},{4,12},{8,0},{12,4},{16,24},{20,28},{24,16},{28,20},{1,9},{5... | collective-permute-start | bytes 1572872 | tf_op jit(solution)/shard_map/ppermute | solution.py:497
  192.8 14.9 %collective-permute-start.26 = (bf16[64,2048]{1,0:T(8,128)(2,1)S(1)}, bf16[64,2048]{1,0:T(8,128)(2,1)S(1)}, u32[]{:S(2)}, u32[]{:S(2)}) collective-permute-start(bf16[64,2048]{1,0:T(8,128)(2,1)S(1)} %get-tuple-element.154), channel_id=1, source_target_pairs={{0,8},{4,12},{8,0},{12,4},{16,24},{20,28},{24,16},{28,20},{1,9},{5... | collective-permute-start | bytes 786440 | tf_op jit(solution)/shard_map/ppermute | solution.py:497
  235.2 16.1 %collective-permute-start.35 = (bf16[8,256,128]{2,1,0:T(8,128)(2,1)S(1)}, bf16[8,256,128]{2,1,0:T(8,128)(2,1)S(1)}, u32[]{:S(2)}, u32[]{:S(2)}) collective-permute-start(bf16[8,256,128]{2,1,0:T(8,128)(2,1)S(1)} %shard_map.146.refs_2_), channel_id=1, source_target_pairs={{0,8},{4,12},{8,0},{12,4},{16,24},{20,28},{24,16},{28,20},{1,9},{5... | collective-permute-start | bytes 1572872 | tf_op jit(solution)/shard_map/ppermute | solution.py:497
  236.5 14.8 %collective-permute-start.36 = (bf16[8,256,128]{2,1,0:T(8,128)(2,1)S(1)}, bf16[8,256,128]{2,1,0:T(8,128)(2,1)S(1)}, u32[]{:S(2)}, u32[]{:S(2)}) collective-permute-start(bf16[8,256,128]{2,1,0:T(8,128)(2,1)S(1)} %shard_map.147.refs_2_), channel_id=1, source_target_pairs={{0,16},{4,20},{8,24},{12,28},{16,0},{20,4},{24,8},{28,12},{1,17},{... | collective-permute-start | bytes 1572872 | tf_op jit(solution)/shard_map/ppermute | solution.py:497
  253.6 21.5 %collective-permute-start.38 = (bf16[8,256,128]{2,1,0:T(8,128)(2,1)}, bf16[8,256,128]{2,1,0:T(8,128)(2,1)}, u32[]{:S(2)}, u32[]{:S(2)}) collective-permute-start(bf16[8,256,128]{2,1,0:T(8,128)(2,1)} %shard_map.149), channel_id=1, source_target_pairs={{0,16},{4,20},{8,24},{12,28},{16,0},{20,4},{24,8},{28,12},{1,17},{... | collective-permute-start | bytes 1572872 | tf_op jit(solution)/shard_map/ppermute | solution.py:497
  256.1 19.1 %collective-permute-start.39 = (bf16[8,256,128]{2,1,0:T(8,128)(2,1)}, bf16[8,256,128]{2,1,0:T(8,128)(2,1)}, u32[]{:S(2)}, u32[]{:S(2)}) collective-permute-start(bf16[8,256,128]{2,1,0:T(8,128)(2,1)} %shard_map.150), channel_id=1, source_target_pairs={{0,8},{4,12},{8,0},{12,4},{16,24},{20,28},{24,16},{28,20},{1,9},{5... | collective-permute-start | bytes 1572872 | tf_op jit(solution)/shard_map/ppermute | solution.py:497
  281.9 27.7 %collective-permute-start.45 = (bf16[256,256]{1,0:T(8,128)(2,1)S(1)}, bf16[256,256]{1,0:T(8,128)(2,1)S(1)}, u32[]{:S(2)}, u32[]{:S(2)}) collective-permute-start(bf16[256,256]{1,0:T(8,128)(2,1)S(1)} %convert_element_type.35), channel_id=1, source_target_pairs={{0,2},{1,3},{2,0},{3,1},{4,6},{5,7},{6,4},{7,5},{8,10},{9,11},{10,... | collective-permute-start | bytes 393224 | tf_op jit(solution)/shard_map/ppermute | solution.py:513
  284.8 24.7 %collective-permute-start.44 = (bf16[256,256]{1,0:T(8,128)(2,1)S(1)}, bf16[256,256]{1,0:T(8,128)(2,1)S(1)}, u32[]{:S(2)}, u32[]{:S(2)}) collective-permute-start(bf16[256,256]{1,0:T(8,128)(2,1)S(1)} %convert_element_type.35), channel_id=1, source_target_pairs={{0,1},{1,0},{2,3},{3,2},{4,5},{5,4},{6,7},{7,6},{8,9},{9,8},{10,11... | collective-permute-start | bytes 393224 | tf_op jit(solution)/shard_map/ppermute | solution.py:513
  286.3 23.2 %collective-permute-start.46 = (bf16[256,256]{1,0:T(8,128)(2,1)S(1)}, bf16[256,256]{1,0:T(8,128)(2,1)S(1)}, u32[]{:S(2)}, u32[]{:S(2)}) collective-permute-start(bf16[256,256]{1,0:T(8,128)(2,1)S(1)} %convert_element_type.35), channel_id=1, source_target_pairs={{0,3},{1,2},{2,1},{3,0},{4,7},{5,6},{6,5},{7,4},{8,11},{9,10},{10,... | collective-permute-start | bytes 393224 | tf_op jit(solution)/shard_map/ppermute | solution.py:513
  (84 other events, 631.0 us)
Sparse Core Ops, SparseCore 0:
  10.4 48.1 all-gather.3
  60.2 44.6 all-gather.5

commit v8 on v7

--- a/solution.py
+++ b/solution.py
@@ -12,7 +12,7 @@
 NN = (((1,), (0,)), ((), ()))
 NT = (((1,), (1,)), ((), ()))
 TN = (((0,), (0,)), ((), ()))
-PARAMS = pltpu.CompilerParams(vmem_limit_bytes=48 << 20)
+PARAMS = pltpu.CompilerParams(vmem_limit_bytes=28 << 20)
 
 
 def mm(a, b, dims):
@@ -128,7 +128,7 @@
             jax.ShapeDtypeStruct((groups * group, span, 2 * span), BF16),
             jax.ShapeDtypeStruct((span, span), F32),
         ],
-        compiler_params=PARAMS,
+        compiler_params=pltpu.CompilerParams(vmem_limit_bytes=60 << 20),
         cost_estimate=cost(
             8 * groups * group * span * span,
             8 * groups * group * span * span,
@@ -571,13 +571,13 @@
             waiting[lane].append((keep, send, across(send, order[0], chips)))
         ahead = [lane[chunk][1] for lane in waiting]
         if chunk == 1:
-            sent, first = reduce(0, ahead)
+            first = reduce(0, ahead)[1]
             full = tie(fulls[1], *ahead)
             own += [blocks_of(full, i * rows, rows, chips, chip) for i in range(2)]
             last = reduce(1, own[2])[1]
-            ahead = [*first, *before([*sent, *own[2]]), *own[3]]
-    reduce(2, [*ahead, *last])
-    reduce(3, None)
+            ahead = [*first, *own[3]]
+    sent, _ = reduce(2, [*ahead, *last])
+    reduce(3, before([*ahead, *sent]))
     ends = waiting[0] + waiting[1]
     return finish([keep for keep, _ in ends], [arrived for _, arrived in ends])
 

time: 328 us -> 335 us (1.021)
  local copies, waits for them, and re-layouts: 37.1 us -> 70.2 us
  waiting for transfers between devices: 74.1 us -> 59.1 us
  Pallas kernels: 133 us -> 121 us
    unnamed x134 -> x204, local copies, waits for them, and re-layouts: 24.9 us -> 59.3 us
    ppermute x36, waiting for transfers between devices: 56.8 us -> 49.7 us  [across(): return lax.ppermute(value, 'seq', pairs)]
    all_gather x2, waiting for transfers between devices: 7.01 us -> 0.01 us  [gather_halves(): lax.all_gather(p, 'head', axis=1, tiled=True)]
    pallas_call x8, Pallas kernels: 48.5 us -> 44.1 us  [partial_sums(): pl.pallas_call(lambda *refs: project_kernel(hops, *refs), grid_spec=pltpu...]
    pallas_call x2, Pallas kernels: 24.4 us -> 20.5 us  [inner_part(): pl.pallas_call(lambda *refs: inner_kernel(not held, last, *refs), grid_sp...]
  transfers between devices with their start and end apart: 49 -> 49, of which waited for: 16 -> 17; matrix products, arithmetic and copies ran while one was open for 5% -> 5% of each run, Pallas kernels for 37% -> 34%
where the time goes in v8:
time: 335 us; the launch traced here: 333 us
  Pallas kernels  121 us (36%)
  local copies, waits for them, and re-layouts  70.2 us (21%)
  waiting for transfers between devices  59.1 us (18%)
  starting transfers between devices  50.6 us (15%)
  between operations  15.1 us (5%)
  blocking collectives  10.6 us (3%)
  other arithmetic  5.42 us (2%)
    unnamed x204, local copies, waits for them, and re-layouts  59.3 us
    ppermute x36, waiting for transfers between devices, across(): return lax.ppermute(value, 'seq', pairs)  49.7 us
    pallas_call x8, Pallas kernels, partial_sums(): pl.pallas_call(lambda *refs: project_kernel(hops, *refs), grid_spec=pltpu...  44.1 us
    ppermute x36, starting transfers between devices, across(): return lax.ppermute(value, 'seq', pairs)  40.4 us
    pallas_call x2, Pallas kernels, inner_part(): pl.pallas_call(lambda *refs: inner_kernel(not held, last, *refs), grid_sp...  20.5 us
    pallas_call x10, Pallas kernels, blend(): pl.pallas_call(lambda *refs: blend_kernel(count, step, *refs), grid_spec=...  17.9 us
    pallas_call x2, Pallas kernels, outer_part(): pl.pallas_call(outer_kernel, grid_spec=pltpu.PrefetchScalarGridSpec(num_s...  12.2 us
    all_gather x1, blocking collectives, local(): ends = lax.all_gather(running[-1], 'seq')  10.6 us
  transfers between devices with their start and end apart: 49, of which 17 were waited for; matrix products, arithmetic and copies ran while one was open for 5% of the time, Pallas kernels for 34%

profile of v8, /device:TPU:0, one launch (start us, length us, event | category | flops | bytes accessed | tf_op | source)
XLA Modules:
  0.0 332.8 jit_solution(8970032333728572789)
XLA Ops:
  11.2 2.5 shard_map.120
  13.9 10.6 %all-gather = f32[8,1,32]{2,1,0:T(1,128)S(1)} all-gather(f32[1,1,32]{2,1,0:T(1,128)S(1)} %bitcast.117), channel_id=1, replica_groups=mesh['seq'=8,'head'=4] {'seq'}, dimensions={0}, use_global_device_ids=true | all-gather | bytes 1152 | tf_op jit(solution)/shard_map/all_gather | solution.py:680
  34.3 9.4 %collective-permute-done.3.refs_3_.refs_6_ = bf16[8,256,128]{2,1,0:T(8,128)(2,1)S(1)} collective-permute-done((bf16[8,256,128]{2,1,0:T(8,128)(2,1)S(1)}, bf16[8,256,128]{2,1,0:T(8,128)(2,1)S(1)}, u32[]{:S(2)}, u32[]{:S(2)}) %collective-permute-start.3) | collective-permute-done | bytes 524320 | tf_op jit(solution)/shard_map/ppermute | solution.py:497
  43.8 2.8 collective-permute-done.2.refs_3_.refs_4_
  52.4 9.8 %collective-permute-done.5.refs_7_ = bf16[8,256,128]{2,1,0:T(8,128)(2,1)S(1)} collective-permute-done((bf16[8,256,128]{2,1,0:T(8,128)(2,1)}, bf16[8,256,128]{2,1,0:T(8,128)(2,1)S(1)}, u32[]{:S(2)}, u32[]{:S(2)}) %collective-permute-start.5) | collective-permute-done | bytes 524320 | tf_op jit(solution)/shard_map/ppermute | solution.py:497
  62.2 2.7 collective-permute-done.4.refs_5_
  70.0 5.5 %collective-permute-done.6.refs_2_ = bf16[64,2048]{1,0:T(8,128)(2,1)S(1)} collective-permute-done((bf16[64,2048]{1,0:T(8,128)(2,1)S(1)}, bf16[64,2048]{1,0:T(8,128)(2,1)S(1)}, u32[]{:S(2)}, u32[]{:S(2)}) %collective-permute-start.6) | collective-permute-done | bytes 262176 | tf_op jit(solution)/shard_map/ppermute | solution.py:497
  75.6 3.1 collective-permute-done.7.refs_3_
  82.3 3.4 %copy-done.2 = bf16[4096,1024]{1,0:T(8,128)(2,1)S(1)} copy-done((bf16[4096,1024]{1,0:T(8,128)(2,1)S(1)}, bf16[4096,1024]{1,0:T(8,128)(2,1)}, u32[]{:S(2)}) %copy-start.2) | copy-done | bytes 8388632
  85.8 5.6 %shard_map.126 = (bf16[128,2048]{1,0:T(8,128)(2,1)}, f32[128,2048]{1,0:T(8,128)S(1)}) custom-call(s32[1]{0:T(128)} %bitcast.1.refs_0_, bf16[64,2048]{1,0:T(8,128)(2,1)S(1)} %get-tuple-element.111.refs_1_, bf16[64,2048]{1,0:T(8,128)(2,1)S(1)} %collective-permute-done.6.refs_2_, bf16[64,2048]{1,0:T(8,128)(2,1)S(1)} %collective-permute-done.7.refs_3_, ...), custom_call_target="tpu_custom_call" | custom-call | flops 8388608 | bytes 38912 | tf_op jit(solution)/shard_map/pallas_call | solution.py:366
  93.6 5.6 %shard_map.125 = (bf16[128,2048]{1,0:T(8,128)(2,1)}, f32[128,2048]{1,0:T(8,128)S(1)}) custom-call(s32[1]{0:T(128)} %bitcast.1.refs_0_, bf16[64,2048]{1,0:T(8,128)(2,1)S(1)} %get-tuple-element.111.refs_1_, bf16[64,2048]{1,0:T(8,128)(2,1)S(1)} %collective-permute-done.6.refs_2_, bf16[64,2048]{1,0:T(8,128)(2,1)S(1)} %collective-permute-done.7.refs_3_, ...), custom_call_target="tpu_custom_call" | custom-call | flops 8388608 | bytes 38912 | tf_op jit(solution)/shard_map/pallas_call | solution.py:366
  101.0 5.6 %shard_map.128 = (bf16[128,2048]{1,0:T(8,128)(2,1)}, f32[128,2048]{1,0:T(8,128)S(1)}) custom-call(s32[1]{0:T(128)} %bitcast.1.refs_0_, bf16[64,2048]{1,0:T(8,128)(2,1)S(1)} %get-tuple-element.118.refs_1_, bf16[64,2048]{1,0:T(8,128)(2,1)S(1)} %collective-permute-done.10.refs_2_, bf16[64,2048]{1,0:T(8,128)(2,1)S(1)} %collective-permute-done.11.refs_3_, ...), custom_call_target="tpu_custom_call" | custom-call | flops 8388608 | bytes 38912 | tf_op jit(solution)/shard_map/pallas_call | solution.py:366
  109.1 5.0 %shard_map.127 = (bf16[128,2048]{1,0:T(8,128)(2,1)S(1)}, f32[128,2048]{1,0:T(8,128)S(1)}) custom-call(s32[1]{0:T(128)} %bitcast.1.refs_0_, bf16[64,2048]{1,0:T(8,128)(2,1)S(1)} %get-tuple-element.118.refs_1_, bf16[64,2048]{1,0:T(8,128)(2,1)S(1)} %collective-permute-done.10.refs_2_, bf16[64,2048]{1,0:T(8,128)(2,1)S(1)} %collective-permute-done.11.refs_3_, ...), custom_call_target="tpu_custom_call" | custom-call | flops 8388608 | bytes 38912 | tf_op jit(solution)/shard_map/pallas_call | solution.py:366
  122.3 3.8 %collective-permute-done.14.refs_2_ = bf16[64,2048]{1,0:T(8,128)(2,1)S(1)} collective-permute-done((bf16[64,2048]{1,0:T(8,128)(2,1)S(1)}, bf16[64,2048]{1,0:T(8,128)(2,1)S(1)}, u32[]{:S(2)}, u32[]{:S(2)}) %collective-permute-start.14) | collective-permute-done | bytes 262176 | tf_op jit(solution)/shard_map/ppermute | solution.py:497
  133.7 3.6 %collective-permute-done.19.refs_12_ = bf16[64,2048]{1,0:T(8,128)(2,1)S(1)} collective-permute-done((bf16[64,2048]{1,0:T(8,128)(2,1)S(1)}, bf16[64,2048]{1,0:T(8,128)(2,1)S(1)}, u32[]{:S(2)}, u32[]{:S(2)}) %collective-permute-start.19) | collective-permute-done | bytes 262176 | tf_op jit(solution)/shard_map/ppermute | solution.py:497
  142.7 3.4 %copy-done.3 = bf16[4096,1024]{1,0:T(8,128)(2,1)S(1)} copy-done((bf16[4096,1024]{1,0:T(8,128)(2,1)S(1)}, bf16[4096,1024]{1,0:T(8,128)(2,1)}, u32[]{:S(2)}) %copy-start.3) | copy-done | bytes 8388632
  146.1 5.6 %shard_map.133 = (bf16[128,2048]{1,0:T(8,128)(2,1)}, f32[128,2048]{1,0:T(8,128)S(1)}) custom-call(s32[1]{0:T(128)} %bitcast.1.refs_0_, bf16[64,2048]{1,0:T(8,128)(2,1)S(1)} %get-tuple-element.134.refs_1_, bf16[64,2048]{1,0:T(8,128)(2,1)S(1)} %collective-permute-done.14.refs_2_, bf16[64,2048]{1,0:T(8,128)(2,1)S(1)} %collective-permute-done.15.refs_3_, ...), custom_call_target="tpu_custom_call" | custom-call | flops 8388608 | bytes 38912 | tf_op jit(solution)/shard_map/pallas_call | solution.py:366
  152.7 5.6 %shard_map.132 = (bf16[128,2048]{1,0:T(8,128)(2,1)}, f32[128,2048]{1,0:T(8,128)S(1)}) custom-call(s32[1]{0:T(128)} %bitcast.1.refs_0_, bf16[64,2048]{1,0:T(8,128)(2,1)S(1)} %get-tuple-element.134.refs_1_, bf16[64,2048]{1,0:T(8,128)(2,1)S(1)} %collective-permute-done.14.refs_2_, bf16[64,2048]{1,0:T(8,128)(2,1)S(1)} %collective-permute-done.15.refs_3_, ...), custom_call_target="tpu_custom_call" | custom-call | flops 8388608 | bytes 38912 | tf_op jit(solution)/shard_map/pallas_call | solution.py:366
  161.2 5.6 %shard_map.135 = (bf16[128,2048]{1,0:T(8,128)(2,1)}, f32[128,2048]{1,0:T(8,128)S(1)}) custom-call(s32[1]{0:T(128)} %bitcast.1.refs_0_, bf16[64,2048]{1,0:T(8,128)(2,1)S(1)} %get-tuple-element.141.refs_1_, bf16[64,2048]{1,0:T(8,128)(2,1)S(1)} %collective-permute-done.21.refs_2_, bf16[64,2048]{1,0:T(8,128)(2,1)S(1)} %collective-permute-done.22.refs_3_, ...), custom_call_target="tpu_custom_call" | custom-call | flops 8388608 | bytes 38912 | tf_op jit(solution)/shard_map/pallas_call | solution.py:366
  169.0 5.6 %shard_map.134 = (bf16[128,2048]{1,0:T(8,128)(2,1)}, f32[128,2048]{1,0:T(8,128)S(1)}) custom-call(s32[1]{0:T(128)} %bitcast.1.refs_0_, bf16[64,2048]{1,0:T(8,128)(2,1)S(1)} %get-tuple-element.141.refs_1_, bf16[64,2048]{1,0:T(8,128)(2,1)S(1)} %collective-permute-done.21.refs_2_, bf16[64,2048]{1,0:T(8,128)(2,1)S(1)} %collective-permute-done.22.refs_3_, ...), custom_call_target="tpu_custom_call" | custom-call | flops 8388608 | bytes 38912 | tf_op jit(solution)/shard_map/pallas_call | solution.py:366
  195.4 3.8 %shard_map.139 = (f32[16,256,128]{2,1,0:T(8,128)S(1)}, f32[16,256,128]{2,1,0:T(8,128)S(1)}) custom-call(s32[1]{0:T(128)} %constant.34.clone.1.refs_0_, f32[12,16]{1,0:T(8,128)S(1)} %stack.112.refs_1_, f32[16,256,128]{2,1,0:T(8,128)S(1)} %copy-done.12, f32[16,256,128]{2,1,0:T(8,128)} %collective-permute-done.1.refs_3_, bf16[8,256,128]{2,1,0:T(8,128)(2,1)S(1)} %copy-done.37, ...), custom_call_target="tpu_custom_call" | custom-call | flops 49152 | bytes 49152 | tf_op jit(solution)/shard_map/pallas_call | solution.py:479
  202.0 8.1 %shard_map.140 = (f32[32,256,256]{2,1,0:T(8,128)}, bf16[32,256,512]{2,1,0:T(8,128)(2,1)}, f32[256,256]{1,0:T(8,128)}) custom-call(f32[4,256,8]{2,1,0:T(8,128)} %bitcast.97, f32[4,8,256]{2,1,0:T(8,128)} %bitcast.109, bf16[256,256]{1,0:T(8,128)(2,1)} %b_ref.2, bf16[256,256]{1,0:T(8,128)(2,1)} %refs_4_.1), custom_call_target="tpu_custom_call" | custom-call | flops 65536 | bytes 65536 | tf_op jit(solution)/shard_map/pallas_call | solution.py:112
  219.2 2.4 collective-permute-done.31.refs_11_
  241.0 9.9 %shard_map.148 = (f32[256,4096]{1,0:T(8,128)S(1)}, f32[4,256,8]{2,1,0:T(8,128)S(1)}, f32[4,256,8]{2,1,0:T(8,128)S(1)}, f32[256,256]{1,0:T(8,128)S(1)}, f32[256,256]{1,0:T(8,128)S(1)}) custom-call(s32[3]{0:T(128)S(1)} %get-tuple-element.272.refs_0_, bf16[256,4096]{1,0:T(8,128)(2,1)S(1)} %copy-done.4, bf16[256,4096]{1,0:T(8,128)(2,1)S(1)} %shard_map.143.v_ref.refs_2_, ...), custom_call_target="tpu_custom_call" | custom-call | flops 7340032 | bytes 57344 | tf_op jit(solution)/shard_map/pallas_call | solution.py:204
  264.0 3.4 %copy-done.15 = f32[32,256,256]{2,1,0:T(8,128)S(1)} copy-done((f32[32,256,256]{2,1,0:T(8,128)S(1)}, f32[32,256,256]{2,1,0:T(8,128)}, u32[]{:S(2)}) %copy-start.15) | copy-done | bytes 8388632
  275.5 10.6 %shard_map.151 = (f32[256,4096]{1,0:T(8,128)S(1)}, f32[4,256,8]{2,1,0:T(8,128)S(1)}, f32[4,256,8]{2,1,0:T(8,128)S(1)}, f32[256,256]{1,0:T(8,128)S(1)}, f32[256,256]{1,0:T(8,128)S(1)}) custom-call(s32[3]{0:T(128)S(1)} %get-tuple-element.273.refs_0_, bf16[256,4096]{1,0:T(8,128)(2,1)S(1)} %copy-done.4, ...), custom_call_target="tpu_custom_call", output_to_operand_aliasing={{0}: (13, {}), {1}: (14, {}), {2}: (15, {})} | custom-call | flops 7340032 | bytes 57344 | tf_op jit(solution)/shard_map/pallas_call | solution.py:204
  288.2 4.1 %shard_map.152 = (f32[16,256,128]{2,1,0:T(8,128)S(1)}, f32[16,256,128]{2,1,0:T(8,128)S(1)}) custom-call(s32[1]{0:T(128)} %constant.34.clone.1.refs_0_, f32[12,16]{1,0:T(8,128)S(1)} %stack.124.refs_1_, f32[16,256,128]{2,1,0:T(8,128)S(1)} %copy-done.14, f32[16,256,128]{2,1,0:T(8,128)S(1)} %copy-done.24, bf16[8,256,128]{2,1,0:T(8,128)(2,1)S(1)} %copy-done.41, ...), custom_call_target="tpu_custom_call" | custom-call | flops 49152 | bytes 49152 | tf_op jit(solution)/shard_map/pallas_call | solution.py:479
  294.1 2.6 collective-permute-start.45
  296.9 6.1 %shard_map.153 = (bf16[256,4096]{1,0:T(8,128)(2,1)}, f32[256,256]{1,0:T(8,128)S(1)}, f32[4,256,8]{2,1,0:T(8,128)S(1)}, f32[4,256,8]{2,1,0:T(8,128)S(1)}) custom-call(s32[1]{0:T(128)} %bitcast.9.at_ref, bf16[256,4096]{1,0:T(8,128)(2,1)S(1)} %copy-done.4, f32[256,4096]{1,0:T(8,128)S(1)} %copy-done.10, bf16[256,256]{1,0:T(8,128)(2,1)S(1)} %copy-done.27, ...), custom_call_target="tpu_custom_call" | custom-call | flops 4194304 | bytes 32768 | tf_op jit(solution)/shard_map/pallas_call | solution.py:302
  303.0 6.1 %shard_map.154 = (bf16[256,4096]{1,0:T(8,128)(2,1)}, f32[256,256]{1,0:T(8,128)S(1)}, f32[4,256,8]{2,1,0:T(8,128)S(1)}, f32[4,256,8]{2,1,0:T(8,128)S(1)}) custom-call(s32[1]{0:T(128)} %bitcast.at_ref, bf16[256,4096]{1,0:T(8,128)(2,1)S(1)} %copy-done.4, f32[256,4096]{1,0:T(8,128)S(1)} %copy-done.10, ...), custom_call_target="tpu_custom_call", output_to_operand_aliasing={{0}: (11, {}), {2}: (12, {}), {3}: (13, {})} | custom-call | flops 4194304 | bytes 32768 | tf_op jit(solution)/shard_map/pallas_call | solution.py:302
  310.7 3.5 %collective-permute-start.42 = (bf16[256,256]{1,0:T(8,128)(2,1)S(1)}, bf16[256,256]{1,0:T(8,128)(2,1)S(1)}, u32[]{:S(2)}, u32[]{:S(2)}) collective-permute-start(bf16[256,256]{1,0:T(8,128)(2,1)S(1)} %convert_element_type.30), channel_id=1, source_target_pairs={{0,2},{1,3},{2,0},{3,1},{4,6},{5,7},{6,4},{7,5},{8,10},{9,11},{10,... | collective-permute-start | bytes 393224 | tf_op jit(solution)/shard_map/ppermute | solution.py:513
  317.0 7.2 %collective-permute-done.42 = bf16[256,256]{1,0:T(8,128)(2,1)S(1)} collective-permute-done((bf16[256,256]{1,0:T(8,128)(2,1)S(1)}, bf16[256,256]{1,0:T(8,128)(2,1)S(1)}, u32[]{:S(2)}, u32[]{:S(2)}) %collective-permute-start.42) | collective-permute-done | bytes 131104 | tf_op jit(solution)/shard_map/ppermute | solution.py:513
  (367 shorter events, 145.1 us)
Async XLA Ops:
  7.2 57.7 %all-gather.4.cloned.1.call-start = ((), (), s32[]{:S(2)}) async-start(), calls=%async_computation | async-start | bytes 2621440 | tf_op jit(solution)/shard_map/all_gather | solution.py:525
  7.3 57.6 %collective-permute-start = (bf16[4096,1024]{1,0:T(8,128)(2,1)}, bf16[4096,1024]{1,0:T(8,128)(2,1)}, u32[]{:S(2)}, u32[]{:S(2)}) collective-permute-start(bf16[4096,1024]{1,0:T(8,128)(2,1)} %refs_5_.15), channel_id=1, source_target_pairs={{0,4},{4,0},{8,12},{12,8},{16,20},{20,16},{24,28},{28,24},{1,5},{5... | collective-permute-start | bytes 25165832 | tf_op jit(solution)/shard_map/ppermute | solution.py:501
  10.2 104.6 %all-gather.6.cloned.1.call-start = ((), (), s32[]{:S(2)}) async-start(), calls=%async_computation.1 | async-start | bytes 2621440 | tf_op jit(solution)/shard_map/all_gather | solution.py:525
  13.8 14.1 %collective-permute-start.1 = (f32[16,256,128]{2,1,0:T(8,128)}, f32[16,256,128]{2,1,0:T(8,128)}, u32[]{:S(2)}, u32[]{:S(2)}) collective-permute-start(f32[16,256,128]{2,1,0:T(8,128)} %shard_map.120), channel_id=1, source_target_pairs={{0,4},{4,0},{8,12},{12,8},{16,20},{20,16},{24,28},{28,24},{1,5},{5... | collective-permute-start | bytes 6291464 | tf_op jit(solution)/shard_map/ppermute | solution.py:501
  29.2 14.6 %collective-permute-start.3 = (bf16[8,256,128]{2,1,0:T(8,128)(2,1)S(1)}, bf16[8,256,128]{2,1,0:T(8,128)(2,1)S(1)}, u32[]{:S(2)}, u32[]{:S(2)}) collective-permute-start(bf16[8,256,128]{2,1,0:T(8,128)(2,1)S(1)} %shard_map.122.refs_2_), channel_id=1, source_target_pairs={{0,16},{4,20},{8,24},{12,28},{16,0},{20,4},{24,8},{28,12},{1,17},{... | collective-permute-start | bytes 1572872 | tf_op jit(solution)/shard_map/ppermute | solution.py:497
  32.7 13.9 %collective-permute-start.2 = (bf16[8,256,128]{2,1,0:T(8,128)(2,1)S(1)}, bf16[8,256,128]{2,1,0:T(8,128)(2,1)S(1)}, u32[]{:S(2)}, u32[]{:S(2)}) collective-permute-start(bf16[8,256,128]{2,1,0:T(8,128)(2,1)S(1)} %shard_map.121.refs_2_), channel_id=1, source_target_pairs={{0,8},{4,12},{8,0},{12,4},{16,24},{20,28},{24,16},{28,20},{1,9},{5... | collective-permute-start | bytes 1572872 | tf_op jit(solution)/shard_map/ppermute | solution.py:497
  48.9 13.3 %collective-permute-start.5 = (bf16[8,256,128]{2,1,0:T(8,128)(2,1)}, bf16[8,256,128]{2,1,0:T(8,128)(2,1)S(1)}, u32[]{:S(2)}, u32[]{:S(2)}) collective-permute-start(bf16[8,256,128]{2,1,0:T(8,128)(2,1)} %shard_map.124), channel_id=1, source_target_pairs={{0,8},{4,12},{8,0},{12,4},{16,24},{20,28},{24,16},{28,20},{1,9},{5... | collective-permute-start | bytes 1572872 | tf_op jit(solution)/shard_map/ppermute | solution.py:497
  51.8 13.0 %collective-permute-start.4 = (bf16[8,256,128]{2,1,0:T(8,128)(2,1)}, bf16[8,256,128]{2,1,0:T(8,128)(2,1)S(1)}, u32[]{:S(2)}, u32[]{:S(2)}) collective-permute-start(bf16[8,256,128]{2,1,0:T(8,128)(2,1)} %shard_map.123), channel_id=1, source_target_pairs={{0,16},{4,20},{8,24},{12,28},{16,0},{20,4},{24,8},{28,12},{1,17},{... | collective-permute-start | bytes 1572872 | tf_op jit(solution)/shard_map/ppermute | solution.py:497
  78.8 22.2 %collective-permute-start.10 = (bf16[64,2048]{1,0:T(8,128)(2,1)S(1)}, bf16[64,2048]{1,0:T(8,128)(2,1)S(1)}, u32[]{:S(2)}, u32[]{:S(2)}) collective-permute-start(bf16[64,2048]{1,0:T(8,128)(2,1)S(1)} %get-tuple-element.224), channel_id=1, source_target_pairs={{0,8},{4,12},{8,0},{12,4},{16,24},{20,28},{24,16},{28,20},{1,9},{5... | collective-permute-start | bytes 786440 | tf_op jit(solution)/shard_map/ppermute | solution.py:497
  80.3 20.7 %collective-permute-start.11 = (bf16[64,2048]{1,0:T(8,128)(2,1)S(1)}, bf16[64,2048]{1,0:T(8,128)(2,1)S(1)}, u32[]{:S(2)}, u32[]{:S(2)}) collective-permute-start(bf16[64,2048]{1,0:T(8,128)(2,1)S(1)} %get-tuple-element.223), channel_id=1, source_target_pairs={{0,16},{4,20},{8,24},{12,28},{16,0},{20,4},{24,8},{28,12},{1,17},{... | collective-permute-start | bytes 786440 | tf_op jit(solution)/shard_map/ppermute | solution.py:497
  80.9 20.1 %collective-permute-start.12 = (bf16[64,2048]{1,0:T(8,128)(2,1)S(1)}, bf16[64,2048]{1,0:T(8,128)(2,1)S(1)}, u32[]{:S(2)}, u32[]{:S(2)}) collective-permute-start(bf16[64,2048]{1,0:T(8,128)(2,1)S(1)} %get-tuple-element.222), channel_id=1, source_target_pairs={{0,24},{4,28},{8,16},{12,20},{16,8},{20,12},{24,0},{28,4},{1,25},{... | collective-permute-start | bytes 786440 | tf_op jit(solution)/shard_map/ppermute | solution.py:497
  92.4 26.2 %collective-permute-start.18 = (bf16[128,2048]{1,0:T(8,128)(2,1)}, bf16[128,2048]{1,0:T(8,128)(2,1)}, u32[]{:S(2)}, u32[]{:S(2)}) collective-permute-start(bf16[128,2048]{1,0:T(8,128)(2,1)} %get-tuple-element.117), channel_id=1, source_target_pairs={{0,16},{4,20},{8,24},{12,28},{16,0},{20,4},{24,8},{28,12},{1,17},{... | collective-permute-start | bytes 1572872 | tf_op jit(solution)/shard_map/ppermute | solution.py:497
  100.1 26.5 %collective-permute-start.9 = (bf16[128,2048]{1,0:T(8,128)(2,1)}, bf16[128,2048]{1,0:T(8,128)(2,1)}, u32[]{:S(2)}, u32[]{:S(2)}) collective-permute-start(bf16[128,2048]{1,0:T(8,128)(2,1)} %get-tuple-element.116), channel_id=1, source_target_pairs={{0,8},{4,12},{8,0},{12,4},{16,24},{20,28},{24,16},{28,20},{1,9},{5... | collective-permute-start | bytes 1572872 | tf_op jit(solution)/shard_map/ppermute | solution.py:497
  107.6 25.2 %collective-permute-start.25 = (bf16[128,2048]{1,0:T(8,128)(2,1)}, bf16[128,2048]{1,0:T(8,128)(2,1)}, u32[]{:S(2)}, u32[]{:S(2)}) collective-permute-start(bf16[128,2048]{1,0:T(8,128)(2,1)} %get-tuple-element.123), channel_id=1, source_target_pairs={{0,16},{4,20},{8,24},{12,28},{16,0},{20,4},{24,8},{28,12},{1,17},{... | collective-permute-start | bytes 1572872 | tf_op jit(solution)/shard_map/ppermute | solution.py:497
  118.6 13.1 %collective-permute-start.16 = (bf16[64,2048]{1,0:T(8,128)(2,1)S(1)}, bf16[64,2048]{1,0:T(8,128)(2,1)S(1)}, u32[]{:S(2)}, u32[]{:S(2)}) collective-permute-start(bf16[64,2048]{1,0:T(8,128)(2,1)S(1)} %get-tuple-element.218), channel_id=1, source_target_pairs={{0,24},{4,28},{8,16},{12,20},{16,8},{20,12},{24,0},{28,4},{1,25},{... | collective-permute-start | bytes 786440 | tf_op jit(solution)/shard_map/ppermute | solution.py:497
  126.6 48.9 %collective-permute-start.13 = (bf16[128,2048]{1,0:T(8,128)(2,1)S(1)}, bf16[128,2048]{1,0:T(8,128)(2,1)S(1)}, u32[]{:S(2)}, u32[]{:S(2)}) collective-permute-start(bf16[128,2048]{1,0:T(8,128)(2,1)S(1)} %copy-done.90), channel_id=1, source_target_pairs={{0,8},{4,12},{8,0},{12,4},{16,24},{20,28},{24,16},{28,20},{1,9},{5... | collective-permute-start | bytes 1572872 | tf_op jit(solution)/shard_map/ppermute | solution.py:497
  131.7 27.5 %collective-permute-start.21 = (bf16[64,2048]{1,0:T(8,128)(2,1)S(1)}, bf16[64,2048]{1,0:T(8,128)(2,1)S(1)}, u32[]{:S(2)}, u32[]{:S(2)}) collective-permute-start(bf16[64,2048]{1,0:T(8,128)(2,1)S(1)} %get-tuple-element.216), channel_id=1, source_target_pairs={{0,8},{4,12},{8,0},{12,4},{16,24},{20,28},{24,16},{28,20},{1,9},{5... | collective-permute-start | bytes 786440 | tf_op jit(solution)/shard_map/ppermute | solution.py:497
  132.9 27.8 %collective-permute-start.22 = (bf16[64,2048]{1,0:T(8,128)(2,1)S(1)}, bf16[64,2048]{1,0:T(8,128)(2,1)S(1)}, u32[]{:S(2)}, u32[]{:S(2)}) collective-permute-start(bf16[64,2048]{1,0:T(8,128)(2,1)S(1)} %get-tuple-element.215), channel_id=1, source_target_pairs={{0,16},{4,20},{8,24},{12,28},{16,0},{20,4},{24,8},{28,12},{1,17},{... | collective-permute-start | bytes 786440 | tf_op jit(solution)/shard_map/ppermute | solution.py:497
  138.0 23.2 %collective-permute-start.23 = (bf16[64,2048]{1,0:T(8,128)(2,1)S(1)}, bf16[64,2048]{1,0:T(8,128)(2,1)S(1)}, u32[]{:S(2)}, u32[]{:S(2)}) collective-permute-start(bf16[64,2048]{1,0:T(8,128)(2,1)S(1)} %get-tuple-element.214), channel_id=1, source_target_pairs={{0,24},{4,28},{8,16},{12,20},{16,8},{20,12},{24,0},{28,4},{1,25},{... | collective-permute-start | bytes 786440 | tf_op jit(solution)/shard_map/ppermute | solution.py:497
  141.9 36.3 %collective-permute-start.26 = (bf16[64,2048]{1,0:T(8,128)(2,1)S(1)}, bf16[64,2048]{1,0:T(8,128)(2,1)S(1)}, u32[]{:S(2)}, u32[]{:S(2)}) collective-permute-start(bf16[64,2048]{1,0:T(8,128)(2,1)S(1)} %get-tuple-element.150), channel_id=1, source_target_pairs={{0,8},{4,12},{8,0},{12,4},{16,24},{20,28},{24,16},{28,20},{1,9},{5... | collective-permute-start | bytes 786440 | tf_op jit(solution)/shard_map/ppermute | solution.py:497
  159.2 26.3 %collective-permute-start.28 = (bf16[128,2048]{1,0:T(8,128)(2,1)}, bf16[128,2048]{1,0:T(8,128)(2,1)}, u32[]{:S(2)}, u32[]{:S(2)}) collective-permute-start(bf16[128,2048]{1,0:T(8,128)(2,1)} %get-tuple-element.140), channel_id=1, source_target_pairs={{0,16},{4,20},{8,24},{12,28},{16,0},{20,4},{24,8},{28,12},{1,17},{... | collective-permute-start | bytes 1572872 | tf_op jit(solution)/shard_map/ppermute | solution.py:497
  160.7 28.8 %collective-permute-start.20 = (bf16[128,2048]{1,0:T(8,128)(2,1)}, bf16[128,2048]{1,0:T(8,128)(2,1)}, u32[]{:S(2)}, u32[]{:S(2)}) collective-permute-start(bf16[128,2048]{1,0:T(8,128)(2,1)} %get-tuple-element.139), channel_id=1, source_target_pairs={{0,8},{4,12},{8,0},{12,4},{16,24},{20,28},{24,16},{28,20},{1,9},{5... | collective-permute-start | bytes 1572872 | tf_op jit(solution)/shard_map/ppermute | solution.py:497
  167.8 42.2 %collective-permute-start.29 = (bf16[128,2048]{1,0:T(8,128)(2,1)}, bf16[128,2048]{1,0:T(8,128)(2,1)}, u32[]{:S(2)}, u32[]{:S(2)}) collective-permute-start(bf16[128,2048]{1,0:T(8,128)(2,1)} %get-tuple-element.146), channel_id=1, source_target_pairs={{0,16},{4,20},{8,24},{12,28},{16,0},{20,4},{24,8},{28,12},{1,17},{... | collective-permute-start | bytes 1572872 | tf_op jit(solution)/shard_map/ppermute | solution.py:497
  175.6 38.4 %collective-permute-start.27 = (bf16[128,2048]{1,0:T(8,128)(2,1)}, bf16[128,2048]{1,0:T(8,128)(2,1)}, u32[]{:S(2)}, u32[]{:S(2)}) collective-permute-start(bf16[128,2048]{1,0:T(8,128)(2,1)} %get-tuple-element.145), channel_id=1, source_target_pairs={{0,8},{4,12},{8,0},{12,4},{16,24},{20,28},{24,16},{28,20},{1,9},{5... | collective-permute-start | bytes 1572872 | tf_op jit(solution)/shard_map/ppermute | solution.py:497
  238.4 16.2 %collective-permute-start.36 = (bf16[8,256,128]{2,1,0:T(8,128)(2,1)S(1)}, bf16[8,256,128]{2,1,0:T(8,128)(2,1)S(1)}, u32[]{:S(2)}, u32[]{:S(2)}) collective-permute-start(bf16[8,256,128]{2,1,0:T(8,128)(2,1)S(1)} %shard_map.147.refs_2_), channel_id=1, source_target_pairs={{0,16},{4,20},{8,24},{12,28},{16,0},{20,4},{24,8},{28,12},{1,17},{... | collective-permute-start | bytes 1572872 | tf_op jit(solution)/shard_map/ppermute | solution.py:497
  239.3 15.3 %collective-permute-start.35 = (bf16[8,256,128]{2,1,0:T(8,128)(2,1)S(1)}, bf16[8,256,128]{2,1,0:T(8,128)(2,1)S(1)}, u32[]{:S(2)}, u32[]{:S(2)}) collective-permute-start(bf16[8,256,128]{2,1,0:T(8,128)(2,1)S(1)} %shard_map.146.refs_2_), channel_id=1, source_target_pairs={{0,8},{4,12},{8,0},{12,4},{16,24},{20,28},{24,16},{28,20},{1,9},{5... | collective-permute-start | bytes 1572872 | tf_op jit(solution)/shard_map/ppermute | solution.py:497
  256.9 31.3 %collective-permute-start.39 = (bf16[8,256,128]{2,1,0:T(8,128)(2,1)}, bf16[8,256,128]{2,1,0:T(8,128)(2,1)}, u32[]{:S(2)}, u32[]{:S(2)}) collective-permute-start(bf16[8,256,128]{2,1,0:T(8,128)(2,1)} %shard_map.150), channel_id=1, source_target_pairs={{0,8},{4,12},{8,0},{12,4},{16,24},{20,28},{24,16},{28,20},{1,9},{5... | collective-permute-start | bytes 1572872 | tf_op jit(solution)/shard_map/ppermute | solution.py:497
  259.0 29.2 %collective-permute-start.38 = (bf16[8,256,128]{2,1,0:T(8,128)(2,1)}, bf16[8,256,128]{2,1,0:T(8,128)(2,1)}, u32[]{:S(2)}, u32[]{:S(2)}) collective-permute-start(bf16[8,256,128]{2,1,0:T(8,128)(2,1)} %shard_map.149), channel_id=1, source_target_pairs={{0,16},{4,20},{8,24},{12,28},{16,0},{20,4},{24,8},{28,12},{1,17},{... | collective-permute-start | bytes 1572872 | tf_op jit(solution)/shard_map/ppermute | solution.py:497
  292.4 21.8 %collective-permute-start.44 = (bf16[256,256]{1,0:T(8,128)(2,1)S(1)}, bf16[256,256]{1,0:T(8,128)(2,1)S(1)}, u32[]{:S(2)}, u32[]{:S(2)}) collective-permute-start(bf16[256,256]{1,0:T(8,128)(2,1)S(1)} %convert_element_type.35), channel_id=1, source_target_pairs={{0,1},{1,0},{2,3},{3,2},{4,5},{5,4},{6,7},{7,6},{8,9},{9,8},{10,11... | collective-permute-start | bytes 393224 | tf_op jit(solution)/shard_map/ppermute | solution.py:513
  294.1 20.3 %collective-permute-start.45 = (bf16[256,256]{1,0:T(8,128)(2,1)S(1)}, bf16[256,256]{1,0:T(8,128)(2,1)S(1)}, u32[]{:S(2)}, u32[]{:S(2)}) collective-permute-start(bf16[256,256]{1,0:T(8,128)(2,1)S(1)} %convert_element_type.35), channel_id=1, source_target_pairs={{0,2},{1,3},{2,0},{3,1},{4,6},{5,7},{6,4},{7,5},{8,10},{9,11},{10,... | collective-permute-start | bytes 393224 | tf_op jit(solution)/shard_map/ppermute | solution.py:513
  296.7 17.7 %collective-permute-start.46 = (bf16[256,256]{1,0:T(8,128)(2,1)S(1)}, bf16[256,256]{1,0:T(8,128)(2,1)S(1)}, u32[]{:S(2)}, u32[]{:S(2)}) collective-permute-start(bf16[256,256]{1,0:T(8,128)(2,1)S(1)} %convert_element_type.35), channel_id=1, source_target_pairs={{0,3},{1,2},{2,1},{3,0},{4,7},{5,6},{6,5},{7,4},{8,11},{9,10},{10,... | collective-permute-start | bytes 393224 | tf_op jit(solution)/shard_map/ppermute | solution.py:513
  310.7 13.5 %collective-permute-start.42 = (bf16[256,256]{1,0:T(8,128)(2,1)S(1)}, bf16[256,256]{1,0:T(8,128)(2,1)S(1)}, u32[]{:S(2)}, u32[]{:S(2)}) collective-permute-start(bf16[256,256]{1,0:T(8,128)(2,1)S(1)} %convert_element_type.30), channel_id=1, source_target_pairs={{0,2},{1,3},{2,0},{3,1},{4,6},{5,7},{6,4},{7,5},{8,10},{9,11},{10,... | collective-permute-start | bytes 393224 | tf_op jit(solution)/shard_map/ppermute | solution.py:513
  (119 other events, 825.4 us)
Sparse Core Ops, SparseCore 0:
  10.3 48.2 all-gather.3
  60.2 44.8 all-gather.5

commit v9 on v5

--- a/solution.py
+++ b/solution.py
@@ -466,6 +466,7 @@
     waiting = [[], []]
 
     def reduce(chunk, rows, after):
+        sends = []
         for lane, (order, _) in enumerate(lanes):
             keep, send, arrived = waiting[lane][chunk]
             for step, bit in enumerate(order):
@@ -479,6 +480,8 @@
                     send = keep[size:].astype(BF16)
                     keep = keep[:size] if size > rows else keep
             waiting[lane][chunk] = (keep, arrived)
+            sends.append(send)
+        return sends
 
     half = fulls[0].shape[0]
     rows = [half, half // 2, half // 2]
@@ -490,15 +493,14 @@
         if chunk == 1:
             full = tie(fulls[1], waiting[0][0][2], *own)
             own = blocks_of(full, rows[1], rows[2], chips, chip)
-            blocks = lax.optimization_barrier((*blocks, *own))[:chips]
+            sends = reduce(0, rows[0], own)
+            blocks = lax.optimization_barrier((*blocks, *own, *sends))[:chips]
         for lane, (order, hops) in enumerate(lanes):
             send, keep = partial_sums(blocks, hops, out_weight, other, lane, core_at)
             waiting[lane].append((keep, send, across(send, order[0], chips)))
         if chunk == 0:
             full = tie(fulls[1], *[lane[0][1] for lane in waiting])
             own = blocks_of(full, 0, rows[1], chips, chip)
-        if chunk == 1:
-            reduce(0, rows[0], own)
     reduce(count - 2, rows[count - 2], None)
     reduce(count - 1, rows[count - 1], None)
     ends = waiting[0] + waiting[1]
@@ -614,8 +616,7 @@
     before = [incoming, cross, steps_g, skip_rows, rise, c_rows]
     grad_y = project(fulls, own, out_weight, other_weight, chips, chip, core, before)
 
-    few = max(1, groups // 4)
-    counts = [few, groups - 2 * few, few]
+    counts = [0, groups - groups // 2, groups // 2]
     held = ()
 
     def fill(step, sent):

time: 317 us -> 304 us (0.959)
  waiting for transfers between devices: 99.3 us -> 89.9 us
  local copies, waits for them, and re-layouts: 39.3 us -> 35.1 us
    ppermute x29, waiting for transfers between devices: 86.2 us -> 76.5 us  [across(): return lax.ppermute(value, 'seq', pairs)]
    unnamed x66 -> x64, local copies, waits for them, and re-layouts: 26.1 us -> 20.6 us
    pallas_call x3 -> x2, Pallas kernels: 21.2 us -> 19.7 us  [inner_part(): pl.pallas_call(lambda *refs: inner_kernel(not held, last, *refs), grid_sp...]
  transfers between devices with their start and end apart: 42 -> 42, of which waited for: 19 -> 20; matrix products, arithmetic and copies ran while one was open for 10% -> 11% of each run, Pallas kernels for 25% -> 23%
where the time goes in v9:
time: 304 us; the launch traced here: 303 us
  waiting for transfers between devices  89.9 us (30%)
  Pallas kernels  79.9 us (26%)
  starting transfers between devices  42.7 us (14%)
  local copies, waits for them, and re-layouts  35.1 us (12%)
  other arithmetic  28.6 us (9%)
  between operations  14.8 us (5%)
  blocking collectives  11.5 us (4%)
    ppermute x29, waiting for transfers between devices, across(): return lax.ppermute(value, 'seq', pairs)  76.5 us
    pallas_call x6, Pallas kernels, partial_sums(): pl.pallas_call(lambda *refs: project_kernel(hops, *refs), grid_spec=pltpu...  35.6 us
    ppermute x29, starting transfers between devices, across(): return lax.ppermute(value, 'seq', pairs)  33.1 us
    unnamed x64, local copies, waits for them, and re-layouts  20.6 us
    pallas_call x2, Pallas kernels, inner_part(): pl.pallas_call(lambda *refs: inner_kernel(not held, last, *refs), grid_sp...  19.7 us
    pallas_call x2, Pallas kernels, outer_part(): pl.pallas_call(outer_kernel, grid_spec=pltpu.PrefetchScalarGridSpec(num_s...  12.3 us
    all_gather x1, blocking collectives, local(): ends = lax.all_gather(running[-1], 'seq')  11.5 us
    ppermute x6, starting transfers between devices, sum_over_heads(): lax.ppermute(value, 'head', [(i, i ^ hop) for i in range(count)])  8.9 us
  transfers between devices with their start and end apart: 42, of which 20 were waited for; matrix products, arithmetic and copies ran while one was open for 11% of the time, Pallas kernels for 23%

profile of v9, /device:TPU:0, one launch (start us, length us, event | category | flops | bytes accessed | tf_op | source)
XLA Modules:
  0.0 302.9 jit_solution(17826662809360457168)
XLA Ops:
  15.6 11.5 %all-gather = f32[8,1,32]{2,1,0:T(1,128)S(1)} all-gather(f32[1,1,32]{2,1,0:T(1,128)S(1)} %bitcast.61), channel_id=1, replica_groups=mesh['seq'=8,'head'=4] {'seq'}, dimensions={0}, use_global_device_ids=true | all-gather | bytes 1152 | tf_op jit(solution)/shard_map/all_gather | solution.py:583
  34.2 11.1 %collective-permute-done.2 = bf16[8,256,128]{2,1,0:T(8,128)(2,1)} collective-permute-done((bf16[8,256,128]{2,1,0:T(8,128)(2,1)}, bf16[8,256,128]{2,1,0:T(8,128)(2,1)}, u32[]{:S(2)}, u32[]{:S(2)}) %collective-permute-start.2) | collective-permute-done | bytes 524320 | tf_op jit(solution)/shard_map/ppermute | solution.py:420
  46.8 2.7 fusion.9
  51.5 7.1 %all-gather.4.cloned.1.call-done = bf16[128,8192]{1,0:T(8,128)(2,1)} async-done(((bf16[128,2048]{1,0:T(8,128)(2,1)}), bf16[128,8192]{1,0:T(8,128)(2,1)}) %all-gather.4.cloned.1.call-update) | async-done | bytes 2097168 | tf_op jit(solution)/shard_map/all_gather | solution.py:448
  58.6 2.9 constant_dynamic-slice_fusion.4
  66.4 2.6 fusion.3
  75.8 2.9 shard_map.121
  78.7 3.3 %copy-done.8 = f32[32,256,256]{2,1,0:T(8,128)} copy-done((f32[32,256,256]{2,1,0:T(8,128)}, f32[32,256,256]{2,1,0:T(8,128)S(1)}, u32[]{:S(2)}) %copy-start.8) | copy-done | bytes 8388632
  82.1 3.3 %copy-done.10 = bf16[32,256,512]{2,1,0:T(8,128)(2,1)} copy-done((bf16[32,256,512]{2,1,0:T(8,128)(2,1)}, bf16[32,256,512]{2,1,0:T(8,128)(2,1)S(1)}, u32[]{:S(2)}) %copy-start.10) | copy-done | bytes 8388632
  85.4 6.4 %maximum_select_fusion.refs_8_.state_ref = f32[32,256,128]{2,1,0:T(8,128)} fusion(f32[16,256,128]{2,1,0:T(8,128)} %collective-permute-done.8, f32[16,256,128]{2,1,0:T(8,128)} %get-tuple-element.132, pred[]{:T(512)S(6)} %eq.4), kind=kLoop, calls=%fused_computation | loop fusion | flops 3145728 | bytes 8388609 | tf_op jit(solution)/shard_map/jit(_where)/select_n | solution.py:610
  91.8 3.5 %collective-permute-done.4.refs_3_ = bf16[128,2048]{1,0:T(8,128)(2,1)} collective-permute-done((bf16[128,2048]{1,0:T(8,128)(2,1)}, bf16[128,2048]{1,0:T(8,128)(2,1)}, u32[]{:S(2)}, u32[]{:S(2)}) %collective-permute-start.4) | collective-permute-done | bytes 524320 | tf_op jit(solution)/shard_map/ppermute | solution.py:420
  95.3 3.4 %copy-done.2 = bf16[4096,1024]{1,0:T(8,128)(2,1)S(1)} copy-done((bf16[4096,1024]{1,0:T(8,128)(2,1)S(1)}, bf16[4096,1024]{1,0:T(8,128)(2,1)}, u32[]{:S(2)}) %copy-start.2) | copy-done | bytes 8388632
  98.7 7.8 %shard_map.122 = (bf16[256,2048]{1,0:T(8,128)(2,1)}, f32[256,2048]{1,0:T(8,128)S(1)}) custom-call(s32[1]{0:T(128)} %bitcast.1.refs_0_, bf16[128,2048]{1,0:T(8,128)(2,1)S(1)} %copy-done.16, bf16[128,2048]{1,0:T(8,128)(2,1)} %collective-permute-done.3.refs_2_, bf16[128,2048]{1,0:T(8,128)(2,1)} %collective-permute-done.4.refs_3_, ...), custom_call_target="tpu_custom_call" | custom-call | flops 16777216 | bytes 45056 | tf_op jit(solution)/shard_map/pallas_call | solution.py:361
  108.8 7.9 %shard_map.123 = (bf16[256,2048]{1,0:T(8,128)(2,1)}, f32[256,2048]{1,0:T(8,128)S(1)}) custom-call(s32[1]{0:T(128)} %bitcast.1.refs_0_, bf16[128,2048]{1,0:T(8,128)(2,1)S(1)} %copy-done.16, bf16[128,2048]{1,0:T(8,128)(2,1)} %collective-permute-done.3.refs_2_, bf16[128,2048]{1,0:T(8,128)(2,1)} %collective-permute-done.4.refs_3_, ...), custom_call_target="tpu_custom_call" | custom-call | flops 16777216 | bytes 45056 | tf_op jit(solution)/shard_map/pallas_call | solution.py:361
  123.8 10.5 %collective-permute-done.10 = bf16[256,2048]{1,0:T(8,128)(2,1)} collective-permute-done((bf16[256,2048]{1,0:T(8,128)(2,1)}, bf16[256,2048]{1,0:T(8,128)(2,1)}, u32[]{:S(2)}, u32[]{:S(2)}) %collective-permute-start.10) | collective-permute-done | bytes 1048608 | tf_op jit(solution)/shard_map/ppermute | solution.py:420
  135.7 14.2 %collective-permute-done.14 = bf16[256,2048]{1,0:T(8,128)(2,1)} collective-permute-done((bf16[256,2048]{1,0:T(8,128)(2,1)}, bf16[256,2048]{1,0:T(8,128)(2,1)}, u32[]{:S(2)}, u32[]{:S(2)}) %collective-permute-start.14) | collective-permute-done | bytes 1048608 | tf_op jit(solution)/shard_map/ppermute | solution.py:420
  154.3 5.0 %shard_map.124 = (bf16[128,2048]{1,0:T(8,128)(2,1)S(1)}, f32[128,2048]{1,0:T(8,128)S(1)}) custom-call(s32[1]{0:T(128)} %bitcast.1.refs_0_, bf16[64,2048]{1,0:T(8,128)(2,1)S(1)} %get-tuple-element.89.refs_1_, bf16[64,2048]{1,0:T(8,128)(2,1)S(1)} %collective-permute-done.11.refs_2_, bf16[64,2048]{1,0:T(8,128)(2,1)S(1)} %collective-permute-done.12.refs_3_, ...), custom_call_target="tpu_custom_call" | custom-call | flops 8388608 | bytes 38912 | tf_op jit(solution)/shard_map/pallas_call | solution.py:361
  163.7 5.0 %shard_map.126 = (bf16[128,2048]{1,0:T(8,128)(2,1)S(1)}, f32[128,2048]{1,0:T(8,128)S(1)}) custom-call(s32[1]{0:T(128)} %bitcast.1.refs_0_, bf16[64,2048]{1,0:T(8,128)(2,1)S(1)} %get-tuple-element.89.refs_1_, bf16[64,2048]{1,0:T(8,128)(2,1)S(1)} %collective-permute-done.11.refs_2_, bf16[64,2048]{1,0:T(8,128)(2,1)S(1)} %collective-permute-done.12.refs_3_, ...), custom_call_target="tpu_custom_call" | custom-call | flops 8388608 | bytes 38912 | tf_op jit(solution)/shard_map/pallas_call | solution.py:361
  170.0 10.1 %collective-permute-done.18.refs_4_ = bf16[64,2048]{1,0:T(8,128)(2,1)S(1)} collective-permute-done((bf16[64,2048]{1,0:T(8,128)(2,1)S(1)}, bf16[64,2048]{1,0:T(8,128)(2,1)S(1)}, u32[]{:S(2)}, u32[]{:S(2)}) %collective-permute-start.18) | collective-permute-done | bytes 262176 | tf_op jit(solution)/shard_map/ppermute | solution.py:420
  182.2 3.3 %collective-permute-done.16.refs_2_ = bf16[64,2048]{1,0:T(8,128)(2,1)S(1)} collective-permute-done((bf16[64,2048]{1,0:T(8,128)(2,1)S(1)}, bf16[64,2048]{1,0:T(8,128)(2,1)S(1)}, u32[]{:S(2)}, u32[]{:S(2)}) %collective-permute-start.16) | collective-permute-done | bytes 262176 | tf_op jit(solution)/shard_map/ppermute | solution.py:420
  185.5 5.0 %shard_map.127 = (bf16[128,2048]{1,0:T(8,128)(2,1)S(1)}, f32[128,2048]{1,0:T(8,128)S(1)}) custom-call(s32[1]{0:T(128)} %bitcast.1.refs_0_, bf16[64,2048]{1,0:T(8,128)(2,1)S(1)} %get-tuple-element.137.refs_1_, bf16[64,2048]{1,0:T(8,128)(2,1)S(1)} %collective-permute-done.16.refs_2_, bf16[64,2048]{1,0:T(8,128)(2,1)S(1)} %collective-permute-done.17.refs_3_, ...), custom_call_target="tpu_custom_call" | custom-call | flops 8388608 | bytes 38912 | tf_op jit(solution)/shard_map/pallas_call | solution.py:361
  191.3 5.0 %shard_map.125 = (bf16[128,2048]{1,0:T(8,128)(2,1)S(1)}, f32[128,2048]{1,0:T(8,128)S(1)}) custom-call(s32[1]{0:T(128)} %bitcast.1.refs_0_, bf16[64,2048]{1,0:T(8,128)(2,1)S(1)} %get-tuple-element.137.refs_1_, bf16[64,2048]{1,0:T(8,128)(2,1)S(1)} %collective-permute-done.16.refs_2_, bf16[64,2048]{1,0:T(8,128)(2,1)S(1)} %collective-permute-done.17.refs_3_, ...), custom_call_target="tpu_custom_call" | custom-call | flops 8388608 | bytes 38912 | tf_op jit(solution)/shard_map/pallas_call | solution.py:361
  198.8 11.8 %collective-permute-done.21 = bf16[128,2048]{1,0:T(8,128)(2,1)S(1)} collective-permute-done((bf16[128,2048]{1,0:T(8,128)(2,1)S(1)}, bf16[128,2048]{1,0:T(8,128)(2,1)S(1)}, u32[]{:S(2)}, u32[]{:S(2)}) %collective-permute-start.21) | collective-permute-done | bytes 524320 | tf_op jit(solution)/shard_map/ppermute | solution.py:420
  217.0 2.8 collective-permute-done.27.refs_11_
  221.1 2.6 shard_map.130
  233.6 3.4 %copy-done.9 = f32[32,256,256]{2,1,0:T(8,128)S(1)} copy-done((f32[32,256,256]{2,1,0:T(8,128)S(1)}, f32[32,256,256]{2,1,0:T(8,128)}, u32[]{:S(2)}) %copy-start.9) | copy-done | bytes 8388632
  237.0 9.6 %shard_map.131 = (f32[256,4096]{1,0:T(8,128)S(1)}, f32[4,256,8]{2,1,0:T(8,128)S(1)}, f32[4,256,8]{2,1,0:T(8,128)S(1)}, f32[256,256]{1,0:T(8,128)S(1)}, f32[256,256]{1,0:T(8,128)S(1)}) custom-call(s32[1]{0:T(128)} %constant.67.clone.1.refs_0_, bf16[256,4096]{1,0:T(8,128)(2,1)S(1)} %copy-done.4, bf16[256,4096]{1,0:T(8,128)(2,1)S(1)} %copy-done.7, ...), custom_call_target="tpu_custom_call" | custom-call | flops 7340032 | bytes 57344 | tf_op jit(solution)/shard_map/pallas_call | solution.py:199
  248.7 10.1 %shard_map.132 = (f32[256,4096]{1,0:T(8,128)S(1)}, f32[4,256,8]{2,1,0:T(8,128)S(1)}, f32[4,256,8]{2,1,0:T(8,128)S(1)}, f32[256,256]{1,0:T(8,128)S(1)}, f32[256,256]{1,0:T(8,128)S(1)}) custom-call(s32[1]{0:T(128)} %constant.54.clone.1.refs_0_, bf16[256,4096]{1,0:T(8,128)(2,1)S(1)} %copy-done.4, ...), custom_call_target="tpu_custom_call", output_to_operand_aliasing={{0}: (12, {}), {1}: (13, {}), {2}: (14, {})} | custom-call | flops 7340032 | bytes 57344 | tf_op jit(solution)/shard_map/pallas_call | solution.py:199
  264.1 2.7 collective-permute-start.38
  268.6 6.1 %shard_map.133 = (bf16[256,4096]{1,0:T(8,128)(2,1)}, f32[256,256]{1,0:T(8,128)S(1)}, f32[4,256,8]{2,1,0:T(8,128)S(1)}, f32[4,256,8]{2,1,0:T(8,128)S(1)}) custom-call(s32[1]{0:T(128)} %bitcast.6.at_ref, bf16[256,4096]{1,0:T(8,128)(2,1)S(1)} %copy-done.4, f32[256,4096]{1,0:T(8,128)S(1)} %get-tuple-element.112.part_ref, bf16[256,256]{1,0:T(8,128)(2,1)S(1)} %copy-done.15, ...), custom_call_target="tpu_custom_call" | custom-call | flops 4194304 | bytes 32768 | tf_op jit(solution)/shard_map/pallas_call | solution.py:297
  274.7 6.1 %shard_map.134 = (bf16[256,4096]{1,0:T(8,128)(2,1)}, f32[256,256]{1,0:T(8,128)S(1)}, f32[4,256,8]{2,1,0:T(8,128)S(1)}, f32[4,256,8]{2,1,0:T(8,128)S(1)}) custom-call(s32[1]{0:T(128)} %bitcast.at_ref, bf16[256,4096]{1,0:T(8,128)(2,1)S(1)} %copy-done.4, ...), custom_call_target="tpu_custom_call", output_to_operand_aliasing={{0}: (11, {}), {2}: (12, {}), {3}: (13, {})} | custom-call | flops 4194304 | bytes 32768 | tf_op jit(solution)/shard_map/pallas_call | solution.py:297
  288.5 4.1 %collective-permute-done.35 = bf16[256,256]{1,0:T(8,128)(2,1)S(1)} collective-permute-done((bf16[256,256]{1,0:T(8,128)(2,1)S(1)}, bf16[256,256]{1,0:T(8,128)(2,1)S(1)}, u32[]{:S(2)}, u32[]{:S(2)}) %collective-permute-start.35) | collective-permute-done | bytes 131104 | tf_op jit(solution)/shard_map/ppermute | solution.py:436
  (200 shorter events, 94.6 us)
Async XLA Ops:
  7.2 51.3 %all-gather.4.cloned.1.call-start = ((), (), s32[]{:S(2)}) async-start(), calls=%async_computation | async-start | bytes 2621440 | tf_op jit(solution)/shard_map/all_gather | solution.py:448
  9.8 109.0 %all-gather.6.cloned.1.call-start = ((), (), s32[]{:S(2)}) async-start(), calls=%async_computation.1 | async-start | bytes 2621440 | tf_op jit(solution)/shard_map/all_gather | solution.py:448
  9.8 85.5 %collective-permute-start.9 = (bf16[4096,1024]{1,0:T(8,128)(2,1)}, bf16[4096,1024]{1,0:T(8,128)(2,1)}, u32[]{:S(2)}, u32[]{:S(2)}) collective-permute-start(bf16[4096,1024]{1,0:T(8,128)(2,1)} %refs_5_.11), channel_id=1, source_target_pairs={{0,4},{4,0},{8,12},{12,8},{16,20},{20,16},{24,28},{28,24},{1,5},{5... | collective-permute-start | bytes 25165832 | tf_op jit(solution)/shard_map/ppermute | solution.py:424
  13.8 13.5 %collective-permute-start = (f32[16,256,128]{2,1,0:T(8,128)}, f32[16,256,128]{2,1,0:T(8,128)}, u32[]{:S(2)}, u32[]{:S(2)}) collective-permute-start(f32[16,256,128]{2,1,0:T(8,128)} %shard_map.120), channel_id=1, source_target_pairs={{0,4},{4,0},{8,12},{12,8},{16,20},{20,16},{24,28},{28,24},{1,5},{5... | collective-permute-start | bytes 6291464 | tf_op jit(solution)/shard_map/ppermute | solution.py:424
  30.5 14.8 %collective-permute-start.2 = (bf16[8,256,128]{2,1,0:T(8,128)(2,1)}, bf16[8,256,128]{2,1,0:T(8,128)(2,1)}, u32[]{:S(2)}, u32[]{:S(2)}) collective-permute-start(bf16[8,256,128]{2,1,0:T(8,128)(2,1)} %get-tuple-element.158), channel_id=1, source_target_pairs={{0,16},{4,20},{8,24},{12,28},{16,0},{20,4},{24,8},{28,12},{1,17},{... | collective-permute-start | bytes 1572872 | tf_op jit(solution)/shard_map/ppermute | solution.py:420
  32.6 14.2 %collective-permute-start.1 = (bf16[8,256,128]{2,1,0:T(8,128)(2,1)}, bf16[8,256,128]{2,1,0:T(8,128)(2,1)}, u32[]{:S(2)}, u32[]{:S(2)}) collective-permute-start(bf16[8,256,128]{2,1,0:T(8,128)(2,1)} %get-tuple-element.159), channel_id=1, source_target_pairs={{0,8},{4,12},{8,0},{12,4},{16,24},{20,28},{24,16},{28,20},{1,9},{5... | collective-permute-start | bytes 1572872 | tf_op jit(solution)/shard_map/ppermute | solution.py:420
  69.0 16.4 %collective-permute-start.8 = (f32[16,256,128]{2,1,0:T(8,128)}, f32[16,256,128]{2,1,0:T(8,128)}, u32[]{:S(2)}, u32[]{:S(2)}) collective-permute-start(f32[16,256,128]{2,1,0:T(8,128)} %get-tuple-element.133), channel_id=1, source_target_pairs={{0,4},{4,0},{8,12},{12,8},{16,20},{20,16},{24,28},{28,24},{1,5},{5... | collective-permute-start | bytes 6291464 | tf_op jit(solution)/shard_map/ppermute | solution.py:424
  69.0 22.8 %collective-permute-start.5 = (bf16[128,2048]{1,0:T(8,128)(2,1)}, bf16[128,2048]{1,0:T(8,128)(2,1)}, u32[]{:S(2)}, u32[]{:S(2)}) collective-permute-start(bf16[128,2048]{1,0:T(8,128)(2,1)} %get-tuple-element.142), channel_id=1, source_target_pairs={{0,24},{4,28},{8,16},{12,20},{16,8},{20,12},{24,0},{28,4},{1,25},{... | collective-permute-start | bytes 1572872 | tf_op jit(solution)/shard_map/ppermute | solution.py:420
  70.2 25.1 %collective-permute-start.4 = (bf16[128,2048]{1,0:T(8,128)(2,1)}, bf16[128,2048]{1,0:T(8,128)(2,1)}, u32[]{:S(2)}, u32[]{:S(2)}) collective-permute-start(bf16[128,2048]{1,0:T(8,128)(2,1)} %get-tuple-element.143), channel_id=1, source_target_pairs={{0,16},{4,20},{8,24},{12,28},{16,0},{20,4},{24,8},{28,12},{1,17},{... | collective-permute-start | bytes 1572872 | tf_op jit(solution)/shard_map/ppermute | solution.py:420
  70.9 24.4 %collective-permute-start.3 = (bf16[128,2048]{1,0:T(8,128)(2,1)}, bf16[128,2048]{1,0:T(8,128)(2,1)}, u32[]{:S(2)}, u32[]{:S(2)}) collective-permute-start(bf16[128,2048]{1,0:T(8,128)(2,1)} %get-tuple-element.144), channel_id=1, source_target_pairs={{0,8},{4,12},{8,0},{12,4},{16,24},{20,28},{24,16},{28,20},{1,9},{5... | collective-permute-start | bytes 1572872 | tf_op jit(solution)/shard_map/ppermute | solution.py:420
  107.9 26.4 %collective-permute-start.10 = (bf16[256,2048]{1,0:T(8,128)(2,1)}, bf16[256,2048]{1,0:T(8,128)(2,1)}, u32[]{:S(2)}, u32[]{:S(2)}) collective-permute-start(bf16[256,2048]{1,0:T(8,128)(2,1)} %get-tuple-element.82), channel_id=1, source_target_pairs={{0,8},{4,12},{8,0},{12,4},{16,24},{20,28},{24,16},{28,20},{1,9},{5... | collective-permute-start | bytes 3145736 | tf_op jit(solution)/shard_map/ppermute | solution.py:420
  118.0 32.0 %collective-permute-start.14 = (bf16[256,2048]{1,0:T(8,128)(2,1)}, bf16[256,2048]{1,0:T(8,128)(2,1)}, u32[]{:S(2)}, u32[]{:S(2)}) collective-permute-start(bf16[256,2048]{1,0:T(8,128)(2,1)} %get-tuple-element.83), channel_id=1, source_target_pairs={{0,16},{4,20},{8,24},{12,28},{16,0},{20,4},{24,8},{28,12},{1,17},{... | collective-permute-start | bytes 3145736 | tf_op jit(solution)/shard_map/ppermute | solution.py:420
  120.3 33.8 %collective-permute-start.13 = (bf16[64,2048]{1,0:T(8,128)(2,1)S(1)}, bf16[64,2048]{1,0:T(8,128)(2,1)S(1)}, u32[]{:S(2)}, u32[]{:S(2)}) collective-permute-start(bf16[64,2048]{1,0:T(8,128)(2,1)S(1)} %get-tuple-element.138), channel_id=1, source_target_pairs={{0,24},{4,28},{8,16},{12,20},{16,8},{20,12},{24,0},{28,4},{1,25},{... | collective-permute-start | bytes 786440 | tf_op jit(solution)/shard_map/ppermute | solution.py:420
  122.1 32.2 %collective-permute-start.12 = (bf16[64,2048]{1,0:T(8,128)(2,1)S(1)}, bf16[64,2048]{1,0:T(8,128)(2,1)S(1)}, u32[]{:S(2)}, u32[]{:S(2)}) collective-permute-start(bf16[64,2048]{1,0:T(8,128)(2,1)S(1)} %get-tuple-element.139), channel_id=1, source_target_pairs={{0,16},{4,20},{8,24},{12,28},{16,0},{20,4},{24,8},{28,12},{1,17},{... | collective-permute-start | bytes 786440 | tf_op jit(solution)/shard_map/ppermute | solution.py:420
  123.2 31.1 %collective-permute-start.11 = (bf16[64,2048]{1,0:T(8,128)(2,1)S(1)}, bf16[64,2048]{1,0:T(8,128)(2,1)S(1)}, u32[]{:S(2)}, u32[]{:S(2)}) collective-permute-start(bf16[64,2048]{1,0:T(8,128)(2,1)S(1)} %get-tuple-element.140), channel_id=1, source_target_pairs={{0,8},{4,12},{8,0},{12,4},{16,24},{20,28},{24,16},{28,20},{1,9},{5... | collective-permute-start | bytes 786440 | tf_op jit(solution)/shard_map/ppermute | solution.py:420
  159.3 37.0 %collective-permute-start.15 = (bf16[128,2048]{1,0:T(8,128)(2,1)S(1)}, bf16[128,2048]{1,0:T(8,128)(2,1)S(1)}, u32[]{:S(2)}, u32[]{:S(2)}) collective-permute-start(bf16[128,2048]{1,0:T(8,128)(2,1)S(1)} %get-tuple-element.94), channel_id=1, source_target_pairs={{0,8},{4,12},{8,0},{12,4},{16,24},{20,28},{24,16},{28,20},{1,9},{5... | collective-permute-start | bytes 1572872 | tf_op jit(solution)/shard_map/ppermute | solution.py:420
  160.3 19.8 %collective-permute-start.18 = (bf16[64,2048]{1,0:T(8,128)(2,1)S(1)}, bf16[64,2048]{1,0:T(8,128)(2,1)S(1)}, u32[]{:S(2)}, u32[]{:S(2)}) collective-permute-start(bf16[64,2048]{1,0:T(8,128)(2,1)S(1)} %get-tuple-element.134), channel_id=1, source_target_pairs={{0,24},{4,28},{8,16},{12,20},{16,8},{20,12},{24,0},{28,4},{1,25},{... | collective-permute-start | bytes 786440 | tf_op jit(solution)/shard_map/ppermute | solution.py:420
  161.6 19.7 %collective-permute-start.17 = (bf16[64,2048]{1,0:T(8,128)(2,1)S(1)}, bf16[64,2048]{1,0:T(8,128)(2,1)S(1)}, u32[]{:S(2)}, u32[]{:S(2)}) collective-permute-start(bf16[64,2048]{1,0:T(8,128)(2,1)S(1)} %get-tuple-element.135), channel_id=1, source_target_pairs={{0,16},{4,20},{8,24},{12,28},{16,0},{20,4},{24,8},{28,12},{1,17},{... | collective-permute-start | bytes 786440 | tf_op jit(solution)/shard_map/ppermute | solution.py:420
  162.8 22.7 %collective-permute-start.16 = (bf16[64,2048]{1,0:T(8,128)(2,1)S(1)}, bf16[64,2048]{1,0:T(8,128)(2,1)S(1)}, u32[]{:S(2)}, u32[]{:S(2)}) collective-permute-start(bf16[64,2048]{1,0:T(8,128)(2,1)S(1)} %get-tuple-element.136), channel_id=1, source_target_pairs={{0,8},{4,12},{8,0},{12,4},{16,24},{20,28},{24,16},{28,20},{1,9},{5... | collective-permute-start | bytes 786440 | tf_op jit(solution)/shard_map/ppermute | solution.py:420
  168.7 29.1 %collective-permute-start.20 = (bf16[128,2048]{1,0:T(8,128)(2,1)S(1)}, bf16[128,2048]{1,0:T(8,128)(2,1)S(1)}, u32[]{:S(2)}, u32[]{:S(2)}) collective-permute-start(bf16[128,2048]{1,0:T(8,128)(2,1)S(1)} %get-tuple-element.98), channel_id=1, source_target_pairs={{0,16},{4,20},{8,24},{12,28},{16,0},{20,4},{24,8},{28,12},{1,17},{... | collective-permute-start | bytes 1572872 | tf_op jit(solution)/shard_map/ppermute | solution.py:420
  180.1 33.0 %collective-permute-start.22 = (bf16[128,2048]{1,0:T(8,128)(2,1)S(1)}, bf16[128,2048]{1,0:T(8,128)(2,1)S(1)}, u32[]{:S(2)}, u32[]{:S(2)}) collective-permute-start(bf16[128,2048]{1,0:T(8,128)(2,1)S(1)} %slice.182), channel_id=1, source_target_pairs={{0,16},{4,20},{8,24},{12,28},{16,0},{20,4},{24,8},{28,12},{1,17},{... | collective-permute-start | bytes 1572872 | tf_op jit(solution)/shard_map/ppermute | solution.py:420
  181.3 33.0 %collective-permute-start.25 = (bf16[128,2048]{1,0:T(8,128)(2,1)S(1)}, bf16[128,2048]{1,0:T(8,128)(2,1)S(1)}, u32[]{:S(2)}, u32[]{:S(2)}) collective-permute-start(bf16[128,2048]{1,0:T(8,128)(2,1)S(1)} %slice.181), channel_id=1, source_target_pairs={{0,8},{4,12},{8,0},{12,4},{16,24},{20,28},{24,16},{28,20},{1,9},{5... | collective-permute-start | bytes 1572872 | tf_op jit(solution)/shard_map/ppermute | solution.py:420
  190.5 20.2 %collective-permute-start.21 = (bf16[128,2048]{1,0:T(8,128)(2,1)S(1)}, bf16[128,2048]{1,0:T(8,128)(2,1)S(1)}, u32[]{:S(2)}, u32[]{:S(2)}) collective-permute-start(bf16[128,2048]{1,0:T(8,128)(2,1)S(1)} %get-tuple-element.100), channel_id=1, source_target_pairs={{0,16},{4,20},{8,24},{12,28},{16,0},{20,4},{24,8},{28,12},{1,17},{... | collective-permute-start | bytes 1572872 | tf_op jit(solution)/shard_map/ppermute | solution.py:420
  196.3 15.6 %collective-permute-start.19 = (bf16[128,2048]{1,0:T(8,128)(2,1)S(1)}, bf16[128,2048]{1,0:T(8,128)(2,1)S(1)}, u32[]{:S(2)}, u32[]{:S(2)}) collective-permute-start(bf16[128,2048]{1,0:T(8,128)(2,1)S(1)} %get-tuple-element.96), channel_id=1, source_target_pairs={{0,8},{4,12},{8,0},{12,4},{16,24},{20,28},{24,16},{28,20},{1,9},{5... | collective-permute-start | bytes 1572872 | tf_op jit(solution)/shard_map/ppermute | solution.py:420
  197.8 18.4 %collective-permute-start.23 = (bf16[64,2048]{1,0:T(8,128)(2,1)S(1)}, bf16[64,2048]{1,0:T(8,128)(2,1)S(1)}, u32[]{:S(2)}, u32[]{:S(2)}) collective-permute-start(bf16[64,2048]{1,0:T(8,128)(2,1)S(1)} %slice.186), channel_id=1, source_target_pairs={{0,16},{4,20},{8,24},{12,28},{16,0},{20,4},{24,8},{28,12},{1,17},{... | collective-permute-start | bytes 786440 | tf_op jit(solution)/shard_map/ppermute | solution.py:420
  230.5 16.1 %collective-permute-start.30 = (bf16[8,256,128]{2,1,0:T(8,128)(2,1)S(1)}, bf16[8,256,128]{2,1,0:T(8,128)(2,1)S(1)}, u32[]{:S(2)}, u32[]{:S(2)}) collective-permute-start(bf16[8,256,128]{2,1,0:T(8,128)(2,1)S(1)} %get-tuple-element.150), channel_id=1, source_target_pairs={{0,16},{4,20},{8,24},{12,28},{16,0},{20,4},{24,8},{28,12},{1,17},{... | collective-permute-start | bytes 1572872 | tf_op jit(solution)/shard_map/ppermute | solution.py:420
  231.9 14.7 %collective-permute-start.29 = (bf16[8,256,128]{2,1,0:T(8,128)(2,1)S(1)}, bf16[8,256,128]{2,1,0:T(8,128)(2,1)S(1)}, u32[]{:S(2)}, u32[]{:S(2)}) collective-permute-start(bf16[8,256,128]{2,1,0:T(8,128)(2,1)S(1)} %get-tuple-element.151), channel_id=1, source_target_pairs={{0,8},{4,12},{8,0},{12,4},{16,24},{20,28},{24,16},{28,20},{1,9},{5... | collective-permute-start | bytes 1572872 | tf_op jit(solution)/shard_map/ppermute | solution.py:420
  247.1 13.5 %collective-permute-start.32 = (bf16[8,256,128]{2,1,0:T(8,128)(2,1)S(1)}, bf16[8,256,128]{2,1,0:T(8,128)(2,1)S(1)}, u32[]{:S(2)}, u32[]{:S(2)}) collective-permute-start(bf16[8,256,128]{2,1,0:T(8,128)(2,1)S(1)} %get-tuple-element.148), channel_id=1, source_target_pairs={{0,8},{4,12},{8,0},{12,4},{16,24},{20,28},{24,16},{28,20},{1,9},{5... | collective-permute-start | bytes 1572872 | tf_op jit(solution)/shard_map/ppermute | solution.py:420
  247.7 13.4 %collective-permute-start.31 = (bf16[8,256,128]{2,1,0:T(8,128)(2,1)S(1)}, bf16[8,256,128]{2,1,0:T(8,128)(2,1)S(1)}, u32[]{:S(2)}, u32[]{:S(2)}) collective-permute-start(bf16[8,256,128]{2,1,0:T(8,128)(2,1)S(1)} %get-tuple-element.149), channel_id=1, source_target_pairs={{0,16},{4,20},{8,24},{12,28},{16,0},{20,4},{24,8},{28,12},{1,17},{... | collective-permute-start | bytes 1572872 | tf_op jit(solution)/shard_map/ppermute | solution.py:420
  264.1 21.8 %collective-permute-start.38 = (bf16[256,256]{1,0:T(8,128)(2,1)S(1)}, bf16[256,256]{1,0:T(8,128)(2,1)S(1)}, u32[]{:S(2)}, u32[]{:S(2)}) collective-permute-start(bf16[256,256]{1,0:T(8,128)(2,1)S(1)} %convert_element_type.141), channel_id=1, source_target_pairs={{0,2},{1,3},{2,0},{3,1},{4,6},{5,7},{6,4},{7,5},{8,10},{9,11},{10,... | collective-permute-start | bytes 393224 | tf_op jit(solution)/shard_map/ppermute | solution.py:436
  266.8 19.4 %collective-permute-start.37 = (bf16[256,256]{1,0:T(8,128)(2,1)S(1)}, bf16[256,256]{1,0:T(8,128)(2,1)S(1)}, u32[]{:S(2)}, u32[]{:S(2)}) collective-permute-start(bf16[256,256]{1,0:T(8,128)(2,1)S(1)} %convert_element_type.141), channel_id=1, source_target_pairs={{0,1},{1,0},{2,3},{3,2},{4,5},{5,4},{6,7},{7,6},{8,9},{9,8},{10,11... | collective-permute-start | bytes 393224 | tf_op jit(solution)/shard_map/ppermute | solution.py:436
  268.3 17.8 %collective-permute-start.39 = (bf16[256,256]{1,0:T(8,128)(2,1)S(1)}, bf16[256,256]{1,0:T(8,128)(2,1)S(1)}, u32[]{:S(2)}, u32[]{:S(2)}) collective-permute-start(bf16[256,256]{1,0:T(8,128)(2,1)S(1)} %convert_element_type.141), channel_id=1, source_target_pairs={{0,3},{1,2},{2,1},{3,0},{4,7},{5,6},{6,5},{7,4},{8,11},{9,10},{10,... | collective-permute-start | bytes 393224 | tf_op jit(solution)/shard_map/ppermute | solution.py:436
  (42 other events, 292.8 us)
Sparse Core Ops, SparseCore 0:
  9.9 48.6 all-gather.3
  60.1 44.6 all-gather.5

commit v10 on v9

--- a/solution.py
+++ b/solution.py
@@ -473,7 +473,7 @@
                 if step:
                     arrived = across(send, bit, chips)
                 elif after:
-                    arrived = tie(arrived, *after)
+                    arrived = tie(arrived, *after, *sends)
                 if step < len(order) - 1:
                     keep = keep + arrived.astype(F32)
                     size = keep.shape[0] // 2
@@ -599,7 +599,7 @@
     def first_blocks(step, sent):
         if step < chips.bit_length() - 2:
             return []
-        own[:] = blocks_of(tie(fulls[0], *sent), 0, span // 2, chips, chip)
+        own[:] = blocks_of(tie(fulls[0], other_weight, *sent), 0, span // 2, chips, chip)
         return own
 
     mine, theirs = span_both(ssm_input, by_group(step_size * tail), b_rows)

time: 304 us -> 302 us (level)
  transfers between devices with their start and end apart: 42 -> 42, of which waited for: 20 -> 19; matrix products, arithmetic and copies ran while one was open for 11% -> 12% of each run, Pallas kernels for 23% -> 24%
where the time goes in v10:
time: 302 us; the launch traced here: 301 us
  waiting for transfers between devices  88.6 us (29%)
  Pallas kernels  79.9 us (26%)
  starting transfers between devices  43.8 us (15%)
  local copies, waits for them, and re-layouts  35 us (12%)
  other arithmetic  28.6 us (9%)
  between operations  14.8 us (5%)
  blocking collectives  10 us (3%)
    ppermute x29, waiting for transfers between devices, across(): return lax.ppermute(value, 'seq', pairs)  74.3 us
    pallas_call x6, Pallas kernels, partial_sums(): pl.pallas_call(lambda *refs: project_kernel(hops, *refs), grid_spec=pltpu...  35.6 us
    ppermute x29, starting transfers between devices, across(): return lax.ppermute(value, 'seq', pairs)  32.8 us
    unnamed x64, local copies, waits for them, and re-layouts  20.5 us
    pallas_call x2, Pallas kernels, inner_part(): pl.pallas_call(lambda *refs: inner_kernel(not held, last, *refs), grid_sp...  19.7 us
    pallas_call x2, Pallas kernels, outer_part(): pl.pallas_call(outer_kernel, grid_spec=pltpu.PrefetchScalarGridSpec(num_s...  12.3 us
    all_gather x1, blocking collectives, local(): ends = lax.all_gather(running[-1], 'seq')  10 us
    all_gather x2, waiting for transfers between devices, gather_halves(): lax.all_gather(p, 'head', axis=1, tiled=True)  9.25 us
  transfers between devices with their start and end apart: 42, of which 19 were waited for; matrix products, arithmetic and copies ran while one was open for 12% of the time, Pallas kernels for 24%

profile of v10, /device:TPU:0, one launch (start us, length us, event | category | flops | bytes accessed | tf_op | source)
XLA Modules:
  0.0 301.0 jit_solution(18334143858557963175)
XLA Ops:
  15.6 10.0 %all-gather = f32[8,1,32]{2,1,0:T(1,128)S(1)} all-gather(f32[1,1,32]{2,1,0:T(1,128)S(1)} %bitcast.61), channel_id=1, replica_groups=mesh['seq'=8,'head'=4] {'seq'}, dimensions={0}, use_global_device_ids=true | all-gather | bytes 1152 | tf_op jit(solution)/shard_map/all_gather | solution.py:583
  32.1 11.4 %collective-permute-done.3 = bf16[8,256,128]{2,1,0:T(8,128)(2,1)} collective-permute-done((bf16[8,256,128]{2,1,0:T(8,128)(2,1)}, bf16[8,256,128]{2,1,0:T(8,128)(2,1)}, u32[]{:S(2)}, u32[]{:S(2)}) %collective-permute-start.3) | collective-permute-done | bytes 524320 | tf_op jit(solution)/shard_map/ppermute | solution.py:420
  44.7 2.7 fusion.9
  49.4 9.3 %all-gather.4.cloned.1.call-done = bf16[128,8192]{1,0:T(8,128)(2,1)} async-done(((bf16[128,2048]{1,0:T(8,128)(2,1)}), bf16[128,8192]{1,0:T(8,128)(2,1)}) %all-gather.4.cloned.1.call-update) | async-done | bytes 2097168 | tf_op jit(solution)/shard_map/all_gather | solution.py:448
  58.7 2.9 constant_dynamic-slice_fusion.4
  63.9 2.6 fusion.3
  74.8 2.9 shard_map.121
  77.7 3.3 %copy-done.8 = f32[32,256,256]{2,1,0:T(8,128)} copy-done((f32[32,256,256]{2,1,0:T(8,128)}, f32[32,256,256]{2,1,0:T(8,128)S(1)}, u32[]{:S(2)}) %copy-start.8) | copy-done | bytes 8388632
  81.0 3.3 %copy-done.10 = bf16[32,256,512]{2,1,0:T(8,128)(2,1)} copy-done((bf16[32,256,512]{2,1,0:T(8,128)(2,1)}, bf16[32,256,512]{2,1,0:T(8,128)(2,1)S(1)}, u32[]{:S(2)}) %copy-start.10) | copy-done | bytes 8388632
  84.3 6.4 %maximum_select_fusion.refs_8_.state_ref = f32[32,256,128]{2,1,0:T(8,128)} fusion(f32[16,256,128]{2,1,0:T(8,128)} %collective-permute-done.9, f32[16,256,128]{2,1,0:T(8,128)} %get-tuple-element.132, pred[]{:T(512)S(6)} %eq.4), kind=kLoop, calls=%fused_computation | loop fusion | flops 3145728 | bytes 8388609 | tf_op jit(solution)/shard_map/jit(_where)/select_n | solution.py:610
  90.7 3.5 %collective-permute-done.5.refs_3_ = bf16[128,2048]{1,0:T(8,128)(2,1)} collective-permute-done((bf16[128,2048]{1,0:T(8,128)(2,1)}, bf16[128,2048]{1,0:T(8,128)(2,1)}, u32[]{:S(2)}, u32[]{:S(2)}) %collective-permute-start.5) | collective-permute-done | bytes 524320 | tf_op jit(solution)/shard_map/ppermute | solution.py:420
  94.3 3.4 %copy-done.2 = bf16[4096,1024]{1,0:T(8,128)(2,1)S(1)} copy-done((bf16[4096,1024]{1,0:T(8,128)(2,1)S(1)}, bf16[4096,1024]{1,0:T(8,128)(2,1)}, u32[]{:S(2)}) %copy-start.2) | copy-done | bytes 8388632
  97.7 7.8 %shard_map.122 = (bf16[256,2048]{1,0:T(8,128)(2,1)}, f32[256,2048]{1,0:T(8,128)S(1)}) custom-call(s32[1]{0:T(128)} %bitcast.1.refs_0_, bf16[128,2048]{1,0:T(8,128)(2,1)S(1)} %copy-done.16, bf16[128,2048]{1,0:T(8,128)(2,1)} %collective-permute-done.4.refs_2_, bf16[128,2048]{1,0:T(8,128)(2,1)} %collective-permute-done.5.refs_3_, ...), custom_call_target="tpu_custom_call" | custom-call | flops 16777216 | bytes 45056 | tf_op jit(solution)/shard_map/pallas_call | solution.py:361
  108.3 7.9 %shard_map.123 = (bf16[256,2048]{1,0:T(8,128)(2,1)}, f32[256,2048]{1,0:T(8,128)S(1)}) custom-call(s32[1]{0:T(128)} %bitcast.1.refs_0_, bf16[128,2048]{1,0:T(8,128)(2,1)S(1)} %copy-done.16, bf16[128,2048]{1,0:T(8,128)(2,1)} %collective-permute-done.4.refs_2_, bf16[128,2048]{1,0:T(8,128)(2,1)} %collective-permute-done.5.refs_3_, ...), custom_call_target="tpu_custom_call" | custom-call | flops 16777216 | bytes 45056 | tf_op jit(solution)/shard_map/pallas_call | solution.py:361
  123.3 9.8 %collective-permute-done.10 = bf16[256,2048]{1,0:T(8,128)(2,1)} collective-permute-done((bf16[256,2048]{1,0:T(8,128)(2,1)}, bf16[256,2048]{1,0:T(8,128)(2,1)}, u32[]{:S(2)}, u32[]{:S(2)}) %collective-permute-start.10) | collective-permute-done | bytes 1048608 | tf_op jit(solution)/shard_map/ppermute | solution.py:420
  136.9 12.6 %collective-permute-done.14 = bf16[256,2048]{1,0:T(8,128)(2,1)} collective-permute-done((bf16[256,2048]{1,0:T(8,128)(2,1)}, bf16[256,2048]{1,0:T(8,128)(2,1)}, u32[]{:S(2)}, u32[]{:S(2)}) %collective-permute-start.14) | collective-permute-done | bytes 1048608 | tf_op jit(solution)/shard_map/ppermute | solution.py:420
  153.7 5.0 %shard_map.124 = (bf16[128,2048]{1,0:T(8,128)(2,1)S(1)}, f32[128,2048]{1,0:T(8,128)S(1)}) custom-call(s32[1]{0:T(128)} %bitcast.1.refs_0_, bf16[64,2048]{1,0:T(8,128)(2,1)S(1)} %get-tuple-element.89.refs_1_, bf16[64,2048]{1,0:T(8,128)(2,1)S(1)} %collective-permute-done.11.refs_2_, bf16[64,2048]{1,0:T(8,128)(2,1)S(1)} %collective-permute-done.12.refs_3_, ...), custom_call_target="tpu_custom_call" | custom-call | flops 8388608 | bytes 38912 | tf_op jit(solution)/shard_map/pallas_call | solution.py:361
  162.8 5.0 %shard_map.126 = (bf16[128,2048]{1,0:T(8,128)(2,1)S(1)}, f32[128,2048]{1,0:T(8,128)S(1)}) custom-call(s32[1]{0:T(128)} %bitcast.1.refs_0_, bf16[64,2048]{1,0:T(8,128)(2,1)S(1)} %get-tuple-element.89.refs_1_, bf16[64,2048]{1,0:T(8,128)(2,1)S(1)} %collective-permute-done.11.refs_2_, bf16[64,2048]{1,0:T(8,128)(2,1)S(1)} %collective-permute-done.12.refs_3_, ...), custom_call_target="tpu_custom_call" | custom-call | flops 8388608 | bytes 38912 | tf_op jit(solution)/shard_map/pallas_call | solution.py:361
  169.3 9.7 %collective-permute-done.18.refs_4_ = bf16[64,2048]{1,0:T(8,128)(2,1)S(1)} collective-permute-done((bf16[64,2048]{1,0:T(8,128)(2,1)S(1)}, bf16[64,2048]{1,0:T(8,128)(2,1)S(1)}, u32[]{:S(2)}, u32[]{:S(2)}) %collective-permute-start.18) | collective-permute-done | bytes 262176 | tf_op jit(solution)/shard_map/ppermute | solution.py:420
  181.3 3.5 %collective-permute-done.16.refs_2_ = bf16[64,2048]{1,0:T(8,128)(2,1)S(1)} collective-permute-done((bf16[64,2048]{1,0:T(8,128)(2,1)S(1)}, bf16[64,2048]{1,0:T(8,128)(2,1)S(1)}, u32[]{:S(2)}, u32[]{:S(2)}) %collective-permute-start.16) | collective-permute-done | bytes 262176 | tf_op jit(solution)/shard_map/ppermute | solution.py:420
  184.9 5.0 %shard_map.127 = (bf16[128,2048]{1,0:T(8,128)(2,1)S(1)}, f32[128,2048]{1,0:T(8,128)S(1)}) custom-call(s32[1]{0:T(128)} %bitcast.1.refs_0_, bf16[64,2048]{1,0:T(8,128)(2,1)S(1)} %get-tuple-element.137.refs_1_, bf16[64,2048]{1,0:T(8,128)(2,1)S(1)} %collective-permute-done.16.refs_2_, bf16[64,2048]{1,0:T(8,128)(2,1)S(1)} %collective-permute-done.17.refs_3_, ...), custom_call_target="tpu_custom_call" | custom-call | flops 8388608 | bytes 38912 | tf_op jit(solution)/shard_map/pallas_call | solution.py:361
  190.2 5.0 %shard_map.125 = (bf16[128,2048]{1,0:T(8,128)(2,1)S(1)}, f32[128,2048]{1,0:T(8,128)S(1)}) custom-call(s32[1]{0:T(128)} %bitcast.1.refs_0_, bf16[64,2048]{1,0:T(8,128)(2,1)S(1)} %get-tuple-element.137.refs_1_, bf16[64,2048]{1,0:T(8,128)(2,1)S(1)} %collective-permute-done.16.refs_2_, bf16[64,2048]{1,0:T(8,128)(2,1)S(1)} %collective-permute-done.17.refs_3_, ...), custom_call_target="tpu_custom_call" | custom-call | flops 8388608 | bytes 38912 | tf_op jit(solution)/shard_map/pallas_call | solution.py:361
  198.0 11.6 %collective-permute-done.21 = bf16[128,2048]{1,0:T(8,128)(2,1)S(1)} collective-permute-done((bf16[128,2048]{1,0:T(8,128)(2,1)S(1)}, bf16[128,2048]{1,0:T(8,128)(2,1)S(1)}, u32[]{:S(2)}, u32[]{:S(2)}) %collective-permute-start.21) | collective-permute-done | bytes 524320 | tf_op jit(solution)/shard_map/ppermute | solution.py:420
  216.6 2.8 collective-permute-done.27.refs_11_
  220.7 2.6 shard_map.130
  232.0 3.4 %copy-done.9 = f32[32,256,256]{2,1,0:T(8,128)S(1)} copy-done((f32[32,256,256]{2,1,0:T(8,128)S(1)}, f32[32,256,256]{2,1,0:T(8,128)}, u32[]{:S(2)}) %copy-start.9) | copy-done | bytes 8388632
  235.4 9.6 %shard_map.131 = (f32[256,4096]{1,0:T(8,128)S(1)}, f32[4,256,8]{2,1,0:T(8,128)S(1)}, f32[4,256,8]{2,1,0:T(8,128)S(1)}, f32[256,256]{1,0:T(8,128)S(1)}, f32[256,256]{1,0:T(8,128)S(1)}) custom-call(s32[1]{0:T(128)} %constant.67.clone.1.refs_0_, bf16[256,4096]{1,0:T(8,128)(2,1)S(1)} %copy-done.4, bf16[256,4096]{1,0:T(8,128)(2,1)S(1)} %copy-done.7, ...), custom_call_target="tpu_custom_call" | custom-call | flops 7340032 | bytes 57344 | tf_op jit(solution)/shard_map/pallas_call | solution.py:199
  248.0 10.1 %shard_map.132 = (f32[256,4096]{1,0:T(8,128)S(1)}, f32[4,256,8]{2,1,0:T(8,128)S(1)}, f32[4,256,8]{2,1,0:T(8,128)S(1)}, f32[256,256]{1,0:T(8,128)S(1)}, f32[256,256]{1,0:T(8,128)S(1)}) custom-call(s32[1]{0:T(128)} %constant.54.clone.1.refs_0_, bf16[256,4096]{1,0:T(8,128)(2,1)S(1)} %copy-done.4, ...), custom_call_target="tpu_custom_call", output_to_operand_aliasing={{0}: (12, {}), {1}: (13, {}), {2}: (14, {})} | custom-call | flops 7340032 | bytes 57344 | tf_op jit(solution)/shard_map/pallas_call | solution.py:199
  268.0 6.1 %shard_map.133 = (bf16[256,4096]{1,0:T(8,128)(2,1)}, f32[256,256]{1,0:T(8,128)S(1)}, f32[4,256,8]{2,1,0:T(8,128)S(1)}, f32[4,256,8]{2,1,0:T(8,128)S(1)}) custom-call(s32[1]{0:T(128)} %bitcast.6.at_ref, bf16[256,4096]{1,0:T(8,128)(2,1)S(1)} %copy-done.4, f32[256,4096]{1,0:T(8,128)S(1)} %get-tuple-element.112.part_ref, bf16[256,256]{1,0:T(8,128)(2,1)S(1)} %copy-done.15, ...), custom_call_target="tpu_custom_call" | custom-call | flops 4194304 | bytes 32768 | tf_op jit(solution)/shard_map/pallas_call | solution.py:297
  274.1 6.1 %shard_map.134 = (bf16[256,4096]{1,0:T(8,128)(2,1)}, f32[256,256]{1,0:T(8,128)S(1)}, f32[4,256,8]{2,1,0:T(8,128)S(1)}, f32[4,256,8]{2,1,0:T(8,128)S(1)}) custom-call(s32[1]{0:T(128)} %bitcast.at_ref, bf16[256,4096]{1,0:T(8,128)(2,1)S(1)} %copy-done.4, ...), custom_call_target="tpu_custom_call", output_to_operand_aliasing={{0}: (11, {}), {2}: (12, {}), {3}: (13, {})} | custom-call | flops 4194304 | bytes 32768 | tf_op jit(solution)/shard_map/pallas_call | solution.py:297
  281.3 2.5 collective-permute-start.34
  287.9 4.5 %collective-permute-done.35 = bf16[256,256]{1,0:T(8,128)(2,1)S(1)} collective-permute-done((bf16[256,256]{1,0:T(8,128)(2,1)S(1)}, bf16[256,256]{1,0:T(8,128)(2,1)S(1)}, u32[]{:S(2)}, u32[]{:S(2)}) %collective-permute-start.35) | collective-permute-done | bytes 131104 | tf_op jit(solution)/shard_map/ppermute | solution.py:436
  (200 shorter events, 94.0 us)
Async XLA Ops:
  7.2 51.5 %all-gather.4.cloned.1.call-start = ((), (), s32[]{:S(2)}) async-start(), calls=%async_computation | async-start | bytes 2621440 | tf_op jit(solution)/shard_map/all_gather | solution.py:448
  7.3 51.4 %collective-permute-start = (bf16[4096,1024]{1,0:T(8,128)(2,1)}, bf16[4096,1024]{1,0:T(8,128)(2,1)}, u32[]{:S(2)}, u32[]{:S(2)}) collective-permute-start(bf16[4096,1024]{1,0:T(8,128)(2,1)} %refs_5_.11), channel_id=1, source_target_pairs={{0,4},{4,0},{8,12},{12,8},{16,20},{20,16},{24,28},{28,24},{1,5},{5... | collective-permute-start | bytes 25165832 | tf_op jit(solution)/shard_map/ppermute | solution.py:424
  10.3 108.0 %all-gather.6.cloned.1.call-start = ((), (), s32[]{:S(2)}) async-start(), calls=%async_computation.1 | async-start | bytes 2621440 | tf_op jit(solution)/shard_map/all_gather | solution.py:448
  29.0 14.4 %collective-permute-start.3 = (bf16[8,256,128]{2,1,0:T(8,128)(2,1)}, bf16[8,256,128]{2,1,0:T(8,128)(2,1)}, u32[]{:S(2)}, u32[]{:S(2)}) collective-permute-start(bf16[8,256,128]{2,1,0:T(8,128)(2,1)} %get-tuple-element.158), channel_id=1, source_target_pairs={{0,16},{4,20},{8,24},{12,28},{16,0},{20,4},{24,8},{28,12},{1,17},{... | collective-permute-start | bytes 1572872 | tf_op jit(solution)/shard_map/ppermute | solution.py:420
  30.5 14.2 %collective-permute-start.2 = (bf16[8,256,128]{2,1,0:T(8,128)(2,1)}, bf16[8,256,128]{2,1,0:T(8,128)(2,1)}, u32[]{:S(2)}, u32[]{:S(2)}) collective-permute-start(bf16[8,256,128]{2,1,0:T(8,128)(2,1)} %get-tuple-element.159), channel_id=1, source_target_pairs={{0,8},{4,12},{8,0},{12,4},{16,24},{20,28},{24,16},{28,20},{1,9},{5... | collective-permute-start | bytes 1572872 | tf_op jit(solution)/shard_map/ppermute | solution.py:420
  47.3 14.2 %collective-permute-start.8 = (bf16[8,256,128]{2,1,0:T(8,128)(2,1)}, bf16[8,256,128]{2,1,0:T(8,128)(2,1)}, u32[]{:S(2)}, u32[]{:S(2)}) collective-permute-start(bf16[8,256,128]{2,1,0:T(8,128)(2,1)} %get-tuple-element.156), channel_id=1, source_target_pairs={{0,8},{4,12},{8,0},{12,4},{16,24},{20,28},{24,16},{28,20},{1,9},{5... | collective-permute-start | bytes 1572872 | tf_op jit(solution)/shard_map/ppermute | solution.py:420
  66.5 17.8 %collective-permute-start.9 = (f32[16,256,128]{2,1,0:T(8,128)}, f32[16,256,128]{2,1,0:T(8,128)}, u32[]{:S(2)}, u32[]{:S(2)}) collective-permute-start(f32[16,256,128]{2,1,0:T(8,128)} %get-tuple-element.133), channel_id=1, source_target_pairs={{0,4},{4,0},{8,12},{12,8},{16,20},{20,16},{24,28},{28,24},{1,5},{5... | collective-permute-start | bytes 6291464 | tf_op jit(solution)/shard_map/ppermute | solution.py:424
  67.9 22.8 %collective-permute-start.6 = (bf16[128,2048]{1,0:T(8,128)(2,1)}, bf16[128,2048]{1,0:T(8,128)(2,1)}, u32[]{:S(2)}, u32[]{:S(2)}) collective-permute-start(bf16[128,2048]{1,0:T(8,128)(2,1)} %get-tuple-element.142), channel_id=1, source_target_pairs={{0,24},{4,28},{8,16},{12,20},{16,8},{20,12},{24,0},{28,4},{1,25},{... | collective-permute-start | bytes 1572872 | tf_op jit(solution)/shard_map/ppermute | solution.py:420
  70.3 23.9 %collective-permute-start.5 = (bf16[128,2048]{1,0:T(8,128)(2,1)}, bf16[128,2048]{1,0:T(8,128)(2,1)}, u32[]{:S(2)}, u32[]{:S(2)}) collective-permute-start(bf16[128,2048]{1,0:T(8,128)(2,1)} %get-tuple-element.143), channel_id=1, source_target_pairs={{0,16},{4,20},{8,24},{12,28},{16,0},{20,4},{24,8},{28,12},{1,17},{... | collective-permute-start | bytes 1572872 | tf_op jit(solution)/shard_map/ppermute | solution.py:420
  70.8 23.4 %collective-permute-start.4 = (bf16[128,2048]{1,0:T(8,128)(2,1)}, bf16[128,2048]{1,0:T(8,128)(2,1)}, u32[]{:S(2)}, u32[]{:S(2)}) collective-permute-start(bf16[128,2048]{1,0:T(8,128)(2,1)} %get-tuple-element.144), channel_id=1, source_target_pairs={{0,8},{4,12},{8,0},{12,4},{16,24},{20,28},{24,16},{28,20},{1,9},{5... | collective-permute-start | bytes 1572872 | tf_op jit(solution)/shard_map/ppermute | solution.py:420
  106.8 26.3 %collective-permute-start.10 = (bf16[256,2048]{1,0:T(8,128)(2,1)}, bf16[256,2048]{1,0:T(8,128)(2,1)}, u32[]{:S(2)}, u32[]{:S(2)}) collective-permute-start(bf16[256,2048]{1,0:T(8,128)(2,1)} %get-tuple-element.82), channel_id=1, source_target_pairs={{0,8},{4,12},{8,0},{12,4},{16,24},{20,28},{24,16},{28,20},{1,9},{5... | collective-permute-start | bytes 3145736 | tf_op jit(solution)/shard_map/ppermute | solution.py:420
  117.5 32.0 %collective-permute-start.14 = (bf16[256,2048]{1,0:T(8,128)(2,1)}, bf16[256,2048]{1,0:T(8,128)(2,1)}, u32[]{:S(2)}, u32[]{:S(2)}) collective-permute-start(bf16[256,2048]{1,0:T(8,128)(2,1)} %get-tuple-element.83), channel_id=1, source_target_pairs={{0,16},{4,20},{8,24},{12,28},{16,0},{20,4},{24,8},{28,12},{1,17},{... | collective-permute-start | bytes 3145736 | tf_op jit(solution)/shard_map/ppermute | solution.py:420
  119.8 31.3 %collective-permute-start.13 = (bf16[64,2048]{1,0:T(8,128)(2,1)S(1)}, bf16[64,2048]{1,0:T(8,128)(2,1)S(1)}, u32[]{:S(2)}, u32[]{:S(2)}) collective-permute-start(bf16[64,2048]{1,0:T(8,128)(2,1)S(1)} %get-tuple-element.138), channel_id=1, source_target_pairs={{0,24},{4,28},{8,16},{12,20},{16,8},{20,12},{24,0},{28,4},{1,25},{... | collective-permute-start | bytes 786440 | tf_op jit(solution)/shard_map/ppermute | solution.py:420
  121.0 32.7 %collective-permute-start.12 = (bf16[64,2048]{1,0:T(8,128)(2,1)S(1)}, bf16[64,2048]{1,0:T(8,128)(2,1)S(1)}, u32[]{:S(2)}, u32[]{:S(2)}) collective-permute-start(bf16[64,2048]{1,0:T(8,128)(2,1)S(1)} %get-tuple-element.139), channel_id=1, source_target_pairs={{0,16},{4,20},{8,24},{12,28},{16,0},{20,4},{24,8},{28,12},{1,17},{... | collective-permute-start | bytes 786440 | tf_op jit(solution)/shard_map/ppermute | solution.py:420
  122.4 31.2 %collective-permute-start.11 = (bf16[64,2048]{1,0:T(8,128)(2,1)S(1)}, bf16[64,2048]{1,0:T(8,128)(2,1)S(1)}, u32[]{:S(2)}, u32[]{:S(2)}) collective-permute-start(bf16[64,2048]{1,0:T(8,128)(2,1)S(1)} %get-tuple-element.140), channel_id=1, source_target_pairs={{0,8},{4,12},{8,0},{12,4},{16,24},{20,28},{24,16},{28,20},{1,9},{5... | collective-permute-start | bytes 786440 | tf_op jit(solution)/shard_map/ppermute | solution.py:420
  158.7 36.5 %collective-permute-start.15 = (bf16[128,2048]{1,0:T(8,128)(2,1)S(1)}, bf16[128,2048]{1,0:T(8,128)(2,1)S(1)}, u32[]{:S(2)}, u32[]{:S(2)}) collective-permute-start(bf16[128,2048]{1,0:T(8,128)(2,1)S(1)} %get-tuple-element.94), channel_id=1, source_target_pairs={{0,8},{4,12},{8,0},{12,4},{16,24},{20,28},{24,16},{28,20},{1,9},{5... | collective-permute-start | bytes 1572872 | tf_op jit(solution)/shard_map/ppermute | solution.py:420
  159.3 19.6 %collective-permute-start.18 = (bf16[64,2048]{1,0:T(8,128)(2,1)S(1)}, bf16[64,2048]{1,0:T(8,128)(2,1)S(1)}, u32[]{:S(2)}, u32[]{:S(2)}) collective-permute-start(bf16[64,2048]{1,0:T(8,128)(2,1)S(1)} %get-tuple-element.134), channel_id=1, source_target_pairs={{0,24},{4,28},{8,16},{12,20},{16,8},{20,12},{24,0},{28,4},{1,25},{... | collective-permute-start | bytes 786440 | tf_op jit(solution)/shard_map/ppermute | solution.py:420
  160.5 20.2 %collective-permute-start.17 = (bf16[64,2048]{1,0:T(8,128)(2,1)S(1)}, bf16[64,2048]{1,0:T(8,128)(2,1)S(1)}, u32[]{:S(2)}, u32[]{:S(2)}) collective-permute-start(bf16[64,2048]{1,0:T(8,128)(2,1)S(1)} %get-tuple-element.135), channel_id=1, source_target_pairs={{0,16},{4,20},{8,24},{12,28},{16,0},{20,4},{24,8},{28,12},{1,17},{... | collective-permute-start | bytes 786440 | tf_op jit(solution)/shard_map/ppermute | solution.py:420
  162.2 22.7 %collective-permute-start.16 = (bf16[64,2048]{1,0:T(8,128)(2,1)S(1)}, bf16[64,2048]{1,0:T(8,128)(2,1)S(1)}, u32[]{:S(2)}, u32[]{:S(2)}) collective-permute-start(bf16[64,2048]{1,0:T(8,128)(2,1)S(1)} %get-tuple-element.136), channel_id=1, source_target_pairs={{0,8},{4,12},{8,0},{12,4},{16,24},{20,28},{24,16},{28,20},{1,9},{5... | collective-permute-start | bytes 786440 | tf_op jit(solution)/shard_map/ppermute | solution.py:420
  167.8 29.3 %collective-permute-start.20 = (bf16[128,2048]{1,0:T(8,128)(2,1)S(1)}, bf16[128,2048]{1,0:T(8,128)(2,1)S(1)}, u32[]{:S(2)}, u32[]{:S(2)}) collective-permute-start(bf16[128,2048]{1,0:T(8,128)(2,1)S(1)} %get-tuple-element.98), channel_id=1, source_target_pairs={{0,16},{4,20},{8,24},{12,28},{16,0},{20,4},{24,8},{28,12},{1,17},{... | collective-permute-start | bytes 1572872 | tf_op jit(solution)/shard_map/ppermute | solution.py:420
  179.0 33.0 %collective-permute-start.22 = (bf16[128,2048]{1,0:T(8,128)(2,1)S(1)}, bf16[128,2048]{1,0:T(8,128)(2,1)S(1)}, u32[]{:S(2)}, u32[]{:S(2)}) collective-permute-start(bf16[128,2048]{1,0:T(8,128)(2,1)S(1)} %slice.182), channel_id=1, source_target_pairs={{0,16},{4,20},{8,24},{12,28},{16,0},{20,4},{24,8},{28,12},{1,17},{... | collective-permute-start | bytes 1572872 | tf_op jit(solution)/shard_map/ppermute | solution.py:420
  180.7 32.8 %collective-permute-start.25 = (bf16[128,2048]{1,0:T(8,128)(2,1)S(1)}, bf16[128,2048]{1,0:T(8,128)(2,1)S(1)}, u32[]{:S(2)}, u32[]{:S(2)}) collective-permute-start(bf16[128,2048]{1,0:T(8,128)(2,1)S(1)} %slice.181), channel_id=1, source_target_pairs={{0,8},{4,12},{8,0},{12,4},{16,24},{20,28},{24,16},{28,20},{1,9},{5... | collective-permute-start | bytes 1572872 | tf_op jit(solution)/shard_map/ppermute | solution.py:420
  189.8 19.7 %collective-permute-start.21 = (bf16[128,2048]{1,0:T(8,128)(2,1)S(1)}, bf16[128,2048]{1,0:T(8,128)(2,1)S(1)}, u32[]{:S(2)}, u32[]{:S(2)}) collective-permute-start(bf16[128,2048]{1,0:T(8,128)(2,1)S(1)} %get-tuple-element.100), channel_id=1, source_target_pairs={{0,16},{4,20},{8,24},{12,28},{16,0},{20,4},{24,8},{28,12},{1,17},{... | collective-permute-start | bytes 1572872 | tf_op jit(solution)/shard_map/ppermute | solution.py:420
  195.2 16.1 %collective-permute-start.19 = (bf16[128,2048]{1,0:T(8,128)(2,1)S(1)}, bf16[128,2048]{1,0:T(8,128)(2,1)S(1)}, u32[]{:S(2)}, u32[]{:S(2)}) collective-permute-start(bf16[128,2048]{1,0:T(8,128)(2,1)S(1)} %get-tuple-element.96), channel_id=1, source_target_pairs={{0,8},{4,12},{8,0},{12,4},{16,24},{20,28},{24,16},{28,20},{1,9},{5... | collective-permute-start | bytes 1572872 | tf_op jit(solution)/shard_map/ppermute | solution.py:420
  197.1 18.0 %collective-permute-start.23 = (bf16[64,2048]{1,0:T(8,128)(2,1)S(1)}, bf16[64,2048]{1,0:T(8,128)(2,1)S(1)}, u32[]{:S(2)}, u32[]{:S(2)}) collective-permute-start(bf16[64,2048]{1,0:T(8,128)(2,1)S(1)} %slice.186), channel_id=1, source_target_pairs={{0,16},{4,20},{8,24},{12,28},{16,0},{20,4},{24,8},{28,12},{1,17},{... | collective-permute-start | bytes 786440 | tf_op jit(solution)/shard_map/ppermute | solution.py:420
  230.1 14.9 %collective-permute-start.30 = (bf16[8,256,128]{2,1,0:T(8,128)(2,1)S(1)}, bf16[8,256,128]{2,1,0:T(8,128)(2,1)S(1)}, u32[]{:S(2)}, u32[]{:S(2)}) collective-permute-start(bf16[8,256,128]{2,1,0:T(8,128)(2,1)S(1)} %get-tuple-element.150), channel_id=1, source_target_pairs={{0,16},{4,20},{8,24},{12,28},{16,0},{20,4},{24,8},{28,12},{1,17},{... | collective-permute-start | bytes 1572872 | tf_op jit(solution)/shard_map/ppermute | solution.py:420
  231.5 13.7 %collective-permute-start.29 = (bf16[8,256,128]{2,1,0:T(8,128)(2,1)S(1)}, bf16[8,256,128]{2,1,0:T(8,128)(2,1)S(1)}, u32[]{:S(2)}, u32[]{:S(2)}) collective-permute-start(bf16[8,256,128]{2,1,0:T(8,128)(2,1)S(1)} %get-tuple-element.151), channel_id=1, source_target_pairs={{0,8},{4,12},{8,0},{12,4},{16,24},{20,28},{24,16},{28,20},{1,9},{5... | collective-permute-start | bytes 1572872 | tf_op jit(solution)/shard_map/ppermute | solution.py:420
  245.7 13.6 %collective-permute-start.32 = (bf16[8,256,128]{2,1,0:T(8,128)(2,1)S(1)}, bf16[8,256,128]{2,1,0:T(8,128)(2,1)S(1)}, u32[]{:S(2)}, u32[]{:S(2)}) collective-permute-start(bf16[8,256,128]{2,1,0:T(8,128)(2,1)S(1)} %get-tuple-element.148), channel_id=1, source_target_pairs={{0,8},{4,12},{8,0},{12,4},{16,24},{20,28},{24,16},{28,20},{1,9},{5... | collective-permute-start | bytes 1572872 | tf_op jit(solution)/shard_map/ppermute | solution.py:420
  247.3 13.1 %collective-permute-start.31 = (bf16[8,256,128]{2,1,0:T(8,128)(2,1)S(1)}, bf16[8,256,128]{2,1,0:T(8,128)(2,1)S(1)}, u32[]{:S(2)}, u32[]{:S(2)}) collective-permute-start(bf16[8,256,128]{2,1,0:T(8,128)(2,1)S(1)} %get-tuple-element.149), channel_id=1, source_target_pairs={{0,16},{4,20},{8,24},{12,28},{16,0},{20,4},{24,8},{28,12},{1,17},{... | collective-permute-start | bytes 1572872 | tf_op jit(solution)/shard_map/ppermute | solution.py:420
  263.5 20.3 %collective-permute-start.38 = (bf16[256,256]{1,0:T(8,128)(2,1)S(1)}, bf16[256,256]{1,0:T(8,128)(2,1)S(1)}, u32[]{:S(2)}, u32[]{:S(2)}) collective-permute-start(bf16[256,256]{1,0:T(8,128)(2,1)S(1)} %convert_element_type.141), channel_id=1, source_target_pairs={{0,2},{1,3},{2,0},{3,1},{4,6},{5,7},{6,4},{7,5},{8,10},{9,11},{10,... | collective-permute-start | bytes 393224 | tf_op jit(solution)/shard_map/ppermute | solution.py:436
  264.6 20.9 %collective-permute-start.37 = (bf16[256,256]{1,0:T(8,128)(2,1)S(1)}, bf16[256,256]{1,0:T(8,128)(2,1)S(1)}, u32[]{:S(2)}, u32[]{:S(2)}) collective-permute-start(bf16[256,256]{1,0:T(8,128)(2,1)S(1)} %convert_element_type.141), channel_id=1, source_target_pairs={{0,1},{1,0},{2,3},{3,2},{4,5},{5,4},{6,7},{7,6},{8,9},{9,8},{10,11... | collective-permute-start | bytes 393224 | tf_op jit(solution)/shard_map/ppermute | solution.py:436
  266.3 19.3 %collective-permute-start.39 = (bf16[256,256]{1,0:T(8,128)(2,1)S(1)}, bf16[256,256]{1,0:T(8,128)(2,1)S(1)}, u32[]{:S(2)}, u32[]{:S(2)}) collective-permute-start(bf16[256,256]{1,0:T(8,128)(2,1)S(1)} %convert_element_type.141), channel_id=1, source_target_pairs={{0,3},{1,2},{2,1},{3,0},{4,7},{5,6},{6,5},{7,4},{8,11},{9,10},{10,... | collective-permute-start | bytes 393224 | tf_op jit(solution)/shard_map/ppermute | solution.py:436
  (42 other events, 304.4 us)
Sparse Core Ops, SparseCore 0:
  10.4 48.1 all-gather.3
  60.2 44.6 all-gather.5
